TPU v7x, 32 devices: a whole 2x2x4 slice. The times are simulated.
32 devices in a mesh: shard: 8 (over y, x, core), tensor: 4 (over z).
Axes of the slice: x: 2, y: 2, z: 4, core: 2. Of those that a mesh axis runs over, the one named last changes fastest.
Arguments:
- hidden_in: bfloat16 [6144, 8192], P('shard'), may hold values from -720 to 720
- policy_weights: bfloat16 [2, 8192, 1024], P(None, 'shard', 'tensor'), may hold values from -6 to 6
- reference_weights: bfloat16 [2, 8192, 1024], P(None, None, 'tensor'), may hold values from -6 to 6
- policy_queries: bfloat16 [6144, 4096], P('shard', 'tensor'), may hold values from -180 to 180
- reference_queries: bfloat16 [6144, 4096], P('shard', 'tensor'), may hold values from -180 to 180
- readout: bfloat16 [6144, 4096], P('shard', 'tensor'), may hold values from -90 to 90
- lengths: int32 [16], P('shard'), may hold values from 96 to 384, as said below
Outputs:
- new_policy: bfloat16 [2, 8192, 1024], P(None, 'shard', 'tensor')
- new_reference: bfloat16 [2, 8192, 1024], P(None, None, 'tensor')
- margins: float32 [8], P('shard')
Inputs may be any that keep to these rules, and one draw needn't show every extreme that they name: The first lengths[s] positions of sequence s are real, the rest padding; some sequence has all 384 real.
All inputs are finite; a program needn't handle non-finite values.
Results may differ from a plain program's by a relative error of at most 0.0087.
Values may be sent and summed in bfloat16 or wider, within the bound.
No kernel may reach another device: no remote copies, remote signals or barrier semaphores. Data moves between devices by JAX's collectives and lax.ppermute only.
A program may use at most 128 MiB of HBM per device.

v0:
```python
import functools
import math

import jax
import jax.numpy as jnp
import numpy as np
from jax import lax
from jax.experimental import pallas as pl
from jax.experimental.pallas import tpu as pltpu
from jax.sharding import PartitionSpec as P

D = 8192
HD = 128
KVH = 8
QH = 32
LEN = 384
TILE = 128

rope_base = 1000000.0
dpo_beta = 0.1
learning_rate = 0.2
mix_alpha = 0.6
norm_eps = 1e-06
width_scale = D ** (-0.5)
logit_scale = 1.0 / math.sqrt(HD)
MIB = 1024 * 1024

NT = (((1,), (1,)), ((), ()))
NN = (((1,), (0,)), ((), ()))
TN = (((0,), (0,)), ((), ()))


def dot(a, b, dims):
    return lax.dot_general(a, b, dims, preferred_element_type=jnp.float32)


def params(mib):
    return pltpu.CompilerParams(vmem_limit_bytes=mib * MIB)


COST = pl.CostEstimate(flops=1, bytes_accessed=1, transcendentals=0)
LONG = pl.CostEstimate(flops=1, bytes_accessed=40 * 1000 * 1000, transcendentals=0)
VMEM = pl.BlockSpec(memory_space=pltpu.VMEM)
SMEM = pl.BlockSpec(memory_space=pltpu.SMEM)
HBM = pl.BlockSpec(memory_space=pl.ANY)


def resident(x):
    return pltpu.with_memory_space_constraint(x, pltpu.VMEM)


def in_hbm(x):
    return pltpu.with_memory_space_constraint(x, pltpu.HBM)


def rope_tables():
    frequency = rope_base ** (-2.0 * np.arange(HD // 2) / HD)
    angles = np.arange(LEN)[:, None] * frequency[None, :]
    cosine, sine = np.cos(angles), np.sin(angles)
    return np.stack([np.concatenate([cosine, cosine], axis=1), np.concatenate([-sine, sine], axis=1)]).astype(np.float32)


def store_heads(acc_ref, cos, sin, key_ref, value_ref):
    for s in range(key_ref.shape[0] // LEN):
        rows = slice(s * LEN, (s + 1) * LEN)
        for h in range(key_ref.shape[1] // HD):
            cols = slice(h * HD, (h + 1) * HD)
            k = acc_ref[0, rows, cols] * width_scale
            key_ref[rows, cols] = (k * cos + pltpu.roll(k, HD // 2, 1) * sin).astype(jnp.bfloat16)
    value_ref[...] = (acc_ref[1] * width_scale).astype(jnp.bfloat16)


def norm_project_kernel(idx_ref, hidden_hbm, weight_hbm, table_hbm, normed_ref, key_ref, value_ref, w, acc, part, table, in_sem, w_sem, table_sem):
    tokens = normed_ref.shape[0]
    step, width, span, chunk = 16, 512, 128, 1024
    reads = []
    for i in range(tokens // span):
        at = pl.ds(i * span, span)
        reads.append(pltpu.make_async_copy(hidden_hbm.at[at], normed_ref.at[at], in_sem.at[i]))
    loads = []
    for c in range(D // chunk):
        at = pl.ds(c * chunk, chunk)
        loads.append(pltpu.make_async_copy(weight_hbm.at[:, at, :], w.at[:, at, :], w_sem.at[c]))
    loads.append(pltpu.make_async_copy(table_hbm, table, table_sem))
    for copy in reads + loads:
        copy.start()

    def row_step(i, carry):
        at = pl.ds(pl.multiple_of(i * step, step), step)
        total = jnp.zeros((step, width), jnp.float32)
        for c in range(D // width):
            v = normed_ref[at, c * width : (c + 1) * width].astype(jnp.float32)
            total = total + v * v
        part[at, :] = functools.reduce(jnp.add, [total[:, c * 128 : (c + 1) * 128] for c in range(width // 128)])
        return carry

    for i, copy in enumerate(reads):
        copy.wait()
        lax.fori_loop(i * (span // step), (i + 1) * (span // step), row_step, 0)
    for copy in loads:
        copy.wait()
    mean = jnp.sum(part[...], axis=1, keepdims=True) * (1.0 / D)
    part[...] = jnp.broadcast_to(lax.rsqrt(mean + norm_eps), part.shape)

    def columns(c):
        return pl.ds(pl.multiple_of(c * chunk, chunk), chunk)

    def normalise(c):
        for i in range(tokens // step):
            rows = slice(i * step, (i + 1) * step)
            scale = jnp.concatenate([part[rows, :]] * (chunk // 128), axis=1)
            normed_ref[rows, columns(c)] = (normed_ref[rows, columns(c)].astype(jnp.float32) * scale).astype(jnp.bfloat16)

    def multiply(c, carry):
        for i in (0, 1):
            acc[i] += dot(normed_ref[:, columns(c)], w[i, columns(c), :], NN)

        @pl.when(c + 1 < D // chunk)
        def _():
            normalise(c + 1)

        return carry

    acc[...] = jnp.zeros_like(acc)
    normalise(0)
    lax.fori_loop(0, D // chunk, multiply, 0)
    store_heads(acc, table[0], table[1], key_ref, value_ref)


def norm_project(idx, hidden, weights, tables):
    tokens = hidden.shape[0]
    cols = weights.shape[2]
    return pl.pallas_call(
        norm_project_kernel,
        in_specs=[SMEM, HBM, HBM, HBM],
        out_specs=[VMEM, VMEM, VMEM],
        out_shape=[
            pltpu.VMEM((tokens, D), jnp.bfloat16),
            pltpu.VMEM((tokens, cols), jnp.bfloat16),
            pltpu.VMEM((tokens, cols), jnp.bfloat16),
        ],
        scratch_shapes=[
            pltpu.VMEM((2, D, cols), jnp.bfloat16),
            pltpu.VMEM((2, tokens, cols), jnp.float32),
            pltpu.VMEM((tokens, 128), jnp.float32),
            pltpu.VMEM(tables.shape, jnp.float32),
            pltpu.SemaphoreType.DMA((tokens // 128,)),
            pltpu.SemaphoreType.DMA((D // 1024,)),
            pltpu.SemaphoreType.DMA,
        ],
        compiler_params=params(16),
        cost_estimate=COST,
        name="norm_project",
    )(idx, in_hbm(hidden), in_hbm(weights), in_hbm(tables))


def is_whole(mask):
    return len(bits_of(mask >> 1)) < 2


def read_rows(sources, target, sems):
    if len(sources) == 1:
        return [pltpu.make_async_copy(sources[0], target, sems[0])]
    return [pltpu.make_async_copy(sources[i], target.at[i], sems[i]) for i in (0, 1)]


def project_kernel(masks, first, last, idx_ref, x_ref, *refs):
    refs = list(refs)
    count = len(masks)
    pieces = [[refs.pop(0) for _ in range(1 if is_whole(m) else 2)] for m in masks]
    held = None if first else refs.pop(0)
    if last:
        table_hbm, key_ref, value_ref, w, acc, table, sem, table_sem = refs
        table_copy = pltpu.make_async_copy(table_hbm, table, table_sem)
        table_copy.start()
    else:
        acc, w, sem = refs
    depth = w.shape[2]
    copies = [read_rows(pieces[n], w.at[n], [sem.at[i, n] for i in (0, 1)]) for n in range(count)]
    for group in copies:
        for copy in group:
            copy.start()
    for n in range(count):
        for copy in copies[n]:
            copy.wait()
        col = pl.multiple_of((idx_ref[0] ^ masks[n]) * depth, depth)
        x = x_ref[:, pl.ds(col, depth)]
        for i in (0, 1):
            term = dot(x, w[n, i], NN)
            if n:
                term = acc[i] + term
            elif not first:
                term = held[i] + term
            acc[i] = term
    if last:
        table_copy.wait()
        store_heads(acc, table[0], table[1], key_ref, value_ref)


def project(idx, normed, masks, pieces, held, tables):
    tokens = normed.shape[0]
    rows, cols = pieces[masks[0]][0].shape[-2:]
    first, last = held is None, tables is not None
    count = len(masks)
    args = [idx, resident(normed)] + [w for m in masks for w in pieces[m]]
    in_specs = [SMEM, VMEM] + [HBM] * (len(args) - 2)
    if not first:
        in_specs.append(VMEM)
        args.append(resident(held))
    acc_shape = (2, tokens, cols)
    scratch = [pltpu.VMEM((count, 2, rows, cols), jnp.bfloat16), pltpu.SemaphoreType.DMA((2, count))]
    if last:
        in_specs.append(HBM)
        args.append(in_hbm(tables))
        out_specs = [VMEM] * 2
        out_shape = [pltpu.VMEM((tokens, cols), jnp.bfloat16)] * 2
        scratch.insert(1, pltpu.VMEM(acc_shape, jnp.float32))
        scratch.insert(2, pltpu.VMEM(tables.shape, jnp.float32))
        scratch.append(pltpu.SemaphoreType.DMA)
    else:
        out_specs = VMEM
        out_shape = pltpu.VMEM(acc_shape, jnp.float32)
    return pl.pallas_call(
        functools.partial(project_kernel, tuple(masks), first, last),
        in_specs=in_specs,
        out_specs=out_specs,
        out_shape=out_shape,
        scratch_shapes=scratch,
        compiler_params=params(10),
        cost_estimate=COST,
        name="project",
    )(*args)


HEADS = 2


def stacked(ref, row, col, r, first, count):
    rows = pl.ds(pl.multiple_of(row + r * TILE, TILE), TILE)
    at = lambda g: pl.ds(pl.multiple_of(col + g * HD, HD), HD)
    return jnp.concatenate([ref[rows, at(g)] for g in range(first, first + count)], axis=0)


def live_readout(ref, row, col, r, first, count, length):
    x = stacked(ref, row, col, r, first, count).astype(jnp.float32)
    at = lax.broadcasted_iota(jnp.int32, x.shape, 0) % TILE + r * TILE
    return jnp.where(at < length, x, 0.0).astype(jnp.bfloat16)


def places(step, q_ref, k_ref):
    heads = k_ref.shape[1] // HD
    seq, h = step // heads, step % heads
    return seq, h, seq * LEN, pl.multiple_of(h * HD, HD), h * (q_ref.shape[1] // heads)


def attend_kernel(keep, len_ref, q_ref, k_ref, v_ref, ro_ref, *rest):
    groups = q_ref.shape[1] // k_ref.shape[1]
    count = min(groups, HEADS)
    if keep:
        before_ref, margin_ref, prob_ref, delta_ref = rest
    else:
        (margin_ref,) = rest

    def one(step, margin):
        seq, h, row, col, q_col = places(step, q_ref, k_ref)
        length = len_ref[seq]
        score = jnp.zeros((1, count * TILE), jnp.float32)
        j = lax.broadcasted_iota(jnp.int32, (TILE, count * TILE), 0)
        i = lax.broadcasted_iota(jnp.int32, (TILE, count * TILE), 1) % TILE
        base = 0
        for r in range(LEN // TILE):
            n = (r + 1) * TILE
            keys = (pl.ds(pl.multiple_of(row, TILE), n), pl.ds(col, HD))
            for g in range(0, groups, count):
                q = stacked(q_ref, row, q_col, r, g, count)
                ro = live_readout(ro_ref, row, q_col, r, g, count, length)
                s = dot(k_ref[keys], q, NT)
                dp = dot(v_ref[keys], ro, NT)
                s = [s[b * TILE : (b + 1) * TILE] for b in range(r + 1)]
                s[r] = jnp.where(j <= i, s[r], -1e30)
                top = functools.reduce(jnp.maximum, [jnp.max(x, axis=0, keepdims=True) for x in s])
                e = [jnp.exp2((x - top) * (logit_scale * math.log2(math.e))) for x in s]
                inverse = 1.0 / functools.reduce(jnp.add, [jnp.sum(x, axis=0, keepdims=True) for x in e])
                cols = slice(g * TILE, (g + count) * TILE)
                delta = jnp.zeros((1, count * TILE), jnp.float32)
                for b in range(r + 1):
                    p = (e[b] * inverse).astype(jnp.bfloat16)
                    if keep:
                        prob_ref[seq, h, base + b * TILE : base + (b + 1) * TILE, cols] = p
                    delta = delta + jnp.sum(p.astype(jnp.float32) * dp[b * TILE : (b + 1) * TILE], axis=0, keepdims=True)
                if keep:
                    delta_ref[seq, h, r : r + 1, cols] = delta
                score = score + delta
            base += n
        side = jnp.where(seq % 2 == 0, 1.0, -1.0) * (dpo_beta / math.sqrt(QH * HD))
        return margin + jnp.sum(score, axis=1, keepdims=True) * side

    steps = k_ref.shape[0] // LEN * (k_ref.shape[1] // HD)
    start = -before_ref[0:1, 0:1] if keep else jnp.zeros((1, 1), jnp.float32)
    margin_ref[...] = jnp.broadcast_to(lax.fori_loop(0, steps, one, start), margin_ref.shape)


def attend(lengths, queries, keys, values, readout, before=None):
    seqs = lengths.shape[0]
    heads = keys.shape[1] // HD
    wide = queries.shape[1] // heads
    tiles = LEN // TILE
    span = TILE * tiles * (tiles + 1) // 2
    keep = before is not None
    args = [lengths] + [resident(x) for x in (queries, keys, values, readout)]
    out_shape = [jax.ShapeDtypeStruct((8, 128), jnp.float32)]
    if keep:
        args.append(before)
        out_shape += [pltpu.VMEM((seqs, heads, span, wide), jnp.bfloat16), pltpu.VMEM((seqs, heads, tiles, wide), jnp.float32)]
    return pl.pallas_call(
        functools.partial(attend_kernel, keep),
        in_specs=[SMEM] + [VMEM] * (len(args) - 1),
        out_specs=[VMEM] * len(out_shape),
        out_shape=out_shape,
        compiler_params=params(8),
        cost_estimate=COST,
        name="attend",
    )(*args)


def attend_back_kernel(len_ref, q_ref, v_ref, ro_ref, prob_ref, delta_ref, table_ref, grad_ref):
    tiles = LEN // TILE
    groups = q_ref.shape[1] // v_ref.shape[1]
    count = min(groups, HEADS)

    def one(step, carry):
        seq, h, row, col, q_col = places(step, q_ref, v_ref)
        length = len_ref[seq]
        dk = [None] * tiles
        dv = [None] * tiles
        base = 0
        for r in range(tiles):
            n = (r + 1) * TILE
            keys = (pl.ds(pl.multiple_of(row, TILE), n), pl.ds(col, HD))
            for g in range(0, groups, count):
                q = stacked(q_ref, row, q_col, r, g, count)
                ro = live_readout(ro_ref, row, q_col, r, g, count, length)
                cols = slice(g * TILE, (g + count) * TILE)
                p = prob_ref[seq, h, base : base + n, cols]
                dp = dot(v_ref[keys], ro, NT)
                ds = (p.astype(jnp.float32) * (dp - delta_ref[seq, h, r : r + 1, cols])).astype(jnp.bfloat16)
                tk = dot(ds, q, NN)
                tv = dot(p, ro, NN)
                for b in range(r + 1):
                    at = slice(b * TILE, (b + 1) * TILE)
                    dk[b] = tk[at] if dk[b] is None else dk[b] + tk[at]
                    dv[b] = tv[at] if dv[b] is None else dv[b] + tv[at]
            base += n
        scale = jnp.where(seq % 2 == 0, -1.0, 1.0) * (1.0 / math.sqrt(QH * HD))
        for b in range(tiles):
            at = slice(b * TILE, (b + 1) * TILE)
            to = (pl.ds(col, HD), pl.ds(pl.multiple_of(row + b * TILE, TILE), TILE))
            k = dk[b] * (scale * logit_scale)
            k = k * table_ref[0, at, :] - pltpu.roll(k, HD // 2, 1) * table_ref[1, at, :]
            grad_ref[(0, *to)] = k.T.astype(jnp.bfloat16)
            grad_ref[(1, *to)] = (dv[b] * scale).T.astype(jnp.bfloat16)
        return carry

    lax.fori_loop(0, v_ref.shape[0] // LEN * (v_ref.shape[1] // HD), one, 0)


def attend_back(lengths, queries, values, readout, probs, delta, tables):
    return pl.pallas_call(
        attend_back_kernel,
        in_specs=[SMEM] + [VMEM] * 6,
        out_specs=VMEM,
        out_shape=pltpu.VMEM((2,) + values.shape[::-1], jnp.bfloat16),
        compiler_params=params(8),
        cost_estimate=COST,
        name="attend_back",
    )(lengths, *[resident(x) for x in (queries, values, readout, probs, delta, tables)])


def gradient_tiles(idx, mask, x_ref, cot_ref, rows, store):
    cols = cot_ref.shape[1]
    tile = min(rows, 256)

    def one(t, carry):
        col = pl.multiple_of((idx ^ mask) * rows + t * tile, tile)
        at = pl.ds(pl.multiple_of(t * tile, tile), tile)
        both = jnp.concatenate([cot_ref[0], cot_ref[1]], axis=0)
        out = dot(both, x_ref[:, pl.ds(col, tile)], NN)
        for i in (0, 1):
            store(i, at, out[i * cols : (i + 1) * cols])
        return carry

    lax.fori_loop(0, rows // tile, one, 0)


def gradient_kernel(masks, idx_ref, x_ref, cot_ref, *outs):
    outs = outs[len(outs) - len(masks) :]
    for mask, out_ref in zip(masks, outs):

        def store(i, at, value):
            out_ref[i, :, at] = value.astype(out_ref.dtype)

        gradient_tiles(idx_ref[0], mask, x_ref, cot_ref, out_ref.shape[2], store)


def merged_kernel(masks, idx_ref, x_ref, cot_ref, mine_ref, their_ref, *refs):
    count = len(masks)
    theirs_hbm, outs = refs[:count], refs[count : 3 * count]
    theirs, sem = refs[3 * count :]
    copies = [pltpu.make_async_copy(theirs_hbm[n], theirs.at[n], sem.at[n]) for n in range(count)]
    for copy in copies:
        copy.start()
    mine, their = (jnp.concatenate([jax.nn.sigmoid(-ref[0:1, :])] * 2, axis=1) for ref in (mine_ref, their_ref))
    for n, mask in enumerate(masks):
        copies[n].wait()

        def store(i, at, value):
            value = value * mine + theirs[n, i, :, at].astype(jnp.float32) * their
            outs[2 * n + i][:, at] = value.astype(outs[2 * n + i].dtype)

        gradient_tiles(idx_ref[0], mask, x_ref, cot_ref, theirs.shape[3], store)


def gradient_blocks(idx, normed, cot, masks, rows, merge=None, earlier=()):
    _, cols, tokens = cot.shape
    args = [idx, resident(normed), resident(cot)]
    in_specs = [SMEM, VMEM, VMEM]
    scratch = []
    if merge is None:
        kernel, name = gradient_kernel, "gradient_block"
        out_shape = [jax.ShapeDtypeStruct((2, cols, rows), jnp.bfloat16) for m in masks]
        args += earlier
        in_specs += [HBM] * len(earlier)
    else:
        kernel, name = merged_kernel, "merged_block"
        margins, theirs = merge
        args += [*margins] + [theirs[m] for m in masks]
        in_specs += [VMEM] * 2 + [HBM] * len(masks)
        out_shape = [
            jax.ShapeDtypeStruct((cols, rows), jnp.bfloat16) if m else pltpu.VMEM((cols, rows), jnp.float32)
            for m in masks
            for i in (0, 1)
        ]
        scratch = [pltpu.VMEM((len(masks), 2, cols, rows), jnp.bfloat16), pltpu.SemaphoreType.DMA((len(masks),))]
    outs = pl.pallas_call(
        functools.partial(kernel, tuple(masks)),
        in_specs=in_specs,
        out_specs=[VMEM] * len(out_shape),
        out_shape=out_shape,
        scratch_shapes=scratch,
        compiler_params=params(10),
        cost_estimate=COST,
        name=name,
    )(*args)
    return outs if merge is None else [outs[2 * n : 2 * n + 2] for n in range(len(masks))]


def finish_kernel(counts, *refs):
    refs = list(refs)
    out_ref, square_ref = refs[-2:]
    refs = refs[:-2]
    square_ref[...] = jnp.zeros_like(square_ref)
    cols, rows = refs[0].shape
    for i in (0, 1):
        terms = [refs.pop(0) for _ in range(1 + counts[i])]
        squares = jnp.zeros((1, 128), jnp.float32)
        for c in range(cols // 128):
            for r in range(rows // 128):
                at = (slice(c * 128, (c + 1) * 128), slice(r * 128, (r + 1) * 128))
                value = functools.reduce(jnp.add, [t[at].astype(jnp.float32) for t in terms])
                squares = squares + jnp.sum(value * value, axis=0, keepdims=True)
                out_ref[i, at[1], at[0]] = value.T.astype(jnp.bfloat16)
        square_ref[i : i + 1, :] = jnp.broadcast_to(jnp.sum(squares, axis=1, keepdims=True), (1, 128))


def finish(base, arrived):
    args = [x for i in (0, 1) for x in (resident(base[i]), *arrived[i])]
    cols, rows = base[0].shape
    return pl.pallas_call(
        functools.partial(finish_kernel, [len(a) for a in arrived]),
        in_specs=[VMEM] * len(args),
        out_specs=[VMEM] * 2,
        out_shape=[jax.ShapeDtypeStruct((2, rows, cols), jnp.bfloat16), jax.ShapeDtypeStruct((8, 128), jnp.float32)],
        compiler_params=params(8),
        cost_estimate=COST,
        name="finish",
    )(*args)


def fetch_kernel(masks, idx_ref, *refs):
    refs = list(refs)
    pieces = [[refs.pop(0) for _ in range(1 if is_whole(m) else 2)] for m in masks]
    ref_hbm, _, w, r, sem = refs
    rows = r.shape[2]
    copies = []
    for n, mask in enumerate(masks):
        at = pl.ds(pl.multiple_of((idx_ref[0] ^ mask) * rows, rows), rows)
        copies += read_rows(pieces[n], w.at[n], [sem.at[i, n] for i in (0, 1)])
        copies.append(pltpu.make_async_copy(ref_hbm.at[:, at, :], r.at[n], sem.at[2, n]))
    for copy in copies:
        copy.start()
    for copy in copies:
        copy.wait()


def fetch(idx, weights, reference, masks, earlier):
    rows, cols = weights[masks[0]][0].shape[-2:]
    count = len(masks)
    args = [idx] + [w for m in masks for w in weights[m]] + [in_hbm(reference), earlier]
    return pl.pallas_call(
        functools.partial(fetch_kernel, tuple(masks)),
        in_specs=[SMEM] + [HBM] * (len(args) - 1),
        out_specs=[VMEM] * 2,
        out_shape=[pltpu.VMEM((count, 2, rows, cols), jnp.bfloat16)] * 2,
        scratch_shapes=[pltpu.SemaphoreType.DMA((3, count))],
        compiler_params=params(4),
        cost_estimate=COST,
        name="fetch",
    )(*args)


def blend_kernel(masks, first, ready, idx_ref, square_ref, *refs):
    refs = list(refs)
    count = len(masks)
    grads = [[refs.pop(0) for _ in range(1 if is_whole(m) else 2)] for m in masks]
    if ready is None:
        weights = [[refs.pop(0) for _ in range(1 if is_whole(m) else 2)] for m in masks]
        ref_hbm = refs.pop(0)
    else:
        w, r = refs.pop(0), refs.pop(0)
    if not first:
        refs.pop(0)
    out_hbm, token_ref = refs.pop(0), refs.pop(0)
    new_hbm = refs.pop(0) if first else None
    if ready is None:
        w, r = refs.pop(0), refs.pop(0)
    g, o, new, sem, out_sem = refs
    rows, cols = g.shape[2:]
    step = 64
    half = rows // 2
    token_ref[...] = jnp.zeros_like(token_ref)

    def reads(n):
        slot = n % 2
        at = pl.ds(pl.multiple_of((idx_ref[0] ^ masks[n]) * rows, rows), rows)
        group = read_rows(grads[n], g.at[slot], [sem.at[i, slot] for i in (0, 1)])
        if ready is None:
            group += read_rows(weights[n], w.at[slot], [sem.at[2 + i, slot] for i in (0, 1)])
            group.append(pltpu.make_async_copy(ref_hbm.at[:, at, :], r.at[slot], sem.at[4, slot]))
        for copy in group:
            copy.start()
        return group

    mean = square_ref[...] * (1.0 / (D * KVH * HD))
    scale = jnp.concatenate([learning_rate * lax.rsqrt(mean + norm_eps)] * (cols // 128), axis=1)
    coming = {n: reads(n) for n in range(min(2, count))}
    writes = {}
    for n in range(count):
        slot = n % 2
        held = slot if ready is None else ready + n
        for copy in coming[n] + writes.pop(n - 2, []):
            copy.wait()
        writes[n] = []
        for part in range(2):

            def mix(t, carry):
                j = pl.ds(pl.multiple_of(part * half + t * step, step), step)
                for i in (0, 1):
                    value = w[held, i, j].astype(jnp.float32) - scale[i : i + 1, :] * g[slot, i, j].astype(jnp.float32)
                    value = value.astype(jnp.bfloat16)
                    if first and n == 0:
                        new[i, j] = value
                    mixed = mix_alpha * value.astype(jnp.float32) + (1.0 - mix_alpha) * r[held, i, j].astype(jnp.float32)
                    o[slot, i, j] = mixed.astype(jnp.bfloat16)
                return carry

            lax.fori_loop(0, half // step, mix, 0)
            at = pl.ds(pl.multiple_of((idx_ref[0] ^ masks[n]) * rows + part * half, half), half)
            copy = pltpu.make_async_copy(o.at[slot, :, pl.ds(part * half, half), :], out_hbm.at[:, at, :], out_sem.at[part, slot])
            copy.start()
            writes[n].append(copy)
        if first and n == 0:
            copy = pltpu.make_async_copy(new, new_hbm, out_sem.at[0, 2])
            copy.start()
            writes[n].append(copy)
        if n + 2 < count:
            coming[n + 2] = reads(n + 2)
    for group in writes.values():
        for copy in group:
            copy.wait()


def blend(idx, squares, weights, grads, reference, held, masks, ready=None):
    rows, cols = weights[masks[0]][0].shape[-2:]
    count = len(masks)
    first = held is None
    args = [idx, squares] + [x for m in masks for x in grads[m]]
    in_specs = [SMEM, VMEM] + [HBM] * (len(args) - 2)
    block = pltpu.VMEM((min(count, 2), 2, rows, cols), jnp.bfloat16)
    scratch = [block, block, pltpu.VMEM((2, rows, cols) if first else (8, 128), jnp.bfloat16)]
    scratch += [pltpu.SemaphoreType.DMA((5, 2)), pltpu.SemaphoreType.DMA((2, 3))]
    if ready is None:
        extra = [w for m in masks for w in weights[m]] + [in_hbm(reference)]
        args += extra
        in_specs += [HBM] * len(extra)
        scratch = [block, block] + scratch
    else:
        args += [resident(x) for x in ready[0]]
        in_specs += [VMEM] * 2
    out_specs = [HBM, VMEM]
    out_shape = [jax.ShapeDtypeStruct(reference.shape, jnp.bfloat16), jax.ShapeDtypeStruct((8, 128), jnp.float32)]
    aliases = {}
    if first:
        out_specs.append(HBM)
        out_shape.append(jax.ShapeDtypeStruct((2, rows, cols), jnp.bfloat16))
    else:
        aliases = {len(args): 0}
        in_specs.append(HBM)
        args.append(held)
    return pl.pallas_call(
        functools.partial(blend_kernel, tuple(masks), first, None if ready is None else ready[1]),
        in_specs=in_specs,
        out_specs=out_specs,
        out_shape=out_shape,
        scratch_shapes=scratch,
        input_output_aliases=aliases,
        compiler_params=params(14),
        cost_estimate=COST,
        name="blend",
    )(*args)


def bits_of(mask):
    return [1 << b for b in range(mask.bit_length()) if mask >> b & 1]


def after(value, *earlier):
    return lax.optimization_barrier((value, earlier))[0]


def body(shards, tensors, hidden_in, policy_weights, reference_weights, policy_queries, reference_queries, readout, lengths):
    rows = policy_weights.shape[1]
    idx = lax.axis_index("shard").astype(jnp.int32).reshape(1)
    tables = jnp.asarray(rope_tables())

    def swap(x, bit, axis="shard", size=shards):
        return lax.ppermute(x, axis, [(i, i ^ bit) for i in range(size)])

    def powers(size):
        return [1 << b for b in range(size.bit_length() - 1)]

    chips = sorted(range(0, shards, 2), key=lambda m: (len(bits_of(m)), m))
    near = [m for m in chips if len(bits_of(m)) == 1]
    far = [m for m in chips if len(bits_of(m)) > 1]
    link = lambda i, m: bits_of(m)[-1] if i == 0 else bits_of(m)[0]

    def send_near(own):
        got = {m: [swap(own, m)] for m in near}
        got[0] = [own]
        got[1] = [swap(own, 1)]
        return got

    def relay(got, m, *earlier):
        got[m] = [None, None]
        for i in (0, 1):
            via = link(i, m)
            source = got[m ^ via]
            source = source[i] if len(source) == 2 else source[0][i]
            got[m][i] = swap(after(source, *earlier), via)

    def to_core(got, m, *earlier):
        got[m | 1] = [swap(after(g, *earlier), 1) for g in got[m]]

    weights = send_near(policy_weights)
    normed, ref_keys, ref_values = norm_project(idx, hidden_in, reference_weights, tables)
    (ref_margin,) = attend(lengths, reference_queries, ref_keys, ref_values, readout)
    for m in far:
        relay(weights, m, ref_margin, *[weights[k] for k in near])
    for m in near:
        to_core(weights, m, ref_margin)
    held = project(idx, normed, [0, 1], weights, None, None)
    held = project(idx, normed, [m | c for m in near for c in (0, 1)], weights, held, None if far else tables)
    if far:
        for m in far:
            to_core(weights, m, held)
        held = project(idx, normed, [m | c for m in far for c in (0, 1)], weights, held, tables)
    pol_keys, pol_values = held
    margin, probs, delta = attend(lengths, policy_queries, pol_keys, pol_values, readout, ref_margin)

    theirs = {}
    order = list(reversed(chips))
    split = max(len(far), 1)

    def other_blocks(masks, *earlier):
        blocks = gradient_blocks(idx, normed, cot, [m | 1 for m in masks], rows, None, earlier)
        theirs.update({m: swap(block, 1) for m, block in zip(masks, blocks)})
        return blocks

    received = [swap(margin, m, "tensor", tensors) for m in range(1, tensors)]
    cot = attend_back(lengths, policy_queries, pol_values, readout, probs, delta, tables)
    terms = [margin] + [after(x, cot) for x in received]
    while len(terms) > 1:
        terms = [a + b for a, b in zip(terms[::2], terms[1::2])]
    (margin,) = terms
    received = swap(margin, 1)
    margins = (margin, after(received, other_blocks(order[:split], margin)))
    other_blocks(order[split:], margins[1])

    chip_sum = {}
    arrived = {m: [[], []] for m in chips}
    waiting = []

    def send(m, i):
        payload = chip_sum[m][i]
        if arrived[m][i]:
            payload = payload.astype(jnp.float32)
            for term in arrived[m][i]:
                payload = payload + term.astype(jnp.float32)
            payload = payload.astype(jnp.bfloat16)
        via = link(i, m)
        arrived[m ^ via][i].append(swap(payload, via))
        return payload

    for masks in (order[:split], order[split:]):
        blocks = gradient_blocks(idx, normed, cot, masks, rows, (margins, theirs))
        chip_sum.update(zip(masks, blocks))
        for m in masks:
            for i in (0, 1):
                if m and not any(k ^ link(i, k) == m for k in far):
                    send(m, i)
                elif m:
                    waiting.append((m, i))
    for m, i in waiting:
        send(m, i)
    own, squares = finish(chip_sum[0], arrived[0])

    grads = send_near(own)
    for bit in powers(tensors):
        squares = squares + swap(squares, bit, "tensor", tensors)
    squares = squares + swap(squares, 1)
    terms = [squares] + [swap(squares, m) for m in chips[1:]]
    while len(terms) > 1:
        terms = [a + b for a, b in zip(terms[::2], terms[1::2])]
    for m in far:
        relay(grads, m, squares, *[grads[k] for k in near])
    (squares,) = terms
    for m in near:
        to_core(grads, m, squares)
    new_reference, token, new_policy = blend(idx, squares, weights, grads, reference_weights, None, [0, 1])
    new_reference, token = blend(idx, squares, weights, grads, reference_weights, new_reference, [m | c for m in near for c in (0, 1)])
    if far:
        ready = fetch(idx, weights, reference_weights, [m | c for c in (0, 1) for m in far], token)
        for m in far:
            to_core(grads, m, ready)
        for c in (0, 1):
            masks = [m | c for m in far]
            new_reference, token = blend(idx, squares, weights, grads, reference_weights, new_reference, masks, (ready, c * len(far)))
    return (new_policy, new_reference, margin[0, :1])


def solution(mesh):
    return jax.shard_map(
        functools.partial(body, mesh.shape["shard"], mesh.shape["tensor"]),
        mesh=mesh,
        in_specs=(
            P("shard", None),
            P(None, "shard", "tensor"),
            P(None, None, "tensor"),
            P("shard", "tensor"),
            P("shard", "tensor"),
            P("shard", "tensor"),
            P("shard"),
        ),
        out_specs=(P(None, "shard", "tensor"), P(None, None, "tensor"), P("shard")),
        check_vma=False,
    )
```

profile of v0, /device:TPU:0, one launch (start us, length us, event | category | flops | bytes accessed | tf_op | source)
XLA Modules:
  0.0 160.2 jit_solution(4741591483714861510)
XLA Ops:
  0.6 3.0 %collective-permute-start = (bf16[2,1024,256]{2,1,0:T(8,128)(2,1)}, bf16[2,1024,256]{2,1,0:T(8,128)(2,1)S(1)}, u32[]{:S(2)}, u32[]{:S(2)}) collective-permute-start(bf16[2,1024,256]{2,1,0:T(8,128)(2,1)} %refs_2_.1), channel_id=1, source_target_pairs={{0,8},{4,12},{8,0},{12,4},{16,24},{20,28},{24,16},{28,20},{1,9},{5... | collective-permute-start | bytes 3145736 | tf_op jit(solution)/shard_map/ppermute | solution.py:646
  3.6 1.5 collective-permute-start.1
  5.2 17.8 %norm_project.1 = (bf16[768,8192]{1,0:T(8,128)(2,1)S(1)}, bf16[768,256]{1,0:T(8,128)(2,1)S(1)}, bf16[768,256]{1,0:T(8,128)(2,1)S(1)}) custom-call(s32[1]{0:T(128)} %bitcast.idx_ref, bf16[768,8192]{1,0:T(8,128)(2,1)} %hidden_hbm.1, bf16[2,8192,256]{2,1,0:T(8,128)(2,1)} %refs_4_.3, f32[2,384,128]{2,1,0:T(8,128)} %constant.8.clone.table_hbm.refs_5_.table_ref), custom_call_target="tpu_custom_call" | custom-call | flops 1 | bytes 1 | tf_op jit(solution)/shard_map/norm_project/pallas_call | solution.py:133
  23.1 4.4 %attend.2.rest_0_ = f32[8,128]{1,0:T(8,128)S(1)} custom-call(s32[2]{0:T(128)S(1)} %copy-done.5, bf16[768,1024]{1,0:T(8,128)(2,1)S(1)} %copy-done.4, bf16[768,256]{1,0:T(8,128)(2,1)S(1)} %get-tuple-element.49.k_ref, bf16[768,256]{1,0:T(8,128)(2,1)S(1)} %get-tuple-element.50.v_ref, bf16[768,1024]{1,0:T(8,128)(2,1)S(1)} %copy-done), custom_call_target="tpu_custom_call" | custom-call | flops 1 | bytes 1 | tf_op jit(solution)/shard_map/attend/pallas_call | solution.py:315
  27.5 0.5 collective-permute-start.4
  28.0 0.5 collective-permute-done.1.refs_2_.refs_6_
  28.5 1.6 collective-permute-start.2
  30.1 0.9 collective-permute-start.3
  31.0 2.0 %project.3.refs_4_ = f32[2,768,256]{2,1,0:T(8,128)S(1)} custom-call(s32[1]{0:T(128)} %bitcast.idx_ref, bf16[768,8192]{1,0:T(8,128)(2,1)S(1)} %get-tuple-element.48.x_ref, bf16[2,1024,256]{2,1,0:T(8,128)(2,1)S(1)} %copy-done.2, bf16[2,1024,256]{2,1,0:T(8,128)(2,1)S(1)} %collective-permute-done.6.refs_1_.refs_3_), custom_call_target="tpu_custom_call" | custom-call | flops 1 | bytes 1 | tf_op jit(solution)/shard_map/project/pallas_call | solution.py:223
  33.1 4.1 %project.4.refs_4_ = f32[2,768,256]{2,1,0:T(8,128)S(1)} custom-call(s32[1]{0:T(128)} %bitcast.idx_ref, bf16[768,8192]{1,0:T(8,128)(2,1)S(1)} %get-tuple-element.48.x_ref, bf16[2,1024,256]{2,1,0:T(8,128)(2,1)S(1)} %collective-permute-done.refs_0_.refs_4_, bf16[2,1024,256]{2,1,0:T(8,128)(2,1)S(1)} %collective-permute-done.4.refs_1_.refs_5_, ...), custom_call_target="tpu_custom_call" | custom-call | flops 1 | bytes 1 | tf_op jit(solution)/shard_map/project/pallas_call | solution.py:223
  37.2 5.7 %collective-permute-done.2.refs_0_ = bf16[1024,256]{1,0:T(8,128)(2,1)S(1)} collective-permute-done((bf16[1024,256]{1,0:T(8,128)(2,1)S(1)}, bf16[1024,256]{1,0:T(8,128)(2,1)S(1)}, u32[]{:S(2)}, u32[]{:S(2)}) %collective-permute-start.2) | collective-permute-done | bytes 524320 | tf_op jit(solution)/shard_map/ppermute | solution.py:646
  42.9 1.3 collective-permute-done.3.refs_1_
  44.3 0.6 collective-permute-done.7.refs_2_
  44.8 1.3 collective-permute-done.8.refs_3_
  46.2 2.4 %project.5 = (bf16[768,256]{1,0:T(8,128)(2,1)S(1)}, bf16[768,256]{1,0:T(8,128)(2,1)S(1)}) custom-call(s32[1]{0:T(128)} %bitcast.idx_ref, bf16[768,8192]{1,0:T(8,128)(2,1)S(1)} %get-tuple-element.48.x_ref, bf16[1024,256]{1,0:T(8,128)(2,1)S(1)} %collective-permute-done.2.refs_0_, bf16[1024,256]{1,0:T(8,128)(2,1)S(1)} %collective-permute-done.3.refs_1_, ...), custom_call_target="tpu_custom_call" | custom-call | flops 1 | bytes 1 | tf_op jit(solution)/shard_map/project/pallas_call | solution.py:223
  48.6 4.7 %attend.3 = (f32[8,128]{1,0:T(8,128)S(1)}, bf16[2,2,768,512]{3,2,1,0:T(8,128)(2,1)S(1)}, f32[2,2,3,512]{3,2,1,0:T(4,128)S(1)}) custom-call(s32[2]{0:T(128)S(1)} %copy-done.5, bf16[768,1024]{1,0:T(8,128)(2,1)S(1)} %copy-done.1, bf16[768,256]{1,0:T(8,128)(2,1)S(1)} %get-tuple-element.58.k_ref, bf16[768,256]{1,0:T(8,128)(2,1)S(1)} %get-tuple-element.57.v_ref, ...), custom_call_target="tpu_custom_call" | custom-call | flops 1 | bytes 1 | tf_op jit(solution)/shard_map/attend/pallas_call | solution.py:315
  53.3 2.7 %collective-permute-start.10 = (f32[8,128]{1,0:T(8,128)S(1)}, f32[8,128]{1,0:T(8,128)S(1)}, u32[]{:S(2)}, u32[]{:S(2)}) collective-permute-start(f32[8,128]{1,0:T(8,128)S(1)} %get-tuple-element.61), channel_id=1, source_target_pairs={{0,2},{1,3},{2,0},{3,1},{4,6},{5,7},{6,4},{7,5},{8,10},{9,11},{10,... | collective-permute-start | bytes 12296 | tf_op jit(solution)/shard_map/ppermute | solution.py:646
  56.0 1.3 collective-permute-start.11
  57.3 0.2 collective-permute-start.9
  57.6 6.2 %attend_back.1.cot_ref = bf16[2,256,768]{2,1,0:T(8,128)(2,1)S(1)} custom-call(s32[2]{0:T(128)S(1)} %copy-done.5, bf16[768,1024]{1,0:T(8,128)(2,1)S(1)} %copy-done.1, bf16[768,256]{1,0:T(8,128)(2,1)S(1)} %get-tuple-element.57.v_ref, bf16[768,1024]{1,0:T(8,128)(2,1)S(1)} %copy-done, bf16[2,2,768,512]{3,2,1,0:T(8,128)(2,1)S(1)} %get-tuple-element.59.prob_ref, ...), custom_call_target="tpu_custom_call" | custom-call | flops 1 | bytes 1 | tf_op jit(solution)/shard_map/attend_back/pallas_call | solution.py:368
  63.9 1.6 gradient_block.2
  65.5 0.5 collective-permute-start.12
  66.0 2.2 %collective-permute-done.12.outs_0_.their_ref = f32[8,128]{1,0:T(8,128)S(1)} collective-permute-done((f32[8,128]{1,0:T(8,128)S(1)}, f32[8,128]{1,0:T(8,128)S(1)}, u32[]{:S(2)}, u32[]{:S(2)}) %collective-permute-start.12) | collective-permute-done | bytes 4128 | tf_op jit(solution)/shard_map/ppermute | solution.py:646
  68.2 4.8 %gradient_block.3 = (bf16[2,256,1024]{2,1,0:T(8,128)(2,1)S(1)}, bf16[2,256,1024]{2,1,0:T(8,128)(2,1)S(1)}, bf16[2,256,1024]{2,1,0:T(8,128)(2,1)S(1)}) custom-call(s32[1]{0:T(128)} %bitcast.idx_ref, bf16[768,8192]{1,0:T(8,128)(2,1)S(1)} %get-tuple-element.48.x_ref, bf16[2,256,768]{2,1,0:T(8,128)(2,1)S(1)} %attend_back.1.cot_ref, ...), custom_call_target="tpu_custom_call" | custom-call | flops 1 | bytes 1 | tf_op jit(solution)/shard_map/gradient_block/pallas_call | solution.py:444
  73.0 0.2 collective-permute-start.13
  73.2 0.4 collective-permute-start.14
  73.7 1.7 %merged_block.3 = (bf16[256,1024]{1,0:T(8,128)(2,1)S(1)}, bf16[256,1024]{1,0:T(8,128)(2,1)S(1)}) custom-call(s32[1]{0:T(128)} %bitcast.idx_ref, bf16[768,8192]{1,0:T(8,128)(2,1)S(1)} %get-tuple-element.48.x_ref, bf16[2,256,768]{2,1,0:T(8,128)(2,1)S(1)} %attend_back.1.cot_ref, f32[8,128]{1,0:T(8,128)S(1)} %add_add_fusion.1.outs_0_.mine_ref, ...), custom_call_target="tpu_custom_call" | custom-call | flops 1 | bytes 1 | tf_op jit(solution)/shard_map/merged_block/pallas_call | solution.py:444
  75.3 1.0 collective-permute-start.18
  76.3 0.5 collective-permute-start.21
  76.9 0.3 collective-permute-done.14.refs_1_
  77.2 1.5 collective-permute-done.15.refs_2_
  78.7 4.9 %merged_block.2 = (bf16[256,1024]{1,0:T(8,128)(2,1)S(1)}, bf16[256,1024]{1,0:T(8,128)(2,1)S(1)}, bf16[256,1024]{1,0:T(8,128)(2,1)S(1)}, bf16[256,1024]{1,0:T(8,1...) custom-call(s32[1]{0:T(128)} %bitcast.idx_ref, bf16[768,8192]{1,0:T(8,128)(2,1)S(1)} %get-tuple-element.48.x_ref, ...), custom_call_target="tpu_custom_call" | custom-call | flops 1 | bytes 1 | tf_op jit(solution)/shard_map/merged_block/pallas_call | solution.py:444
  83.6 1.0 collective-permute-start.16
  84.6 0.5 collective-permute-start.20
  85.1 5.0 %collective-permute-done.18 = bf16[256,1024]{1,0:T(8,128)(2,1)S(1)} collective-permute-done((bf16[256,1024]{1,0:T(8,128)(2,1)S(1)}, bf16[256,1024]{1,0:T(8,128)(2,1)S(1)}, u32[]{:S(2)}, u32[]{:S(2)}) %collective-permute-start.18) | collective-permute-done | bytes 524320 | tf_op jit(solution)/shard_map/ppermute | solution.py:646
  90.4 0.6 collective-permute-start.19
  91.3 1.2 collective-permute-start.22
  92.5 8.9 %collective-permute-done.16.refs_1_ = bf16[256,1024]{1,0:T(8,128)(2,1)S(1)} collective-permute-done((bf16[256,1024]{1,0:T(8,128)(2,1)S(1)}, bf16[256,1024]{1,0:T(8,128)(2,1)S(1)}, u32[]{:S(2)}, u32[]{:S(2)}) %collective-permute-start.16) | collective-permute-done | bytes 524320 | tf_op jit(solution)/shard_map/ppermute | solution.py:646
  101.4 1.0 collective-permute-done.20.refs_4_
  102.4 10.4 %collective-permute-done.19.refs_2_ = bf16[256,1024]{1,0:T(8,128)(2,1)S(1)} collective-permute-done((bf16[256,1024]{1,0:T(8,128)(2,1)S(1)}, bf16[256,1024]{1,0:T(8,128)(2,1)S(1)}, u32[]{:S(2)}, u32[]{:S(2)}) %collective-permute-start.19) | collective-permute-done | bytes 524320 | tf_op jit(solution)/shard_map/ppermute | solution.py:646
  112.7 0.7 finish.1
  113.4 0.6 collective-permute-start.30
  114.0 1.1 collective-permute-start.31
  115.1 1.8 %collective-permute-start.23 = (f32[8,128]{1,0:T(8,128)S(1)}, f32[8,128]{1,0:T(8,128)S(1)}, u32[]{:S(2)}, u32[]{:S(2)}) collective-permute-start(f32[8,128]{1,0:T(8,128)S(1)} %get-tuple-element.77), channel_id=1, source_target_pairs={{0,1},{1,0},{2,3},{3,2},{4,5},{5,4},{6,7},{7,6},{8,9},{9,8},{10,11... | collective-permute-start | bytes 12296 | tf_op jit(solution)/shard_map/ppermute | solution.py:646
  116.9 1.8 %collective-permute-done.23 = f32[8,128]{1,0:T(8,128)S(1)} collective-permute-done((f32[8,128]{1,0:T(8,128)S(1)}, f32[8,128]{1,0:T(8,128)S(1)}, u32[]{:S(2)}, u32[]{:S(2)}) %collective-permute-start.23) | collective-permute-done | bytes 4128 | tf_op jit(solution)/shard_map/ppermute | solution.py:646
  118.7 2.8 %collective-permute-start.24 = (f32[8,128]{1,0:T(8,128)S(1)}, f32[8,128]{1,0:T(8,128)S(1)}, u32[]{:S(2)}, u32[]{:S(2)}) collective-permute-start(f32[8,128]{1,0:T(8,128)S(1)} %add.38), channel_id=1, source_target_pairs={{0,2},{1,3},{2,0},{3,1},{4,6},{5,7},{6,4},{7,5},{8,10},{9,11},{10,... | collective-permute-start | bytes 12296 | tf_op jit(solution)/shard_map/ppermute | solution.py:646
  121.5 1.7 %collective-permute-done.24 = f32[8,128]{1,0:T(8,128)S(1)} collective-permute-done((f32[8,128]{1,0:T(8,128)S(1)}, f32[8,128]{1,0:T(8,128)S(1)}, u32[]{:S(2)}, u32[]{:S(2)}) %collective-permute-start.24) | collective-permute-done | bytes 4128 | tf_op jit(solution)/shard_map/ppermute | solution.py:646
  123.2 1.2 collective-permute-done.25
  124.4 0.9 collective-permute-start.27
  125.3 2.0 %collective-permute-start.28 = (f32[8,128]{1,0:T(8,128)S(1)}, f32[8,128]{1,0:T(8,128)S(1)}, u32[]{:S(2)}, u32[]{:S(2)}) collective-permute-start(f32[8,128]{1,0:T(8,128)S(1)} %add.40), channel_id=1, source_target_pairs={{0,24},{4,28},{8,16},{12,20},{16,8},{20,12},{24,0},{28,4},{1,25},{... | collective-permute-start | bytes 12296 | tf_op jit(solution)/shard_map/ppermute | solution.py:646
  127.3 0.5 collective-permute-start.26
  127.9 10.3 %collective-permute-done.27 = f32[8,128]{1,0:T(8,128)S(1)} collective-permute-done((f32[8,128]{1,0:T(8,128)S(1)}, f32[8,128]{1,0:T(8,128)S(1)}, u32[]{:S(2)}, u32[]{:S(2)}) %collective-permute-start.27) | collective-permute-done | bytes 4128 | tf_op jit(solution)/shard_map/ppermute | solution.py:646
  138.1 0.3 collective-permute-done.28
  138.4 0.3 collective-permute-start.33
  138.7 0.3 collective-permute-start.34
  139.1 1.0 collective-permute-start.32
  140.1 1.6 collective-permute-start.36
  141.7 4.5 %blend.4 = (bf16[2,8192,256]{2,1,0:T(8,128)(2,1)}, f32[8,128]{1,0:T(8,128)}, bf16[2,1024,256]{2,1,0:T(8,128)(2,1)}) custom-call(s32[1]{0:T(128)} %bitcast.idx_ref, f32[8,128]{1,0:T(8,128)S(1)} %add_add_fusion.square_ref, bf16[2,1024,256]{2,1,0:T(8,128)(2,1)S(1)} %get-tuple-element.78.refs_0_, bf16[2,1024,256]{2,1,0:T(8,128)(2,1)S(1)} %collective-permute-done.29.refs_1_, ...), custom_call_target="tpu_custom_call" | custom-call | flops 1 | bytes 1 | tf_op jit(solution)/shard_map/blend/pallas_call | solution.py:619
  146.2 6.3 %blend.5 = (bf16[2,8192,256]{2,1,0:T(8,128)(2,1)}, f32[8,128]{1,0:T(8,128)S(1)}) custom-call(s32[1]{0:T(128)} %bitcast.idx_ref, f32[8,128]{1,0:T(8,128)S(1)} %add_add_fusion.square_ref, bf16[2,1024,256]{2,1,0:T(8,128)(2,1)S(1)} %collective-permute-done.30.refs_0_, ...), custom_call_target="tpu_custom_call", output_to_operand_aliasing={{0}: (11, {})} | custom-call | flops 1 | bytes 1 | tf_op jit(solution)/shard_map/blend/pallas_call | solution.py:619
  152.5 1.7 %fetch.1 = (bf16[2,2,1024,256]{3,2,1,0:T(8,128)(2,1)S(1)}, bf16[2,2,1024,256]{3,2,1,0:T(8,128)(2,1)S(1)}) custom-call(s32[1]{0:T(128)} %bitcast.idx_ref, bf16[1024,256]{1,0:T(8,128)(2,1)S(1)} %collective-permute-done.2.refs_0_, bf16[1024,256]{1,0:T(8,128)(2,1)S(1)} %collective-permute-done.3.refs_1_, bf16[1024,256]{1,0:T(8,128)(2,1)S(1)} %collective-permute-done.7.refs_2_, ...), custom_call_target="tpu_custom_call" | custom-call | flops 1 | bytes 1 | tf_op jit(solution)/shard_map/fetch/pallas_call | solution.py:509
  154.3 0.5 collective-permute-start.37
  154.8 0.5 slice.19
  155.3 2.4 %blend.6 = (bf16[2,8192,256]{2,1,0:T(8,128)(2,1)}, f32[8,128]{1,0:T(8,128)}) custom-call(s32[1]{0:T(128)} %bitcast.idx_ref, f32[8,128]{1,0:T(8,128)S(1)} %add_add_fusion.square_ref, bf16[1024,256]{1,0:T(8,128)(2,1)S(1)} %collective-permute-done.32.refs_0_, bf16[1024,256]{1,0:T(8,128)(2,1)S(1)} %collective-permute-done.36.refs_1_, ...), custom_call_target="tpu_custom_call", output_to_operand_aliasing={{0}: (6, {})} | custom-call | flops 1 | bytes 1 | tf_op jit(solution)/shard_map/blend/pallas_call | solution.py:619
  157.7 2.4 %blend.7 = (bf16[2,8192,256]{2,1,0:T(8,128)(2,1)}, f32[8,128]{1,0:T(8,128)}) custom-call(s32[1]{0:T(128)} %bitcast.idx_ref, f32[8,128]{1,0:T(8,128)S(1)} %add_add_fusion.square_ref, bf16[1024,256]{1,0:T(8,128)(2,1)S(1)} %collective-permute-done.35.refs_0_, bf16[1024,256]{1,0:T(8,128)(2,1)S(1)} %collective-permute-done.37.refs_1_, ...), custom_call_target="tpu_custom_call", output_to_operand_aliasing={{0}: (6, {})} | custom-call | flops 1 | bytes 1 | tf_op jit(solution)/shard_map/blend/pallas_call | solution.py:619
  (53 shorter events, 1.1 us)
Async XLA Ops:
  0.6 26.9 %collective-permute-start = (bf16[2,1024,256]{2,1,0:T(8,128)(2,1)}, bf16[2,1024,256]{2,1,0:T(8,128)(2,1)S(1)}, u32[]{:S(2)}, u32[]{:S(2)}) collective-permute-start(bf16[2,1024,256]{2,1,0:T(8,128)(2,1)} %refs_2_.1), channel_id=1, source_target_pairs={{0,8},{4,12},{8,0},{12,4},{16,24},{20,28},{24,16},{28,20},{1,9},{5... | collective-permute-start | bytes 3145736 | tf_op jit(solution)/shard_map/ppermute | solution.py:646
  3.6 24.8 %collective-permute-start.1 = (bf16[2,1024,256]{2,1,0:T(8,128)(2,1)}, bf16[2,1024,256]{2,1,0:T(8,128)(2,1)S(1)}, u32[]{:S(2)}, u32[]{:S(2)}) collective-permute-start(bf16[2,1024,256]{2,1,0:T(8,128)(2,1)} %refs_2_.1), channel_id=1, source_target_pairs={{0,16},{4,20},{8,24},{12,28},{16,0},{20,4},{24,8},{28,12},{1,17},{... | collective-permute-start | bytes 3145736 | tf_op jit(solution)/shard_map/ppermute | solution.py:646
  5.2 25.8 %collective-permute-start.6 = (bf16[2,1024,256]{2,1,0:T(8,128)(2,1)}, bf16[2,1024,256]{2,1,0:T(8,128)(2,1)S(1)}, u32[]{:S(2)}, u32[]{:S(2)}) collective-permute-start(bf16[2,1024,256]{2,1,0:T(8,128)(2,1)} %refs_2_.1), channel_id=1, source_target_pairs={{0,4},{4,0},{8,12},{12,8},{16,20},{20,16},{24,28},{28,24},{1,5},{5... | collective-permute-start | bytes 3145736 | tf_op jit(solution)/shard_map/ppermute | solution.py:646
  5.2 17.9 %copy-start = (bf16[768,1024]{1,0:T(8,128)(2,1)S(1)}, bf16[768,1024]{1,0:T(8,128)(2,1)}, u32[]{:S(2)}) copy-start(bf16[768,1024]{1,0:T(8,128)(2,1)} %ro_ref.5) | copy-start | bytes 4718596
  5.2 17.9 %copy-start.4 = (bf16[768,1024]{1,0:T(8,128)(2,1)S(1)}, bf16[768,1024]{1,0:T(8,128)(2,1)}, u32[]{:S(2)}) copy-start(bf16[768,1024]{1,0:T(8,128)(2,1)} %q_ref.3) | copy-start | bytes 4718596
  5.2 17.9 %copy-start.5 = (s32[2]{0:T(128)S(1)}, s32[2]{0:T(128)}, u32[]{:S(2)}) copy-start(s32[2]{0:T(128)} %len_ref.5) | copy-start | bytes 28
  23.0 8.0 %copy-start.2 = (bf16[2,1024,256]{2,1,0:T(8,128)(2,1)S(1)}, bf16[2,1024,256]{2,1,0:T(8,128)(2,1)}, u32[]{:S(2)}) copy-start(bf16[2,1024,256]{2,1,0:T(8,128)(2,1)} %refs_2_.1) | copy-start | bytes 3145732
  27.5 5.5 %collective-permute-start.4 = (bf16[2,1024,256]{2,1,0:T(8,128)(2,1)S(1)}, bf16[2,1024,256]{2,1,0:T(8,128)(2,1)S(1)}, u32[]{:S(2)}, u32[]{:S(2)}) collective-permute-start(bf16[2,1024,256]{2,1,0:T(8,128)(2,1)S(1)} %collective-permute-done.refs_0_.refs_4_), channel_id=1, source_target_pairs={{0,4},{4,0},{8,12},{12,8},{16,20},{20,16},{24,28},{28,24},{1,5},{5... | collective-permute-start | bytes 3145736 | tf_op jit(solution)/shard_map/ppermute | solution.py:646
  28.5 4.6 %collective-permute-start.5 = (bf16[2,1024,256]{2,1,0:T(8,128)(2,1)S(1)}, bf16[2,1024,256]{2,1,0:T(8,128)(2,1)S(1)}, u32[]{:S(2)}, u32[]{:S(2)}) collective-permute-start(bf16[2,1024,256]{2,1,0:T(8,128)(2,1)S(1)} %collective-permute-done.1.refs_2_.refs_6_), channel_id=1, source_target_pairs={{0,4},{4,0},{8,12},{12,8},{16,20},{20,16},{24,28},{28,24},{1,5},{5... | collective-permute-start | bytes 3145736 | tf_op jit(solution)/shard_map/ppermute | solution.py:646
  28.5 14.4 %collective-permute-start.2 = (bf16[1024,256]{1,0:T(8,128)(2,1)S(1)}, bf16[1024,256]{1,0:T(8,128)(2,1)S(1)}, u32[]{:S(2)}, u32[]{:S(2)}) collective-permute-start(bf16[1024,256]{1,0:T(8,128)(2,1)S(1)} %slice_bitcast_fusion.3), channel_id=1, source_target_pairs={{0,16},{4,20},{8,24},{12,28},{16,0},{20,4},{24,8},{28,12},{1,17},{... | collective-permute-start | bytes 1572872 | tf_op jit(solution)/shard_map/ppermute | solution.py:646
  30.1 14.1 %collective-permute-start.3 = (bf16[1024,256]{1,0:T(8,128)(2,1)S(1)}, bf16[1024,256]{1,0:T(8,128)(2,1)S(1)}, u32[]{:S(2)}, u32[]{:S(2)}) collective-permute-start(bf16[1024,256]{1,0:T(8,128)(2,1)S(1)} %slice_bitcast_fusion.2), channel_id=1, source_target_pairs={{0,8},{4,12},{8,0},{12,4},{16,24},{20,28},{24,16},{28,20},{1,9},{5... | collective-permute-start | bytes 1572872 | tf_op jit(solution)/shard_map/ppermute | solution.py:646
  37.2 11.5 %copy-start.1 = (bf16[768,1024]{1,0:T(8,128)(2,1)S(1)}, bf16[768,1024]{1,0:T(8,128)(2,1)}, u32[]{:S(2)}) copy-start(bf16[768,1024]{1,0:T(8,128)(2,1)} %q_ref.5) | copy-start | bytes 4718596
  42.9 1.9 %collective-permute-start.7 = (bf16[1024,256]{1,0:T(8,128)(2,1)S(1)}, bf16[1024,256]{1,0:T(8,128)(2,1)S(1)}, u32[]{:S(2)}, u32[]{:S(2)}) collective-permute-start(bf16[1024,256]{1,0:T(8,128)(2,1)S(1)} %collective-permute-done.2.refs_0_), channel_id=1, source_target_pairs={{0,4},{4,0},{8,12},{12,8},{16,20},{20,16},{24,28},{28,24},{1,5},{5... | collective-permute-start | bytes 1572872 | tf_op jit(solution)/shard_map/ppermute | solution.py:646
  44.3 1.9 %collective-permute-start.8 = (bf16[1024,256]{1,0:T(8,128)(2,1)S(1)}, bf16[1024,256]{1,0:T(8,128)(2,1)S(1)}, u32[]{:S(2)}, u32[]{:S(2)}) collective-permute-start(bf16[1024,256]{1,0:T(8,128)(2,1)S(1)} %collective-permute-done.3.refs_1_), channel_id=1, source_target_pairs={{0,4},{4,0},{8,12},{12,8},{16,20},{20,16},{24,28},{28,24},{1,5},{5... | collective-permute-start | bytes 1572872 | tf_op jit(solution)/shard_map/ppermute | solution.py:646
  48.6 8.9 %copy-start.3 = (f32[2,384,128]{2,1,0:T(8,128)S(1)}, f32[2,384,128]{2,1,0:T(8,128)}, u32[]{:S(2)}) copy-start(f32[2,384,128]{2,1,0:T(8,128)} %constant.8.clone.table_hbm.refs_5_.table_ref) | copy-start | bytes 1179652
  53.3 10.5 %collective-permute-start.10 = (f32[8,128]{1,0:T(8,128)S(1)}, f32[8,128]{1,0:T(8,128)S(1)}, u32[]{:S(2)}, u32[]{:S(2)}) collective-permute-start(f32[8,128]{1,0:T(8,128)S(1)} %get-tuple-element.61), channel_id=1, source_target_pairs={{0,2},{1,3},{2,0},{3,1},{4,6},{5,7},{6,4},{7,5},{8,10},{9,11},{10,... | collective-permute-start | bytes 12296 | tf_op jit(solution)/shard_map/ppermute | solution.py:646
  56.0 7.9 %collective-permute-start.11 = (f32[8,128]{1,0:T(8,128)S(1)}, f32[8,128]{1,0:T(8,128)S(1)}, u32[]{:S(2)}, u32[]{:S(2)}) collective-permute-start(f32[8,128]{1,0:T(8,128)S(1)} %get-tuple-element.61), channel_id=1, source_target_pairs={{0,3},{1,2},{2,1},{3,0},{4,7},{5,6},{6,5},{7,4},{8,11},{9,10},{10,... | collective-permute-start | bytes 12296 | tf_op jit(solution)/shard_map/ppermute | solution.py:646
  57.3 6.5 %collective-permute-start.9 = (f32[8,128]{1,0:T(8,128)S(1)}, f32[8,128]{1,0:T(8,128)S(1)}, u32[]{:S(2)}, u32[]{:S(2)}) collective-permute-start(f32[8,128]{1,0:T(8,128)S(1)} %get-tuple-element.61), channel_id=1, source_target_pairs={{0,1},{1,0},{2,3},{3,2},{4,5},{5,4},{6,7},{7,6},{8,9},{9,8},{10,11... | collective-permute-start | bytes 12296 | tf_op jit(solution)/shard_map/ppermute | solution.py:646
  65.4 8.3 %collective-permute-start.17 = (bf16[2,256,1024]{2,1,0:T(8,128)(2,1)S(1)}, bf16[2,256,1024]{2,1,0:T(8,128)(2,1)S(1)}, u32[]{:S(2)}, u32[]{:S(2)}) collective-permute-start(bf16[2,256,1024]{2,1,0:T(8,128)(2,1)S(1)} %gradient_block.2), channel_id=1, source_target_pairs={{0,4},{4,0},{8,12},{12,8},{16,20},{20,16},{24,28},{28,24},{1,5},{5... | collective-permute-start | bytes 3145736 | tf_op jit(solution)/shard_map/ppermute | solution.py:646
  65.5 2.7 %collective-permute-start.12 = (f32[8,128]{1,0:T(8,128)S(1)}, f32[8,128]{1,0:T(8,128)S(1)}, u32[]{:S(2)}, u32[]{:S(2)}) collective-permute-start(f32[8,128]{1,0:T(8,128)S(1)} %add_add_fusion.1.outs_0_.mine_ref), channel_id=1, source_target_pairs={{0,4},{4,0},{8,12},{12,8},{16,20},{20,16},{24,28},{28,24},{1,5},{5... | collective-permute-start | bytes 12296 | tf_op jit(solution)/shard_map/ppermute | solution.py:646
  73.0 3.9 %collective-permute-start.13 = (bf16[2,256,1024]{2,1,0:T(8,128)(2,1)S(1)}, bf16[2,256,1024]{2,1,0:T(8,128)(2,1)S(1)}, u32[]{:S(2)}, u32[]{:S(2)}) collective-permute-start(bf16[2,256,1024]{2,1,0:T(8,128)(2,1)S(1)} %get-tuple-element.66), channel_id=1, source_target_pairs={{0,4},{4,0},{8,12},{12,8},{16,20},{20,16},{24,28},{28,24},{1,5},{5... | collective-permute-start | bytes 3145736 | tf_op jit(solution)/shard_map/ppermute | solution.py:646
  73.2 4.0 %collective-permute-start.14 = (bf16[2,256,1024]{2,1,0:T(8,128)(2,1)S(1)}, bf16[2,256,1024]{2,1,0:T(8,128)(2,1)S(1)}, u32[]{:S(2)}, u32[]{:S(2)}) collective-permute-start(bf16[2,256,1024]{2,1,0:T(8,128)(2,1)S(1)} %get-tuple-element.67), channel_id=1, source_target_pairs={{0,4},{4,0},{8,12},{12,8},{16,20},{20,16},{24,28},{28,24},{1,5},{5... | collective-permute-start | bytes 3145736 | tf_op jit(solution)/shard_map/ppermute | solution.py:646
  73.5 5.1 %collective-permute-start.15 = (bf16[2,256,1024]{2,1,0:T(8,128)(2,1)S(1)}, bf16[2,256,1024]{2,1,0:T(8,128)(2,1)S(1)}, u32[]{:S(2)}, u32[]{:S(2)}) collective-permute-start(bf16[2,256,1024]{2,1,0:T(8,128)(2,1)S(1)} %get-tuple-element.68), channel_id=1, source_target_pairs={{0,4},{4,0},{8,12},{12,8},{16,20},{20,16},{24,28},{28,24},{1,5},{5... | collective-permute-start | bytes 3145736 | tf_op jit(solution)/shard_map/ppermute | solution.py:646
  75.3 14.8 %collective-permute-start.18 = (bf16[256,1024]{1,0:T(8,128)(2,1)S(1)}, bf16[256,1024]{1,0:T(8,128)(2,1)S(1)}, u32[]{:S(2)}, u32[]{:S(2)}) collective-permute-start(bf16[256,1024]{1,0:T(8,128)(2,1)S(1)} %get-tuple-element.72), channel_id=1, source_target_pairs={{0,16},{4,20},{8,24},{12,28},{16,0},{20,4},{24,8},{28,12},{1,17},{... | collective-permute-start | bytes 1572872 | tf_op jit(solution)/shard_map/ppermute | solution.py:646
  76.3 14.8 %collective-permute-start.21 = (bf16[256,1024]{1,0:T(8,128)(2,1)S(1)}, bf16[256,1024]{1,0:T(8,128)(2,1)S(1)}, u32[]{:S(2)}, u32[]{:S(2)}) collective-permute-start(bf16[256,1024]{1,0:T(8,128)(2,1)S(1)} %get-tuple-element.76), channel_id=1, source_target_pairs={{0,8},{4,12},{8,0},{12,4},{16,24},{20,28},{24,16},{28,20},{1,9},{5... | collective-permute-start | bytes 1572872 | tf_op jit(solution)/shard_map/ppermute | solution.py:646
  83.6 17.8 %collective-permute-start.16 = (bf16[256,1024]{1,0:T(8,128)(2,1)S(1)}, bf16[256,1024]{1,0:T(8,128)(2,1)S(1)}, u32[]{:S(2)}, u32[]{:S(2)}) collective-permute-start(bf16[256,1024]{1,0:T(8,128)(2,1)S(1)} %get-tuple-element.70), channel_id=1, source_target_pairs={{0,16},{4,20},{8,24},{12,28},{16,0},{20,4},{24,8},{28,12},{1,17},{... | collective-permute-start | bytes 1572872 | tf_op jit(solution)/shard_map/ppermute | solution.py:646
  84.6 17.7 %collective-permute-start.20 = (bf16[256,1024]{1,0:T(8,128)(2,1)S(1)}, bf16[256,1024]{1,0:T(8,128)(2,1)S(1)}, u32[]{:S(2)}, u32[]{:S(2)}) collective-permute-start(bf16[256,1024]{1,0:T(8,128)(2,1)S(1)} %get-tuple-element.74), channel_id=1, source_target_pairs={{0,8},{4,12},{8,0},{12,4},{16,24},{20,28},{24,16},{28,20},{1,9},{5... | collective-permute-start | bytes 1572872 | tf_op jit(solution)/shard_map/ppermute | solution.py:646
  90.4 22.4 %collective-permute-start.19 = (bf16[256,1024]{1,0:T(8,128)(2,1)S(1)}, bf16[256,1024]{1,0:T(8,128)(2,1)S(1)}, u32[]{:S(2)}, u32[]{:S(2)}) collective-permute-start(bf16[256,1024]{1,0:T(8,128)(2,1)S(1)} %add_convert_fusion.1), channel_id=1, source_target_pairs={{0,8},{4,12},{8,0},{12,4},{16,24},{20,28},{24,16},{28,20},{1,9},{5... | collective-permute-start | bytes 1572872 | tf_op jit(solution)/shard_map/ppermute | solution.py:646
  91.3 21.4 %collective-permute-start.22 = (bf16[256,1024]{1,0:T(8,128)(2,1)S(1)}, bf16[256,1024]{1,0:T(8,128)(2,1)S(1)}, u32[]{:S(2)}, u32[]{:S(2)}) collective-permute-start(bf16[256,1024]{1,0:T(8,128)(2,1)S(1)} %add_convert_fusion), channel_id=1, source_target_pairs={{0,16},{4,20},{8,24},{12,28},{16,0},{20,4},{24,8},{28,12},{1,17},{... | collective-permute-start | bytes 1572872 | tf_op jit(solution)/shard_map/ppermute | solution.py:646
  113.4 25.0 %collective-permute-start.30 = (bf16[2,1024,256]{2,1,0:T(8,128)(2,1)S(1)}, bf16[2,1024,256]{2,1,0:T(8,128)(2,1)S(1)}, u32[]{:S(2)}, u32[]{:S(2)}) collective-permute-start(bf16[2,1024,256]{2,1,0:T(8,128)(2,1)S(1)} %get-tuple-element.78.refs_0_), channel_id=1, source_target_pairs={{0,8},{4,12},{8,0},{12,4},{16,24},{20,28},{24,16},{28,20},{1,9},{5... | collective-permute-start | bytes 3145736 | tf_op jit(solution)/shard_map/ppermute | solution.py:646
  114.0 24.8 %collective-permute-start.31 = (bf16[2,1024,256]{2,1,0:T(8,128)(2,1)S(1)}, bf16[2,1024,256]{2,1,0:T(8,128)(2,1)S(1)}, u32[]{:S(2)}, u32[]{:S(2)}) collective-permute-start(bf16[2,1024,256]{2,1,0:T(8,128)(2,1)S(1)} %get-tuple-element.78.refs_0_), channel_id=1, source_target_pairs={{0,16},{4,20},{8,24},{12,28},{16,0},{20,4},{24,8},{28,12},{1,17},{... | collective-permute-start | bytes 3145736 | tf_op jit(solution)/shard_map/ppermute | solution.py:646
  115.1 3.6 %collective-permute-start.23 = (f32[8,128]{1,0:T(8,128)S(1)}, f32[8,128]{1,0:T(8,128)S(1)}, u32[]{:S(2)}, u32[]{:S(2)}) collective-permute-start(f32[8,128]{1,0:T(8,128)S(1)} %get-tuple-element.77), channel_id=1, source_target_pairs={{0,1},{1,0},{2,3},{3,2},{4,5},{5,4},{6,7},{7,6},{8,9},{9,8},{10,11... | collective-permute-start | bytes 12296 | tf_op jit(solution)/shard_map/ppermute | solution.py:646
  118.7 4.5 %collective-permute-start.24 = (f32[8,128]{1,0:T(8,128)S(1)}, f32[8,128]{1,0:T(8,128)S(1)}, u32[]{:S(2)}, u32[]{:S(2)}) collective-permute-start(f32[8,128]{1,0:T(8,128)S(1)} %add.38), channel_id=1, source_target_pairs={{0,2},{1,3},{2,0},{3,1},{4,6},{5,7},{6,4},{7,5},{8,10},{9,11},{10,... | collective-permute-start | bytes 12296 | tf_op jit(solution)/shard_map/ppermute | solution.py:646
  123.2 1.2 collective-permute-start.25
  124.4 13.8 %collective-permute-start.27 = (f32[8,128]{1,0:T(8,128)S(1)}, f32[8,128]{1,0:T(8,128)S(1)}, u32[]{:S(2)}, u32[]{:S(2)}) collective-permute-start(f32[8,128]{1,0:T(8,128)S(1)} %add.40), channel_id=1, source_target_pairs={{0,16},{4,20},{8,24},{12,28},{16,0},{20,4},{24,8},{28,12},{1,17},{... | collective-permute-start | bytes 12296 | tf_op jit(solution)/shard_map/ppermute | solution.py:646
  125.3 13.1 %collective-permute-start.28 = (f32[8,128]{1,0:T(8,128)S(1)}, f32[8,128]{1,0:T(8,128)S(1)}, u32[]{:S(2)}, u32[]{:S(2)}) collective-permute-start(f32[8,128]{1,0:T(8,128)S(1)} %add.40), channel_id=1, source_target_pairs={{0,24},{4,28},{8,16},{12,20},{16,8},{20,12},{24,0},{28,4},{1,25},{... | collective-permute-start | bytes 12296 | tf_op jit(solution)/shard_map/ppermute | solution.py:646
  127.3 11.1 %collective-permute-start.26 = (f32[8,128]{1,0:T(8,128)S(1)}, f32[8,128]{1,0:T(8,128)S(1)}, u32[]{:S(2)}, u32[]{:S(2)}) collective-permute-start(f32[8,128]{1,0:T(8,128)S(1)} %add.40), channel_id=1, source_target_pairs={{0,8},{4,12},{8,0},{12,4},{16,24},{20,28},{24,16},{28,20},{1,9},{5... | collective-permute-start | bytes 12296 | tf_op jit(solution)/shard_map/ppermute | solution.py:646
  138.1 3.5 %collective-permute-start.29 = (bf16[2,1024,256]{2,1,0:T(8,128)(2,1)S(1)}, bf16[2,1024,256]{2,1,0:T(8,128)(2,1)S(1)}, u32[]{:S(2)}, u32[]{:S(2)}) collective-permute-start(bf16[2,1024,256]{2,1,0:T(8,128)(2,1)S(1)} %get-tuple-element.78.refs_0_), channel_id=1, source_target_pairs={{0,4},{4,0},{8,12},{12,8},{16,20},{20,16},{24,28},{28,24},{1,5},{5... | collective-permute-start | bytes 3145736 | tf_op jit(solution)/shard_map/ppermute | solution.py:646
  138.4 7.7 %collective-permute-start.33 = (bf16[2,1024,256]{2,1,0:T(8,128)(2,1)S(1)}, bf16[2,1024,256]{2,1,0:T(8,128)(2,1)S(1)}, u32[]{:S(2)}, u32[]{:S(2)}) collective-permute-start(bf16[2,1024,256]{2,1,0:T(8,128)(2,1)S(1)} %collective-permute-done.30.refs_0_), channel_id=1, source_target_pairs={{0,4},{4,0},{8,12},{12,8},{16,20},{20,16},{24,28},{28,24},{1,5},{5... | collective-permute-start | bytes 3145736 | tf_op jit(solution)/shard_map/ppermute | solution.py:646
  138.7 7.4 %collective-permute-start.34 = (bf16[2,1024,256]{2,1,0:T(8,128)(2,1)S(1)}, bf16[2,1024,256]{2,1,0:T(8,128)(2,1)S(1)}, u32[]{:S(2)}, u32[]{:S(2)}) collective-permute-start(bf16[2,1024,256]{2,1,0:T(8,128)(2,1)S(1)} %collective-permute-done.31.refs_2_), channel_id=1, source_target_pairs={{0,4},{4,0},{8,12},{12,8},{16,20},{20,16},{24,28},{28,24},{1,5},{5... | collective-permute-start | bytes 3145736 | tf_op jit(solution)/shard_map/ppermute | solution.py:646
  139.1 15.1 %collective-permute-start.32 = (bf16[1024,256]{1,0:T(8,128)(2,1)S(1)}, bf16[1024,256]{1,0:T(8,128)(2,1)S(1)}, u32[]{:S(2)}, u32[]{:S(2)}) collective-permute-start(bf16[1024,256]{1,0:T(8,128)(2,1)S(1)} %slice_bitcast_fusion.1), channel_id=1, source_target_pairs={{0,16},{4,20},{8,24},{12,28},{16,0},{20,4},{24,8},{28,12},{1,17},{... | collective-permute-start | bytes 1572872 | tf_op jit(solution)/shard_map/ppermute | solution.py:646
  140.1 14.2 %collective-permute-start.36 = (bf16[1024,256]{1,0:T(8,128)(2,1)S(1)}, bf16[1024,256]{1,0:T(8,128)(2,1)S(1)}, u32[]{:S(2)}, u32[]{:S(2)}) collective-permute-start(bf16[1024,256]{1,0:T(8,128)(2,1)S(1)} %slice_bitcast_fusion), channel_id=1, source_target_pairs={{0,8},{4,12},{8,0},{12,4},{16,24},{20,28},{24,16},{28,20},{1,9},{5... | collective-permute-start | bytes 1572872 | tf_op jit(solution)/shard_map/ppermute | solution.py:646
  154.2 3.5 %collective-permute-start.35 = (bf16[1024,256]{1,0:T(8,128)(2,1)S(1)}, bf16[1024,256]{1,0:T(8,128)(2,1)S(1)}, u32[]{:S(2)}, u32[]{:S(2)}) collective-permute-start(bf16[1024,256]{1,0:T(8,128)(2,1)S(1)} %collective-permute-done.32.refs_0_), channel_id=1, source_target_pairs={{0,4},{4,0},{8,12},{12,8},{16,20},{20,16},{24,28},{28,24},{1,5},{5... | collective-permute-start | bytes 1572872 | tf_op jit(solution)/shard_map/ppermute | solution.py:646
  154.3 3.4 %collective-permute-start.37 = (bf16[1024,256]{1,0:T(8,128)(2,1)S(1)}, bf16[1024,256]{1,0:T(8,128)(2,1)S(1)}, u32[]{:S(2)}, u32[]{:S(2)}) collective-permute-start(bf16[1024,256]{1,0:T(8,128)(2,1)S(1)} %collective-permute-done.36.refs_1_), channel_id=1, source_target_pairs={{0,4},{4,0},{8,12},{12,8},{16,20},{20,16},{24,28},{28,24},{1,5},{5... | collective-permute-start | bytes 1572872 | tf_op jit(solution)/shard_map/ppermute | solution.py:646
where the time goes:
time: 160 us
  Pallas kernels  72.6 us (45%)
  waiting for transfers between devices  54.1 us (34%)
  starting transfers between devices  31.3 us (20%)
    ppermute x38, waiting for transfers between devices, swap(): return lax.ppermute(x, axis, [(i, i ^ bit) for i in range(size)])  54.1 us
    ppermute x38, starting transfers between devices, swap(): return lax.ppermute(x, axis, [(i, i ^ bit) for i in range(size)])  31.3 us
    pallas_call x1, Pallas kernels, norm_project(): pl.pallas_call(norm_project_kernel, in_specs=[SMEM, HBM, HBM, HBM], out_s...  17.8 us
    pallas_call x4, Pallas kernels, blend(): pl.pallas_call(functools.partial(blend_kernel, tuple(masks), first, None...  15.5 us
    pallas_call x4, Pallas kernels, gradient_blocks(): pl.pallas_call(functools.partial(kernel, tuple(masks)), in_specs=in_specs...  12.9 us
    pallas_call x2, Pallas kernels, attend(): pl.pallas_call(functools.partial(attend_kernel, keep), in_specs=[SMEM] +...  9.11 us
    pallas_call x3, Pallas kernels, project(): pl.pallas_call(functools.partial(project_kernel, tuple(masks), first, las...  8.59 us
    pallas_call x1, Pallas kernels, attend_back(): pl.pallas_call(attend_back_kernel, in_specs=[SMEM] + [VMEM] * 6, out_spec...  6.25 us
  transfers between devices with their start and end apart: 38, of which 18 were waited for; matrix products, arithmetic and copies ran while one was open for 1% of the time, Pallas kernels for 38%

commit v1 on v0

--- a/solution.py
+++ b/solution.py
@@ -161,7 +161,10 @@
 def read_rows(sources, target, sems):
     if len(sources) == 1:
         return [pltpu.make_async_copy(sources[0], target, sems[0])]
-    return [pltpu.make_async_copy(sources[i], target.at[i], sems[i]) for i in (0, 1)]
+    if len(sources[0].shape) == 2:
+        return [pltpu.make_async_copy(sources[i], target.at[i], sems[i]) for i in (0, 1)]
+    half = sources[0].shape[1]
+    return [pltpu.make_async_copy(sources[h], target.at[:, pl.ds(h * half, half), :], sems[h]) for h in (0, 1)]
 
 
 def project_kernel(masks, first, last, idx_ref, x_ref, *refs):
@@ -297,7 +300,7 @@
 
     steps = k_ref.shape[0] // LEN * (k_ref.shape[1] // HD)
     start = -before_ref[0:1, 0:1] if keep else jnp.zeros((1, 1), jnp.float32)
-    margin_ref[...] = jnp.broadcast_to(lax.fori_loop(0, steps, one, start), margin_ref.shape)
+    margin_ref[...] = jnp.broadcast_to(lax.fori_loop(0, steps, one, start, unroll=min(steps, 2) if keep else 1), margin_ref.shape)
 
 
 def attend(lengths, queries, keys, values, readout, before=None):
@@ -361,7 +364,8 @@
             grad_ref[(1, *to)] = (dv[b] * scale).T.astype(jnp.bfloat16)
         return carry
 
-    lax.fori_loop(0, v_ref.shape[0] // LEN * (v_ref.shape[1] // HD), one, 0)
+    steps = v_ref.shape[0] // LEN * (v_ref.shape[1] // HD)
+    lax.fori_loop(0, steps, one, 0, unroll=min(steps, 2))
 
 
 def attend_back(lengths, queries, values, readout, probs, delta, tables):
@@ -376,48 +380,40 @@
     )(lengths, *[resident(x) for x in (queries, values, readout, probs, delta, tables)])
 
 
-def gradient_tiles(idx, mask, x_ref, cot_ref, rows, store):
+def gradient_tiles(idx, mask, x_ref, cot_ref, rows):
     cols = cot_ref.shape[1]
+    both = jnp.concatenate([cot_ref[0], cot_ref[1]], axis=0)
     tile = min(rows, 256)
-
-    def one(t, carry):
+    for t in range(rows // tile):
         col = pl.multiple_of((idx ^ mask) * rows + t * tile, tile)
-        at = pl.ds(pl.multiple_of(t * tile, tile), tile)
-        both = jnp.concatenate([cot_ref[0], cot_ref[1]], axis=0)
         out = dot(both, x_ref[:, pl.ds(col, tile)], NN)
         for i in (0, 1):
-            store(i, at, out[i * cols : (i + 1) * cols])
-        return carry
-
-    lax.fori_loop(0, rows // tile, one, 0)
+            yield i, t * tile, tile, out[i * cols : (i + 1) * cols]
 
 
 def gradient_kernel(masks, idx_ref, x_ref, cot_ref, *outs):
     outs = outs[len(outs) - len(masks) :]
     for mask, out_ref in zip(masks, outs):
-
-        def store(i, at, value):
-            out_ref[i, :, at] = value.astype(out_ref.dtype)
-
-        gradient_tiles(idx_ref[0], mask, x_ref, cot_ref, out_ref.shape[2], store)
+        for i, start, tile, value in gradient_tiles(idx_ref[0], mask, x_ref, cot_ref, out_ref.shape[2]):
+            out_ref[i, :, start : start + tile] = value.astype(out_ref.dtype)
 
 
 def merged_kernel(masks, idx_ref, x_ref, cot_ref, mine_ref, their_ref, *refs):
     count = len(masks)
     theirs_hbm, outs = refs[:count], refs[count : 3 * count]
     theirs, sem = refs[3 * count :]
+    rows = theirs.shape[3]
     copies = [pltpu.make_async_copy(theirs_hbm[n], theirs.at[n], sem.at[n]) for n in range(count)]
     for copy in copies:
         copy.start()
-    mine, their = (jnp.concatenate([jax.nn.sigmoid(-ref[0:1, :])] * 2, axis=1) for ref in (mine_ref, their_ref))
+    mine, their = (ref[0:1, :] for ref in (mine_ref, their_ref))
+    mine, their = (jax.nn.sigmoid(-x) for x in (mine, their))
     for n, mask in enumerate(masks):
         copies[n].wait()
-
-        def store(i, at, value):
-            value = value * mine + theirs[n, i, :, at].astype(jnp.float32) * their
-            outs[2 * n + i][:, at] = value.astype(outs[2 * n + i].dtype)
-
-        gradient_tiles(idx_ref[0], mask, x_ref, cot_ref, theirs.shape[3], store)
+        for i, start, tile, value in gradient_tiles(idx_ref[0], mask, x_ref, cot_ref, rows):
+            wide = lambda x: jnp.concatenate([x] * (tile // 128), axis=1)
+            value = value * wide(mine) + theirs[n, i, :, start : start + tile].astype(jnp.float32) * wide(their)
+            outs[2 * n + i][:, start : start + tile] = value.astype(outs[2 * n + i].dtype)
 
 
 def gradient_blocks(idx, normed, cot, masks, rows, merge=None, earlier=()):
@@ -454,36 +450,68 @@
     return outs if merge is None else [outs[2 * n : 2 * n + 2] for n in range(len(masks))]
 
 
-def finish_kernel(counts, *refs):
+def finish_kernel(half, counts, *refs):
     refs = list(refs)
     out_ref, square_ref = refs[-2:]
     refs = refs[:-2]
     square_ref[...] = jnp.zeros_like(square_ref)
-    cols, rows = refs[0].shape
+    _, rows, cols = out_ref.shape
     for i in (0, 1):
         terms = [refs.pop(0) for _ in range(1 + counts[i])]
         squares = jnp.zeros((1, 128), jnp.float32)
-        for c in range(cols // 128):
-            for r in range(rows // 128):
-                at = (slice(c * 128, (c + 1) * 128), slice(r * 128, (r + 1) * 128))
-                value = functools.reduce(jnp.add, [t[at].astype(jnp.float32) for t in terms])
+        for c in range(0, cols, 128):
+            for r in range(0, rows, 128):
+                at = [slice(x, x + 128) for x in (r if t.shape[1] == rows else half * rows + r for t in terms)]
+                value = functools.reduce(jnp.add, [t[c : c + 128, x].astype(jnp.float32) for t, x in zip(terms, at)])
                 squares = squares + jnp.sum(value * value, axis=0, keepdims=True)
-                out_ref[i, at[1], at[0]] = value.T.astype(jnp.bfloat16)
+                out_ref[i, r : r + 128, c : c + 128] = value.T.astype(jnp.bfloat16)
         square_ref[i : i + 1, :] = jnp.broadcast_to(jnp.sum(squares, axis=1, keepdims=True), (1, 128))
 
 
-def finish(base, arrived):
+def finish(base, arrived, half):
     args = [x for i in (0, 1) for x in (resident(base[i]), *arrived[i])]
     cols, rows = base[0].shape
     return pl.pallas_call(
-        functools.partial(finish_kernel, [len(a) for a in arrived]),
+        functools.partial(finish_kernel, half, [len(a) for a in arrived]),
         in_specs=[VMEM] * len(args),
         out_specs=[VMEM] * 2,
-        out_shape=[jax.ShapeDtypeStruct((2, rows, cols), jnp.bfloat16), jax.ShapeDtypeStruct((8, 128), jnp.float32)],
+        out_shape=[jax.ShapeDtypeStruct((2, rows // 2, cols), jnp.bfloat16), jax.ShapeDtypeStruct((8, 128), jnp.float32)],
         compiler_params=params(8),
         cost_estimate=COST,
         name="finish",
     )(*args)
+
+
+def pack_kernel(takes, *refs):
+    sources, outs, sem = refs[: 2 * len(takes)], refs[2 * len(takes) + 1 : -1], refs[-1]
+    copies = []
+    for n, i in enumerate(takes):
+        half = sources[2 * n].shape[1]
+        for h in (0, 1):
+            source, at = sources[2 * n + h], pl.ds(h * half, half)
+            if i is None:
+                copies.append(pltpu.make_async_copy(source, outs[n].at[:, at, :], sem.at[n, h]))
+            else:
+                copies.append(pltpu.make_async_copy(source.at[i], outs[n].at[at, :], sem.at[n, h]))
+    for copy in copies:
+        copy.start()
+    for copy in copies:
+        copy.wait()
+
+
+def pack(sources, takes, earlier):
+    _, half, cols = sources[0][0].shape
+    shapes = [(2, 2 * half, cols) if i is None else (2 * half, cols) for i in takes]
+    return pl.pallas_call(
+        functools.partial(pack_kernel, tuple(takes)),
+        in_specs=[HBM] * (2 * len(takes) + 1),
+        out_specs=[HBM] * len(takes),
+        out_shape=[jax.ShapeDtypeStruct(shape, jnp.bfloat16) for shape in shapes],
+        scratch_shapes=[pltpu.SemaphoreType.DMA((len(takes), 2))],
+        compiler_params=params(2),
+        cost_estimate=COST,
+        name="pack",
+    )(*[x for pair in sources for x in pair], earlier)
 
 
 def fetch_kernel(masks, idx_ref, *refs):
@@ -521,7 +549,7 @@
 def blend_kernel(masks, first, ready, idx_ref, square_ref, *refs):
     refs = list(refs)
     count = len(masks)
-    grads = [[refs.pop(0) for _ in range(1 if is_whole(m) else 2)] for m in masks]
+    grads = [[refs.pop(0) for _ in range(1 if m & 1 and is_whole(m) else 2)] for m in masks]
     if ready is None:
         weights = [[refs.pop(0) for _ in range(1 if is_whole(m) else 2)] for m in masks]
         ref_hbm = refs.pop(0)
@@ -664,7 +692,7 @@
         for i in (0, 1):
             via = link(i, m)
             source = got[m ^ via]
-            source = source[i] if len(source) == 2 else source[0][i]
+            source = source[i] if source[0].ndim == 2 else source[0][i]
             got[m][i] = swap(after(source, *earlier), via)
 
     def to_core(got, m, *earlier):
@@ -706,23 +734,26 @@
     other_blocks(order[split:], margins[1])
 
     chip_sum = {}
-    arrived = {m: [[], []] for m in chips}
+    arrived = {m: ([], []) for m in chips}
+    halves = ([[], []], [[], []])
     waiting = []
 
-    def send(m, i):
-        payload = chip_sum[m][i]
-        if arrived[m][i]:
-            payload = payload.astype(jnp.float32)
-            for term in arrived[m][i]:
-                payload = payload + term.astype(jnp.float32)
-            payload = payload.astype(jnp.bfloat16)
+    def send(m, i, half=None):
+        terms = [chip_sum[m][i], *arrived[m][i]]
+        if half is not None:
+            terms = [t[:, half * rows // 2 : (half + 1) * rows // 2] for t in terms]
+        payload = terms[0]
+        if len(terms) > 1:
+            payload = sum(t.astype(jnp.float32) for t in terms).astype(jnp.bfloat16)
         via = link(i, m)
-        arrived[m ^ via][i].append(swap(payload, via))
-        return payload
+        received = swap(payload, via)
+        if half is None:
+            arrived[m ^ via][i].append(received)
+        else:
+            halves[half][i].append(received)
 
     for masks in (order[:split], order[split:]):
-        blocks = gradient_blocks(idx, normed, cot, masks, rows, (margins, theirs))
-        chip_sum.update(zip(masks, blocks))
+        chip_sum.update(zip(masks, gradient_blocks(idx, normed, cot, masks, rows, (margins, theirs))))
         for m in masks:
             for i in (0, 1):
                 if m and not any(k ^ link(i, k) == m for k in far):
@@ -730,21 +761,38 @@
                 elif m:
                     waiting.append((m, i))
     for m, i in waiting:
-        send(m, i)
-    own, squares = finish(chip_sum[0], arrived[0])
-
-    grads = send_near(own)
+        if m in far:
+            send(m, i)
+
+    for half in (0, 1):
+        for m, i in waiting:
+            if m in near:
+                send(m, i, half)
+    grads = {m: [] for m in [0] + near}
+    parts = []
+    for half in (0, 1):
+        own, part = finish(chip_sum[0], [arrived[0][i] + halves[half][i] for i in (0, 1)], half)
+        parts.append(part)
+        grads[0].append(own)
+        for m in near:
+            grads[m].append(swap(own, m))
+    squares = parts[0] + parts[1]
     for bit in powers(tensors):
         squares = squares + swap(squares, bit, "tensor", tensors)
     squares = squares + swap(squares, 1)
-    terms = [squares] + [swap(squares, m) for m in chips[1:]]
-    while len(terms) > 1:
-        terms = [a + b for a, b in zip(terms[::2], terms[1::2])]
+    total = squares
+    for bit in powers(shards)[1:]:
+        total = total + swap(total, bit)
+    squares = total
+    two = [m for m in far if len(bits_of(m)) == 2]
+    ends = [(m, i) for m in two for i in (0, 1)]
+    whole = [0] + near
+    packed = pack([grads[m ^ link(i, m)] for m, i in ends] + [grads[m] for m in whole], [i for m, i in ends] + [None] * len(whole), total)
+    packed = dict(zip(ends + whole, packed))
     for m in far:
-        relay(grads, m, squares, *[grads[k] for k in near])
-    (squares,) = terms
-    for m in near:
-        to_core(grads, m, squares)
+        grads[m] = [swap(packed[m, i] if m in two else grads[m ^ link(i, m)][i], link(i, m)) for i in (0, 1)]
+    for m in whole:
+        grads[m | 1] = [swap(packed[m], 1)]
     new_reference, token, new_policy = blend(idx, squares, weights, grads, reference_weights, None, [0, 1])
     new_reference, token = blend(idx, squares, weights, grads, reference_weights, new_reference, [m | c for m in near for c in (0, 1)])
     if far:

time: 160 us -> 157 us (0.981)
  Pallas kernels: 72.6 us -> 67.4 us
  waiting for transfers between devices: 54.1 us -> 57.4 us
    pallas_call x4, Pallas kernels: 12.9 us -> 8.07 us  [gradient_blocks(): pl.pallas_call(functools.partial(kernel, tuple(masks)), in_specs=in_specs...]
    ppermute x38 -> x41, waiting for transfers between devices: 54.1 us -> 57.4 us  [swap(): return lax.ppermute(x, axis, [(i, i ^ bit) for i in range(size)])]
    ppermute x38 -> x41, starting transfers between devices: 31.3 us -> 30.1 us  [swap(): return lax.ppermute(x, axis, [(i, i ^ bit) for i in range(size)])]
  transfers between devices with their start and end apart: 38 -> 41, of which waited for: 18 -> 18; matrix products, arithmetic and copies ran while one was open for 1% -> 1% of each run, Pallas kernels for 38% -> 36%
where the time goes in v1:
time: 157 us
  Pallas kernels  67.4 us (43%)
  waiting for transfers between devices  57.4 us (37%)
  starting transfers between devices  30.1 us (19%)
    ppermute x41, waiting for transfers between devices, swap(): return lax.ppermute(x, axis, [(i, i ^ bit) for i in range(size)])  57.4 us
    ppermute x41, starting transfers between devices, swap(): return lax.ppermute(x, axis, [(i, i ^ bit) for i in range(size)])  30.1 us
    pallas_call x1, Pallas kernels, norm_project(): pl.pallas_call(norm_project_kernel, in_specs=[SMEM, HBM, HBM, HBM], out_s...  17.8 us
    pallas_call x4, Pallas kernels, blend(): pl.pallas_call(functools.partial(blend_kernel, tuple(masks), first, None...  15.5 us
    pallas_call x2, Pallas kernels, attend(): pl.pallas_call(functools.partial(attend_kernel, keep), in_specs=[SMEM] +...  8.86 us
    pallas_call x3, Pallas kernels, project(): pl.pallas_call(functools.partial(project_kernel, tuple(masks), first, las...  8.58 us
    pallas_call x4, Pallas kernels, gradient_blocks(): pl.pallas_call(functools.partial(kernel, tuple(masks)), in_specs=in_specs...  8.07 us
    pallas_call x1, Pallas kernels, attend_back(): pl.pallas_call(attend_back_kernel, in_specs=[SMEM] + [VMEM] * 6, out_spec...  5.72 us
  transfers between devices with their start and end apart: 41, of which 18 were waited for; matrix products, arithmetic and copies ran while one was open for 1% of the time, Pallas kernels for 36%

profile of v1, /device:TPU:0, one launch (start us, length us, event | category | flops | bytes accessed | tf_op | source)
XLA Modules:
  0.0 156.9 jit_solution(17278573920068573116)
XLA Ops:
  0.6 3.0 %collective-permute-start.1 = (bf16[2,1024,256]{2,1,0:T(8,128)(2,1)}, bf16[2,1024,256]{2,1,0:T(8,128)(2,1)S(1)}, u32[]{:S(2)}, u32[]{:S(2)}) collective-permute-start(bf16[2,1024,256]{2,1,0:T(8,128)(2,1)} %refs_3_.1), channel_id=1, source_target_pairs={{0,16},{4,20},{8,24},{12,28},{16,0},{20,4},{24,8},{28,12},{1,17},{... | collective-permute-start | bytes 3145736 | tf_op jit(solution)/shard_map/ppermute | solution.py:674
  3.7 1.5 collective-permute-start
  5.2 17.8 %norm_project.1 = (bf16[768,8192]{1,0:T(8,128)(2,1)S(1)}, bf16[768,256]{1,0:T(8,128)(2,1)S(1)}, bf16[768,256]{1,0:T(8,128)(2,1)S(1)}) custom-call(s32[1]{0:T(128)} %bitcast.idx_ref, bf16[768,8192]{1,0:T(8,128)(2,1)} %hidden_hbm.1, bf16[2,8192,256]{2,1,0:T(8,128)(2,1)} %refs_4_.1, f32[2,384,128]{2,1,0:T(8,128)} %constant.8.clone.table_hbm.refs_5_.table_ref), custom_call_target="tpu_custom_call" | custom-call | flops 1 | bytes 1 | tf_op jit(solution)/shard_map/norm_project/pallas_call | solution.py:133
  23.1 4.4 %attend.2.rest_0_ = f32[8,128]{1,0:T(8,128)S(1)} custom-call(s32[2]{0:T(128)S(1)} %copy-done.5, bf16[768,1024]{1,0:T(8,128)(2,1)S(1)} %copy-done.4, bf16[768,256]{1,0:T(8,128)(2,1)S(1)} %get-tuple-element.52.k_ref, bf16[768,256]{1,0:T(8,128)(2,1)S(1)} %get-tuple-element.53.v_ref, bf16[768,1024]{1,0:T(8,128)(2,1)S(1)} %copy-done), custom_call_target="tpu_custom_call" | custom-call | flops 1 | bytes 1 | tf_op jit(solution)/shard_map/attend/pallas_call | solution.py:318
  27.5 1.0 collective-permute-done.refs_0_.refs_6_
  28.5 0.5 collective-permute-start.5
  29.0 1.6 collective-permute-start.3
  30.6 0.6 collective-permute-start.2
  31.2 2.0 %project.3.refs_4_ = f32[2,768,256]{2,1,0:T(8,128)S(1)} custom-call(s32[1]{0:T(128)} %bitcast.idx_ref, bf16[768,8192]{1,0:T(8,128)(2,1)S(1)} %get-tuple-element.51.x_ref, bf16[2,1024,256]{2,1,0:T(8,128)(2,1)S(1)} %copy-done.2, bf16[2,1024,256]{2,1,0:T(8,128)(2,1)S(1)} %collective-permute-done.6.refs_1_.refs_4_), custom_call_target="tpu_custom_call" | custom-call | flops 1 | bytes 1 | tf_op jit(solution)/shard_map/project/pallas_call | solution.py:226
  33.3 4.1 %project.4.refs_4_ = f32[2,768,256]{2,1,0:T(8,128)S(1)} custom-call(s32[1]{0:T(128)} %bitcast.idx_ref, bf16[768,8192]{1,0:T(8,128)(2,1)S(1)} %get-tuple-element.51.x_ref, bf16[2,1024,256]{2,1,0:T(8,128)(2,1)S(1)} %collective-permute-done.refs_0_.refs_6_, bf16[2,1024,256]{2,1,0:T(8,128)(2,1)S(1)} %collective-permute-done.4.refs_1_.refs_7_, ...), custom_call_target="tpu_custom_call" | custom-call | flops 1 | bytes 1 | tf_op jit(solution)/shard_map/project/pallas_call | solution.py:226
  37.4 5.5 %collective-permute-done.3.refs_1_ = bf16[1024,256]{1,0:T(8,128)(2,1)S(1)} collective-permute-done((bf16[1024,256]{1,0:T(8,128)(2,1)S(1)}, bf16[1024,256]{1,0:T(8,128)(2,1)S(1)}, u32[]{:S(2)}, u32[]{:S(2)}) %collective-permute-start.3) | collective-permute-done | bytes 524320 | tf_op jit(solution)/shard_map/ppermute | solution.py:674
  42.9 1.3 collective-permute-done.2.refs_0_
  44.3 0.5 collective-permute-start.8
  44.8 1.4 collective-permute-done.7.refs_2_
  46.2 0.7 collective-permute-done.8.refs_3_
  46.9 2.4 %project.5 = (bf16[768,256]{1,0:T(8,128)(2,1)S(1)}, bf16[768,256]{1,0:T(8,128)(2,1)S(1)}) custom-call(s32[1]{0:T(128)} %bitcast.idx_ref, bf16[768,8192]{1,0:T(8,128)(2,1)S(1)} %get-tuple-element.51.x_ref, bf16[1024,256]{1,0:T(8,128)(2,1)S(1)} %collective-permute-done.2.refs_0_, bf16[1024,256]{1,0:T(8,128)(2,1)S(1)} %collective-permute-done.3.refs_1_, ...), custom_call_target="tpu_custom_call" | custom-call | flops 1 | bytes 1 | tf_op jit(solution)/shard_map/project/pallas_call | solution.py:226
  49.4 4.4 %attend.3 = (f32[8,128]{1,0:T(8,128)S(1)}, bf16[2,2,768,512]{3,2,1,0:T(8,128)(2,1)S(1)}, f32[2,2,3,512]{3,2,1,0:T(4,128)S(1)}) custom-call(s32[2]{0:T(128)S(1)} %copy-done.5, bf16[768,1024]{1,0:T(8,128)(2,1)S(1)} %copy-done.1, bf16[768,256]{1,0:T(8,128)(2,1)S(1)} %get-tuple-element.61.k_ref, bf16[768,256]{1,0:T(8,128)(2,1)S(1)} %get-tuple-element.60.v_ref, ...), custom_call_target="tpu_custom_call" | custom-call | flops 1 | bytes 1 | tf_op jit(solution)/shard_map/attend/pallas_call | solution.py:318
  53.8 3.7 %collective-permute-start.11 = (f32[8,128]{1,0:T(8,128)S(1)}, f32[8,128]{1,0:T(8,128)S(1)}, u32[]{:S(2)}, u32[]{:S(2)}) collective-permute-start(f32[8,128]{1,0:T(8,128)S(1)} %get-tuple-element.64), channel_id=1, source_target_pairs={{0,3},{1,2},{2,1},{3,0},{4,7},{5,6},{6,5},{7,4},{8,11},{9,10},{10,... | collective-permute-start | bytes 12296 | tf_op jit(solution)/shard_map/ppermute | solution.py:674
  57.5 0.8 collective-permute-start.9
  58.3 5.7 %attend_back.1.cot_ref = bf16[2,256,768]{2,1,0:T(8,128)(2,1)S(1)} custom-call(s32[2]{0:T(128)S(1)} %copy-done.5, bf16[768,1024]{1,0:T(8,128)(2,1)S(1)} %copy-done.1, bf16[768,256]{1,0:T(8,128)(2,1)S(1)} %get-tuple-element.60.v_ref, bf16[768,1024]{1,0:T(8,128)(2,1)S(1)} %copy-done, bf16[2,2,768,512]{3,2,1,0:T(8,128)(2,1)S(1)} %get-tuple-element.62.prob_ref, ...), custom_call_target="tpu_custom_call" | custom-call | flops 1 | bytes 1 | tf_op jit(solution)/shard_map/attend_back/pallas_call | solution.py:372
  64.0 1.0 gradient_block.2
  65.1 0.5 collective-permute-start.12
  65.6 2.2 %collective-permute-done.12.outs_0_.their_ref = f32[8,128]{1,0:T(8,128)S(1)} collective-permute-done((f32[8,128]{1,0:T(8,128)S(1)}, f32[8,128]{1,0:T(8,128)S(1)}, u32[]{:S(2)}, u32[]{:S(2)}) %collective-permute-start.12) | collective-permute-done | bytes 4128 | tf_op jit(solution)/shard_map/ppermute | solution.py:674
  67.8 2.7 %gradient_block.3 = (bf16[2,256,1024]{2,1,0:T(8,128)(2,1)S(1)}, bf16[2,256,1024]{2,1,0:T(8,128)(2,1)S(1)}, bf16[2,256,1024]{2,1,0:T(8,128)(2,1)S(1)}) custom-call(s32[1]{0:T(128)} %bitcast.idx_ref, bf16[768,8192]{1,0:T(8,128)(2,1)S(1)} %get-tuple-element.51.x_ref, bf16[2,256,768]{2,1,0:T(8,128)(2,1)S(1)} %attend_back.1.cot_ref, ...), custom_call_target="tpu_custom_call" | custom-call | flops 1 | bytes 1 | tf_op jit(solution)/shard_map/gradient_block/pallas_call | solution.py:440
  70.7 0.4 collective-permute-start.14
  71.2 1.1 merged_block.3
  72.3 0.6 collective-permute-start.21
  73.3 1.4 collective-permute-done.14.refs_1_
  74.7 1.5 collective-permute-done.15.refs_2_
  76.2 3.3 %merged_block.2 = (bf16[256,1024]{1,0:T(8,128)(2,1)S(1)}, bf16[256,1024]{1,0:T(8,128)(2,1)S(1)}, bf16[256,1024]{1,0:T(8,128)(2,1)S(1)}, bf16[256,1024]{1,0:T(8,1...) custom-call(s32[1]{0:T(128)} %bitcast.idx_ref, bf16[768,8192]{1,0:T(8,128)(2,1)S(1)} %get-tuple-element.51.x_ref, ...), custom_call_target="tpu_custom_call" | custom-call | flops 1 | bytes 1 | tf_op jit(solution)/shard_map/merged_block/pallas_call | solution.py:440
  79.5 0.6 collective-permute-start.16
  80.1 0.4 collective-permute-start.20
  80.5 6.6 %collective-permute-done.21 = bf16[256,1024]{1,0:T(8,128)(2,1)S(1)} collective-permute-done((bf16[256,1024]{1,0:T(8,128)(2,1)S(1)}, bf16[256,1024]{1,0:T(8,128)(2,1)S(1)}, u32[]{:S(2)}, u32[]{:S(2)}) %collective-permute-start.21) | collective-permute-done | bytes 524320 | tf_op jit(solution)/shard_map/ppermute | solution.py:674
  87.3 0.6 collective-permute-start.24
  88.0 1.4 collective-permute-start.23
  89.4 0.7 collective-permute-start.22
  90.1 8.8 %collective-permute-done.16.refs_1_ = bf16[256,1024]{1,0:T(8,128)(2,1)S(1)} collective-permute-done((bf16[256,1024]{1,0:T(8,128)(2,1)S(1)}, bf16[256,1024]{1,0:T(8,128)(2,1)S(1)}, u32[]{:S(2)}, u32[]{:S(2)}) %collective-permute-start.16) | collective-permute-done | bytes 524320 | tf_op jit(solution)/shard_map/ppermute | solution.py:674
  98.9 1.5 collective-permute-start.19
  100.4 4.1 %collective-permute-done.24.refs_5_ = bf16[256,512]{1,0:T(8,128)(2,1)S(1)} collective-permute-done((bf16[256,512]{1,0:T(8,128)(2,1)S(1)}, bf16[256,512]{1,0:T(8,128)(2,1)S(1)}, u32[]{:S(2)}, u32[]{:S(2)}) %collective-permute-start.24) | collective-permute-done | bytes 262176 | tf_op jit(solution)/shard_map/ppermute | solution.py:674
  104.9 0.4 collective-permute-start.33
  105.3 1.6 %collective-permute-start.31 = (bf16[2,512,256]{2,1,0:T(8,128)(2,1)S(1)}, bf16[2,512,256]{2,1,0:T(8,128)(2,1)S(1)}, u32[]{:S(2)}, u32[]{:S(2)}) collective-permute-start(bf16[2,512,256]{2,1,0:T(8,128)(2,1)S(1)} %get-tuple-element.83.refs_5_.refs_1_), channel_id=1, source_target_pairs={{0,8},{4,12},{8,0},{12,4},{16,24},{20,28},{24,16},{28,20},{1,9},{5... | collective-permute-start | bytes 1572872 | tf_op jit(solution)/shard_map/ppermute | solution.py:674
  107.0 3.2 %collective-permute-done.22.refs_5_ = bf16[256,512]{1,0:T(8,128)(2,1)S(1)} collective-permute-done((bf16[256,512]{1,0:T(8,128)(2,1)S(1)}, bf16[256,512]{1,0:T(8,128)(2,1)S(1)}, u32[]{:S(2)}, u32[]{:S(2)}) %collective-permute-start.22) | collective-permute-done | bytes 262176 | tf_op jit(solution)/shard_map/ppermute | solution.py:674
  110.5 0.4 collective-permute-start.32
  111.0 1.6 %collective-permute-start.30 = (bf16[2,512,256]{2,1,0:T(8,128)(2,1)S(1)}, bf16[2,512,256]{2,1,0:T(8,128)(2,1)S(1)}, u32[]{:S(2)}, u32[]{:S(2)}) collective-permute-start(bf16[2,512,256]{2,1,0:T(8,128)(2,1)S(1)} %get-tuple-element.82.refs_4_.refs_0_), channel_id=1, source_target_pairs={{0,8},{4,12},{8,0},{12,4},{16,24},{20,28},{24,16},{28,20},{1,9},{5... | collective-permute-start | bytes 1572872 | tf_op jit(solution)/shard_map/ppermute | solution.py:674
  112.6 1.2 collective-permute-start.25
  113.8 2.4 %collective-permute-done.25 = f32[8,128]{1,0:T(8,128)S(1)} collective-permute-done((f32[8,128]{1,0:T(8,128)S(1)}, f32[8,128]{1,0:T(8,128)S(1)}, u32[]{:S(2)}, u32[]{:S(2)}) %collective-permute-start.25) | collective-permute-done | bytes 4128 | tf_op jit(solution)/shard_map/ppermute | solution.py:674
  116.2 2.2 %collective-permute-start.26 = (f32[8,128]{1,0:T(8,128)S(1)}, f32[8,128]{1,0:T(8,128)S(1)}, u32[]{:S(2)}, u32[]{:S(2)}) collective-permute-start(f32[8,128]{1,0:T(8,128)S(1)} %add.47), channel_id=1, source_target_pairs={{0,2},{1,3},{2,0},{3,1},{4,6},{5,7},{6,4},{7,5},{8,10},{9,11},{10,... | collective-permute-start | bytes 12296 | tf_op jit(solution)/shard_map/ppermute | solution.py:674
  118.3 2.4 %collective-permute-done.26 = f32[8,128]{1,0:T(8,128)S(1)} collective-permute-done((f32[8,128]{1,0:T(8,128)S(1)}, f32[8,128]{1,0:T(8,128)S(1)}, u32[]{:S(2)}, u32[]{:S(2)}) %collective-permute-start.26) | collective-permute-done | bytes 4128 | tf_op jit(solution)/shard_map/ppermute | solution.py:674
  120.7 1.2 collective-permute-done.27
  121.9 0.4 collective-permute-start.28
  122.3 9.3 %collective-permute-done.28 = f32[8,128]{1,0:T(8,128)S(1)} collective-permute-done((f32[8,128]{1,0:T(8,128)S(1)}, f32[8,128]{1,0:T(8,128)S(1)}, u32[]{:S(2)}, u32[]{:S(2)}) %collective-permute-start.28) | collective-permute-done | bytes 4128 | tf_op jit(solution)/shard_map/ppermute | solution.py:674
  131.6 0.5 collective-permute-start.29
  132.1 3.1 %collective-permute-done.29 = f32[8,128]{1,0:T(8,128)S(1)} collective-permute-done((f32[8,128]{1,0:T(8,128)S(1)}, f32[8,128]{1,0:T(8,128)S(1)}, u32[]{:S(2)}, u32[]{:S(2)}) %collective-permute-start.29) | collective-permute-done | bytes 4128 | tf_op jit(solution)/shard_map/ppermute | solution.py:674
  135.2 0.4 pack.1
  135.7 0.5 collective-permute-start.36
  136.3 0.5 collective-permute-start.39
  137.2 1.2 collective-permute-done.34.refs_2_
  138.4 4.5 %blend.4 = (bf16[2,8192,256]{2,1,0:T(8,128)(2,1)}, f32[8,128]{1,0:T(8,128)}, bf16[2,1024,256]{2,1,0:T(8,128)(2,1)}) custom-call(s32[1]{0:T(128)} %bitcast.idx_ref, f32[8,128]{1,0:T(8,128)S(1)} %add.51.refs_10_.square_ref, bf16[2,512,256]{2,1,0:T(8,128)(2,1)S(1)} %get-tuple-element.82.refs_4_.refs_0_, ...), custom_call_target="tpu_custom_call" | custom-call | flops 1 | bytes 1 | tf_op jit(solution)/shard_map/blend/pallas_call | solution.py:647
  142.9 6.3 %blend.5 = (bf16[2,8192,256]{2,1,0:T(8,128)(2,1)}, f32[8,128]{1,0:T(8,128)S(1)}) custom-call(s32[1]{0:T(128)} %bitcast.idx_ref, f32[8,128]{1,0:T(8,128)S(1)} %add.51.refs_10_.square_ref, bf16[2,512,256]{2,1,0:T(8,128)(2,1)S(1)} %collective-permute-done.30.refs_0_.refs_6_, ...), custom_call_target="tpu_custom_call", output_to_operand_aliasing={{0}: (13, {})} | custom-call | flops 1 | bytes 1 | tf_op jit(solution)/shard_map/blend/pallas_call | solution.py:647
  149.2 1.7 %fetch.1 = (bf16[2,2,1024,256]{3,2,1,0:T(8,128)(2,1)S(1)}, bf16[2,2,1024,256]{3,2,1,0:T(8,128)(2,1)S(1)}) custom-call(s32[1]{0:T(128)} %bitcast.idx_ref, bf16[1024,256]{1,0:T(8,128)(2,1)S(1)} %collective-permute-done.2.refs_0_, bf16[1024,256]{1,0:T(8,128)(2,1)S(1)} %collective-permute-done.3.refs_1_, bf16[1024,256]{1,0:T(8,128)(2,1)S(1)} %collective-permute-done.7.refs_2_, ...), custom_call_target="tpu_custom_call" | custom-call | flops 1 | bytes 1 | tf_op jit(solution)/shard_map/fetch/pallas_call | solution.py:537
  151.1 0.4 collective-permute-start.40
  151.5 0.5 slice.43
  152.0 2.4 %blend.6 = (bf16[2,8192,256]{2,1,0:T(8,128)(2,1)}, f32[8,128]{1,0:T(8,128)}) custom-call(s32[1]{0:T(128)} %bitcast.idx_ref, f32[8,128]{1,0:T(8,128)S(1)} %add.51.refs_10_.square_ref, bf16[1024,256]{1,0:T(8,128)(2,1)S(1)} %collective-permute-done.35.refs_0_, bf16[1024,256]{1,0:T(8,128)(2,1)S(1)} %collective-permute-done.39.refs_1_, ...), custom_call_target="tpu_custom_call", output_to_operand_aliasing={{0}: (6, {})} | custom-call | flops 1 | bytes 1 | tf_op jit(solution)/shard_map/blend/pallas_call | solution.py:647
  154.4 2.4 %blend.7 = (bf16[2,8192,256]{2,1,0:T(8,128)(2,1)}, f32[8,128]{1,0:T(8,128)}) custom-call(s32[1]{0:T(128)} %bitcast.idx_ref, f32[8,128]{1,0:T(8,128)S(1)} %add.51.refs_10_.square_ref, bf16[1024,256]{1,0:T(8,128)(2,1)S(1)} %collective-permute-done.38.refs_0_, bf16[1024,256]{1,0:T(8,128)(2,1)S(1)} %collective-permute-done.40.refs_1_, ...), custom_call_target="tpu_custom_call", output_to_operand_aliasing={{0}: (6, {})} | custom-call | flops 1 | bytes 1 | tf_op jit(solution)/shard_map/blend/pallas_call | solution.py:647
  (61 shorter events, 2.7 us)
Async XLA Ops:
  0.6 26.9 %collective-permute-start.1 = (bf16[2,1024,256]{2,1,0:T(8,128)(2,1)}, bf16[2,1024,256]{2,1,0:T(8,128)(2,1)S(1)}, u32[]{:S(2)}, u32[]{:S(2)}) collective-permute-start(bf16[2,1024,256]{2,1,0:T(8,128)(2,1)} %refs_3_.1), channel_id=1, source_target_pairs={{0,16},{4,20},{8,24},{12,28},{16,0},{20,4},{24,8},{28,12},{1,17},{... | collective-permute-start | bytes 3145736 | tf_op jit(solution)/shard_map/ppermute | solution.py:674
  3.7 24.8 %collective-permute-start = (bf16[2,1024,256]{2,1,0:T(8,128)(2,1)}, bf16[2,1024,256]{2,1,0:T(8,128)(2,1)S(1)}, u32[]{:S(2)}, u32[]{:S(2)}) collective-permute-start(bf16[2,1024,256]{2,1,0:T(8,128)(2,1)} %refs_3_.1), channel_id=1, source_target_pairs={{0,8},{4,12},{8,0},{12,4},{16,24},{20,28},{24,16},{28,20},{1,9},{5... | collective-permute-start | bytes 3145736 | tf_op jit(solution)/shard_map/ppermute | solution.py:674
  5.2 26.1 %collective-permute-start.6 = (bf16[2,1024,256]{2,1,0:T(8,128)(2,1)}, bf16[2,1024,256]{2,1,0:T(8,128)(2,1)S(1)}, u32[]{:S(2)}, u32[]{:S(2)}) collective-permute-start(bf16[2,1024,256]{2,1,0:T(8,128)(2,1)} %refs_3_.1), channel_id=1, source_target_pairs={{0,4},{4,0},{8,12},{12,8},{16,20},{20,16},{24,28},{28,24},{1,5},{5... | collective-permute-start | bytes 3145736 | tf_op jit(solution)/shard_map/ppermute | solution.py:674
  5.2 17.9 %copy-start = (bf16[768,1024]{1,0:T(8,128)(2,1)S(1)}, bf16[768,1024]{1,0:T(8,128)(2,1)}, u32[]{:S(2)}) copy-start(bf16[768,1024]{1,0:T(8,128)(2,1)} %ro_ref.5) | copy-start | bytes 4718596
  5.2 17.9 %copy-start.4 = (bf16[768,1024]{1,0:T(8,128)(2,1)S(1)}, bf16[768,1024]{1,0:T(8,128)(2,1)}, u32[]{:S(2)}) copy-start(bf16[768,1024]{1,0:T(8,128)(2,1)} %q_ref.3) | copy-start | bytes 4718596
  5.2 17.9 %copy-start.5 = (s32[2]{0:T(128)S(1)}, s32[2]{0:T(128)}, u32[]{:S(2)}) copy-start(s32[2]{0:T(128)} %len_ref.5) | copy-start | bytes 28
  23.0 8.2 %copy-start.2 = (bf16[2,1024,256]{2,1,0:T(8,128)(2,1)S(1)}, bf16[2,1024,256]{2,1,0:T(8,128)(2,1)}, u32[]{:S(2)}) copy-start(bf16[2,1024,256]{2,1,0:T(8,128)(2,1)} %refs_3_.1) | copy-start | bytes 3145732
  28.5 4.8 %collective-permute-start.4 = (bf16[2,1024,256]{2,1,0:T(8,128)(2,1)S(1)}, bf16[2,1024,256]{2,1,0:T(8,128)(2,1)S(1)}, u32[]{:S(2)}, u32[]{:S(2)}) collective-permute-start(bf16[2,1024,256]{2,1,0:T(8,128)(2,1)S(1)} %collective-permute-done.refs_0_.refs_6_), channel_id=1, source_target_pairs={{0,4},{4,0},{8,12},{12,8},{16,20},{20,16},{24,28},{28,24},{1,5},{5... | collective-permute-start | bytes 3145736 | tf_op jit(solution)/shard_map/ppermute | solution.py:674
  28.5 4.8 %collective-permute-start.5 = (bf16[2,1024,256]{2,1,0:T(8,128)(2,1)S(1)}, bf16[2,1024,256]{2,1,0:T(8,128)(2,1)S(1)}, u32[]{:S(2)}, u32[]{:S(2)}) collective-permute-start(bf16[2,1024,256]{2,1,0:T(8,128)(2,1)S(1)} %collective-permute-done.1.refs_2_.refs_8_), channel_id=1, source_target_pairs={{0,4},{4,0},{8,12},{12,8},{16,20},{20,16},{24,28},{28,24},{1,5},{5... | collective-permute-start | bytes 3145736 | tf_op jit(solution)/shard_map/ppermute | solution.py:674
  29.0 13.9 %collective-permute-start.3 = (bf16[1024,256]{1,0:T(8,128)(2,1)S(1)}, bf16[1024,256]{1,0:T(8,128)(2,1)S(1)}, u32[]{:S(2)}, u32[]{:S(2)}) collective-permute-start(bf16[1024,256]{1,0:T(8,128)(2,1)S(1)} %slice_bitcast_fusion), channel_id=1, source_target_pairs={{0,8},{4,12},{8,0},{12,4},{16,24},{20,28},{24,16},{28,20},{1,9},{5... | collective-permute-start | bytes 1572872 | tf_op jit(solution)/shard_map/ppermute | solution.py:674
  30.6 13.6 %collective-permute-start.2 = (bf16[1024,256]{1,0:T(8,128)(2,1)S(1)}, bf16[1024,256]{1,0:T(8,128)(2,1)S(1)}, u32[]{:S(2)}, u32[]{:S(2)}) collective-permute-start(bf16[1024,256]{1,0:T(8,128)(2,1)S(1)} %slice_bitcast_fusion.1), channel_id=1, source_target_pairs={{0,16},{4,20},{8,24},{12,28},{16,0},{20,4},{24,8},{28,12},{1,17},{... | collective-permute-start | bytes 1572872 | tf_op jit(solution)/shard_map/ppermute | solution.py:674
  37.4 12.0 %copy-start.1 = (bf16[768,1024]{1,0:T(8,128)(2,1)S(1)}, bf16[768,1024]{1,0:T(8,128)(2,1)}, u32[]{:S(2)}) copy-start(bf16[768,1024]{1,0:T(8,128)(2,1)} %q_ref.5) | copy-start | bytes 4718596
  44.3 1.9 %collective-permute-start.7 = (bf16[1024,256]{1,0:T(8,128)(2,1)S(1)}, bf16[1024,256]{1,0:T(8,128)(2,1)S(1)}, u32[]{:S(2)}, u32[]{:S(2)}) collective-permute-start(bf16[1024,256]{1,0:T(8,128)(2,1)S(1)} %collective-permute-done.2.refs_0_), channel_id=1, source_target_pairs={{0,4},{4,0},{8,12},{12,8},{16,20},{20,16},{24,28},{28,24},{1,5},{5... | collective-permute-start | bytes 1572872 | tf_op jit(solution)/shard_map/ppermute | solution.py:674
  44.3 2.7 %collective-permute-start.8 = (bf16[1024,256]{1,0:T(8,128)(2,1)S(1)}, bf16[1024,256]{1,0:T(8,128)(2,1)S(1)}, u32[]{:S(2)}, u32[]{:S(2)}) collective-permute-start(bf16[1024,256]{1,0:T(8,128)(2,1)S(1)} %collective-permute-done.3.refs_1_), channel_id=1, source_target_pairs={{0,4},{4,0},{8,12},{12,8},{16,20},{20,16},{24,28},{28,24},{1,5},{5... | collective-permute-start | bytes 1572872 | tf_op jit(solution)/shard_map/ppermute | solution.py:674
  49.4 8.9 %copy-start.3 = (f32[2,384,128]{2,1,0:T(8,128)S(1)}, f32[2,384,128]{2,1,0:T(8,128)}, u32[]{:S(2)}) copy-start(f32[2,384,128]{2,1,0:T(8,128)} %constant.8.clone.table_hbm.refs_5_.table_ref) | copy-start | bytes 1179652
  53.8 10.2 %collective-permute-start.11 = (f32[8,128]{1,0:T(8,128)S(1)}, f32[8,128]{1,0:T(8,128)S(1)}, u32[]{:S(2)}, u32[]{:S(2)}) collective-permute-start(f32[8,128]{1,0:T(8,128)S(1)} %get-tuple-element.64), channel_id=1, source_target_pairs={{0,3},{1,2},{2,1},{3,0},{4,7},{5,6},{6,5},{7,4},{8,11},{9,10},{10,... | collective-permute-start | bytes 12296 | tf_op jit(solution)/shard_map/ppermute | solution.py:674
  57.5 6.5 %collective-permute-start.10 = (f32[8,128]{1,0:T(8,128)S(1)}, f32[8,128]{1,0:T(8,128)S(1)}, u32[]{:S(2)}, u32[]{:S(2)}) collective-permute-start(f32[8,128]{1,0:T(8,128)S(1)} %get-tuple-element.64), channel_id=1, source_target_pairs={{0,2},{1,3},{2,0},{3,1},{4,6},{5,7},{6,4},{7,5},{8,10},{9,11},{10,... | collective-permute-start | bytes 12296 | tf_op jit(solution)/shard_map/ppermute | solution.py:674
  57.5 6.5 %collective-permute-start.9 = (f32[8,128]{1,0:T(8,128)S(1)}, f32[8,128]{1,0:T(8,128)S(1)}, u32[]{:S(2)}, u32[]{:S(2)}) collective-permute-start(f32[8,128]{1,0:T(8,128)S(1)} %get-tuple-element.64), channel_id=1, source_target_pairs={{0,1},{1,0},{2,3},{3,2},{4,5},{5,4},{6,7},{7,6},{8,9},{9,8},{10,11... | collective-permute-start | bytes 12296 | tf_op jit(solution)/shard_map/ppermute | solution.py:674
  65.1 6.1 %collective-permute-start.17 = (bf16[2,256,1024]{2,1,0:T(8,128)(2,1)S(1)}, bf16[2,256,1024]{2,1,0:T(8,128)(2,1)S(1)}, u32[]{:S(2)}, u32[]{:S(2)}) collective-permute-start(bf16[2,256,1024]{2,1,0:T(8,128)(2,1)S(1)} %gradient_block.2), channel_id=1, source_target_pairs={{0,4},{4,0},{8,12},{12,8},{16,20},{20,16},{24,28},{28,24},{1,5},{5... | collective-permute-start | bytes 3145736 | tf_op jit(solution)/shard_map/ppermute | solution.py:674
  65.1 2.7 %collective-permute-start.12 = (f32[8,128]{1,0:T(8,128)S(1)}, f32[8,128]{1,0:T(8,128)S(1)}, u32[]{:S(2)}, u32[]{:S(2)}) collective-permute-start(f32[8,128]{1,0:T(8,128)S(1)} %add_add_fusion.outs_0_.mine_ref), channel_id=1, source_target_pairs={{0,4},{4,0},{8,12},{12,8},{16,20},{20,16},{24,28},{28,24},{1,5},{5... | collective-permute-start | bytes 12296 | tf_op jit(solution)/shard_map/ppermute | solution.py:674
  70.5 2.8 %collective-permute-start.13 = (bf16[2,256,1024]{2,1,0:T(8,128)(2,1)S(1)}, bf16[2,256,1024]{2,1,0:T(8,128)(2,1)S(1)}, u32[]{:S(2)}, u32[]{:S(2)}) collective-permute-start(bf16[2,256,1024]{2,1,0:T(8,128)(2,1)S(1)} %get-tuple-element.69), channel_id=1, source_target_pairs={{0,4},{4,0},{8,12},{12,8},{16,20},{20,16},{24,28},{28,24},{1,5},{5... | collective-permute-start | bytes 3145736 | tf_op jit(solution)/shard_map/ppermute | solution.py:674
  70.7 4.0 %collective-permute-start.14 = (bf16[2,256,1024]{2,1,0:T(8,128)(2,1)S(1)}, bf16[2,256,1024]{2,1,0:T(8,128)(2,1)S(1)}, u32[]{:S(2)}, u32[]{:S(2)}) collective-permute-start(bf16[2,256,1024]{2,1,0:T(8,128)(2,1)S(1)} %get-tuple-element.70), channel_id=1, source_target_pairs={{0,4},{4,0},{8,12},{12,8},{16,20},{20,16},{24,28},{28,24},{1,5},{5... | collective-permute-start | bytes 3145736 | tf_op jit(solution)/shard_map/ppermute | solution.py:674
  71.0 5.1 %collective-permute-start.15 = (bf16[2,256,1024]{2,1,0:T(8,128)(2,1)S(1)}, bf16[2,256,1024]{2,1,0:T(8,128)(2,1)S(1)}, u32[]{:S(2)}, u32[]{:S(2)}) collective-permute-start(bf16[2,256,1024]{2,1,0:T(8,128)(2,1)S(1)} %get-tuple-element.71), channel_id=1, source_target_pairs={{0,4},{4,0},{8,12},{12,8},{16,20},{20,16},{24,28},{28,24},{1,5},{5... | collective-permute-start | bytes 3145736 | tf_op jit(solution)/shard_map/ppermute | solution.py:674
  72.3 14.8 %collective-permute-start.21 = (bf16[256,1024]{1,0:T(8,128)(2,1)S(1)}, bf16[256,1024]{1,0:T(8,128)(2,1)S(1)}, u32[]{:S(2)}, u32[]{:S(2)}) collective-permute-start(bf16[256,1024]{1,0:T(8,128)(2,1)S(1)} %get-tuple-element.79), channel_id=1, source_target_pairs={{0,8},{4,12},{8,0},{12,4},{16,24},{20,28},{24,16},{28,20},{1,9},{5... | collective-permute-start | bytes 1572872 | tf_op jit(solution)/shard_map/ppermute | solution.py:674
  72.9 14.9 %collective-permute-start.18 = (bf16[256,1024]{1,0:T(8,128)(2,1)S(1)}, bf16[256,1024]{1,0:T(8,128)(2,1)S(1)}, u32[]{:S(2)}, u32[]{:S(2)}) collective-permute-start(bf16[256,1024]{1,0:T(8,128)(2,1)S(1)} %get-tuple-element.75), channel_id=1, source_target_pairs={{0,16},{4,20},{8,24},{12,28},{16,0},{20,4},{24,8},{28,12},{1,17},{... | collective-permute-start | bytes 1572872 | tf_op jit(solution)/shard_map/ppermute | solution.py:674
  79.5 19.4 %collective-permute-start.16 = (bf16[256,1024]{1,0:T(8,128)(2,1)S(1)}, bf16[256,1024]{1,0:T(8,128)(2,1)S(1)}, u32[]{:S(2)}, u32[]{:S(2)}) collective-permute-start(bf16[256,1024]{1,0:T(8,128)(2,1)S(1)} %get-tuple-element.73), channel_id=1, source_target_pairs={{0,16},{4,20},{8,24},{12,28},{16,0},{20,4},{24,8},{28,12},{1,17},{... | collective-permute-start | bytes 1572872 | tf_op jit(solution)/shard_map/ppermute | solution.py:674
  80.1 20.3 %collective-permute-start.20 = (bf16[256,1024]{1,0:T(8,128)(2,1)S(1)}, bf16[256,1024]{1,0:T(8,128)(2,1)S(1)}, u32[]{:S(2)}, u32[]{:S(2)}) collective-permute-start(bf16[256,1024]{1,0:T(8,128)(2,1)S(1)} %get-tuple-element.77), channel_id=1, source_target_pairs={{0,8},{4,12},{8,0},{12,4},{16,24},{20,28},{24,16},{28,20},{1,9},{5... | collective-permute-start | bytes 1572872 | tf_op jit(solution)/shard_map/ppermute | solution.py:674
  87.3 17.3 %collective-permute-start.24 = (bf16[256,512]{1,0:T(8,128)(2,1)S(1)}, bf16[256,512]{1,0:T(8,128)(2,1)S(1)}, u32[]{:S(2)}, u32[]{:S(2)}) collective-permute-start(bf16[256,512]{1,0:T(8,128)(2,1)S(1)} %get-tuple-element.99), channel_id=1, source_target_pairs={{0,16},{4,20},{8,24},{12,28},{16,0},{20,4},{24,8},{28,12},{1,17},{... | collective-permute-start | bytes 786440 | tf_op jit(solution)/shard_map/ppermute | solution.py:674
  88.0 16.6 %collective-permute-start.23 = (bf16[256,512]{1,0:T(8,128)(2,1)S(1)}, bf16[256,512]{1,0:T(8,128)(2,1)S(1)}, u32[]{:S(2)}, u32[]{:S(2)}) collective-permute-start(bf16[256,512]{1,0:T(8,128)(2,1)S(1)} %get-tuple-element.101), channel_id=1, source_target_pairs={{0,8},{4,12},{8,0},{12,4},{16,24},{20,28},{24,16},{28,20},{1,9},{5... | collective-permute-start | bytes 786440 | tf_op jit(solution)/shard_map/ppermute | solution.py:674
  89.4 20.8 %collective-permute-start.22 = (bf16[256,512]{1,0:T(8,128)(2,1)S(1)}, bf16[256,512]{1,0:T(8,128)(2,1)S(1)}, u32[]{:S(2)}, u32[]{:S(2)}) collective-permute-start(bf16[256,512]{1,0:T(8,128)(2,1)S(1)} %get-tuple-element.100), channel_id=1, source_target_pairs={{0,16},{4,20},{8,24},{12,28},{16,0},{20,4},{24,8},{28,12},{1,17},{... | collective-permute-start | bytes 786440 | tf_op jit(solution)/shard_map/ppermute | solution.py:674
  98.9 11.2 %collective-permute-start.19 = (bf16[256,512]{1,0:T(8,128)(2,1)S(1)}, bf16[256,512]{1,0:T(8,128)(2,1)S(1)}, u32[]{:S(2)}, u32[]{:S(2)}) collective-permute-start(bf16[256,512]{1,0:T(8,128)(2,1)S(1)} %get-tuple-element.102), channel_id=1, source_target_pairs={{0,8},{4,12},{8,0},{12,4},{16,24},{20,28},{24,16},{28,20},{1,9},{5... | collective-permute-start | bytes 786440 | tf_op jit(solution)/shard_map/ppermute | solution.py:674
  104.9 30.3 %collective-permute-start.33 = (bf16[2,512,256]{2,1,0:T(8,128)(2,1)S(1)}, bf16[2,512,256]{2,1,0:T(8,128)(2,1)S(1)}, u32[]{:S(2)}, u32[]{:S(2)}) collective-permute-start(bf16[2,512,256]{2,1,0:T(8,128)(2,1)S(1)} %get-tuple-element.83.refs_5_.refs_1_), channel_id=1, source_target_pairs={{0,16},{4,20},{8,24},{12,28},{16,0},{20,4},{24,8},{28,12},{1,17},{... | collective-permute-start | bytes 1572872 | tf_op jit(solution)/shard_map/ppermute | solution.py:674
  105.3 29.9 %collective-permute-start.31 = (bf16[2,512,256]{2,1,0:T(8,128)(2,1)S(1)}, bf16[2,512,256]{2,1,0:T(8,128)(2,1)S(1)}, u32[]{:S(2)}, u32[]{:S(2)}) collective-permute-start(bf16[2,512,256]{2,1,0:T(8,128)(2,1)S(1)} %get-tuple-element.83.refs_5_.refs_1_), channel_id=1, source_target_pairs={{0,8},{4,12},{8,0},{12,4},{16,24},{20,28},{24,16},{28,20},{1,9},{5... | collective-permute-start | bytes 1572872 | tf_op jit(solution)/shard_map/ppermute | solution.py:674
  110.5 24.7 %collective-permute-start.32 = (bf16[2,512,256]{2,1,0:T(8,128)(2,1)S(1)}, bf16[2,512,256]{2,1,0:T(8,128)(2,1)S(1)}, u32[]{:S(2)}, u32[]{:S(2)}) collective-permute-start(bf16[2,512,256]{2,1,0:T(8,128)(2,1)S(1)} %get-tuple-element.82.refs_4_.refs_0_), channel_id=1, source_target_pairs={{0,16},{4,20},{8,24},{12,28},{16,0},{20,4},{24,8},{28,12},{1,17},{... | collective-permute-start | bytes 1572872 | tf_op jit(solution)/shard_map/ppermute | solution.py:674
  111.0 24.3 %collective-permute-start.30 = (bf16[2,512,256]{2,1,0:T(8,128)(2,1)S(1)}, bf16[2,512,256]{2,1,0:T(8,128)(2,1)S(1)}, u32[]{:S(2)}, u32[]{:S(2)}) collective-permute-start(bf16[2,512,256]{2,1,0:T(8,128)(2,1)S(1)} %get-tuple-element.82.refs_4_.refs_0_), channel_id=1, source_target_pairs={{0,8},{4,12},{8,0},{12,4},{16,24},{20,28},{24,16},{28,20},{1,9},{5... | collective-permute-start | bytes 1572872 | tf_op jit(solution)/shard_map/ppermute | solution.py:674
  112.6 3.6 %collective-permute-start.25 = (f32[8,128]{1,0:T(8,128)S(1)}, f32[8,128]{1,0:T(8,128)S(1)}, u32[]{:S(2)}, u32[]{:S(2)}) collective-permute-start(f32[8,128]{1,0:T(8,128)S(1)} %add.46), channel_id=1, source_target_pairs={{0,1},{1,0},{2,3},{3,2},{4,5},{5,4},{6,7},{7,6},{8,9},{9,8},{10,11... | collective-permute-start | bytes 12296 | tf_op jit(solution)/shard_map/ppermute | solution.py:674
  116.2 4.5 %collective-permute-start.26 = (f32[8,128]{1,0:T(8,128)S(1)}, f32[8,128]{1,0:T(8,128)S(1)}, u32[]{:S(2)}, u32[]{:S(2)}) collective-permute-start(f32[8,128]{1,0:T(8,128)S(1)} %add.47), channel_id=1, source_target_pairs={{0,2},{1,3},{2,0},{3,1},{4,6},{5,7},{6,4},{7,5},{8,10},{9,11},{10,... | collective-permute-start | bytes 12296 | tf_op jit(solution)/shard_map/ppermute | solution.py:674
  120.7 1.2 collective-permute-start.27
  121.9 9.7 %collective-permute-start.28 = (f32[8,128]{1,0:T(8,128)S(1)}, f32[8,128]{1,0:T(8,128)S(1)}, u32[]{:S(2)}, u32[]{:S(2)}) collective-permute-start(f32[8,128]{1,0:T(8,128)S(1)} %add.49), channel_id=1, source_target_pairs={{0,8},{4,12},{8,0},{12,4},{16,24},{20,28},{24,16},{28,20},{1,9},{5... | collective-permute-start | bytes 12296 | tf_op jit(solution)/shard_map/ppermute | solution.py:674
  131.6 3.6 %collective-permute-start.29 = (f32[8,128]{1,0:T(8,128)S(1)}, f32[8,128]{1,0:T(8,128)S(1)}, u32[]{:S(2)}, u32[]{:S(2)}) collective-permute-start(f32[8,128]{1,0:T(8,128)S(1)} %add.50), channel_id=1, source_target_pairs={{0,16},{4,20},{8,24},{12,28},{16,0},{20,4},{24,8},{28,12},{1,17},{... | collective-permute-start | bytes 12296 | tf_op jit(solution)/shard_map/ppermute | solution.py:674
  135.6 2.7 %collective-permute-start.34 = (bf16[2,1024,256]{2,1,0:T(8,128)(2,1)S(1)}, bf16[2,1024,256]{2,1,0:T(8,128)(2,1)S(1)}, u32[]{:S(2)}, u32[]{:S(2)}) collective-permute-start(bf16[2,1024,256]{2,1,0:T(8,128)(2,1)S(1)} %get-tuple-element.84), channel_id=1, source_target_pairs={{0,4},{4,0},{8,12},{12,8},{16,20},{20,16},{24,28},{28,24},{1,5},{5... | collective-permute-start | bytes 3145736 | tf_op jit(solution)/shard_map/ppermute | solution.py:674
  135.7 7.1 %collective-permute-start.36 = (bf16[2,1024,256]{2,1,0:T(8,128)(2,1)S(1)}, bf16[2,1024,256]{2,1,0:T(8,128)(2,1)S(1)}, u32[]{:S(2)}, u32[]{:S(2)}) collective-permute-start(bf16[2,1024,256]{2,1,0:T(8,128)(2,1)S(1)} %get-tuple-element.87), channel_id=1, source_target_pairs={{0,4},{4,0},{8,12},{12,8},{16,20},{20,16},{24,28},{28,24},{1,5},{5... | collective-permute-start | bytes 3145736 | tf_op jit(solution)/shard_map/ppermute | solution.py:674
  136.2 6.7 %collective-permute-start.37 = (bf16[2,1024,256]{2,1,0:T(8,128)(2,1)S(1)}, bf16[2,1024,256]{2,1,0:T(8,128)(2,1)S(1)}, u32[]{:S(2)}, u32[]{:S(2)}) collective-permute-start(bf16[2,1024,256]{2,1,0:T(8,128)(2,1)S(1)} %get-tuple-element.88), channel_id=1, source_target_pairs={{0,4},{4,0},{8,12},{12,8},{16,20},{20,16},{24,28},{28,24},{1,5},{5... | collective-permute-start | bytes 3145736 | tf_op jit(solution)/shard_map/ppermute | solution.py:674
  136.3 14.6 %collective-permute-start.39 = (bf16[1024,256]{1,0:T(8,128)(2,1)S(1)}, bf16[1024,256]{1,0:T(8,128)(2,1)S(1)}, u32[]{:S(2)}, u32[]{:S(2)}) collective-permute-start(bf16[1024,256]{1,0:T(8,128)(2,1)S(1)} %get-tuple-element.94), channel_id=1, source_target_pairs={{0,8},{4,12},{8,0},{12,4},{16,24},{20,28},{24,16},{28,20},{1,9},{5... | collective-permute-start | bytes 1572872 | tf_op jit(solution)/shard_map/ppermute | solution.py:674
  136.8 14.0 %collective-permute-start.35 = (bf16[1024,256]{1,0:T(8,128)(2,1)S(1)}, bf16[1024,256]{1,0:T(8,128)(2,1)S(1)}, u32[]{:S(2)}, u32[]{:S(2)}) collective-permute-start(bf16[1024,256]{1,0:T(8,128)(2,1)S(1)} %get-tuple-element.86), channel_id=1, source_target_pairs={{0,16},{4,20},{8,24},{12,28},{16,0},{20,4},{24,8},{28,12},{1,17},{... | collective-permute-start | bytes 1572872 | tf_op jit(solution)/shard_map/ppermute | solution.py:674
  150.9 3.5 %collective-permute-start.38 = (bf16[1024,256]{1,0:T(8,128)(2,1)S(1)}, bf16[1024,256]{1,0:T(8,128)(2,1)S(1)}, u32[]{:S(2)}, u32[]{:S(2)}) collective-permute-start(bf16[1024,256]{1,0:T(8,128)(2,1)S(1)} %collective-permute-done.35.refs_0_), channel_id=1, source_target_pairs={{0,4},{4,0},{8,12},{12,8},{16,20},{20,16},{24,28},{28,24},{1,5},{5... | collective-permute-start | bytes 1572872 | tf_op jit(solution)/shard_map/ppermute | solution.py:674
  151.1 3.3 %collective-permute-start.40 = (bf16[1024,256]{1,0:T(8,128)(2,1)S(1)}, bf16[1024,256]{1,0:T(8,128)(2,1)S(1)}, u32[]{:S(2)}, u32[]{:S(2)}) collective-permute-start(bf16[1024,256]{1,0:T(8,128)(2,1)S(1)} %collective-permute-done.39.refs_1_), channel_id=1, source_target_pairs={{0,4},{4,0},{8,12},{12,8},{16,20},{20,16},{24,28},{28,24},{1,5},{5... | collective-permute-start | bytes 1572872 | tf_op jit(solution)/shard_map/ppermute | solution.py:674

commit v2 on v1

--- a/solution.py
+++ b/solution.py
@@ -365,7 +365,7 @@
         return carry
 
     steps = v_ref.shape[0] // LEN * (v_ref.shape[1] // HD)
-    lax.fori_loop(0, steps, one, 0, unroll=min(steps, 2))
+    lax.fori_loop(0, steps, one, 0, unroll=True)
 
 
 def attend_back(lengths, queries, values, readout, probs, delta, tables):
@@ -482,8 +482,26 @@
     )(*args)
 
 
+def gate_kernel(value_ref, margin_ref, *refs):
+    out_ref, first_ref = refs[-2:]
+    out_ref[...] = value_ref[...]
+    first_ref[0] = margin_ref[0, 0]
+
+
+def gate(value, margin, *earlier):
+    return pl.pallas_call(
+        gate_kernel,
+        in_specs=[VMEM, VMEM] + [HBM] * len(earlier),
+        out_specs=[VMEM, SMEM],
+        out_shape=[jax.ShapeDtypeStruct(value.shape, value.dtype), jax.ShapeDtypeStruct((1,), jnp.float32)],
+        compiler_params=params(2),
+        cost_estimate=COST,
+        name="gate",
+    )(value, margin, *earlier)
+
+
 def pack_kernel(takes, *refs):
-    sources, outs, sem = refs[: 2 * len(takes)], refs[2 * len(takes) + 1 : -1], refs[-1]
+    sources, outs, sem = refs[: 2 * len(takes)], refs[-1 - len(takes) : -1], refs[-1]
     copies = []
     for n, i in enumerate(takes):
         half = sources[2 * n].shape[1]
@@ -499,19 +517,19 @@
         copy.wait()
 
 
-def pack(sources, takes, earlier):
+def pack(sources, takes, *earlier):
     _, half, cols = sources[0][0].shape
     shapes = [(2, 2 * half, cols) if i is None else (2 * half, cols) for i in takes]
     return pl.pallas_call(
         functools.partial(pack_kernel, tuple(takes)),
-        in_specs=[HBM] * (2 * len(takes) + 1),
+        in_specs=[HBM] * (2 * len(takes) + len(earlier)),
         out_specs=[HBM] * len(takes),
         out_shape=[jax.ShapeDtypeStruct(shape, jnp.bfloat16) for shape in shapes],
         scratch_shapes=[pltpu.SemaphoreType.DMA((len(takes), 2))],
         compiler_params=params(2),
         cost_estimate=COST,
         name="pack",
-    )(*[x for pair in sources for x in pair], earlier)
+    )(*[x for pair in sources for x in pair], *earlier)
 
 
 def fetch_kernel(masks, idx_ref, *refs):
@@ -546,94 +564,63 @@
     )(*args)
 
 
-def blend_kernel(masks, first, ready, idx_ref, square_ref, *refs):
+def blend_kernel(masks, first, offset, idx_ref, square_ref, *refs):
     refs = list(refs)
     count = len(masks)
     grads = [[refs.pop(0) for _ in range(1 if m & 1 and is_whole(m) else 2)] for m in masks]
-    if ready is None:
-        weights = [[refs.pop(0) for _ in range(1 if is_whole(m) else 2)] for m in masks]
-        ref_hbm = refs.pop(0)
-    else:
-        w, r = refs.pop(0), refs.pop(0)
+    w, r = refs.pop(0), refs.pop(0)
     if not first:
         refs.pop(0)
     out_hbm, token_ref = refs.pop(0), refs.pop(0)
     new_hbm = refs.pop(0) if first else None
-    if ready is None:
-        w, r = refs.pop(0), refs.pop(0)
     g, o, new, sem, out_sem = refs
     rows, cols = g.shape[2:]
     step = 64
     half = rows // 2
     token_ref[...] = jnp.zeros_like(token_ref)
-
-    def reads(n):
-        slot = n % 2
-        at = pl.ds(pl.multiple_of((idx_ref[0] ^ masks[n]) * rows, rows), rows)
-        group = read_rows(grads[n], g.at[slot], [sem.at[i, slot] for i in (0, 1)])
-        if ready is None:
-            group += read_rows(weights[n], w.at[slot], [sem.at[2 + i, slot] for i in (0, 1)])
-            group.append(pltpu.make_async_copy(ref_hbm.at[:, at, :], r.at[slot], sem.at[4, slot]))
+    coming = [read_rows(grads[n], g.at[n], [sem.at[i, n] for i in (0, 1)]) for n in range(count)]
+    for group in coming:
         for copy in group:
             copy.start()
-        return group
-
     mean = square_ref[...] * (1.0 / (D * KVH * HD))
     scale = jnp.concatenate([learning_rate * lax.rsqrt(mean + norm_eps)] * (cols // 128), axis=1)
-    coming = {n: reads(n) for n in range(min(2, count))}
-    writes = {}
+    writes = []
     for n in range(count):
-        slot = n % 2
-        held = slot if ready is None else ready + n
-        for copy in coming[n] + writes.pop(n - 2, []):
+        for copy in coming[n]:
             copy.wait()
-        writes[n] = []
         for part in range(2):
 
             def mix(t, carry):
                 j = pl.ds(pl.multiple_of(part * half + t * step, step), step)
                 for i in (0, 1):
-                    value = w[held, i, j].astype(jnp.float32) - scale[i : i + 1, :] * g[slot, i, j].astype(jnp.float32)
+                    value = w[offset + n, i, j].astype(jnp.float32) - scale[i : i + 1, :] * g[n, i, j].astype(jnp.float32)
                     value = value.astype(jnp.bfloat16)
                     if first and n == 0:
                         new[i, j] = value
-                    mixed = mix_alpha * value.astype(jnp.float32) + (1.0 - mix_alpha) * r[held, i, j].astype(jnp.float32)
-                    o[slot, i, j] = mixed.astype(jnp.bfloat16)
+                    mixed = mix_alpha * value.astype(jnp.float32) + (1.0 - mix_alpha) * r[offset + n, i, j].astype(jnp.float32)
+                    o[n, i, j] = mixed.astype(jnp.bfloat16)
                 return carry
 
-            lax.fori_loop(0, half // step, mix, 0)
+            lax.fori_loop(0, half // step, mix, 0, unroll=2)
             at = pl.ds(pl.multiple_of((idx_ref[0] ^ masks[n]) * rows + part * half, half), half)
-            copy = pltpu.make_async_copy(o.at[slot, :, pl.ds(part * half, half), :], out_hbm.at[:, at, :], out_sem.at[part, slot])
-            copy.start()
-            writes[n].append(copy)
+            writes.append(pltpu.make_async_copy(o.at[n, :, pl.ds(part * half, half), :], out_hbm.at[:, at, :], out_sem.at[part, n]))
+            writes[-1].start()
         if first and n == 0:
-            copy = pltpu.make_async_copy(new, new_hbm, out_sem.at[0, 2])
-            copy.start()
-            writes[n].append(copy)
-        if n + 2 < count:
-            coming[n + 2] = reads(n + 2)
-    for group in writes.values():
-        for copy in group:
-            copy.wait()
-
-
-def blend(idx, squares, weights, grads, reference, held, masks, ready=None):
-    rows, cols = weights[masks[0]][0].shape[-2:]
+            writes.append(pltpu.make_async_copy(new, new_hbm, out_sem.at[0, count]))
+            writes[-1].start()
+    for copy in writes:
+        copy.wait()
+
+
+def blend(idx, squares, grads, reference, held, masks, ready, offset):
+    w, r = ready
+    _, _, rows, cols = w.shape
     count = len(masks)
     first = held is None
     args = [idx, squares] + [x for m in masks for x in grads[m]]
     in_specs = [SMEM, VMEM] + [HBM] * (len(args) - 2)
-    block = pltpu.VMEM((min(count, 2), 2, rows, cols), jnp.bfloat16)
-    scratch = [block, block, pltpu.VMEM((2, rows, cols) if first else (8, 128), jnp.bfloat16)]
-    scratch += [pltpu.SemaphoreType.DMA((5, 2)), pltpu.SemaphoreType.DMA((2, 3))]
-    if ready is None:
-        extra = [w for m in masks for w in weights[m]] + [in_hbm(reference)]
-        args += extra
-        in_specs += [HBM] * len(extra)
-        scratch = [block, block] + scratch
-    else:
-        args += [resident(x) for x in ready[0]]
-        in_specs += [VMEM] * 2
+    args += [resident(w), resident(r)]
+    in_specs += [VMEM] * 2
     out_specs = [HBM, VMEM]
     out_shape = [jax.ShapeDtypeStruct(reference.shape, jnp.bfloat16), jax.ShapeDtypeStruct((8, 128), jnp.float32)]
     aliases = {}
@@ -644,14 +631,21 @@
         aliases = {len(args): 0}
         in_specs.append(HBM)
         args.append(held)
+    block = pltpu.VMEM((count, 2, rows, cols), jnp.bfloat16)
     return pl.pallas_call(
-        functools.partial(blend_kernel, tuple(masks), first, None if ready is None else ready[1]),
+        functools.partial(blend_kernel, tuple(masks), first, offset),
         in_specs=in_specs,
         out_specs=out_specs,
         out_shape=out_shape,
-        scratch_shapes=scratch,
+        scratch_shapes=[
+            block,
+            block,
+            pltpu.VMEM((2, rows, cols) if first else (8, 128), jnp.bfloat16),
+            pltpu.SemaphoreType.DMA((2, count)),
+            pltpu.SemaphoreType.DMA((2, count + 1)),
+        ],
         input_output_aliases=aliases,
-        compiler_params=params(14),
+        compiler_params=params(12),
         cost_estimate=COST,
         name="blend",
     )(*args)
@@ -780,29 +774,34 @@
     for bit in powers(tensors):
         squares = squares + swap(squares, bit, "tensor", tensors)
     squares = squares + swap(squares, 1)
-    total = squares
-    for bit in powers(shards)[1:]:
-        total = total + swap(total, bit)
-    squares = total
+    squares, margin_out = gate(squares, margin, *[grads[m][0] for m in near])
+    masks = [m | c for m in [0] + near for c in (0, 1)] + [m | c for c in (0, 1) for m in far]
+    ready = fetch(idx, weights, reference_weights, masks, squares)
+    terms = [squares] + [swap(squares, m) for m in chips[1:]]
+    while len(terms) > 1:
+        terms = [a + b for a, b in zip(terms[::2], terms[1::2])]
+    (squares,) = terms
     two = [m for m in far if len(bits_of(m)) == 2]
     ends = [(m, i) for m in two for i in (0, 1)]
     whole = [0] + near
-    packed = pack([grads[m ^ link(i, m)] for m, i in ends] + [grads[m] for m in whole], [i for m, i in ends] + [None] * len(whole), total)
+    packed = pack([grads[m ^ link(i, m)] for m, i in ends] + [grads[m] for m in whole], [i for m, i in ends] + [None] * len(whole), squares, ready[0])
     packed = dict(zip(ends + whole, packed))
     for m in far:
         grads[m] = [swap(packed[m, i] if m in two else grads[m ^ link(i, m)][i], link(i, m)) for i in (0, 1)]
     for m in whole:
         grads[m | 1] = [swap(packed[m], 1)]
-    new_reference, token, new_policy = blend(idx, squares, weights, grads, reference_weights, None, [0, 1])
-    new_reference, token = blend(idx, squares, weights, grads, reference_weights, new_reference, [m | c for m in near for c in (0, 1)])
-    if far:
-        ready = fetch(idx, weights, reference_weights, [m | c for c in (0, 1) for m in far], token)
-        for m in far:
-            to_core(grads, m, ready)
-        for c in (0, 1):
-            masks = [m | c for m in far]
-            new_reference, token = blend(idx, squares, weights, grads, reference_weights, new_reference, masks, (ready, c * len(far)))
-    return (new_policy, new_reference, margin[0, :1])
+    groups = [[0, 1], [m | c for m in near for c in (0, 1)]] + [[m | c for m in far] for c in (0, 1)]
+    new_reference, at = None, 0
+    for group in groups:
+        if group == far and far:
+            for m in far:
+                to_core(grads, m, token)
+        if group:
+            outs = blend(idx, squares, grads, reference_weights, new_reference, group, ready, at)
+            new_reference, token = outs[:2]
+            new_policy = outs[2] if at == 0 else new_policy
+            at += len(group)
+    return (new_policy, new_reference, margin_out)
 
 
 def solution(mesh):

time: 157 us -> 153 us (0.975)
  waiting for transfers between devices: 57.4 us -> 51.2 us
  starting transfers between devices: 30.1 us -> 33.7 us
    ppermute x41 -> x42, waiting for transfers between devices: 57.4 us -> 51.2 us  [swap(): return lax.ppermute(x, axis, [(i, i ^ bit) for i in range(size)])]
    ppermute x41 -> x42, starting transfers between devices: 30.1 us -> 33.7 us  [swap(): return lax.ppermute(x, axis, [(i, i ^ bit) for i in range(size)])]
    pallas_call x4 -> x5, Pallas kernels: 15.5 us -> 13 us  [the longest x4 12.5 us: blend(): pl.pallas_call(functools.partial(blend_kernel, tuple(masks), first, offse...]
    pallas_call x1, Pallas kernels: 1.69 us -> 3.81 us  [fetch(): pl.pallas_call(functools.partial(fetch_kernel, tuple(masks)), in_specs=[S...]
  transfers between devices with their start and end apart: 41 -> 42, of which waited for: 18 -> 20; matrix products, arithmetic and copies ran while one was open for 1% -> 0% of each run, Pallas kernels for 36% -> 37%
where the time goes in v2:
time: 153 us
  Pallas kernels  66.7 us (44%)
  waiting for transfers between devices  51.2 us (33%)
  starting transfers between devices  33.7 us (22%)
    ppermute x42, waiting for transfers between devices, swap(): return lax.ppermute(x, axis, [(i, i ^ bit) for i in range(size)])  51.2 us
    ppermute x42, starting transfers between devices, swap(): return lax.ppermute(x, axis, [(i, i ^ bit) for i in range(size)])  33.7 us
    pallas_call x1, Pallas kernels, norm_project(): pl.pallas_call(norm_project_kernel, in_specs=[SMEM, HBM, HBM, HBM], out_s...  17.8 us
    pallas_call x4, Pallas kernels, blend(): pl.pallas_call(functools.partial(blend_kernel, tuple(masks), first, offse...  12.5 us
    pallas_call x2, Pallas kernels, attend(): pl.pallas_call(functools.partial(attend_kernel, keep), in_specs=[SMEM] +...  8.96 us
    pallas_call x3, Pallas kernels, project(): pl.pallas_call(functools.partial(project_kernel, tuple(masks), first, las...  8.58 us
    pallas_call x4, Pallas kernels, gradient_blocks(): pl.pallas_call(functools.partial(kernel, tuple(masks)), in_specs=in_specs...  8.29 us
    pallas_call x1, Pallas kernels, attend_back(): pl.pallas_call(attend_back_kernel, in_specs=[SMEM] + [VMEM] * 6, out_spec...  5.04 us
  transfers between devices with their start and end apart: 42, of which 20 were waited for; matrix products, arithmetic and copies ran while one was open for 0% of the time, Pallas kernels for 37%

profile of v2, /device:TPU:0, one launch (start us, length us, event | category | flops | bytes accessed | tf_op | source)
XLA Modules:
  0.0 153.2 jit_solution(4804649504639839679)
XLA Ops:
  0.6 3.0 %collective-permute-start.1 = (bf16[2,1024,256]{2,1,0:T(8,128)(2,1)}, bf16[2,1024,256]{2,1,0:T(8,128)(2,1)S(1)}, u32[]{:S(2)}, u32[]{:S(2)}) collective-permute-start(bf16[2,1024,256]{2,1,0:T(8,128)(2,1)} %refs_0_.3), channel_id=1, source_target_pairs={{0,16},{4,20},{8,24},{12,28},{16,0},{20,4},{24,8},{28,12},{1,17},{... | collective-permute-start | bytes 3145736 | tf_op jit(solution)/shard_map/ppermute | solution.py:668
  3.7 1.5 collective-permute-start
  5.2 17.8 %norm_project.1 = (bf16[768,8192]{1,0:T(8,128)(2,1)S(1)}, bf16[768,256]{1,0:T(8,128)(2,1)S(1)}, bf16[768,256]{1,0:T(8,128)(2,1)S(1)}) custom-call(s32[1]{0:T(128)} %bitcast.idx_ref, bf16[768,8192]{1,0:T(8,128)(2,1)} %hidden_hbm.1, bf16[2,8192,256]{2,1,0:T(8,128)(2,1)} %refs_10_.1, f32[2,384,128]{2,1,0:T(8,128)} %constant.8.clone.table_hbm.refs_5_.table_ref), custom_call_target="tpu_custom_call" | custom-call | flops 1 | bytes 1 | tf_op jit(solution)/shard_map/norm_project/pallas_call | solution.py:133
  23.1 4.4 %attend.2.rest_0_ = f32[8,128]{1,0:T(8,128)S(1)} custom-call(s32[2]{0:T(128)S(1)} %copy-done.5, bf16[768,1024]{1,0:T(8,128)(2,1)S(1)} %copy-done.4, bf16[768,256]{1,0:T(8,128)(2,1)S(1)} %get-tuple-element.54.k_ref, bf16[768,256]{1,0:T(8,128)(2,1)S(1)} %get-tuple-element.55.v_ref, bf16[768,1024]{1,0:T(8,128)(2,1)S(1)} %copy-done), custom_call_target="tpu_custom_call" | custom-call | flops 1 | bytes 1 | tf_op jit(solution)/shard_map/attend/pallas_call | solution.py:318
  27.5 1.0 collective-permute-done.refs_0_.refs_2_
  28.5 0.5 collective-permute-start.5
  29.0 1.6 %collective-permute-start.3 = (bf16[1024,256]{1,0:T(8,128)(2,1)S(1)}, bf16[1024,256]{1,0:T(8,128)(2,1)S(1)}, u32[]{:S(2)}, u32[]{:S(2)}) collective-permute-start(bf16[1024,256]{1,0:T(8,128)(2,1)S(1)} %slice_bitcast_fusion), channel_id=1, source_target_pairs={{0,8},{4,12},{8,0},{12,4},{16,24},{20,28},{24,16},{28,20},{1,9},{5... | collective-permute-start | bytes 1572872 | tf_op jit(solution)/shard_map/ppermute | solution.py:668
  30.6 0.6 collective-permute-start.2
  31.2 2.0 %project.3.refs_4_ = f32[2,768,256]{2,1,0:T(8,128)S(1)} custom-call(s32[1]{0:T(128)} %bitcast.idx_ref, bf16[768,8192]{1,0:T(8,128)(2,1)S(1)} %get-tuple-element.53.x_ref, bf16[2,1024,256]{2,1,0:T(8,128)(2,1)S(1)} %copy-done.2, bf16[2,1024,256]{2,1,0:T(8,128)(2,1)S(1)} %collective-permute-done.6.refs_1_), custom_call_target="tpu_custom_call" | custom-call | flops 1 | bytes 1 | tf_op jit(solution)/shard_map/project/pallas_call | solution.py:226
  33.3 4.1 %project.4.refs_4_ = f32[2,768,256]{2,1,0:T(8,128)S(1)} custom-call(s32[1]{0:T(128)} %bitcast.idx_ref, bf16[768,8192]{1,0:T(8,128)(2,1)S(1)} %get-tuple-element.53.x_ref, bf16[2,1024,256]{2,1,0:T(8,128)(2,1)S(1)} %collective-permute-done.refs_0_.refs_2_, bf16[2,1024,256]{2,1,0:T(8,128)(2,1)S(1)} %collective-permute-done.4.refs_1_.refs_3_, ...), custom_call_target="tpu_custom_call" | custom-call | flops 1 | bytes 1 | tf_op jit(solution)/shard_map/project/pallas_call | solution.py:226
  37.4 5.5 %collective-permute-done.3.refs_1_.refs_7_ = bf16[1024,256]{1,0:T(8,128)(2,1)S(1)} collective-permute-done((bf16[1024,256]{1,0:T(8,128)(2,1)S(1)}, bf16[1024,256]{1,0:T(8,128)(2,1)S(1)}, u32[]{:S(2)}, u32[]{:S(2)}) %collective-permute-start.3) | collective-permute-done | bytes 524320 | tf_op jit(solution)/shard_map/ppermute | solution.py:668
  42.9 1.3 collective-permute-done.2.refs_0_.refs_6_
  44.3 0.5 collective-permute-start.8
  44.8 1.4 collective-permute-done.7.refs_2_.refs_8_
  46.2 0.7 collective-permute-done.8.refs_3_.refs_9_
  46.9 2.4 %project.5 = (bf16[768,256]{1,0:T(8,128)(2,1)S(1)}, bf16[768,256]{1,0:T(8,128)(2,1)S(1)}) custom-call(s32[1]{0:T(128)} %bitcast.idx_ref, bf16[768,8192]{1,0:T(8,128)(2,1)S(1)} %get-tuple-element.53.x_ref, bf16[1024,256]{1,0:T(8,128)(2,1)S(1)} %collective-permute-done.2.refs_0_.refs_6_, bf16[1024,256]{1,0:T(8,128)(2,1)S(1)} %collective-permute-done.3.refs_1_.refs_7_, ...), custom_call_target="tpu_custom_call" | custom-call | flops 1 | bytes 1 | tf_op jit(solution)/shard_map/project/pallas_call | solution.py:226
  49.4 4.5 %attend.3 = (f32[8,128]{1,0:T(8,128)S(1)}, bf16[2,2,768,512]{3,2,1,0:T(8,128)(2,1)S(1)}, f32[2,2,3,512]{3,2,1,0:T(4,128)S(1)}) custom-call(s32[2]{0:T(128)S(1)} %copy-done.5, bf16[768,1024]{1,0:T(8,128)(2,1)S(1)} %copy-done.1, bf16[768,256]{1,0:T(8,128)(2,1)S(1)} %get-tuple-element.63.k_ref, bf16[768,256]{1,0:T(8,128)(2,1)S(1)} %get-tuple-element.62.v_ref, ...), custom_call_target="tpu_custom_call" | custom-call | flops 1 | bytes 1 | tf_op jit(solution)/shard_map/attend/pallas_call | solution.py:318
  53.9 3.7 %collective-permute-start.11 = (f32[8,128]{1,0:T(8,128)S(1)}, f32[8,128]{1,0:T(8,128)S(1)}, u32[]{:S(2)}, u32[]{:S(2)}) collective-permute-start(f32[8,128]{1,0:T(8,128)S(1)} %get-tuple-element.66), channel_id=1, source_target_pairs={{0,3},{1,2},{2,1},{3,0},{4,7},{5,6},{6,5},{7,4},{8,11},{9,10},{10,... | collective-permute-start | bytes 12296 | tf_op jit(solution)/shard_map/ppermute | solution.py:668
  57.6 0.8 collective-permute-start.9
  58.4 5.0 %attend_back.1.cot_ref = bf16[2,256,768]{2,1,0:T(8,128)(2,1)S(1)} custom-call(s32[2]{0:T(128)S(1)} %copy-done.5, bf16[768,1024]{1,0:T(8,128)(2,1)S(1)} %copy-done.1, bf16[768,256]{1,0:T(8,128)(2,1)S(1)} %get-tuple-element.62.v_ref, bf16[768,1024]{1,0:T(8,128)(2,1)S(1)} %copy-done, bf16[2,2,768,512]{3,2,1,0:T(8,128)(2,1)S(1)} %get-tuple-element.64.prob_ref, ...), custom_call_target="tpu_custom_call" | custom-call | flops 1 | bytes 1 | tf_op jit(solution)/shard_map/attend_back/pallas_call | solution.py:372
  63.5 1.0 gradient_block.2
  64.5 0.5 collective-permute-start.12
  65.0 2.2 %collective-permute-done.12.outs_0_.their_ref = f32[8,128]{1,0:T(8,128)S(1)} collective-permute-done((f32[8,128]{1,0:T(8,128)S(1)}, f32[8,128]{1,0:T(8,128)S(1)}, u32[]{:S(2)}, u32[]{:S(2)}) %collective-permute-start.12) | collective-permute-done | bytes 4128 | tf_op jit(solution)/shard_map/ppermute | solution.py:668
  67.2 2.7 %gradient_block.3 = (bf16[2,256,1024]{2,1,0:T(8,128)(2,1)S(1)}, bf16[2,256,1024]{2,1,0:T(8,128)(2,1)S(1)}, bf16[2,256,1024]{2,1,0:T(8,128)(2,1)S(1)}) custom-call(s32[1]{0:T(128)} %bitcast.idx_ref, bf16[768,8192]{1,0:T(8,128)(2,1)S(1)} %get-tuple-element.53.x_ref, bf16[2,256,768]{2,1,0:T(8,128)(2,1)S(1)} %attend_back.1.cot_ref, ...), custom_call_target="tpu_custom_call" | custom-call | flops 1 | bytes 1 | tf_op jit(solution)/shard_map/gradient_block/pallas_call | solution.py:440
  70.6 1.1 merged_block.3
  71.7 0.6 collective-permute-start.21
  72.7 1.4 collective-permute-done.14.refs_1_
  74.1 1.5 collective-permute-done.15.refs_2_
  75.6 3.5 %merged_block.2 = (bf16[256,1024]{1,0:T(8,128)(2,1)S(1)}, bf16[256,1024]{1,0:T(8,128)(2,1)S(1)}, bf16[256,1024]{1,0:T(8,128)(2,1)S(1)}, bf16[256,1024]{1,0:T(8,1...) custom-call(s32[1]{0:T(128)} %bitcast.idx_ref, bf16[768,8192]{1,0:T(8,128)(2,1)S(1)} %get-tuple-element.53.x_ref, ...), custom_call_target="tpu_custom_call" | custom-call | flops 1 | bytes 1 | tf_op jit(solution)/shard_map/merged_block/pallas_call | solution.py:440
  79.1 0.6 collective-permute-start.16
  80.1 6.4 %collective-permute-done.21 = bf16[256,1024]{1,0:T(8,128)(2,1)S(1)} collective-permute-done((bf16[256,1024]{1,0:T(8,128)(2,1)S(1)}, bf16[256,1024]{1,0:T(8,128)(2,1)S(1)}, u32[]{:S(2)}, u32[]{:S(2)}) %collective-permute-start.21) | collective-permute-done | bytes 524320 | tf_op jit(solution)/shard_map/ppermute | solution.py:668
  86.7 0.6 collective-permute-start.22
  87.4 1.4 collective-permute-start.19
  88.8 0.7 collective-permute-start.24
  89.5 8.8 %collective-permute-done.16.refs_1_ = bf16[256,1024]{1,0:T(8,128)(2,1)S(1)} collective-permute-done((bf16[256,1024]{1,0:T(8,128)(2,1)S(1)}, bf16[256,1024]{1,0:T(8,128)(2,1)S(1)}, u32[]{:S(2)}, u32[]{:S(2)}) %collective-permute-start.16) | collective-permute-done | bytes 524320 | tf_op jit(solution)/shard_map/ppermute | solution.py:668
  98.3 1.5 collective-permute-start.23
  99.8 4.1 %collective-permute-done.22.refs_5_ = bf16[256,512]{1,0:T(8,128)(2,1)S(1)} collective-permute-done((bf16[256,512]{1,0:T(8,128)(2,1)S(1)}, bf16[256,512]{1,0:T(8,128)(2,1)S(1)}, u32[]{:S(2)}, u32[]{:S(2)}) %collective-permute-start.22) | collective-permute-done | bytes 262176 | tf_op jit(solution)/shard_map/ppermute | solution.py:668
  104.3 0.4 collective-permute-start.29
  104.7 1.6 %collective-permute-start.28 = (bf16[2,512,256]{2,1,0:T(8,128)(2,1)S(1)}, bf16[2,512,256]{2,1,0:T(8,128)(2,1)S(1)}, u32[]{:S(2)}, u32[]{:S(2)}) collective-permute-start(bf16[2,512,256]{2,1,0:T(8,128)(2,1)S(1)} %get-tuple-element.84.refs_4_.refs_0_), channel_id=1, source_target_pairs={{0,8},{4,12},{8,0},{12,4},{16,24},{20,28},{24,16},{28,20},{1,9},{5... | collective-permute-start | bytes 1572872 | tf_op jit(solution)/shard_map/ppermute | solution.py:668
  106.4 3.2 %collective-permute-done.24.refs_5_ = bf16[256,512]{1,0:T(8,128)(2,1)S(1)} collective-permute-done((bf16[256,512]{1,0:T(8,128)(2,1)S(1)}, bf16[256,512]{1,0:T(8,128)(2,1)S(1)}, u32[]{:S(2)}, u32[]{:S(2)}) %collective-permute-start.24) | collective-permute-done | bytes 262176 | tf_op jit(solution)/shard_map/ppermute | solution.py:668
  109.9 0.4 collective-permute-start.34
  110.3 1.6 %collective-permute-start.33 = (bf16[2,512,256]{2,1,0:T(8,128)(2,1)S(1)}, bf16[2,512,256]{2,1,0:T(8,128)(2,1)S(1)}, u32[]{:S(2)}, u32[]{:S(2)}) collective-permute-start(bf16[2,512,256]{2,1,0:T(8,128)(2,1)S(1)} %get-tuple-element.86.refs_5_.refs_1_), channel_id=1, source_target_pairs={{0,8},{4,12},{8,0},{12,4},{16,24},{20,28},{24,16},{28,20},{1,9},{5... | collective-permute-start | bytes 1572872 | tf_op jit(solution)/shard_map/ppermute | solution.py:668
  112.0 1.2 collective-permute-start.25
  113.2 2.4 %collective-permute-done.25 = f32[8,128]{1,0:T(8,128)S(1)} collective-permute-done((f32[8,128]{1,0:T(8,128)S(1)}, f32[8,128]{1,0:T(8,128)S(1)}, u32[]{:S(2)}, u32[]{:S(2)}) %collective-permute-start.25) | collective-permute-done | bytes 4128 | tf_op jit(solution)/shard_map/ppermute | solution.py:668
  115.6 2.1 %collective-permute-start.26 = (f32[8,128]{1,0:T(8,128)S(1)}, f32[8,128]{1,0:T(8,128)S(1)}, u32[]{:S(2)}, u32[]{:S(2)}) collective-permute-start(f32[8,128]{1,0:T(8,128)S(1)} %add.50), channel_id=1, source_target_pairs={{0,2},{1,3},{2,0},{3,1},{4,6},{5,7},{6,4},{7,5},{8,10},{9,11},{10,... | collective-permute-start | bytes 12296 | tf_op jit(solution)/shard_map/ppermute | solution.py:668
  117.7 2.4 %collective-permute-done.26 = f32[8,128]{1,0:T(8,128)S(1)} collective-permute-done((f32[8,128]{1,0:T(8,128)S(1)}, f32[8,128]{1,0:T(8,128)S(1)}, u32[]{:S(2)}, u32[]{:S(2)}) %collective-permute-start.26) | collective-permute-done | bytes 4128 | tf_op jit(solution)/shard_map/ppermute | solution.py:668
  120.1 1.2 collective-permute-done.27
  121.3 0.6 gate.1
  121.8 1.5 %collective-permute-start.32 = (f32[8,128]{1,0:T(8,128)S(1)}, f32[8,128]{1,0:T(8,128)S(1)}, u32[]{:S(2)}, u32[]{:S(2)}) collective-permute-start(f32[8,128]{1,0:T(8,128)S(1)} %get-tuple-element.85.refs_11_), channel_id=1, source_target_pairs={{0,24},{4,28},{8,16},{12,20},{16,8},{20,12},{24,0},{28,4},{1,25},{... | collective-permute-start | bytes 12296 | tf_op jit(solution)/shard_map/ppermute | solution.py:668
  123.4 1.0 collective-permute-start.31
  124.4 1.0 collective-permute-start.30
  125.4 3.8 %fetch.1 = (bf16[8,2,1024,256]{3,2,1,0:T(8,128)(2,1)S(1)}, bf16[8,2,1024,256]{3,2,1,0:T(8,128)(2,1)S(1)}) custom-call(s32[1]{0:T(128)} %bitcast.idx_ref, bf16[2,1024,256]{2,1,0:T(8,128)(2,1)S(1)} %copy-done.2, bf16[2,1024,256]{2,1,0:T(8,128)(2,1)S(1)} %collective-permute-done.6.refs_1_, bf16[2,1024,256]{2,1,0:T(8,128)(2,1)S(1)} %collective-permute-done.refs_0_.refs_2_, ...), custom_call_target="tpu_custom_call" | custom-call | flops 1 | bytes 1 | tf_op jit(solution)/shard_map/fetch/pallas_call | solution.py:555
  129.2 1.9 %collective-permute-done.32 = f32[8,128]{1,0:T(8,128)S(1)} collective-permute-done((f32[8,128]{1,0:T(8,128)S(1)}, f32[8,128]{1,0:T(8,128)S(1)}, u32[]{:S(2)}, u32[]{:S(2)}) %collective-permute-start.32) | collective-permute-done | bytes 4128 | tf_op jit(solution)/shard_map/ppermute | solution.py:668
  131.4 0.4 pack.1
  131.8 0.5 collective-permute-start.37
  132.4 1.5 collective-permute-start.40
  133.9 0.5 collective-permute-start.36
  134.5 3.1 %blend.4 = (bf16[2,8192,256]{2,1,0:T(8,128)(2,1)}, f32[8,128]{1,0:T(8,128)}, bf16[2,1024,256]{2,1,0:T(8,128)(2,1)}) custom-call(s32[1]{0:T(128)} %bitcast.idx_ref, f32[8,128]{1,0:T(8,128)S(1)} %add_add_fusion.refs_10_.square_ref, bf16[2,512,256]{2,1,0:T(8,128)(2,1)S(1)} %get-tuple-element.84.refs_4_.refs_0_, ...), custom_call_target="tpu_custom_call" | custom-call | flops 1 | bytes 1 | tf_op jit(solution)/shard_map/blend/pallas_call | solution.py:635
  137.7 4.8 %blend.5 = (bf16[2,8192,256]{2,1,0:T(8,128)(2,1)}, f32[8,128]{1,0:T(8,128)}) custom-call(s32[1]{0:T(128)} %bitcast.idx_ref, f32[8,128]{1,0:T(8,128)S(1)} %add_add_fusion.refs_10_.square_ref, bf16[2,512,256]{2,1,0:T(8,128)(2,1)S(1)} %collective-permute-done.28.refs_0_.refs_6_, ...), custom_call_target="tpu_custom_call", output_to_operand_aliasing={{0}: (10, {})} | custom-call | flops 1 | bytes 1 | tf_op jit(solution)/shard_map/blend/pallas_call | solution.py:635
  142.5 4.2 %collective-permute-done.40.refs_1_ = bf16[1024,256]{1,0:T(8,128)(2,1)S(1)} collective-permute-done((bf16[1024,256]{1,0:T(8,128)(2,1)S(1)}, bf16[1024,256]{1,0:T(8,128)(2,1)S(1)}, u32[]{:S(2)}, u32[]{:S(2)}) %collective-permute-start.40) | collective-permute-done | bytes 524320 | tf_op jit(solution)/shard_map/ppermute | solution.py:668
  146.7 1.2 collective-permute-done.36.refs_0_
  147.9 0.5 collective-permute-start.41
  148.4 2.3 %blend.6 = (bf16[2,8192,256]{2,1,0:T(8,128)(2,1)}, f32[8,128]{1,0:T(8,128)}) custom-call(s32[1]{0:T(128)} %bitcast.idx_ref, f32[8,128]{1,0:T(8,128)S(1)} %add_add_fusion.refs_10_.square_ref, bf16[1024,256]{1,0:T(8,128)(2,1)S(1)} %collective-permute-done.36.refs_0_, ...), custom_call_target="tpu_custom_call", output_to_operand_aliasing={{0}: (6, {})} | custom-call | flops 1 | bytes 1 | tf_op jit(solution)/shard_map/blend/pallas_call | solution.py:635
  150.7 2.3 %blend.7 = (bf16[2,8192,256]{2,1,0:T(8,128)(2,1)}, f32[8,128]{1,0:T(8,128)}) custom-call(s32[1]{0:T(128)} %bitcast.idx_ref, f32[8,128]{1,0:T(8,128)S(1)} %add_add_fusion.refs_10_.square_ref, bf16[1024,256]{1,0:T(8,128)(2,1)S(1)} %collective-permute-done.39.refs_0_, ...), custom_call_target="tpu_custom_call", output_to_operand_aliasing={{0}: (6, {})} | custom-call | flops 1 | bytes 1 | tf_op jit(solution)/shard_map/blend/pallas_call | solution.py:635
  (62 shorter events, 3.2 us)
Async XLA Ops:
  0.6 26.9 %collective-permute-start.1 = (bf16[2,1024,256]{2,1,0:T(8,128)(2,1)}, bf16[2,1024,256]{2,1,0:T(8,128)(2,1)S(1)}, u32[]{:S(2)}, u32[]{:S(2)}) collective-permute-start(bf16[2,1024,256]{2,1,0:T(8,128)(2,1)} %refs_0_.3), channel_id=1, source_target_pairs={{0,16},{4,20},{8,24},{12,28},{16,0},{20,4},{24,8},{28,12},{1,17},{... | collective-permute-start | bytes 3145736 | tf_op jit(solution)/shard_map/ppermute | solution.py:668
  3.7 24.8 %collective-permute-start = (bf16[2,1024,256]{2,1,0:T(8,128)(2,1)}, bf16[2,1024,256]{2,1,0:T(8,128)(2,1)S(1)}, u32[]{:S(2)}, u32[]{:S(2)}) collective-permute-start(bf16[2,1024,256]{2,1,0:T(8,128)(2,1)} %refs_0_.3), channel_id=1, source_target_pairs={{0,8},{4,12},{8,0},{12,4},{16,24},{20,28},{24,16},{28,20},{1,9},{5... | collective-permute-start | bytes 3145736 | tf_op jit(solution)/shard_map/ppermute | solution.py:668
  5.2 26.1 %collective-permute-start.6 = (bf16[2,1024,256]{2,1,0:T(8,128)(2,1)}, bf16[2,1024,256]{2,1,0:T(8,128)(2,1)S(1)}, u32[]{:S(2)}, u32[]{:S(2)}) collective-permute-start(bf16[2,1024,256]{2,1,0:T(8,128)(2,1)} %refs_0_.3), channel_id=1, source_target_pairs={{0,4},{4,0},{8,12},{12,8},{16,20},{20,16},{24,28},{28,24},{1,5},{5... | collective-permute-start | bytes 3145736 | tf_op jit(solution)/shard_map/ppermute | solution.py:668
  5.2 17.9 %copy-start = (bf16[768,1024]{1,0:T(8,128)(2,1)S(1)}, bf16[768,1024]{1,0:T(8,128)(2,1)}, u32[]{:S(2)}) copy-start(bf16[768,1024]{1,0:T(8,128)(2,1)} %ro_ref.5) | copy-start | bytes 4718596
  5.2 17.9 %copy-start.4 = (bf16[768,1024]{1,0:T(8,128)(2,1)S(1)}, bf16[768,1024]{1,0:T(8,128)(2,1)}, u32[]{:S(2)}) copy-start(bf16[768,1024]{1,0:T(8,128)(2,1)} %q_ref.3) | copy-start | bytes 4718596
  5.2 17.9 %copy-start.5 = (s32[2]{0:T(128)S(1)}, s32[2]{0:T(128)}, u32[]{:S(2)}) copy-start(s32[2]{0:T(128)} %len_ref.5) | copy-start | bytes 28
  5.2 26.0 %copy-start.2 = (bf16[2,1024,256]{2,1,0:T(8,128)(2,1)S(1)}, bf16[2,1024,256]{2,1,0:T(8,128)(2,1)}, u32[]{:S(2)}) copy-start(bf16[2,1024,256]{2,1,0:T(8,128)(2,1)} %refs_0_.3) | copy-start | bytes 3145732
  28.5 4.8 %collective-permute-start.4 = (bf16[2,1024,256]{2,1,0:T(8,128)(2,1)S(1)}, bf16[2,1024,256]{2,1,0:T(8,128)(2,1)S(1)}, u32[]{:S(2)}, u32[]{:S(2)}) collective-permute-start(bf16[2,1024,256]{2,1,0:T(8,128)(2,1)S(1)} %collective-permute-done.refs_0_.refs_2_), channel_id=1, source_target_pairs={{0,4},{4,0},{8,12},{12,8},{16,20},{20,16},{24,28},{28,24},{1,5},{5... | collective-permute-start | bytes 3145736 | tf_op jit(solution)/shard_map/ppermute | solution.py:668
  28.5 4.8 %collective-permute-start.5 = (bf16[2,1024,256]{2,1,0:T(8,128)(2,1)S(1)}, bf16[2,1024,256]{2,1,0:T(8,128)(2,1)S(1)}, u32[]{:S(2)}, u32[]{:S(2)}) collective-permute-start(bf16[2,1024,256]{2,1,0:T(8,128)(2,1)S(1)} %collective-permute-done.1.refs_2_.refs_4_), channel_id=1, source_target_pairs={{0,4},{4,0},{8,12},{12,8},{16,20},{20,16},{24,28},{28,24},{1,5},{5... | collective-permute-start | bytes 3145736 | tf_op jit(solution)/shard_map/ppermute | solution.py:668
  29.0 13.9 %collective-permute-start.3 = (bf16[1024,256]{1,0:T(8,128)(2,1)S(1)}, bf16[1024,256]{1,0:T(8,128)(2,1)S(1)}, u32[]{:S(2)}, u32[]{:S(2)}) collective-permute-start(bf16[1024,256]{1,0:T(8,128)(2,1)S(1)} %slice_bitcast_fusion), channel_id=1, source_target_pairs={{0,8},{4,12},{8,0},{12,4},{16,24},{20,28},{24,16},{28,20},{1,9},{5... | collective-permute-start | bytes 1572872 | tf_op jit(solution)/shard_map/ppermute | solution.py:668
  30.6 13.6 %collective-permute-start.2 = (bf16[1024,256]{1,0:T(8,128)(2,1)S(1)}, bf16[1024,256]{1,0:T(8,128)(2,1)S(1)}, u32[]{:S(2)}, u32[]{:S(2)}) collective-permute-start(bf16[1024,256]{1,0:T(8,128)(2,1)S(1)} %slice_bitcast_fusion.1), channel_id=1, source_target_pairs={{0,16},{4,20},{8,24},{12,28},{16,0},{20,4},{24,8},{28,12},{1,17},{... | collective-permute-start | bytes 1572872 | tf_op jit(solution)/shard_map/ppermute | solution.py:668
  37.4 12.0 %copy-start.1 = (bf16[768,1024]{1,0:T(8,128)(2,1)S(1)}, bf16[768,1024]{1,0:T(8,128)(2,1)}, u32[]{:S(2)}) copy-start(bf16[768,1024]{1,0:T(8,128)(2,1)} %q_ref.5) | copy-start | bytes 4718596
  37.4 21.0 %copy-start.3 = (f32[2,384,128]{2,1,0:T(8,128)S(1)}, f32[2,384,128]{2,1,0:T(8,128)}, u32[]{:S(2)}) copy-start(f32[2,384,128]{2,1,0:T(8,128)} %constant.8.clone.table_hbm.refs_5_.table_ref) | copy-start | bytes 1179652
  44.3 1.9 %collective-permute-start.7 = (bf16[1024,256]{1,0:T(8,128)(2,1)S(1)}, bf16[1024,256]{1,0:T(8,128)(2,1)S(1)}, u32[]{:S(2)}, u32[]{:S(2)}) collective-permute-start(bf16[1024,256]{1,0:T(8,128)(2,1)S(1)} %collective-permute-done.2.refs_0_.refs_6_), channel_id=1, source_target_pairs={{0,4},{4,0},{8,12},{12,8},{16,20},{20,16},{24,28},{28,24},{1,5},{5... | collective-permute-start | bytes 1572872 | tf_op jit(solution)/shard_map/ppermute | solution.py:668
  44.3 2.7 %collective-permute-start.8 = (bf16[1024,256]{1,0:T(8,128)(2,1)S(1)}, bf16[1024,256]{1,0:T(8,128)(2,1)S(1)}, u32[]{:S(2)}, u32[]{:S(2)}) collective-permute-start(bf16[1024,256]{1,0:T(8,128)(2,1)S(1)} %collective-permute-done.3.refs_1_.refs_7_), channel_id=1, source_target_pairs={{0,4},{4,0},{8,12},{12,8},{16,20},{20,16},{24,28},{28,24},{1,5},{5... | collective-permute-start | bytes 1572872 | tf_op jit(solution)/shard_map/ppermute | solution.py:668
  53.9 9.5 %collective-permute-start.11 = (f32[8,128]{1,0:T(8,128)S(1)}, f32[8,128]{1,0:T(8,128)S(1)}, u32[]{:S(2)}, u32[]{:S(2)}) collective-permute-start(f32[8,128]{1,0:T(8,128)S(1)} %get-tuple-element.66), channel_id=1, source_target_pairs={{0,3},{1,2},{2,1},{3,0},{4,7},{5,6},{6,5},{7,4},{8,11},{9,10},{10,... | collective-permute-start | bytes 12296 | tf_op jit(solution)/shard_map/ppermute | solution.py:668
  57.6 5.9 %collective-permute-start.10 = (f32[8,128]{1,0:T(8,128)S(1)}, f32[8,128]{1,0:T(8,128)S(1)}, u32[]{:S(2)}, u32[]{:S(2)}) collective-permute-start(f32[8,128]{1,0:T(8,128)S(1)} %get-tuple-element.66), channel_id=1, source_target_pairs={{0,2},{1,3},{2,0},{3,1},{4,6},{5,7},{6,4},{7,5},{8,10},{9,11},{10,... | collective-permute-start | bytes 12296 | tf_op jit(solution)/shard_map/ppermute | solution.py:668
  57.6 5.9 %collective-permute-start.9 = (f32[8,128]{1,0:T(8,128)S(1)}, f32[8,128]{1,0:T(8,128)S(1)}, u32[]{:S(2)}, u32[]{:S(2)}) collective-permute-start(f32[8,128]{1,0:T(8,128)S(1)} %get-tuple-element.66), channel_id=1, source_target_pairs={{0,1},{1,0},{2,3},{3,2},{4,5},{5,4},{6,7},{7,6},{8,9},{9,8},{10,11... | collective-permute-start | bytes 12296 | tf_op jit(solution)/shard_map/ppermute | solution.py:668
  64.5 6.1 %collective-permute-start.17 = (bf16[2,256,1024]{2,1,0:T(8,128)(2,1)S(1)}, bf16[2,256,1024]{2,1,0:T(8,128)(2,1)S(1)}, u32[]{:S(2)}, u32[]{:S(2)}) collective-permute-start(bf16[2,256,1024]{2,1,0:T(8,128)(2,1)S(1)} %gradient_block.2), channel_id=1, source_target_pairs={{0,4},{4,0},{8,12},{12,8},{16,20},{20,16},{24,28},{28,24},{1,5},{5... | collective-permute-start | bytes 3145736 | tf_op jit(solution)/shard_map/ppermute | solution.py:668
  64.5 2.7 %collective-permute-start.12 = (f32[8,128]{1,0:T(8,128)S(1)}, f32[8,128]{1,0:T(8,128)S(1)}, u32[]{:S(2)}, u32[]{:S(2)}) collective-permute-start(f32[8,128]{1,0:T(8,128)S(1)} %add_add_fusion.1.outs_0_.mine_ref.margin_ref), channel_id=1, source_target_pairs={{0,4},{4,0},{8,12},{12,8},{16,20},{20,16},{24,28},{28,24},{1,5},{5... | collective-permute-start | bytes 12296 | tf_op jit(solution)/shard_map/ppermute | solution.py:668
  69.9 2.8 %collective-permute-start.13 = (bf16[2,256,1024]{2,1,0:T(8,128)(2,1)S(1)}, bf16[2,256,1024]{2,1,0:T(8,128)(2,1)S(1)}, u32[]{:S(2)}, u32[]{:S(2)}) collective-permute-start(bf16[2,256,1024]{2,1,0:T(8,128)(2,1)S(1)} %get-tuple-element.71), channel_id=1, source_target_pairs={{0,4},{4,0},{8,12},{12,8},{16,20},{20,16},{24,28},{28,24},{1,5},{5... | collective-permute-start | bytes 3145736 | tf_op jit(solution)/shard_map/ppermute | solution.py:668
  70.1 4.0 %collective-permute-start.14 = (bf16[2,256,1024]{2,1,0:T(8,128)(2,1)S(1)}, bf16[2,256,1024]{2,1,0:T(8,128)(2,1)S(1)}, u32[]{:S(2)}, u32[]{:S(2)}) collective-permute-start(bf16[2,256,1024]{2,1,0:T(8,128)(2,1)S(1)} %get-tuple-element.72), channel_id=1, source_target_pairs={{0,4},{4,0},{8,12},{12,8},{16,20},{20,16},{24,28},{28,24},{1,5},{5... | collective-permute-start | bytes 3145736 | tf_op jit(solution)/shard_map/ppermute | solution.py:668
  70.4 5.1 %collective-permute-start.15 = (bf16[2,256,1024]{2,1,0:T(8,128)(2,1)S(1)}, bf16[2,256,1024]{2,1,0:T(8,128)(2,1)S(1)}, u32[]{:S(2)}, u32[]{:S(2)}) collective-permute-start(bf16[2,256,1024]{2,1,0:T(8,128)(2,1)S(1)} %get-tuple-element.73), channel_id=1, source_target_pairs={{0,4},{4,0},{8,12},{12,8},{16,20},{20,16},{24,28},{28,24},{1,5},{5... | collective-permute-start | bytes 3145736 | tf_op jit(solution)/shard_map/ppermute | solution.py:668
  71.7 14.8 %collective-permute-start.21 = (bf16[256,1024]{1,0:T(8,128)(2,1)S(1)}, bf16[256,1024]{1,0:T(8,128)(2,1)S(1)}, u32[]{:S(2)}, u32[]{:S(2)}) collective-permute-start(bf16[256,1024]{1,0:T(8,128)(2,1)S(1)} %get-tuple-element.81), channel_id=1, source_target_pairs={{0,8},{4,12},{8,0},{12,4},{16,24},{20,28},{24,16},{28,20},{1,9},{5... | collective-permute-start | bytes 1572872 | tf_op jit(solution)/shard_map/ppermute | solution.py:668
  72.3 14.9 %collective-permute-start.18 = (bf16[256,1024]{1,0:T(8,128)(2,1)S(1)}, bf16[256,1024]{1,0:T(8,128)(2,1)S(1)}, u32[]{:S(2)}, u32[]{:S(2)}) collective-permute-start(bf16[256,1024]{1,0:T(8,128)(2,1)S(1)} %get-tuple-element.77), channel_id=1, source_target_pairs={{0,16},{4,20},{8,24},{12,28},{16,0},{20,4},{24,8},{28,12},{1,17},{... | collective-permute-start | bytes 1572872 | tf_op jit(solution)/shard_map/ppermute | solution.py:668
  79.1 19.2 %collective-permute-start.16 = (bf16[256,1024]{1,0:T(8,128)(2,1)S(1)}, bf16[256,1024]{1,0:T(8,128)(2,1)S(1)}, u32[]{:S(2)}, u32[]{:S(2)}) collective-permute-start(bf16[256,1024]{1,0:T(8,128)(2,1)S(1)} %get-tuple-element.75), channel_id=1, source_target_pairs={{0,16},{4,20},{8,24},{12,28},{16,0},{20,4},{24,8},{28,12},{1,17},{... | collective-permute-start | bytes 1572872 | tf_op jit(solution)/shard_map/ppermute | solution.py:668
  79.7 20.1 %collective-permute-start.20 = (bf16[256,1024]{1,0:T(8,128)(2,1)S(1)}, bf16[256,1024]{1,0:T(8,128)(2,1)S(1)}, u32[]{:S(2)}, u32[]{:S(2)}) collective-permute-start(bf16[256,1024]{1,0:T(8,128)(2,1)S(1)} %get-tuple-element.79), channel_id=1, source_target_pairs={{0,8},{4,12},{8,0},{12,4},{16,24},{20,28},{24,16},{28,20},{1,9},{5... | collective-permute-start | bytes 1572872 | tf_op jit(solution)/shard_map/ppermute | solution.py:668
  86.7 17.3 %collective-permute-start.22 = (bf16[256,512]{1,0:T(8,128)(2,1)S(1)}, bf16[256,512]{1,0:T(8,128)(2,1)S(1)}, u32[]{:S(2)}, u32[]{:S(2)}) collective-permute-start(bf16[256,512]{1,0:T(8,128)(2,1)S(1)} %get-tuple-element.104), channel_id=1, source_target_pairs={{0,16},{4,20},{8,24},{12,28},{16,0},{20,4},{24,8},{28,12},{1,17},{... | collective-permute-start | bytes 786440 | tf_op jit(solution)/shard_map/ppermute | solution.py:668
  87.4 16.6 %collective-permute-start.19 = (bf16[256,512]{1,0:T(8,128)(2,1)S(1)}, bf16[256,512]{1,0:T(8,128)(2,1)S(1)}, u32[]{:S(2)}, u32[]{:S(2)}) collective-permute-start(bf16[256,512]{1,0:T(8,128)(2,1)S(1)} %get-tuple-element.106), channel_id=1, source_target_pairs={{0,8},{4,12},{8,0},{12,4},{16,24},{20,28},{24,16},{28,20},{1,9},{5... | collective-permute-start | bytes 786440 | tf_op jit(solution)/shard_map/ppermute | solution.py:668
  88.8 20.8 %collective-permute-start.24 = (bf16[256,512]{1,0:T(8,128)(2,1)S(1)}, bf16[256,512]{1,0:T(8,128)(2,1)S(1)}, u32[]{:S(2)}, u32[]{:S(2)}) collective-permute-start(bf16[256,512]{1,0:T(8,128)(2,1)S(1)} %get-tuple-element.103), channel_id=1, source_target_pairs={{0,16},{4,20},{8,24},{12,28},{16,0},{20,4},{24,8},{28,12},{1,17},{... | collective-permute-start | bytes 786440 | tf_op jit(solution)/shard_map/ppermute | solution.py:668
  98.3 11.2 %collective-permute-start.23 = (bf16[256,512]{1,0:T(8,128)(2,1)S(1)}, bf16[256,512]{1,0:T(8,128)(2,1)S(1)}, u32[]{:S(2)}, u32[]{:S(2)}) collective-permute-start(bf16[256,512]{1,0:T(8,128)(2,1)S(1)} %get-tuple-element.105), channel_id=1, source_target_pairs={{0,8},{4,12},{8,0},{12,4},{16,24},{20,28},{24,16},{28,20},{1,9},{5... | collective-permute-start | bytes 786440 | tf_op jit(solution)/shard_map/ppermute | solution.py:668
  104.3 17.0 %collective-permute-start.29 = (bf16[2,512,256]{2,1,0:T(8,128)(2,1)S(1)}, bf16[2,512,256]{2,1,0:T(8,128)(2,1)S(1)}, u32[]{:S(2)}, u32[]{:S(2)}) collective-permute-start(bf16[2,512,256]{2,1,0:T(8,128)(2,1)S(1)} %get-tuple-element.84.refs_4_.refs_0_), channel_id=1, source_target_pairs={{0,16},{4,20},{8,24},{12,28},{16,0},{20,4},{24,8},{28,12},{1,17},{... | collective-permute-start | bytes 1572872 | tf_op jit(solution)/shard_map/ppermute | solution.py:668
  104.7 16.6 %collective-permute-start.28 = (bf16[2,512,256]{2,1,0:T(8,128)(2,1)S(1)}, bf16[2,512,256]{2,1,0:T(8,128)(2,1)S(1)}, u32[]{:S(2)}, u32[]{:S(2)}) collective-permute-start(bf16[2,512,256]{2,1,0:T(8,128)(2,1)S(1)} %get-tuple-element.84.refs_4_.refs_0_), channel_id=1, source_target_pairs={{0,8},{4,12},{8,0},{12,4},{16,24},{20,28},{24,16},{28,20},{1,9},{5... | collective-permute-start | bytes 1572872 | tf_op jit(solution)/shard_map/ppermute | solution.py:668
  109.9 21.4 %collective-permute-start.34 = (bf16[2,512,256]{2,1,0:T(8,128)(2,1)S(1)}, bf16[2,512,256]{2,1,0:T(8,128)(2,1)S(1)}, u32[]{:S(2)}, u32[]{:S(2)}) collective-permute-start(bf16[2,512,256]{2,1,0:T(8,128)(2,1)S(1)} %get-tuple-element.86.refs_5_.refs_1_), channel_id=1, source_target_pairs={{0,16},{4,20},{8,24},{12,28},{16,0},{20,4},{24,8},{28,12},{1,17},{... | collective-permute-start | bytes 1572872 | tf_op jit(solution)/shard_map/ppermute | solution.py:668
  110.3 21.0 %collective-permute-start.33 = (bf16[2,512,256]{2,1,0:T(8,128)(2,1)S(1)}, bf16[2,512,256]{2,1,0:T(8,128)(2,1)S(1)}, u32[]{:S(2)}, u32[]{:S(2)}) collective-permute-start(bf16[2,512,256]{2,1,0:T(8,128)(2,1)S(1)} %get-tuple-element.86.refs_5_.refs_1_), channel_id=1, source_target_pairs={{0,8},{4,12},{8,0},{12,4},{16,24},{20,28},{24,16},{28,20},{1,9},{5... | collective-permute-start | bytes 1572872 | tf_op jit(solution)/shard_map/ppermute | solution.py:668
  112.0 3.6 %collective-permute-start.25 = (f32[8,128]{1,0:T(8,128)S(1)}, f32[8,128]{1,0:T(8,128)S(1)}, u32[]{:S(2)}, u32[]{:S(2)}) collective-permute-start(f32[8,128]{1,0:T(8,128)S(1)} %add.49), channel_id=1, source_target_pairs={{0,1},{1,0},{2,3},{3,2},{4,5},{5,4},{6,7},{7,6},{8,9},{9,8},{10,11... | collective-permute-start | bytes 12296 | tf_op jit(solution)/shard_map/ppermute | solution.py:668
  115.6 4.5 %collective-permute-start.26 = (f32[8,128]{1,0:T(8,128)S(1)}, f32[8,128]{1,0:T(8,128)S(1)}, u32[]{:S(2)}, u32[]{:S(2)}) collective-permute-start(f32[8,128]{1,0:T(8,128)S(1)} %add.50), channel_id=1, source_target_pairs={{0,2},{1,3},{2,0},{3,1},{4,6},{5,7},{6,4},{7,5},{8,10},{9,11},{10,... | collective-permute-start | bytes 12296 | tf_op jit(solution)/shard_map/ppermute | solution.py:668
  120.1 1.2 collective-permute-start.27
  121.8 9.2 %collective-permute-start.32 = (f32[8,128]{1,0:T(8,128)S(1)}, f32[8,128]{1,0:T(8,128)S(1)}, u32[]{:S(2)}, u32[]{:S(2)}) collective-permute-start(f32[8,128]{1,0:T(8,128)S(1)} %get-tuple-element.85.refs_11_), channel_id=1, source_target_pairs={{0,24},{4,28},{8,16},{12,20},{16,8},{20,12},{24,0},{28,4},{1,25},{... | collective-permute-start | bytes 12296 | tf_op jit(solution)/shard_map/ppermute | solution.py:668
  123.4 7.9 %collective-permute-start.31 = (f32[8,128]{1,0:T(8,128)S(1)}, f32[8,128]{1,0:T(8,128)S(1)}, u32[]{:S(2)}, u32[]{:S(2)}) collective-permute-start(f32[8,128]{1,0:T(8,128)S(1)} %get-tuple-element.85.refs_11_), channel_id=1, source_target_pairs={{0,16},{4,20},{8,24},{12,28},{16,0},{20,4},{24,8},{28,12},{1,17},{... | collective-permute-start | bytes 12296 | tf_op jit(solution)/shard_map/ppermute | solution.py:668
  124.4 6.9 %collective-permute-start.30 = (f32[8,128]{1,0:T(8,128)S(1)}, f32[8,128]{1,0:T(8,128)S(1)}, u32[]{:S(2)}, u32[]{:S(2)}) collective-permute-start(f32[8,128]{1,0:T(8,128)S(1)} %get-tuple-element.85.refs_11_), channel_id=1, source_target_pairs={{0,8},{4,12},{8,0},{12,4},{16,24},{20,28},{24,16},{28,20},{1,9},{5... | collective-permute-start | bytes 12296 | tf_op jit(solution)/shard_map/ppermute | solution.py:668
  131.8 2.7 %collective-permute-start.35 = (bf16[2,1024,256]{2,1,0:T(8,128)(2,1)S(1)}, bf16[2,1024,256]{2,1,0:T(8,128)(2,1)S(1)}, u32[]{:S(2)}, u32[]{:S(2)}) collective-permute-start(bf16[2,1024,256]{2,1,0:T(8,128)(2,1)S(1)} %get-tuple-element.88), channel_id=1, source_target_pairs={{0,4},{4,0},{8,12},{12,8},{16,20},{20,16},{24,28},{28,24},{1,5},{5... | collective-permute-start | bytes 3145736 | tf_op jit(solution)/shard_map/ppermute | solution.py:668
  131.8 5.8 %collective-permute-start.37 = (bf16[2,1024,256]{2,1,0:T(8,128)(2,1)S(1)}, bf16[2,1024,256]{2,1,0:T(8,128)(2,1)S(1)}, u32[]{:S(2)}, u32[]{:S(2)}) collective-permute-start(bf16[2,1024,256]{2,1,0:T(8,128)(2,1)S(1)} %get-tuple-element.92), channel_id=1, source_target_pairs={{0,4},{4,0},{8,12},{12,8},{16,20},{20,16},{24,28},{28,24},{1,5},{5... | collective-permute-start | bytes 3145736 | tf_op jit(solution)/shard_map/ppermute | solution.py:668
  132.3 5.3 %collective-permute-start.38 = (bf16[2,1024,256]{2,1,0:T(8,128)(2,1)S(1)}, bf16[2,1024,256]{2,1,0:T(8,128)(2,1)S(1)}, u32[]{:S(2)}, u32[]{:S(2)}) collective-permute-start(bf16[2,1024,256]{2,1,0:T(8,128)(2,1)S(1)} %get-tuple-element.93), channel_id=1, source_target_pairs={{0,4},{4,0},{8,12},{12,8},{16,20},{20,16},{24,28},{28,24},{1,5},{5... | collective-permute-start | bytes 3145736 | tf_op jit(solution)/shard_map/ppermute | solution.py:668
  132.4 14.3 %collective-permute-start.40 = (bf16[1024,256]{1,0:T(8,128)(2,1)S(1)}, bf16[1024,256]{1,0:T(8,128)(2,1)S(1)}, u32[]{:S(2)}, u32[]{:S(2)}) collective-permute-start(bf16[1024,256]{1,0:T(8,128)(2,1)S(1)} %get-tuple-element.97), channel_id=1, source_target_pairs={{0,8},{4,12},{8,0},{12,4},{16,24},{20,28},{24,16},{28,20},{1,9},{5... | collective-permute-start | bytes 1572872 | tf_op jit(solution)/shard_map/ppermute | solution.py:668
  133.9 14.0 %collective-permute-start.36 = (bf16[1024,256]{1,0:T(8,128)(2,1)S(1)}, bf16[1024,256]{1,0:T(8,128)(2,1)S(1)}, u32[]{:S(2)}, u32[]{:S(2)}) collective-permute-start(bf16[1024,256]{1,0:T(8,128)(2,1)S(1)} %get-tuple-element.91), channel_id=1, source_target_pairs={{0,16},{4,20},{8,24},{12,28},{16,0},{20,4},{24,8},{28,12},{1,17},{... | collective-permute-start | bytes 1572872 | tf_op jit(solution)/shard_map/ppermute | solution.py:668
  147.9 2.8 %collective-permute-start.39 = (bf16[1024,256]{1,0:T(8,128)(2,1)S(1)}, bf16[1024,256]{1,0:T(8,128)(2,1)S(1)}, u32[]{:S(2)}, u32[]{:S(2)}) collective-permute-start(bf16[1024,256]{1,0:T(8,128)(2,1)S(1)} %collective-permute-done.36.refs_0_), channel_id=1, source_target_pairs={{0,4},{4,0},{8,12},{12,8},{16,20},{20,16},{24,28},{28,24},{1,5},{5... | collective-permute-start | bytes 1572872 | tf_op jit(solution)/shard_map/ppermute | solution.py:668
  147.9 2.8 %collective-permute-start.41 = (bf16[1024,256]{1,0:T(8,128)(2,1)S(1)}, bf16[1024,256]{1,0:T(8,128)(2,1)S(1)}, u32[]{:S(2)}, u32[]{:S(2)}) collective-permute-start(bf16[1024,256]{1,0:T(8,128)(2,1)S(1)} %collective-permute-done.40.refs_1_), channel_id=1, source_target_pairs={{0,4},{4,0},{8,12},{12,8},{16,20},{20,16},{24,28},{28,24},{1,5},{5... | collective-permute-start | bytes 1572872 | tf_op jit(solution)/shard_map/ppermute | solution.py:668

commit v3 on v2

--- a/solution.py
+++ b/solution.py
@@ -300,7 +300,7 @@
 
     steps = k_ref.shape[0] // LEN * (k_ref.shape[1] // HD)
     start = -before_ref[0:1, 0:1] if keep else jnp.zeros((1, 1), jnp.float32)
-    margin_ref[...] = jnp.broadcast_to(lax.fori_loop(0, steps, one, start, unroll=min(steps, 2) if keep else 1), margin_ref.shape)
+    margin_ref[...] = jnp.broadcast_to(lax.fori_loop(0, steps, one, start, unroll=keep), margin_ref.shape)
 
 
 def attend(lengths, queries, keys, values, readout, before=None):
@@ -482,6 +482,24 @@
     )(*args)
 
 
+def hand_on_kernel(count, *refs):
+    pass
+
+
+def hand_on(arrays, earlier):
+    count = len(arrays)
+    return pl.pallas_call(
+        functools.partial(hand_on_kernel, count),
+        in_specs=[HBM] * (count + 1),
+        out_specs=[HBM] * count,
+        out_shape=[jax.ShapeDtypeStruct(x.shape, x.dtype) for x in arrays],
+        input_output_aliases={n: n for n in range(count)},
+        compiler_params=params(2),
+        cost_estimate=COST,
+        name="hand_on",
+    )(*arrays, earlier)
+
+
 def gate_kernel(value_ref, margin_ref, *refs):
     out_ref, first_ref = refs[-2:]
     out_ref[...] = value_ref[...]
@@ -500,13 +518,13 @@
     )(value, margin, *earlier)
 
 
-def pack_kernel(takes, *refs):
-    sources, outs, sem = refs[: 2 * len(takes)], refs[-1 - len(takes) : -1], refs[-1]
+def pack_kernel(takes, parts, *refs):
+    sources, outs, sem = refs[: parts * len(takes)], refs[-1 - len(takes) : -1], refs[-1]
     copies = []
     for n, i in enumerate(takes):
-        half = sources[2 * n].shape[1]
-        for h in (0, 1):
-            source, at = sources[2 * n + h], pl.ds(h * half, half)
+        half = sources[parts * n].shape[1]
+        for h in range(parts):
+            source, at = sources[parts * n + h], pl.ds(h * half, half)
             if i is None:
                 copies.append(pltpu.make_async_copy(source, outs[n].at[:, at, :], sem.at[n, h]))
             else:
@@ -518,11 +536,12 @@
 
 
 def pack(sources, takes, *earlier):
+    parts = len(sources[0])
     _, half, cols = sources[0][0].shape
-    shapes = [(2, 2 * half, cols) if i is None else (2 * half, cols) for i in takes]
-    return pl.pallas_call(
-        functools.partial(pack_kernel, tuple(takes)),
-        in_specs=[HBM] * (2 * len(takes) + len(earlier)),
+    shapes = [(2, parts * half, cols) if i is None else (parts * half, cols) for i in takes]
+    return pl.pallas_call(
+        functools.partial(pack_kernel, tuple(takes), parts),
+        in_specs=[HBM] * (parts * len(takes) + len(earlier)),
         out_specs=[HBM] * len(takes),
         out_shape=[jax.ShapeDtypeStruct(shape, jnp.bfloat16) for shape in shapes],
         scratch_shapes=[pltpu.SemaphoreType.DMA((len(takes), 2))],
@@ -578,7 +597,8 @@
     step = 64
     half = rows // 2
     token_ref[...] = jnp.zeros_like(token_ref)
-    coming = [read_rows(grads[n], g.at[n], [sem.at[i, n] for i in (0, 1)]) for n in range(count)]
+    here = [not is_whole(m) for m in masks]
+    coming = [[] if here[n] else read_rows(grads[n], g.at[n], [sem.at[i, n] for i in (0, 1)]) for n in range(count)]
     for group in coming:
         for copy in group:
             copy.start()
@@ -593,7 +613,8 @@
             def mix(t, carry):
                 j = pl.ds(pl.multiple_of(part * half + t * step, step), step)
                 for i in (0, 1):
-                    value = w[offset + n, i, j].astype(jnp.float32) - scale[i : i + 1, :] * g[n, i, j].astype(jnp.float32)
+                    slope = grads[n][i][j, :] if here[n] else g[n, i, j]
+                    value = w[offset + n, i, j].astype(jnp.float32) - scale[i : i + 1, :] * slope.astype(jnp.float32)
                     value = value.astype(jnp.bfloat16)
                     if first and n == 0:
                         new[i, j] = value
@@ -617,8 +638,8 @@
     _, _, rows, cols = w.shape
     count = len(masks)
     first = held is None
-    args = [idx, squares] + [x for m in masks for x in grads[m]]
-    in_specs = [SMEM, VMEM] + [HBM] * (len(args) - 2)
+    args = [idx, squares] + [x if is_whole(m) else resident(x) for m in masks for x in grads[m]]
+    in_specs = [SMEM, VMEM] + [HBM if is_whole(m) else VMEM for m in masks for x in grads[m]]
     args += [resident(w), resident(r)]
     in_specs += [VMEM] * 2
     out_specs = [HBM, VMEM]
@@ -695,8 +716,13 @@
     weights = send_near(policy_weights)
     normed, ref_keys, ref_values = norm_project(idx, hidden_in, reference_weights, tables)
     (ref_margin,) = attend(lengths, reference_queries, ref_keys, ref_values, readout)
+    two = [m for m in far if len(bits_of(m)) == 2]
+    ends = [(m, i) for m in two for i in (0, 1)]
+    packed = {}
+    if two:
+        packed = dict(zip(ends, pack([weights[m ^ link(i, m)] for m, i in ends], [i for m, i in ends], ref_margin)))
     for m in far:
-        relay(weights, m, ref_margin, *[weights[k] for k in near])
+        weights[m] = [swap(packed[m, i] if m in two else weights[m ^ link(i, m)][i], link(i, m)) for i in (0, 1)]
     for m in near:
         to_core(weights, m, ref_margin)
     held = project(idx, normed, [0, 1], weights, None, None)
@@ -712,8 +738,10 @@
     order = list(reversed(chips))
     split = max(len(far), 1)
 
-    def other_blocks(masks, *earlier):
-        blocks = gradient_blocks(idx, normed, cot, [m | 1 for m in masks], rows, None, earlier)
+    def other_blocks(masks, margin, other=None):
+        blocks = gradient_blocks(idx, normed, cot, [m | 1 for m in masks], rows, None, (margin,))
+        if other is not None:
+            blocks = hand_on(blocks, other)
         theirs.update({m: swap(block, 1) for m, block in zip(masks, blocks)})
         return blocks
 
@@ -725,7 +753,7 @@
     (margin,) = terms
     received = swap(margin, 1)
     margins = (margin, after(received, other_blocks(order[:split], margin)))
-    other_blocks(order[split:], margins[1])
+    other_blocks(order[split:], margin, margins[1])
 
     chip_sum = {}
     arrived = {m: ([], []) for m in chips}

time: 153 us -> 151 us (0.987)
  waiting for transfers between devices: 51.2 us -> 49.4 us
    ppermute x42, waiting for transfers between devices: 51.2 us -> 49.4 us  [swap(): return lax.ppermute(x, axis, [(i, i ^ bit) for i in range(size)])]
  transfers between devices with their start and end apart: 42 -> 42, of which waited for: 20 -> 19; matrix products, arithmetic and copies ran while one was open for 0% -> 0% of each run, Pallas kernels for 37% -> 37%
where the time goes in v3:
time: 151 us
  Pallas kernels  66.4 us (44%)
  waiting for transfers between devices  49.4 us (33%)
  starting transfers between devices  33.6 us (22%)
    ppermute x42, waiting for transfers between devices, swap(): return lax.ppermute(x, axis, [(i, i ^ bit) for i in range(size)])  49.4 us
    ppermute x42, starting transfers between devices, swap(): return lax.ppermute(x, axis, [(i, i ^ bit) for i in range(size)])  33.6 us
    pallas_call x1, Pallas kernels, norm_project(): pl.pallas_call(norm_project_kernel, in_specs=[SMEM, HBM, HBM, HBM], out_s...  17.8 us
    pallas_call x4, Pallas kernels, blend(): pl.pallas_call(functools.partial(blend_kernel, tuple(masks), first, offse...  12.3 us
    pallas_call x3, Pallas kernels, project(): pl.pallas_call(functools.partial(project_kernel, tuple(masks), first, las...  8.76 us
    pallas_call x2, Pallas kernels, attend(): pl.pallas_call(functools.partial(attend_kernel, keep), in_specs=[SMEM] +...  8.72 us
    pallas_call x4, Pallas kernels, gradient_blocks(): pl.pallas_call(functools.partial(kernel, tuple(masks)), in_specs=in_specs...  8.08 us
    pallas_call x1, Pallas kernels, attend_back(): pl.pallas_call(attend_back_kernel, in_specs=[SMEM] + [VMEM] * 6, out_spec...  5.04 us
  transfers between devices with their start and end apart: 42, of which 19 were waited for; matrix products, arithmetic and copies ran while one was open for 0% of the time, Pallas kernels for 37%

profile of v3, /device:TPU:0, one launch (start us, length us, event | category | flops | bytes accessed | tf_op | source)
XLA Modules:
  0.0 150.8 jit_solution(8355577268956072036)
XLA Ops:
  0.6 3.0 %collective-permute-start.1 = (bf16[2,1024,256]{2,1,0:T(8,128)(2,1)}, bf16[2,1024,256]{2,1,0:T(8,128)(2,1)S(1)}, u32[]{:S(2)}, u32[]{:S(2)}) collective-permute-start(bf16[2,1024,256]{2,1,0:T(8,128)(2,1)} %refs_0_.3), channel_id=1, source_target_pairs={{0,16},{4,20},{8,24},{12,28},{16,0},{20,4},{24,8},{28,12},{1,17},{... | collective-permute-start | bytes 3145736 | tf_op jit(solution)/shard_map/ppermute | solution.py:689
  3.7 1.5 collective-permute-start
  5.2 17.8 %norm_project.1 = (bf16[768,8192]{1,0:T(8,128)(2,1)S(1)}, bf16[768,256]{1,0:T(8,128)(2,1)S(1)}, bf16[768,256]{1,0:T(8,128)(2,1)S(1)}) custom-call(s32[1]{0:T(128)} %bitcast.idx_ref, bf16[768,8192]{1,0:T(8,128)(2,1)} %hidden_hbm.1, bf16[2,8192,256]{2,1,0:T(8,128)(2,1)} %refs_10_.1, f32[2,384,128]{2,1,0:T(8,128)} %constant.8.clone.table_hbm.refs_5_.table_ref), custom_call_target="tpu_custom_call" | custom-call | flops 1 | bytes 1 | tf_op jit(solution)/shard_map/norm_project/pallas_call | solution.py:133
  23.1 4.4 %attend.2.refs_2_.rest_0_ = f32[8,128]{1,0:T(8,128)S(1)} custom-call(s32[2]{0:T(128)S(1)} %copy-done.5, bf16[768,1024]{1,0:T(8,128)(2,1)S(1)} %copy-done.4, bf16[768,256]{1,0:T(8,128)(2,1)S(1)} %get-tuple-element.57.k_ref, bf16[768,256]{1,0:T(8,128)(2,1)S(1)} %get-tuple-element.58.v_ref, bf16[768,1024]{1,0:T(8,128)(2,1)S(1)} %copy-done), custom_call_target="tpu_custom_call" | custom-call | flops 1 | bytes 1 | tf_op jit(solution)/shard_map/attend/pallas_call | solution.py:318
  27.5 1.0 collective-permute-done.refs_0_.refs_2_
  28.5 0.5 collective-permute-start.5
  29.1 1.6 %collective-permute-start.3 = (bf16[1024,256]{1,0:T(8,128)(2,1)S(1)}, bf16[1024,256]{1,0:T(8,128)(2,1)S(1)}, u32[]{:S(2)}, u32[]{:S(2)}) collective-permute-start(bf16[1024,256]{1,0:T(8,128)(2,1)S(1)} %get-tuple-element.60), channel_id=1, source_target_pairs={{0,8},{4,12},{8,0},{12,4},{16,24},{20,28},{24,16},{28,20},{1,9},{5... | collective-permute-start | bytes 1572872 | tf_op jit(solution)/shard_map/ppermute | solution.py:689
  30.7 0.5 collective-permute-start.2
  31.2 2.0 %project.3.refs_4_ = f32[2,768,256]{2,1,0:T(8,128)S(1)} custom-call(s32[1]{0:T(128)} %bitcast.idx_ref, bf16[768,8192]{1,0:T(8,128)(2,1)S(1)} %get-tuple-element.56.x_ref, bf16[2,1024,256]{2,1,0:T(8,128)(2,1)S(1)} %copy-done.2, bf16[2,1024,256]{2,1,0:T(8,128)(2,1)S(1)} %collective-permute-done.6.refs_1_), custom_call_target="tpu_custom_call" | custom-call | flops 1 | bytes 1 | tf_op jit(solution)/shard_map/project/pallas_call | solution.py:226
  33.3 4.1 %project.4.refs_4_ = f32[2,768,256]{2,1,0:T(8,128)S(1)} custom-call(s32[1]{0:T(128)} %bitcast.idx_ref, bf16[768,8192]{1,0:T(8,128)(2,1)S(1)} %get-tuple-element.56.x_ref, bf16[2,1024,256]{2,1,0:T(8,128)(2,1)S(1)} %collective-permute-done.refs_0_.refs_2_, bf16[2,1024,256]{2,1,0:T(8,128)(2,1)S(1)} %collective-permute-done.4.refs_1_.refs_3_, ...), custom_call_target="tpu_custom_call" | custom-call | flops 1 | bytes 1 | tf_op jit(solution)/shard_map/project/pallas_call | solution.py:226
  37.4 5.6 %collective-permute-done.3.refs_1_.refs_7_ = bf16[1024,256]{1,0:T(8,128)(2,1)S(1)} collective-permute-done((bf16[1024,256]{1,0:T(8,128)(2,1)S(1)}, bf16[1024,256]{1,0:T(8,128)(2,1)S(1)}, u32[]{:S(2)}, u32[]{:S(2)}) %collective-permute-start.3) | collective-permute-done | bytes 524320 | tf_op jit(solution)/shard_map/ppermute | solution.py:689
  43.0 1.2 collective-permute-done.2.refs_0_.refs_6_
  44.2 0.5 collective-permute-start.8
  44.7 1.4 collective-permute-done.7.refs_2_.refs_8_
  46.1 0.7 collective-permute-done.8.refs_3_.refs_9_
  46.9 2.6 %project.5 = (bf16[768,256]{1,0:T(8,128)(2,1)S(1)}, bf16[768,256]{1,0:T(8,128)(2,1)S(1)}) custom-call(s32[1]{0:T(128)} %bitcast.idx_ref, bf16[768,8192]{1,0:T(8,128)(2,1)S(1)} %get-tuple-element.56.x_ref, bf16[1024,256]{1,0:T(8,128)(2,1)S(1)} %collective-permute-done.2.refs_0_.refs_6_, bf16[1024,256]{1,0:T(8,128)(2,1)S(1)} %collective-permute-done.3.refs_1_.refs_7_, ...), custom_call_target="tpu_custom_call" | custom-call | flops 1 | bytes 1 | tf_op jit(solution)/shard_map/project/pallas_call | solution.py:226
  49.5 4.3 %attend.3 = (f32[8,128]{1,0:T(8,128)S(1)}, bf16[2,2,768,512]{3,2,1,0:T(8,128)(2,1)S(1)}, f32[2,2,3,512]{3,2,1,0:T(4,128)S(1)}) custom-call(s32[2]{0:T(128)S(1)} %copy-done.5, bf16[768,1024]{1,0:T(8,128)(2,1)S(1)} %copy-done.1, bf16[768,256]{1,0:T(8,128)(2,1)S(1)} %get-tuple-element.66.k_ref, bf16[768,256]{1,0:T(8,128)(2,1)S(1)} %get-tuple-element.65.v_ref, ...), custom_call_target="tpu_custom_call" | custom-call | flops 1 | bytes 1 | tf_op jit(solution)/shard_map/attend/pallas_call | solution.py:318
  53.8 3.7 %collective-permute-start.11 = (f32[8,128]{1,0:T(8,128)S(1)}, f32[8,128]{1,0:T(8,128)S(1)}, u32[]{:S(2)}, u32[]{:S(2)}) collective-permute-start(f32[8,128]{1,0:T(8,128)S(1)} %get-tuple-element.69), channel_id=1, source_target_pairs={{0,3},{1,2},{2,1},{3,0},{4,7},{5,6},{6,5},{7,4},{8,11},{9,10},{10,... | collective-permute-start | bytes 12296 | tf_op jit(solution)/shard_map/ppermute | solution.py:689
  57.5 0.8 collective-permute-start.9
  58.3 5.0 %attend_back.1.cot_ref = bf16[2,256,768]{2,1,0:T(8,128)(2,1)S(1)} custom-call(s32[2]{0:T(128)S(1)} %copy-done.5, bf16[768,1024]{1,0:T(8,128)(2,1)S(1)} %copy-done.1, bf16[768,256]{1,0:T(8,128)(2,1)S(1)} %get-tuple-element.65.v_ref, bf16[768,1024]{1,0:T(8,128)(2,1)S(1)} %copy-done, bf16[2,2,768,512]{3,2,1,0:T(8,128)(2,1)S(1)} %get-tuple-element.67.prob_ref, ...), custom_call_target="tpu_custom_call" | custom-call | flops 1 | bytes 1 | tf_op jit(solution)/shard_map/attend_back/pallas_call | solution.py:372
  63.4 1.0 gradient_block.2
  64.5 0.5 collective-permute-start.12
  65.0 2.7 %gradient_block.3 = (bf16[2,256,1024]{2,1,0:T(8,128)(2,1)S(1)}, bf16[2,256,1024]{2,1,0:T(8,128)(2,1)S(1)}, bf16[2,256,1024]{2,1,0:T(8,128)(2,1)S(1)}) custom-call(s32[1]{0:T(128)} %bitcast.idx_ref, bf16[768,8192]{1,0:T(8,128)(2,1)S(1)} %get-tuple-element.56.x_ref, bf16[2,256,768]{2,1,0:T(8,128)(2,1)S(1)} %attend_back.1.cot_ref, ...), custom_call_target="tpu_custom_call" | custom-call | flops 1 | bytes 1 | tf_op jit(solution)/shard_map/gradient_block/pallas_call | solution.py:440
  67.8 0.4 collective-permute-start.14
  68.3 1.1 merged_block.3
  69.4 0.6 collective-permute-start.21
  70.4 1.5 collective-permute-done.14.refs_1_
  71.9 1.5 collective-permute-done.15.refs_2_
  73.4 3.3 %merged_block.2 = (bf16[256,1024]{1,0:T(8,128)(2,1)S(1)}, bf16[256,1024]{1,0:T(8,128)(2,1)S(1)}, bf16[256,1024]{1,0:T(8,128)(2,1)S(1)}, bf16[256,1024]{1,0:T(8,1...) custom-call(s32[1]{0:T(128)} %bitcast.idx_ref, bf16[768,8192]{1,0:T(8,128)(2,1)S(1)} %get-tuple-element.56.x_ref, ...), custom_call_target="tpu_custom_call" | custom-call | flops 1 | bytes 1 | tf_op jit(solution)/shard_map/merged_block/pallas_call | solution.py:440
  76.7 0.6 collective-permute-start.16
  77.6 6.6 %collective-permute-done.21 = bf16[256,1024]{1,0:T(8,128)(2,1)S(1)} collective-permute-done((bf16[256,1024]{1,0:T(8,128)(2,1)S(1)}, bf16[256,1024]{1,0:T(8,128)(2,1)S(1)}, u32[]{:S(2)}, u32[]{:S(2)}) %collective-permute-start.21) | collective-permute-done | bytes 524320 | tf_op jit(solution)/shard_map/ppermute | solution.py:689
  84.4 0.6 collective-permute-start.22
  85.1 1.4 collective-permute-start.19
  86.5 0.7 collective-permute-start.24
  87.2 8.8 %collective-permute-done.16.refs_1_ = bf16[256,1024]{1,0:T(8,128)(2,1)S(1)} collective-permute-done((bf16[256,1024]{1,0:T(8,128)(2,1)S(1)}, bf16[256,1024]{1,0:T(8,128)(2,1)S(1)}, u32[]{:S(2)}, u32[]{:S(2)}) %collective-permute-start.16) | collective-permute-done | bytes 524320 | tf_op jit(solution)/shard_map/ppermute | solution.py:689
  96.0 1.5 collective-permute-start.23
  97.5 4.1 %collective-permute-done.22.refs_5_ = bf16[256,512]{1,0:T(8,128)(2,1)S(1)} collective-permute-done((bf16[256,512]{1,0:T(8,128)(2,1)S(1)}, bf16[256,512]{1,0:T(8,128)(2,1)S(1)}, u32[]{:S(2)}, u32[]{:S(2)}) %collective-permute-start.22) | collective-permute-done | bytes 262176 | tf_op jit(solution)/shard_map/ppermute | solution.py:689
  102.0 0.4 collective-permute-start.29
  102.4 1.6 %collective-permute-start.28 = (bf16[2,512,256]{2,1,0:T(8,128)(2,1)S(1)}, bf16[2,512,256]{2,1,0:T(8,128)(2,1)S(1)}, u32[]{:S(2)}, u32[]{:S(2)}) collective-permute-start(bf16[2,512,256]{2,1,0:T(8,128)(2,1)S(1)} %get-tuple-element.90.refs_4_.refs_0_), channel_id=1, source_target_pairs={{0,8},{4,12},{8,0},{12,4},{16,24},{20,28},{24,16},{28,20},{1,9},{5... | collective-permute-start | bytes 1572872 | tf_op jit(solution)/shard_map/ppermute | solution.py:689
  104.1 3.2 %collective-permute-done.24.refs_5_ = bf16[256,512]{1,0:T(8,128)(2,1)S(1)} collective-permute-done((bf16[256,512]{1,0:T(8,128)(2,1)S(1)}, bf16[256,512]{1,0:T(8,128)(2,1)S(1)}, u32[]{:S(2)}, u32[]{:S(2)}) %collective-permute-start.24) | collective-permute-done | bytes 262176 | tf_op jit(solution)/shard_map/ppermute | solution.py:689
  107.6 0.4 collective-permute-start.34
  108.0 1.6 %collective-permute-start.33 = (bf16[2,512,256]{2,1,0:T(8,128)(2,1)S(1)}, bf16[2,512,256]{2,1,0:T(8,128)(2,1)S(1)}, u32[]{:S(2)}, u32[]{:S(2)}) collective-permute-start(bf16[2,512,256]{2,1,0:T(8,128)(2,1)S(1)} %get-tuple-element.92.refs_5_.refs_1_), channel_id=1, source_target_pairs={{0,8},{4,12},{8,0},{12,4},{16,24},{20,28},{24,16},{28,20},{1,9},{5... | collective-permute-start | bytes 1572872 | tf_op jit(solution)/shard_map/ppermute | solution.py:689
  109.7 1.2 collective-permute-start.25
  110.9 2.4 %collective-permute-done.25 = f32[8,128]{1,0:T(8,128)S(1)} collective-permute-done((f32[8,128]{1,0:T(8,128)S(1)}, f32[8,128]{1,0:T(8,128)S(1)}, u32[]{:S(2)}, u32[]{:S(2)}) %collective-permute-start.25) | collective-permute-done | bytes 4128 | tf_op jit(solution)/shard_map/ppermute | solution.py:689
  113.3 2.1 %collective-permute-start.26 = (f32[8,128]{1,0:T(8,128)S(1)}, f32[8,128]{1,0:T(8,128)S(1)}, u32[]{:S(2)}, u32[]{:S(2)}) collective-permute-start(f32[8,128]{1,0:T(8,128)S(1)} %add.50), channel_id=1, source_target_pairs={{0,2},{1,3},{2,0},{3,1},{4,6},{5,7},{6,4},{7,5},{8,10},{9,11},{10,... | collective-permute-start | bytes 12296 | tf_op jit(solution)/shard_map/ppermute | solution.py:689
  115.4 2.4 %collective-permute-done.26 = f32[8,128]{1,0:T(8,128)S(1)} collective-permute-done((f32[8,128]{1,0:T(8,128)S(1)}, f32[8,128]{1,0:T(8,128)S(1)}, u32[]{:S(2)}, u32[]{:S(2)}) %collective-permute-start.26) | collective-permute-done | bytes 4128 | tf_op jit(solution)/shard_map/ppermute | solution.py:689
  117.8 1.2 collective-permute-done.27
  119.0 0.6 gate.1
  119.5 1.6 %collective-permute-start.32 = (f32[8,128]{1,0:T(8,128)S(1)}, f32[8,128]{1,0:T(8,128)S(1)}, u32[]{:S(2)}, u32[]{:S(2)}) collective-permute-start(f32[8,128]{1,0:T(8,128)S(1)} %get-tuple-element.91.refs_11_), channel_id=1, source_target_pairs={{0,24},{4,28},{8,16},{12,20},{16,8},{20,12},{24,0},{28,4},{1,25},{... | collective-permute-start | bytes 12296 | tf_op jit(solution)/shard_map/ppermute | solution.py:689
  121.1 1.0 collective-permute-start.31
  122.1 1.0 collective-permute-start.30
  123.1 3.8 %fetch.1 = (bf16[8,2,1024,256]{3,2,1,0:T(8,128)(2,1)S(1)}, bf16[8,2,1024,256]{3,2,1,0:T(8,128)(2,1)S(1)}) custom-call(s32[1]{0:T(128)} %bitcast.idx_ref, bf16[2,1024,256]{2,1,0:T(8,128)(2,1)S(1)} %copy-done.2, bf16[2,1024,256]{2,1,0:T(8,128)(2,1)S(1)} %collective-permute-done.6.refs_1_, bf16[2,1024,256]{2,1,0:T(8,128)(2,1)S(1)} %collective-permute-done.refs_0_.refs_2_, ...), custom_call_target="tpu_custom_call" | custom-call | flops 1 | bytes 1 | tf_op jit(solution)/shard_map/fetch/pallas_call | solution.py:574
  126.9 2.0 %collective-permute-done.32 = f32[8,128]{1,0:T(8,128)S(1)} collective-permute-done((f32[8,128]{1,0:T(8,128)S(1)}, f32[8,128]{1,0:T(8,128)S(1)}, u32[]{:S(2)}, u32[]{:S(2)}) %collective-permute-start.32) | collective-permute-done | bytes 4128 | tf_op jit(solution)/shard_map/ppermute | solution.py:689
  129.2 0.4 pack.3
  129.7 0.5 collective-permute-start.37
  130.2 1.5 collective-permute-start.40
  131.7 0.5 collective-permute-start.36
  132.3 3.2 %blend.4 = (bf16[2,8192,256]{2,1,0:T(8,128)(2,1)}, f32[8,128]{1,0:T(8,128)}, bf16[2,1024,256]{2,1,0:T(8,128)(2,1)}) custom-call(s32[1]{0:T(128)} %bitcast.idx_ref, f32[8,128]{1,0:T(8,128)S(1)} %add_add_fusion.refs_10_.square_ref, bf16[2,512,256]{2,1,0:T(8,128)(2,1)S(1)} %get-tuple-element.90.refs_4_.refs_0_, ...), custom_call_target="tpu_custom_call" | custom-call | flops 1 | bytes 1 | tf_op jit(solution)/shard_map/blend/pallas_call | solution.py:656
  135.5 4.8 %blend.5 = (bf16[2,8192,256]{2,1,0:T(8,128)(2,1)}, f32[8,128]{1,0:T(8,128)}) custom-call(s32[1]{0:T(128)} %bitcast.idx_ref, f32[8,128]{1,0:T(8,128)S(1)} %add_add_fusion.refs_10_.square_ref, bf16[2,512,256]{2,1,0:T(8,128)(2,1)S(1)} %collective-permute-done.28.refs_0_.refs_6_, ...), custom_call_target="tpu_custom_call", output_to_operand_aliasing={{0}: (10, {})} | custom-call | flops 1 | bytes 1 | tf_op jit(solution)/shard_map/blend/pallas_call | solution.py:656
  140.3 4.2 %collective-permute-done.40.refs_1_ = bf16[1024,256]{1,0:T(8,128)(2,1)S(1)} collective-permute-done((bf16[1024,256]{1,0:T(8,128)(2,1)S(1)}, bf16[1024,256]{1,0:T(8,128)(2,1)S(1)}, u32[]{:S(2)}, u32[]{:S(2)}) %collective-permute-start.40) | collective-permute-done | bytes 524320 | tf_op jit(solution)/shard_map/ppermute | solution.py:689
  144.5 1.2 collective-permute-done.36.refs_0_
  145.7 0.5 collective-permute-start.41
  146.2 2.2 %blend.6 = (bf16[2,8192,256]{2,1,0:T(8,128)(2,1)}, f32[8,128]{1,0:T(8,128)}) custom-call(s32[1]{0:T(128)} %bitcast.idx_ref, f32[8,128]{1,0:T(8,128)S(1)} %add_add_fusion.refs_10_.square_ref, bf16[1024,256]{1,0:T(8,128)(2,1)S(1)} %collective-permute-done.36.refs_0_, ...), custom_call_target="tpu_custom_call", output_to_operand_aliasing={{0}: (6, {})} | custom-call | flops 1 | bytes 1 | tf_op jit(solution)/shard_map/blend/pallas_call | solution.py:656
  148.4 2.2 %blend.7 = (bf16[2,8192,256]{2,1,0:T(8,128)(2,1)}, f32[8,128]{1,0:T(8,128)}) custom-call(s32[1]{0:T(128)} %bitcast.idx_ref, f32[8,128]{1,0:T(8,128)S(1)} %add_add_fusion.refs_10_.square_ref, bf16[1024,256]{1,0:T(8,128)(2,1)S(1)} %collective-permute-done.39.refs_0_, ...), custom_call_target="tpu_custom_call", output_to_operand_aliasing={{0}: (6, {})} | custom-call | flops 1 | bytes 1 | tf_op jit(solution)/shard_map/blend/pallas_call | solution.py:656
  (62 shorter events, 2.8 us)
Async XLA Ops:
  0.6 26.9 %collective-permute-start.1 = (bf16[2,1024,256]{2,1,0:T(8,128)(2,1)}, bf16[2,1024,256]{2,1,0:T(8,128)(2,1)S(1)}, u32[]{:S(2)}, u32[]{:S(2)}) collective-permute-start(bf16[2,1024,256]{2,1,0:T(8,128)(2,1)} %refs_0_.3), channel_id=1, source_target_pairs={{0,16},{4,20},{8,24},{12,28},{16,0},{20,4},{24,8},{28,12},{1,17},{... | collective-permute-start | bytes 3145736 | tf_op jit(solution)/shard_map/ppermute | solution.py:689
  3.7 24.8 %collective-permute-start = (bf16[2,1024,256]{2,1,0:T(8,128)(2,1)}, bf16[2,1024,256]{2,1,0:T(8,128)(2,1)S(1)}, u32[]{:S(2)}, u32[]{:S(2)}) collective-permute-start(bf16[2,1024,256]{2,1,0:T(8,128)(2,1)} %refs_0_.3), channel_id=1, source_target_pairs={{0,8},{4,12},{8,0},{12,4},{16,24},{20,28},{24,16},{28,20},{1,9},{5... | collective-permute-start | bytes 3145736 | tf_op jit(solution)/shard_map/ppermute | solution.py:689
  5.2 26.0 %collective-permute-start.6 = (bf16[2,1024,256]{2,1,0:T(8,128)(2,1)}, bf16[2,1024,256]{2,1,0:T(8,128)(2,1)S(1)}, u32[]{:S(2)}, u32[]{:S(2)}) collective-permute-start(bf16[2,1024,256]{2,1,0:T(8,128)(2,1)} %refs_0_.3), channel_id=1, source_target_pairs={{0,4},{4,0},{8,12},{12,8},{16,20},{20,16},{24,28},{28,24},{1,5},{5... | collective-permute-start | bytes 3145736 | tf_op jit(solution)/shard_map/ppermute | solution.py:689
  5.2 17.9 %copy-start = (bf16[768,1024]{1,0:T(8,128)(2,1)S(1)}, bf16[768,1024]{1,0:T(8,128)(2,1)}, u32[]{:S(2)}) copy-start(bf16[768,1024]{1,0:T(8,128)(2,1)} %ro_ref.5) | copy-start | bytes 4718596
  5.2 17.9 %copy-start.4 = (bf16[768,1024]{1,0:T(8,128)(2,1)S(1)}, bf16[768,1024]{1,0:T(8,128)(2,1)}, u32[]{:S(2)}) copy-start(bf16[768,1024]{1,0:T(8,128)(2,1)} %q_ref.3) | copy-start | bytes 4718596
  5.2 17.9 %copy-start.5 = (s32[2]{0:T(128)S(1)}, s32[2]{0:T(128)}, u32[]{:S(2)}) copy-start(s32[2]{0:T(128)} %len_ref.5) | copy-start | bytes 28
  5.2 26.0 %copy-start.2 = (bf16[2,1024,256]{2,1,0:T(8,128)(2,1)S(1)}, bf16[2,1024,256]{2,1,0:T(8,128)(2,1)}, u32[]{:S(2)}) copy-start(bf16[2,1024,256]{2,1,0:T(8,128)(2,1)} %refs_0_.3) | copy-start | bytes 3145732
  28.5 4.8 %collective-permute-start.4 = (bf16[2,1024,256]{2,1,0:T(8,128)(2,1)S(1)}, bf16[2,1024,256]{2,1,0:T(8,128)(2,1)S(1)}, u32[]{:S(2)}, u32[]{:S(2)}) collective-permute-start(bf16[2,1024,256]{2,1,0:T(8,128)(2,1)S(1)} %collective-permute-done.refs_0_.refs_2_), channel_id=1, source_target_pairs={{0,4},{4,0},{8,12},{12,8},{16,20},{20,16},{24,28},{28,24},{1,5},{5... | collective-permute-start | bytes 3145736 | tf_op jit(solution)/shard_map/ppermute | solution.py:689
  28.5 4.8 %collective-permute-start.5 = (bf16[2,1024,256]{2,1,0:T(8,128)(2,1)S(1)}, bf16[2,1024,256]{2,1,0:T(8,128)(2,1)S(1)}, u32[]{:S(2)}, u32[]{:S(2)}) collective-permute-start(bf16[2,1024,256]{2,1,0:T(8,128)(2,1)S(1)} %collective-permute-done.1.refs_1_.refs_2_.refs_4_), channel_id=1, source_target_pairs={{0,4},{4,0},{8,12},{12,8},{16,20},{20,16},{24,28},{28,24},{1,5},{5... | collective-permute-start | bytes 3145736 | tf_op jit(solution)/shard_map/ppermute | solution.py:689
  29.1 13.9 %collective-permute-start.3 = (bf16[1024,256]{1,0:T(8,128)(2,1)S(1)}, bf16[1024,256]{1,0:T(8,128)(2,1)S(1)}, u32[]{:S(2)}, u32[]{:S(2)}) collective-permute-start(bf16[1024,256]{1,0:T(8,128)(2,1)S(1)} %get-tuple-element.60), channel_id=1, source_target_pairs={{0,8},{4,12},{8,0},{12,4},{16,24},{20,28},{24,16},{28,20},{1,9},{5... | collective-permute-start | bytes 1572872 | tf_op jit(solution)/shard_map/ppermute | solution.py:689
  30.7 13.6 %collective-permute-start.2 = (bf16[1024,256]{1,0:T(8,128)(2,1)S(1)}, bf16[1024,256]{1,0:T(8,128)(2,1)S(1)}, u32[]{:S(2)}, u32[]{:S(2)}) collective-permute-start(bf16[1024,256]{1,0:T(8,128)(2,1)S(1)} %get-tuple-element.59), channel_id=1, source_target_pairs={{0,16},{4,20},{8,24},{12,28},{16,0},{20,4},{24,8},{28,12},{1,17},{... | collective-permute-start | bytes 1572872 | tf_op jit(solution)/shard_map/ppermute | solution.py:689
  37.4 12.2 %copy-start.1 = (bf16[768,1024]{1,0:T(8,128)(2,1)S(1)}, bf16[768,1024]{1,0:T(8,128)(2,1)}, u32[]{:S(2)}) copy-start(bf16[768,1024]{1,0:T(8,128)(2,1)} %q_ref.5) | copy-start | bytes 4718596
  37.4 20.9 %copy-start.3 = (f32[2,384,128]{2,1,0:T(8,128)S(1)}, f32[2,384,128]{2,1,0:T(8,128)}, u32[]{:S(2)}) copy-start(f32[2,384,128]{2,1,0:T(8,128)} %constant.8.clone.table_hbm.refs_5_.table_ref) | copy-start | bytes 1179652
  44.2 1.9 %collective-permute-start.7 = (bf16[1024,256]{1,0:T(8,128)(2,1)S(1)}, bf16[1024,256]{1,0:T(8,128)(2,1)S(1)}, u32[]{:S(2)}, u32[]{:S(2)}) collective-permute-start(bf16[1024,256]{1,0:T(8,128)(2,1)S(1)} %collective-permute-done.2.refs_0_.refs_6_), channel_id=1, source_target_pairs={{0,4},{4,0},{8,12},{12,8},{16,20},{20,16},{24,28},{28,24},{1,5},{5... | collective-permute-start | bytes 1572872 | tf_op jit(solution)/shard_map/ppermute | solution.py:689
  44.2 2.7 %collective-permute-start.8 = (bf16[1024,256]{1,0:T(8,128)(2,1)S(1)}, bf16[1024,256]{1,0:T(8,128)(2,1)S(1)}, u32[]{:S(2)}, u32[]{:S(2)}) collective-permute-start(bf16[1024,256]{1,0:T(8,128)(2,1)S(1)} %collective-permute-done.3.refs_1_.refs_7_), channel_id=1, source_target_pairs={{0,4},{4,0},{8,12},{12,8},{16,20},{20,16},{24,28},{28,24},{1,5},{5... | collective-permute-start | bytes 1572872 | tf_op jit(solution)/shard_map/ppermute | solution.py:689
  53.8 9.5 %collective-permute-start.11 = (f32[8,128]{1,0:T(8,128)S(1)}, f32[8,128]{1,0:T(8,128)S(1)}, u32[]{:S(2)}, u32[]{:S(2)}) collective-permute-start(f32[8,128]{1,0:T(8,128)S(1)} %get-tuple-element.69), channel_id=1, source_target_pairs={{0,3},{1,2},{2,1},{3,0},{4,7},{5,6},{6,5},{7,4},{8,11},{9,10},{10,... | collective-permute-start | bytes 12296 | tf_op jit(solution)/shard_map/ppermute | solution.py:689
  57.5 5.9 %collective-permute-start.10 = (f32[8,128]{1,0:T(8,128)S(1)}, f32[8,128]{1,0:T(8,128)S(1)}, u32[]{:S(2)}, u32[]{:S(2)}) collective-permute-start(f32[8,128]{1,0:T(8,128)S(1)} %get-tuple-element.69), channel_id=1, source_target_pairs={{0,2},{1,3},{2,0},{3,1},{4,6},{5,7},{6,4},{7,5},{8,10},{9,11},{10,... | collective-permute-start | bytes 12296 | tf_op jit(solution)/shard_map/ppermute | solution.py:689
  57.5 5.9 %collective-permute-start.9 = (f32[8,128]{1,0:T(8,128)S(1)}, f32[8,128]{1,0:T(8,128)S(1)}, u32[]{:S(2)}, u32[]{:S(2)}) collective-permute-start(f32[8,128]{1,0:T(8,128)S(1)} %get-tuple-element.69), channel_id=1, source_target_pairs={{0,1},{1,0},{2,3},{3,2},{4,5},{5,4},{6,7},{7,6},{8,9},{9,8},{10,11... | collective-permute-start | bytes 12296 | tf_op jit(solution)/shard_map/ppermute | solution.py:689
  64.4 3.9 %collective-permute-start.17 = (bf16[2,256,1024]{2,1,0:T(8,128)(2,1)S(1)}, bf16[2,256,1024]{2,1,0:T(8,128)(2,1)S(1)}, u32[]{:S(2)}, u32[]{:S(2)}) collective-permute-start(bf16[2,256,1024]{2,1,0:T(8,128)(2,1)S(1)} %gradient_block.2), channel_id=1, source_target_pairs={{0,4},{4,0},{8,12},{12,8},{16,20},{20,16},{24,28},{28,24},{1,5},{5... | collective-permute-start | bytes 3145736 | tf_op jit(solution)/shard_map/ppermute | solution.py:689
  64.5 3.2 %collective-permute-start.12 = (f32[8,128]{1,0:T(8,128)S(1)}, f32[8,128]{1,0:T(8,128)S(1)}, u32[]{:S(2)}, u32[]{:S(2)}) collective-permute-start(f32[8,128]{1,0:T(8,128)S(1)} %add_add_fusion.1.outs_0_.mine_ref.margin_ref), channel_id=1, source_target_pairs={{0,4},{4,0},{8,12},{12,8},{16,20},{20,16},{24,28},{28,24},{1,5},{5... | collective-permute-start | bytes 12296 | tf_op jit(solution)/shard_map/ppermute | solution.py:689
  67.6 2.7 %collective-permute-start.13 = (bf16[2,256,1024]{2,1,0:T(8,128)(2,1)S(1)}, bf16[2,256,1024]{2,1,0:T(8,128)(2,1)S(1)}, u32[]{:S(2)}, u32[]{:S(2)}) collective-permute-start(bf16[2,256,1024]{2,1,0:T(8,128)(2,1)S(1)} %get-tuple-element.77), channel_id=1, source_target_pairs={{0,4},{4,0},{8,12},{12,8},{16,20},{20,16},{24,28},{28,24},{1,5},{5... | collective-permute-start | bytes 3145736 | tf_op jit(solution)/shard_map/ppermute | solution.py:689
  67.8 4.1 %collective-permute-start.14 = (bf16[2,256,1024]{2,1,0:T(8,128)(2,1)S(1)}, bf16[2,256,1024]{2,1,0:T(8,128)(2,1)S(1)}, u32[]{:S(2)}, u32[]{:S(2)}) collective-permute-start(bf16[2,256,1024]{2,1,0:T(8,128)(2,1)S(1)} %get-tuple-element.78), channel_id=1, source_target_pairs={{0,4},{4,0},{8,12},{12,8},{16,20},{20,16},{24,28},{28,24},{1,5},{5... | collective-permute-start | bytes 3145736 | tf_op jit(solution)/shard_map/ppermute | solution.py:689
  68.2 5.1 %collective-permute-start.15 = (bf16[2,256,1024]{2,1,0:T(8,128)(2,1)S(1)}, bf16[2,256,1024]{2,1,0:T(8,128)(2,1)S(1)}, u32[]{:S(2)}, u32[]{:S(2)}) collective-permute-start(bf16[2,256,1024]{2,1,0:T(8,128)(2,1)S(1)} %get-tuple-element.79), channel_id=1, source_target_pairs={{0,4},{4,0},{8,12},{12,8},{16,20},{20,16},{24,28},{28,24},{1,5},{5... | collective-permute-start | bytes 3145736 | tf_op jit(solution)/shard_map/ppermute | solution.py:689
  69.4 14.8 %collective-permute-start.21 = (bf16[256,1024]{1,0:T(8,128)(2,1)S(1)}, bf16[256,1024]{1,0:T(8,128)(2,1)S(1)}, u32[]{:S(2)}, u32[]{:S(2)}) collective-permute-start(bf16[256,1024]{1,0:T(8,128)(2,1)S(1)} %get-tuple-element.87), channel_id=1, source_target_pairs={{0,8},{4,12},{8,0},{12,4},{16,24},{20,28},{24,16},{28,20},{1,9},{5... | collective-permute-start | bytes 1572872 | tf_op jit(solution)/shard_map/ppermute | solution.py:689
  70.0 14.9 %collective-permute-start.18 = (bf16[256,1024]{1,0:T(8,128)(2,1)S(1)}, bf16[256,1024]{1,0:T(8,128)(2,1)S(1)}, u32[]{:S(2)}, u32[]{:S(2)}) collective-permute-start(bf16[256,1024]{1,0:T(8,128)(2,1)S(1)} %get-tuple-element.83), channel_id=1, source_target_pairs={{0,16},{4,20},{8,24},{12,28},{16,0},{20,4},{24,8},{28,12},{1,17},{... | collective-permute-start | bytes 1572872 | tf_op jit(solution)/shard_map/ppermute | solution.py:689
  76.7 19.3 %collective-permute-start.16 = (bf16[256,1024]{1,0:T(8,128)(2,1)S(1)}, bf16[256,1024]{1,0:T(8,128)(2,1)S(1)}, u32[]{:S(2)}, u32[]{:S(2)}) collective-permute-start(bf16[256,1024]{1,0:T(8,128)(2,1)S(1)} %get-tuple-element.81), channel_id=1, source_target_pairs={{0,16},{4,20},{8,24},{12,28},{16,0},{20,4},{24,8},{28,12},{1,17},{... | collective-permute-start | bytes 1572872 | tf_op jit(solution)/shard_map/ppermute | solution.py:689
  77.3 20.3 %collective-permute-start.20 = (bf16[256,1024]{1,0:T(8,128)(2,1)S(1)}, bf16[256,1024]{1,0:T(8,128)(2,1)S(1)}, u32[]{:S(2)}, u32[]{:S(2)}) collective-permute-start(bf16[256,1024]{1,0:T(8,128)(2,1)S(1)} %get-tuple-element.85), channel_id=1, source_target_pairs={{0,8},{4,12},{8,0},{12,4},{16,24},{20,28},{24,16},{28,20},{1,9},{5... | collective-permute-start | bytes 1572872 | tf_op jit(solution)/shard_map/ppermute | solution.py:689
  84.4 17.3 %collective-permute-start.22 = (bf16[256,512]{1,0:T(8,128)(2,1)S(1)}, bf16[256,512]{1,0:T(8,128)(2,1)S(1)}, u32[]{:S(2)}, u32[]{:S(2)}) collective-permute-start(bf16[256,512]{1,0:T(8,128)(2,1)S(1)} %get-tuple-element.110), channel_id=1, source_target_pairs={{0,16},{4,20},{8,24},{12,28},{16,0},{20,4},{24,8},{28,12},{1,17},{... | collective-permute-start | bytes 786440 | tf_op jit(solution)/shard_map/ppermute | solution.py:689
  85.1 16.6 %collective-permute-start.19 = (bf16[256,512]{1,0:T(8,128)(2,1)S(1)}, bf16[256,512]{1,0:T(8,128)(2,1)S(1)}, u32[]{:S(2)}, u32[]{:S(2)}) collective-permute-start(bf16[256,512]{1,0:T(8,128)(2,1)S(1)} %get-tuple-element.112), channel_id=1, source_target_pairs={{0,8},{4,12},{8,0},{12,4},{16,24},{20,28},{24,16},{28,20},{1,9},{5... | collective-permute-start | bytes 786440 | tf_op jit(solution)/shard_map/ppermute | solution.py:689
  86.5 20.8 %collective-permute-start.24 = (bf16[256,512]{1,0:T(8,128)(2,1)S(1)}, bf16[256,512]{1,0:T(8,128)(2,1)S(1)}, u32[]{:S(2)}, u32[]{:S(2)}) collective-permute-start(bf16[256,512]{1,0:T(8,128)(2,1)S(1)} %get-tuple-element.109), channel_id=1, source_target_pairs={{0,16},{4,20},{8,24},{12,28},{16,0},{20,4},{24,8},{28,12},{1,17},{... | collective-permute-start | bytes 786440 | tf_op jit(solution)/shard_map/ppermute | solution.py:689
  96.0 11.2 %collective-permute-start.23 = (bf16[256,512]{1,0:T(8,128)(2,1)S(1)}, bf16[256,512]{1,0:T(8,128)(2,1)S(1)}, u32[]{:S(2)}, u32[]{:S(2)}) collective-permute-start(bf16[256,512]{1,0:T(8,128)(2,1)S(1)} %get-tuple-element.111), channel_id=1, source_target_pairs={{0,8},{4,12},{8,0},{12,4},{16,24},{20,28},{24,16},{28,20},{1,9},{5... | collective-permute-start | bytes 786440 | tf_op jit(solution)/shard_map/ppermute | solution.py:689
  102.0 17.0 %collective-permute-start.29 = (bf16[2,512,256]{2,1,0:T(8,128)(2,1)S(1)}, bf16[2,512,256]{2,1,0:T(8,128)(2,1)S(1)}, u32[]{:S(2)}, u32[]{:S(2)}) collective-permute-start(bf16[2,512,256]{2,1,0:T(8,128)(2,1)S(1)} %get-tuple-element.90.refs_4_.refs_0_), channel_id=1, source_target_pairs={{0,16},{4,20},{8,24},{12,28},{16,0},{20,4},{24,8},{28,12},{1,17},{... | collective-permute-start | bytes 1572872 | tf_op jit(solution)/shard_map/ppermute | solution.py:689
  102.4 16.6 %collective-permute-start.28 = (bf16[2,512,256]{2,1,0:T(8,128)(2,1)S(1)}, bf16[2,512,256]{2,1,0:T(8,128)(2,1)S(1)}, u32[]{:S(2)}, u32[]{:S(2)}) collective-permute-start(bf16[2,512,256]{2,1,0:T(8,128)(2,1)S(1)} %get-tuple-element.90.refs_4_.refs_0_), channel_id=1, source_target_pairs={{0,8},{4,12},{8,0},{12,4},{16,24},{20,28},{24,16},{28,20},{1,9},{5... | collective-permute-start | bytes 1572872 | tf_op jit(solution)/shard_map/ppermute | solution.py:689
  107.6 21.5 %collective-permute-start.34 = (bf16[2,512,256]{2,1,0:T(8,128)(2,1)S(1)}, bf16[2,512,256]{2,1,0:T(8,128)(2,1)S(1)}, u32[]{:S(2)}, u32[]{:S(2)}) collective-permute-start(bf16[2,512,256]{2,1,0:T(8,128)(2,1)S(1)} %get-tuple-element.92.refs_5_.refs_1_), channel_id=1, source_target_pairs={{0,16},{4,20},{8,24},{12,28},{16,0},{20,4},{24,8},{28,12},{1,17},{... | collective-permute-start | bytes 1572872 | tf_op jit(solution)/shard_map/ppermute | solution.py:689
  108.0 21.1 %collective-permute-start.33 = (bf16[2,512,256]{2,1,0:T(8,128)(2,1)S(1)}, bf16[2,512,256]{2,1,0:T(8,128)(2,1)S(1)}, u32[]{:S(2)}, u32[]{:S(2)}) collective-permute-start(bf16[2,512,256]{2,1,0:T(8,128)(2,1)S(1)} %get-tuple-element.92.refs_5_.refs_1_), channel_id=1, source_target_pairs={{0,8},{4,12},{8,0},{12,4},{16,24},{20,28},{24,16},{28,20},{1,9},{5... | collective-permute-start | bytes 1572872 | tf_op jit(solution)/shard_map/ppermute | solution.py:689
  109.7 3.6 %collective-permute-start.25 = (f32[8,128]{1,0:T(8,128)S(1)}, f32[8,128]{1,0:T(8,128)S(1)}, u32[]{:S(2)}, u32[]{:S(2)}) collective-permute-start(f32[8,128]{1,0:T(8,128)S(1)} %add.49), channel_id=1, source_target_pairs={{0,1},{1,0},{2,3},{3,2},{4,5},{5,4},{6,7},{7,6},{8,9},{9,8},{10,11... | collective-permute-start | bytes 12296 | tf_op jit(solution)/shard_map/ppermute | solution.py:689
  113.3 4.5 %collective-permute-start.26 = (f32[8,128]{1,0:T(8,128)S(1)}, f32[8,128]{1,0:T(8,128)S(1)}, u32[]{:S(2)}, u32[]{:S(2)}) collective-permute-start(f32[8,128]{1,0:T(8,128)S(1)} %add.50), channel_id=1, source_target_pairs={{0,2},{1,3},{2,0},{3,1},{4,6},{5,7},{6,4},{7,5},{8,10},{9,11},{10,... | collective-permute-start | bytes 12296 | tf_op jit(solution)/shard_map/ppermute | solution.py:689
  117.8 1.2 collective-permute-start.27
  119.5 9.3 %collective-permute-start.32 = (f32[8,128]{1,0:T(8,128)S(1)}, f32[8,128]{1,0:T(8,128)S(1)}, u32[]{:S(2)}, u32[]{:S(2)}) collective-permute-start(f32[8,128]{1,0:T(8,128)S(1)} %get-tuple-element.91.refs_11_), channel_id=1, source_target_pairs={{0,24},{4,28},{8,16},{12,20},{16,8},{20,12},{24,0},{28,4},{1,25},{... | collective-permute-start | bytes 12296 | tf_op jit(solution)/shard_map/ppermute | solution.py:689
  121.1 8.0 %collective-permute-start.31 = (f32[8,128]{1,0:T(8,128)S(1)}, f32[8,128]{1,0:T(8,128)S(1)}, u32[]{:S(2)}, u32[]{:S(2)}) collective-permute-start(f32[8,128]{1,0:T(8,128)S(1)} %get-tuple-element.91.refs_11_), channel_id=1, source_target_pairs={{0,16},{4,20},{8,24},{12,28},{16,0},{20,4},{24,8},{28,12},{1,17},{... | collective-permute-start | bytes 12296 | tf_op jit(solution)/shard_map/ppermute | solution.py:689
  122.1 7.1 %collective-permute-start.30 = (f32[8,128]{1,0:T(8,128)S(1)}, f32[8,128]{1,0:T(8,128)S(1)}, u32[]{:S(2)}, u32[]{:S(2)}) collective-permute-start(f32[8,128]{1,0:T(8,128)S(1)} %get-tuple-element.91.refs_11_), channel_id=1, source_target_pairs={{0,8},{4,12},{8,0},{12,4},{16,24},{20,28},{24,16},{28,20},{1,9},{5... | collective-permute-start | bytes 12296 | tf_op jit(solution)/shard_map/ppermute | solution.py:689
  129.6 2.7 %collective-permute-start.35 = (bf16[2,1024,256]{2,1,0:T(8,128)(2,1)S(1)}, bf16[2,1024,256]{2,1,0:T(8,128)(2,1)S(1)}, u32[]{:S(2)}, u32[]{:S(2)}) collective-permute-start(bf16[2,1024,256]{2,1,0:T(8,128)(2,1)S(1)} %get-tuple-element.94), channel_id=1, source_target_pairs={{0,4},{4,0},{8,12},{12,8},{16,20},{20,16},{24,28},{28,24},{1,5},{5... | collective-permute-start | bytes 3145736 | tf_op jit(solution)/shard_map/ppermute | solution.py:689
  129.7 5.8 %collective-permute-start.37 = (bf16[2,1024,256]{2,1,0:T(8,128)(2,1)S(1)}, bf16[2,1024,256]{2,1,0:T(8,128)(2,1)S(1)}, u32[]{:S(2)}, u32[]{:S(2)}) collective-permute-start(bf16[2,1024,256]{2,1,0:T(8,128)(2,1)S(1)} %get-tuple-element.98), channel_id=1, source_target_pairs={{0,4},{4,0},{8,12},{12,8},{16,20},{20,16},{24,28},{28,24},{1,5},{5... | collective-permute-start | bytes 3145736 | tf_op jit(solution)/shard_map/ppermute | solution.py:689
  130.2 5.3 %collective-permute-start.38 = (bf16[2,1024,256]{2,1,0:T(8,128)(2,1)S(1)}, bf16[2,1024,256]{2,1,0:T(8,128)(2,1)S(1)}, u32[]{:S(2)}, u32[]{:S(2)}) collective-permute-start(bf16[2,1024,256]{2,1,0:T(8,128)(2,1)S(1)} %get-tuple-element.99), channel_id=1, source_target_pairs={{0,4},{4,0},{8,12},{12,8},{16,20},{20,16},{24,28},{28,24},{1,5},{5... | collective-permute-start | bytes 3145736 | tf_op jit(solution)/shard_map/ppermute | solution.py:689
  130.2 14.3 %collective-permute-start.40 = (bf16[1024,256]{1,0:T(8,128)(2,1)S(1)}, bf16[1024,256]{1,0:T(8,128)(2,1)S(1)}, u32[]{:S(2)}, u32[]{:S(2)}) collective-permute-start(bf16[1024,256]{1,0:T(8,128)(2,1)S(1)} %get-tuple-element.103), channel_id=1, source_target_pairs={{0,8},{4,12},{8,0},{12,4},{16,24},{20,28},{24,16},{28,20},{1,9},{5... | collective-permute-start | bytes 1572872 | tf_op jit(solution)/shard_map/ppermute | solution.py:689
  131.7 14.0 %collective-permute-start.36 = (bf16[1024,256]{1,0:T(8,128)(2,1)S(1)}, bf16[1024,256]{1,0:T(8,128)(2,1)S(1)}, u32[]{:S(2)}, u32[]{:S(2)}) collective-permute-start(bf16[1024,256]{1,0:T(8,128)(2,1)S(1)} %get-tuple-element.97), channel_id=1, source_target_pairs={{0,16},{4,20},{8,24},{12,28},{16,0},{20,4},{24,8},{28,12},{1,17},{... | collective-permute-start | bytes 1572872 | tf_op jit(solution)/shard_map/ppermute | solution.py:689
  145.7 2.7 %collective-permute-start.39 = (bf16[1024,256]{1,0:T(8,128)(2,1)S(1)}, bf16[1024,256]{1,0:T(8,128)(2,1)S(1)}, u32[]{:S(2)}, u32[]{:S(2)}) collective-permute-start(bf16[1024,256]{1,0:T(8,128)(2,1)S(1)} %collective-permute-done.36.refs_0_), channel_id=1, source_target_pairs={{0,4},{4,0},{8,12},{12,8},{16,20},{20,16},{24,28},{28,24},{1,5},{5... | collective-permute-start | bytes 1572872 | tf_op jit(solution)/shard_map/ppermute | solution.py:689
  145.7 2.7 %collective-permute-start.41 = (bf16[1024,256]{1,0:T(8,128)(2,1)S(1)}, bf16[1024,256]{1,0:T(8,128)(2,1)S(1)}, u32[]{:S(2)}, u32[]{:S(2)}) collective-permute-start(bf16[1024,256]{1,0:T(8,128)(2,1)S(1)} %collective-permute-done.40.refs_1_), channel_id=1, source_target_pairs={{0,4},{4,0},{8,12},{12,8},{16,20},{20,16},{24,28},{28,24},{1,5},{5... | collective-permute-start | bytes 1572872 | tf_op jit(solution)/shard_map/ppermute | solution.py:689

commit v4 on v3

--- a/solution.py
+++ b/solution.py
@@ -235,7 +235,7 @@
     )(*args)
 
 
-HEADS = 2
+HEADS = 1
 
 
 def stacked(ref, row, col, r, first, count):
@@ -730,7 +730,8 @@
     if far:
         for m in far:
             to_core(weights, m, held)
-        held = project(idx, normed, [m | c for m in far for c in (0, 1)], weights, held, tables)
+        held = project(idx, normed, far, weights, held, None)
+        held = project(idx, normed, [m | 1 for m in far], weights, held, tables)
     pol_keys, pol_values = held
     margin, probs, delta = attend(lengths, policy_queries, pol_keys, pol_values, readout, ref_margin)
 

time: 151 us -> 151 us (level)
    pallas_call x3 -> x4, Pallas kernels: 8.76 us -> 8.81 us  [project(): pl.pallas_call(functools.partial(project_kernel, tuple(masks), first, las...]
  transfers between devices with their start and end apart: 42 -> 42, of which waited for: 19 -> 19; matrix products, arithmetic and copies ran while one was open for 0% -> 0% of each run, Pallas kernels for 37% -> 39%
where the time goes in v4:
time: 151 us
  Pallas kernels  67.6 us (45%)
  waiting for transfers between devices  47.9 us (32%)
  starting transfers between devices  33.6 us (22%)
    ppermute x42, waiting for transfers between devices, swap(): return lax.ppermute(x, axis, [(i, i ^ bit) for i in range(size)])  47.9 us
    ppermute x42, starting transfers between devices, swap(): return lax.ppermute(x, axis, [(i, i ^ bit) for i in range(size)])  33.6 us
    pallas_call x1, Pallas kernels, norm_project(): pl.pallas_call(norm_project_kernel, in_specs=[SMEM, HBM, HBM, HBM], out_s...  17.8 us
    pallas_call x4, Pallas kernels, blend(): pl.pallas_call(functools.partial(blend_kernel, tuple(masks), first, offse...  12.3 us
    pallas_call x2, Pallas kernels, attend(): pl.pallas_call(functools.partial(attend_kernel, keep), in_specs=[SMEM] +...  8.92 us
    pallas_call x4, Pallas kernels, project(): pl.pallas_call(functools.partial(project_kernel, tuple(masks), first, las...  8.81 us
    pallas_call x4, Pallas kernels, gradient_blocks(): pl.pallas_call(functools.partial(kernel, tuple(masks)), in_specs=in_specs...  8.29 us
    pallas_call x1, Pallas kernels, attend_back(): pl.pallas_call(attend_back_kernel, in_specs=[SMEM] + [VMEM] * 6, out_spec...  5.79 us
  transfers between devices with their start and end apart: 42, of which 19 were waited for; matrix products, arithmetic and copies ran while one was open for 0% of the time, Pallas kernels for 39%

profile of v4, /device:TPU:0, one launch (start us, length us, event | category | flops | bytes accessed | tf_op | source)
XLA Modules:
  0.0 150.6 jit_solution(15024202817890664261)
XLA Ops:
  0.6 3.0 %collective-permute-start.1 = (bf16[2,1024,256]{2,1,0:T(8,128)(2,1)}, bf16[2,1024,256]{2,1,0:T(8,128)(2,1)S(1)}, u32[]{:S(2)}, u32[]{:S(2)}) collective-permute-start(bf16[2,1024,256]{2,1,0:T(8,128)(2,1)} %refs_0_.3), channel_id=1, source_target_pairs={{0,16},{4,20},{8,24},{12,28},{16,0},{20,4},{24,8},{28,12},{1,17},{... | collective-permute-start | bytes 3145736 | tf_op jit(solution)/shard_map/ppermute | solution.py:689
  3.7 1.5 collective-permute-start
  5.2 17.8 %norm_project.1 = (bf16[768,8192]{1,0:T(8,128)(2,1)S(1)}, bf16[768,256]{1,0:T(8,128)(2,1)S(1)}, bf16[768,256]{1,0:T(8,128)(2,1)S(1)}) custom-call(s32[1]{0:T(128)} %bitcast.idx_ref, bf16[768,8192]{1,0:T(8,128)(2,1)} %hidden_hbm.1, bf16[2,8192,256]{2,1,0:T(8,128)(2,1)} %refs_10_.1, f32[2,384,128]{2,1,0:T(8,128)} %constant.8.clone.table_hbm.refs_3_.table_ref), custom_call_target="tpu_custom_call" | custom-call | flops 1 | bytes 1 | tf_op jit(solution)/shard_map/norm_project/pallas_call | solution.py:133
  23.1 4.8 %attend.2.refs_2_.rest_0_ = f32[8,128]{1,0:T(8,128)S(1)} custom-call(s32[2]{0:T(128)S(1)} %copy-done.5, bf16[768,1024]{1,0:T(8,128)(2,1)S(1)} %copy-done.4, bf16[768,256]{1,0:T(8,128)(2,1)S(1)} %get-tuple-element.57.k_ref, bf16[768,256]{1,0:T(8,128)(2,1)S(1)} %get-tuple-element.58.v_ref, bf16[768,1024]{1,0:T(8,128)(2,1)S(1)} %copy-done), custom_call_target="tpu_custom_call" | custom-call | flops 1 | bytes 1 | tf_op jit(solution)/shard_map/attend/pallas_call | solution.py:318
  27.8 0.7 collective-permute-done.refs_0_.refs_2_
  28.5 0.5 collective-permute-start.4
  29.1 1.6 %collective-permute-start.7 = (bf16[1024,256]{1,0:T(8,128)(2,1)S(1)}, bf16[1024,256]{1,0:T(8,128)(2,1)S(1)}, u32[]{:S(2)}, u32[]{:S(2)}) collective-permute-start(bf16[1024,256]{1,0:T(8,128)(2,1)S(1)} %get-tuple-element.63), channel_id=1, source_target_pairs={{0,8},{4,12},{8,0},{12,4},{16,24},{20,28},{24,16},{28,20},{1,9},{5... | collective-permute-start | bytes 1572872 | tf_op jit(solution)/shard_map/ppermute | solution.py:689
  30.7 0.5 collective-permute-start.2
  31.2 2.0 %project.4.refs_4_ = f32[2,768,256]{2,1,0:T(8,128)S(1)} custom-call(s32[1]{0:T(128)} %bitcast.idx_ref, bf16[768,8192]{1,0:T(8,128)(2,1)S(1)} %get-tuple-element.56.x_ref, bf16[2,1024,256]{2,1,0:T(8,128)(2,1)S(1)} %copy-done.2, bf16[2,1024,256]{2,1,0:T(8,128)(2,1)S(1)} %collective-permute-done.5.refs_1_), custom_call_target="tpu_custom_call" | custom-call | flops 1 | bytes 1 | tf_op jit(solution)/shard_map/project/pallas_call | solution.py:226
  33.3 4.1 %project.5.refs_2_ = f32[2,768,256]{2,1,0:T(8,128)S(1)} custom-call(s32[1]{0:T(128)} %bitcast.idx_ref, bf16[768,8192]{1,0:T(8,128)(2,1)S(1)} %get-tuple-element.56.x_ref, bf16[2,1024,256]{2,1,0:T(8,128)(2,1)S(1)} %collective-permute-done.refs_0_.refs_2_, bf16[2,1024,256]{2,1,0:T(8,128)(2,1)S(1)} %collective-permute-done.3.refs_1_.refs_3_, ...), custom_call_target="tpu_custom_call" | custom-call | flops 1 | bytes 1 | tf_op jit(solution)/shard_map/project/pallas_call | solution.py:226
  37.4 5.7 %collective-permute-done.7.refs_1_.refs_7_ = bf16[1024,256]{1,0:T(8,128)(2,1)S(1)} collective-permute-done((bf16[1024,256]{1,0:T(8,128)(2,1)S(1)}, bf16[1024,256]{1,0:T(8,128)(2,1)S(1)}, u32[]{:S(2)}, u32[]{:S(2)}) %collective-permute-start.7) | collective-permute-done | bytes 524320 | tf_op jit(solution)/shard_map/ppermute | solution.py:689
  43.0 1.2 collective-permute-done.2.refs_0_.refs_6_
  44.2 0.5 collective-permute-start.8
  44.7 1.1 project.6.refs_2_
  46.1 0.7 collective-permute-done.8.refs_1_.refs_9_
  46.9 1.6 %project.7 = (bf16[768,256]{1,0:T(8,128)(2,1)S(1)}, bf16[768,256]{1,0:T(8,128)(2,1)S(1)}) custom-call(s32[1]{0:T(128)} %bitcast.idx_ref, bf16[768,8192]{1,0:T(8,128)(2,1)S(1)} %get-tuple-element.56.x_ref, bf16[1024,256]{1,0:T(8,128)(2,1)S(1)} %collective-permute-done.6.refs_0_.refs_8_, bf16[1024,256]{1,0:T(8,128)(2,1)S(1)} %collective-permute-done.8.refs_1_.refs_9_, ...), custom_call_target="tpu_custom_call" | custom-call | flops 1 | bytes 1 | tf_op jit(solution)/shard_map/project/pallas_call | solution.py:226
  48.5 4.2 %attend.3 = (f32[8,128]{1,0:T(8,128)S(1)}, bf16[2,2,768,512]{3,2,1,0:T(8,128)(2,1)S(1)}, f32[2,2,3,512]{3,2,1,0:T(4,128)S(1)}) custom-call(s32[2]{0:T(128)S(1)} %copy-done.5, bf16[768,1024]{1,0:T(8,128)(2,1)S(1)} %copy-done.1, bf16[768,256]{1,0:T(8,128)(2,1)S(1)} %get-tuple-element.66.k_ref, bf16[768,256]{1,0:T(8,128)(2,1)S(1)} %get-tuple-element.65.v_ref, ...), custom_call_target="tpu_custom_call" | custom-call | flops 1 | bytes 1 | tf_op jit(solution)/shard_map/attend/pallas_call | solution.py:318
  52.7 3.7 %collective-permute-start.11 = (f32[8,128]{1,0:T(8,128)S(1)}, f32[8,128]{1,0:T(8,128)S(1)}, u32[]{:S(2)}, u32[]{:S(2)}) collective-permute-start(f32[8,128]{1,0:T(8,128)S(1)} %get-tuple-element.69), channel_id=1, source_target_pairs={{0,3},{1,2},{2,1},{3,0},{4,7},{5,6},{6,5},{7,4},{8,11},{9,10},{10,... | collective-permute-start | bytes 12296 | tf_op jit(solution)/shard_map/ppermute | solution.py:689
  56.3 0.8 collective-permute-start.9
  57.1 5.8 %attend_back.1.cot_ref = bf16[2,256,768]{2,1,0:T(8,128)(2,1)S(1)} custom-call(s32[2]{0:T(128)S(1)} %copy-done.5, bf16[768,1024]{1,0:T(8,128)(2,1)S(1)} %copy-done.1, bf16[768,256]{1,0:T(8,128)(2,1)S(1)} %get-tuple-element.65.v_ref, bf16[768,1024]{1,0:T(8,128)(2,1)S(1)} %copy-done, bf16[2,2,768,512]{3,2,1,0:T(8,128)(2,1)S(1)} %get-tuple-element.67.prob_ref, ...), custom_call_target="tpu_custom_call" | custom-call | flops 1 | bytes 1 | tf_op jit(solution)/shard_map/attend_back/pallas_call | solution.py:372
  63.0 1.0 gradient_block.2
  64.1 0.5 collective-permute-start.12
  64.6 2.7 %gradient_block.3 = (bf16[2,256,1024]{2,1,0:T(8,128)(2,1)S(1)}, bf16[2,256,1024]{2,1,0:T(8,128)(2,1)S(1)}, bf16[2,256,1024]{2,1,0:T(8,128)(2,1)S(1)}) custom-call(s32[1]{0:T(128)} %bitcast.idx_ref, bf16[768,8192]{1,0:T(8,128)(2,1)S(1)} %get-tuple-element.56.x_ref, bf16[2,256,768]{2,1,0:T(8,128)(2,1)S(1)} %attend_back.1.cot_ref, ...), custom_call_target="tpu_custom_call" | custom-call | flops 1 | bytes 1 | tf_op jit(solution)/shard_map/gradient_block/pallas_call | solution.py:440
  67.4 0.4 collective-permute-start.14
  67.9 1.3 merged_block.3
  69.2 0.6 collective-permute-start.21
  70.2 1.3 collective-permute-done.14.refs_1_
  71.5 1.5 collective-permute-done.15.refs_2_
  73.0 3.3 %merged_block.2 = (bf16[256,1024]{1,0:T(8,128)(2,1)S(1)}, bf16[256,1024]{1,0:T(8,128)(2,1)S(1)}, bf16[256,1024]{1,0:T(8,128)(2,1)S(1)}, bf16[256,1024]{1,0:T(8,1...) custom-call(s32[1]{0:T(128)} %bitcast.idx_ref, bf16[768,8192]{1,0:T(8,128)(2,1)S(1)} %get-tuple-element.56.x_ref, ...), custom_call_target="tpu_custom_call" | custom-call | flops 1 | bytes 1 | tf_op jit(solution)/shard_map/merged_block/pallas_call | solution.py:440
  76.3 0.6 collective-permute-start.16
  76.8 0.4 collective-permute-start.20
  77.2 6.8 %collective-permute-done.21 = bf16[256,1024]{1,0:T(8,128)(2,1)S(1)} collective-permute-done((bf16[256,1024]{1,0:T(8,128)(2,1)S(1)}, bf16[256,1024]{1,0:T(8,128)(2,1)S(1)}, u32[]{:S(2)}, u32[]{:S(2)}) %collective-permute-start.21) | collective-permute-done | bytes 524320 | tf_op jit(solution)/shard_map/ppermute | solution.py:689
  84.2 0.6 collective-permute-start.22
  84.9 1.4 collective-permute-start.19
  86.3 0.7 collective-permute-start.24
  87.0 8.8 %collective-permute-done.16.refs_1_ = bf16[256,1024]{1,0:T(8,128)(2,1)S(1)} collective-permute-done((bf16[256,1024]{1,0:T(8,128)(2,1)S(1)}, bf16[256,1024]{1,0:T(8,128)(2,1)S(1)}, u32[]{:S(2)}, u32[]{:S(2)}) %collective-permute-start.16) | collective-permute-done | bytes 524320 | tf_op jit(solution)/shard_map/ppermute | solution.py:689
  95.8 1.5 collective-permute-start.23
  97.3 4.1 %collective-permute-done.22.refs_5_ = bf16[256,512]{1,0:T(8,128)(2,1)S(1)} collective-permute-done((bf16[256,512]{1,0:T(8,128)(2,1)S(1)}, bf16[256,512]{1,0:T(8,128)(2,1)S(1)}, u32[]{:S(2)}, u32[]{:S(2)}) %collective-permute-start.22) | collective-permute-done | bytes 262176 | tf_op jit(solution)/shard_map/ppermute | solution.py:689
  101.8 0.4 collective-permute-start.29
  102.2 1.6 %collective-permute-start.28 = (bf16[2,512,256]{2,1,0:T(8,128)(2,1)S(1)}, bf16[2,512,256]{2,1,0:T(8,128)(2,1)S(1)}, u32[]{:S(2)}, u32[]{:S(2)}) collective-permute-start(bf16[2,512,256]{2,1,0:T(8,128)(2,1)S(1)} %get-tuple-element.90.refs_4_.refs_0_), channel_id=1, source_target_pairs={{0,8},{4,12},{8,0},{12,4},{16,24},{20,28},{24,16},{28,20},{1,9},{5... | collective-permute-start | bytes 1572872 | tf_op jit(solution)/shard_map/ppermute | solution.py:689
  103.9 3.2 %collective-permute-done.24.refs_5_ = bf16[256,512]{1,0:T(8,128)(2,1)S(1)} collective-permute-done((bf16[256,512]{1,0:T(8,128)(2,1)S(1)}, bf16[256,512]{1,0:T(8,128)(2,1)S(1)}, u32[]{:S(2)}, u32[]{:S(2)}) %collective-permute-start.24) | collective-permute-done | bytes 262176 | tf_op jit(solution)/shard_map/ppermute | solution.py:689
  107.4 0.4 collective-permute-start.34
  107.9 1.6 %collective-permute-start.33 = (bf16[2,512,256]{2,1,0:T(8,128)(2,1)S(1)}, bf16[2,512,256]{2,1,0:T(8,128)(2,1)S(1)}, u32[]{:S(2)}, u32[]{:S(2)}) collective-permute-start(bf16[2,512,256]{2,1,0:T(8,128)(2,1)S(1)} %get-tuple-element.92.refs_5_.refs_1_), channel_id=1, source_target_pairs={{0,8},{4,12},{8,0},{12,4},{16,24},{20,28},{24,16},{28,20},{1,9},{5... | collective-permute-start | bytes 1572872 | tf_op jit(solution)/shard_map/ppermute | solution.py:689
  109.5 1.3 collective-permute-start.25
  110.7 2.4 %collective-permute-done.25 = f32[8,128]{1,0:T(8,128)S(1)} collective-permute-done((f32[8,128]{1,0:T(8,128)S(1)}, f32[8,128]{1,0:T(8,128)S(1)}, u32[]{:S(2)}, u32[]{:S(2)}) %collective-permute-start.25) | collective-permute-done | bytes 4128 | tf_op jit(solution)/shard_map/ppermute | solution.py:689
  113.1 2.1 %collective-permute-start.26 = (f32[8,128]{1,0:T(8,128)S(1)}, f32[8,128]{1,0:T(8,128)S(1)}, u32[]{:S(2)}, u32[]{:S(2)}) collective-permute-start(f32[8,128]{1,0:T(8,128)S(1)} %add.50), channel_id=1, source_target_pairs={{0,2},{1,3},{2,0},{3,1},{4,6},{5,7},{6,4},{7,5},{8,10},{9,11},{10,... | collective-permute-start | bytes 12296 | tf_op jit(solution)/shard_map/ppermute | solution.py:689
  115.2 2.4 %collective-permute-done.26 = f32[8,128]{1,0:T(8,128)S(1)} collective-permute-done((f32[8,128]{1,0:T(8,128)S(1)}, f32[8,128]{1,0:T(8,128)S(1)}, u32[]{:S(2)}, u32[]{:S(2)}) %collective-permute-start.26) | collective-permute-done | bytes 4128 | tf_op jit(solution)/shard_map/ppermute | solution.py:689
  117.6 1.2 collective-permute-done.27
  118.8 0.6 gate.1
  119.4 1.6 %collective-permute-start.32 = (f32[8,128]{1,0:T(8,128)S(1)}, f32[8,128]{1,0:T(8,128)S(1)}, u32[]{:S(2)}, u32[]{:S(2)}) collective-permute-start(f32[8,128]{1,0:T(8,128)S(1)} %get-tuple-element.91.refs_11_), channel_id=1, source_target_pairs={{0,24},{4,28},{8,16},{12,20},{16,8},{20,12},{24,0},{28,4},{1,25},{... | collective-permute-start | bytes 12296 | tf_op jit(solution)/shard_map/ppermute | solution.py:689
  120.9 1.0 collective-permute-start.31
  121.9 1.0 collective-permute-start.30
  122.9 3.8 %fetch.1 = (bf16[8,2,1024,256]{3,2,1,0:T(8,128)(2,1)S(1)}, bf16[8,2,1024,256]{3,2,1,0:T(8,128)(2,1)S(1)}) custom-call(s32[1]{0:T(128)} %bitcast.idx_ref, bf16[2,1024,256]{2,1,0:T(8,128)(2,1)S(1)} %copy-done.2, bf16[2,1024,256]{2,1,0:T(8,128)(2,1)S(1)} %collective-permute-done.5.refs_1_, bf16[2,1024,256]{2,1,0:T(8,128)(2,1)S(1)} %collective-permute-done.refs_0_.refs_2_, ...), custom_call_target="tpu_custom_call" | custom-call | flops 1 | bytes 1 | tf_op jit(solution)/shard_map/fetch/pallas_call | solution.py:574
  126.7 2.0 %collective-permute-done.32 = f32[8,128]{1,0:T(8,128)S(1)} collective-permute-done((f32[8,128]{1,0:T(8,128)S(1)}, f32[8,128]{1,0:T(8,128)S(1)}, u32[]{:S(2)}, u32[]{:S(2)}) %collective-permute-start.32) | collective-permute-done | bytes 4128 | tf_op jit(solution)/shard_map/ppermute | solution.py:689
  129.5 0.5 collective-permute-start.37
  130.0 1.5 collective-permute-start.40
  131.5 0.5 collective-permute-start.36
  132.1 3.2 %blend.4 = (bf16[2,8192,256]{2,1,0:T(8,128)(2,1)}, f32[8,128]{1,0:T(8,128)}, bf16[2,1024,256]{2,1,0:T(8,128)(2,1)}) custom-call(s32[1]{0:T(128)} %bitcast.idx_ref, f32[8,128]{1,0:T(8,128)S(1)} %add_add_fusion.refs_10_.square_ref, bf16[2,512,256]{2,1,0:T(8,128)(2,1)S(1)} %get-tuple-element.90.refs_4_.refs_0_, ...), custom_call_target="tpu_custom_call" | custom-call | flops 1 | bytes 1 | tf_op jit(solution)/shard_map/blend/pallas_call | solution.py:656
  135.3 4.8 %blend.5 = (bf16[2,8192,256]{2,1,0:T(8,128)(2,1)}, f32[8,128]{1,0:T(8,128)}) custom-call(s32[1]{0:T(128)} %bitcast.idx_ref, f32[8,128]{1,0:T(8,128)S(1)} %add_add_fusion.refs_10_.square_ref, bf16[2,512,256]{2,1,0:T(8,128)(2,1)S(1)} %collective-permute-done.28.refs_0_.refs_6_, ...), custom_call_target="tpu_custom_call", output_to_operand_aliasing={{0}: (10, {})} | custom-call | flops 1 | bytes 1 | tf_op jit(solution)/shard_map/blend/pallas_call | solution.py:656
  140.1 4.2 %collective-permute-done.40.refs_1_ = bf16[1024,256]{1,0:T(8,128)(2,1)S(1)} collective-permute-done((bf16[1024,256]{1,0:T(8,128)(2,1)S(1)}, bf16[1024,256]{1,0:T(8,128)(2,1)S(1)}, u32[]{:S(2)}, u32[]{:S(2)}) %collective-permute-start.40) | collective-permute-done | bytes 524320 | tf_op jit(solution)/shard_map/ppermute | solution.py:689
  144.3 1.2 collective-permute-done.36.refs_0_
  145.5 0.5 collective-permute-start.41
  146.0 2.2 %blend.6 = (bf16[2,8192,256]{2,1,0:T(8,128)(2,1)}, f32[8,128]{1,0:T(8,128)}) custom-call(s32[1]{0:T(128)} %bitcast.idx_ref, f32[8,128]{1,0:T(8,128)S(1)} %add_add_fusion.refs_10_.square_ref, bf16[1024,256]{1,0:T(8,128)(2,1)S(1)} %collective-permute-done.36.refs_0_, ...), custom_call_target="tpu_custom_call", output_to_operand_aliasing={{0}: (6, {})} | custom-call | flops 1 | bytes 1 | tf_op jit(solution)/shard_map/blend/pallas_call | solution.py:656
  148.2 2.2 %blend.7 = (bf16[2,8192,256]{2,1,0:T(8,128)(2,1)}, f32[8,128]{1,0:T(8,128)}) custom-call(s32[1]{0:T(128)} %bitcast.idx_ref, f32[8,128]{1,0:T(8,128)S(1)} %add_add_fusion.refs_10_.square_ref, bf16[1024,256]{1,0:T(8,128)(2,1)S(1)} %collective-permute-done.39.refs_0_, ...), custom_call_target="tpu_custom_call", output_to_operand_aliasing={{0}: (6, {})} | custom-call | flops 1 | bytes 1 | tf_op jit(solution)/shard_map/blend/pallas_call | solution.py:656
  (63 shorter events, 3.1 us)
Async XLA Ops:
  0.6 27.2 %collective-permute-start.1 = (bf16[2,1024,256]{2,1,0:T(8,128)(2,1)}, bf16[2,1024,256]{2,1,0:T(8,128)(2,1)S(1)}, u32[]{:S(2)}, u32[]{:S(2)}) collective-permute-start(bf16[2,1024,256]{2,1,0:T(8,128)(2,1)} %refs_0_.3), channel_id=1, source_target_pairs={{0,16},{4,20},{8,24},{12,28},{16,0},{20,4},{24,8},{28,12},{1,17},{... | collective-permute-start | bytes 3145736 | tf_op jit(solution)/shard_map/ppermute | solution.py:689
  3.7 24.8 %collective-permute-start = (bf16[2,1024,256]{2,1,0:T(8,128)(2,1)}, bf16[2,1024,256]{2,1,0:T(8,128)(2,1)S(1)}, u32[]{:S(2)}, u32[]{:S(2)}) collective-permute-start(bf16[2,1024,256]{2,1,0:T(8,128)(2,1)} %refs_0_.3), channel_id=1, source_target_pairs={{0,8},{4,12},{8,0},{12,4},{16,24},{20,28},{24,16},{28,20},{1,9},{5... | collective-permute-start | bytes 3145736 | tf_op jit(solution)/shard_map/ppermute | solution.py:689
  5.2 26.0 %collective-permute-start.5 = (bf16[2,1024,256]{2,1,0:T(8,128)(2,1)}, bf16[2,1024,256]{2,1,0:T(8,128)(2,1)S(1)}, u32[]{:S(2)}, u32[]{:S(2)}) collective-permute-start(bf16[2,1024,256]{2,1,0:T(8,128)(2,1)} %refs_0_.3), channel_id=1, source_target_pairs={{0,4},{4,0},{8,12},{12,8},{16,20},{20,16},{24,28},{28,24},{1,5},{5... | collective-permute-start | bytes 3145736 | tf_op jit(solution)/shard_map/ppermute | solution.py:689
  5.2 17.9 %copy-start = (bf16[768,1024]{1,0:T(8,128)(2,1)S(1)}, bf16[768,1024]{1,0:T(8,128)(2,1)}, u32[]{:S(2)}) copy-start(bf16[768,1024]{1,0:T(8,128)(2,1)} %ro_ref.5) | copy-start | bytes 4718596
  5.2 17.9 %copy-start.4 = (bf16[768,1024]{1,0:T(8,128)(2,1)S(1)}, bf16[768,1024]{1,0:T(8,128)(2,1)}, u32[]{:S(2)}) copy-start(bf16[768,1024]{1,0:T(8,128)(2,1)} %q_ref.3) | copy-start | bytes 4718596
  5.2 17.9 %copy-start.5 = (s32[2]{0:T(128)S(1)}, s32[2]{0:T(128)}, u32[]{:S(2)}) copy-start(s32[2]{0:T(128)} %len_ref.5) | copy-start | bytes 28
  5.2 26.0 %copy-start.2 = (bf16[2,1024,256]{2,1,0:T(8,128)(2,1)S(1)}, bf16[2,1024,256]{2,1,0:T(8,128)(2,1)}, u32[]{:S(2)}) copy-start(bf16[2,1024,256]{2,1,0:T(8,128)(2,1)} %refs_0_.3) | copy-start | bytes 3145732
  28.5 4.8 %collective-permute-start.3 = (bf16[2,1024,256]{2,1,0:T(8,128)(2,1)S(1)}, bf16[2,1024,256]{2,1,0:T(8,128)(2,1)S(1)}, u32[]{:S(2)}, u32[]{:S(2)}) collective-permute-start(bf16[2,1024,256]{2,1,0:T(8,128)(2,1)S(1)} %collective-permute-done.refs_0_.refs_2_), channel_id=1, source_target_pairs={{0,4},{4,0},{8,12},{12,8},{16,20},{20,16},{24,28},{28,24},{1,5},{5... | collective-permute-start | bytes 3145736 | tf_op jit(solution)/shard_map/ppermute | solution.py:689
  28.5 4.8 %collective-permute-start.4 = (bf16[2,1024,256]{2,1,0:T(8,128)(2,1)S(1)}, bf16[2,1024,256]{2,1,0:T(8,128)(2,1)S(1)}, u32[]{:S(2)}, u32[]{:S(2)}) collective-permute-start(bf16[2,1024,256]{2,1,0:T(8,128)(2,1)S(1)} %collective-permute-done.1.refs_1_.refs_2_.refs_4_), channel_id=1, source_target_pairs={{0,4},{4,0},{8,12},{12,8},{16,20},{20,16},{24,28},{28,24},{1,5},{5... | collective-permute-start | bytes 3145736 | tf_op jit(solution)/shard_map/ppermute | solution.py:689
  29.1 13.9 %collective-permute-start.7 = (bf16[1024,256]{1,0:T(8,128)(2,1)S(1)}, bf16[1024,256]{1,0:T(8,128)(2,1)S(1)}, u32[]{:S(2)}, u32[]{:S(2)}) collective-permute-start(bf16[1024,256]{1,0:T(8,128)(2,1)S(1)} %get-tuple-element.63), channel_id=1, source_target_pairs={{0,8},{4,12},{8,0},{12,4},{16,24},{20,28},{24,16},{28,20},{1,9},{5... | collective-permute-start | bytes 1572872 | tf_op jit(solution)/shard_map/ppermute | solution.py:689
  30.7 13.6 %collective-permute-start.2 = (bf16[1024,256]{1,0:T(8,128)(2,1)S(1)}, bf16[1024,256]{1,0:T(8,128)(2,1)S(1)}, u32[]{:S(2)}, u32[]{:S(2)}) collective-permute-start(bf16[1024,256]{1,0:T(8,128)(2,1)S(1)} %get-tuple-element.59), channel_id=1, source_target_pairs={{0,16},{4,20},{8,24},{12,28},{16,0},{20,4},{24,8},{28,12},{1,17},{... | collective-permute-start | bytes 1572872 | tf_op jit(solution)/shard_map/ppermute | solution.py:689
  44.2 1.9 %collective-permute-start.6 = (bf16[1024,256]{1,0:T(8,128)(2,1)S(1)}, bf16[1024,256]{1,0:T(8,128)(2,1)S(1)}, u32[]{:S(2)}, u32[]{:S(2)}) collective-permute-start(bf16[1024,256]{1,0:T(8,128)(2,1)S(1)} %collective-permute-done.2.refs_0_.refs_6_), channel_id=1, source_target_pairs={{0,4},{4,0},{8,12},{12,8},{16,20},{20,16},{24,28},{28,24},{1,5},{5... | collective-permute-start | bytes 1572872 | tf_op jit(solution)/shard_map/ppermute | solution.py:689
  44.2 2.7 %collective-permute-start.8 = (bf16[1024,256]{1,0:T(8,128)(2,1)S(1)}, bf16[1024,256]{1,0:T(8,128)(2,1)S(1)}, u32[]{:S(2)}, u32[]{:S(2)}) collective-permute-start(bf16[1024,256]{1,0:T(8,128)(2,1)S(1)} %collective-permute-done.7.refs_1_.refs_7_), channel_id=1, source_target_pairs={{0,4},{4,0},{8,12},{12,8},{16,20},{20,16},{24,28},{28,24},{1,5},{5... | collective-permute-start | bytes 1572872 | tf_op jit(solution)/shard_map/ppermute | solution.py:689
  45.8 2.6 %copy-start.1 = (bf16[768,1024]{1,0:T(8,128)(2,1)S(1)}, bf16[768,1024]{1,0:T(8,128)(2,1)}, u32[]{:S(2)}) copy-start(bf16[768,1024]{1,0:T(8,128)(2,1)} %q_ref.5) | copy-start | bytes 4718596
  45.9 11.3 %copy-start.3 = (f32[2,384,128]{2,1,0:T(8,128)S(1)}, f32[2,384,128]{2,1,0:T(8,128)}, u32[]{:S(2)}) copy-start(f32[2,384,128]{2,1,0:T(8,128)} %constant.8.clone.table_hbm.refs_3_.table_ref) | copy-start | bytes 1179652
  52.7 10.3 %collective-permute-start.11 = (f32[8,128]{1,0:T(8,128)S(1)}, f32[8,128]{1,0:T(8,128)S(1)}, u32[]{:S(2)}, u32[]{:S(2)}) collective-permute-start(f32[8,128]{1,0:T(8,128)S(1)} %get-tuple-element.69), channel_id=1, source_target_pairs={{0,3},{1,2},{2,1},{3,0},{4,7},{5,6},{6,5},{7,4},{8,11},{9,10},{10,... | collective-permute-start | bytes 12296 | tf_op jit(solution)/shard_map/ppermute | solution.py:689
  56.3 6.6 %collective-permute-start.10 = (f32[8,128]{1,0:T(8,128)S(1)}, f32[8,128]{1,0:T(8,128)S(1)}, u32[]{:S(2)}, u32[]{:S(2)}) collective-permute-start(f32[8,128]{1,0:T(8,128)S(1)} %get-tuple-element.69), channel_id=1, source_target_pairs={{0,2},{1,3},{2,0},{3,1},{4,6},{5,7},{6,4},{7,5},{8,10},{9,11},{10,... | collective-permute-start | bytes 12296 | tf_op jit(solution)/shard_map/ppermute | solution.py:689
  56.3 6.6 %collective-permute-start.9 = (f32[8,128]{1,0:T(8,128)S(1)}, f32[8,128]{1,0:T(8,128)S(1)}, u32[]{:S(2)}, u32[]{:S(2)}) collective-permute-start(f32[8,128]{1,0:T(8,128)S(1)} %get-tuple-element.69), channel_id=1, source_target_pairs={{0,1},{1,0},{2,3},{3,2},{4,5},{5,4},{6,7},{7,6},{8,9},{9,8},{10,11... | collective-permute-start | bytes 12296 | tf_op jit(solution)/shard_map/ppermute | solution.py:689
  64.0 3.9 %collective-permute-start.17 = (bf16[2,256,1024]{2,1,0:T(8,128)(2,1)S(1)}, bf16[2,256,1024]{2,1,0:T(8,128)(2,1)S(1)}, u32[]{:S(2)}, u32[]{:S(2)}) collective-permute-start(bf16[2,256,1024]{2,1,0:T(8,128)(2,1)S(1)} %gradient_block.2), channel_id=1, source_target_pairs={{0,4},{4,0},{8,12},{12,8},{16,20},{20,16},{24,28},{28,24},{1,5},{5... | collective-permute-start | bytes 3145736 | tf_op jit(solution)/shard_map/ppermute | solution.py:689
  64.1 3.2 %collective-permute-start.12 = (f32[8,128]{1,0:T(8,128)S(1)}, f32[8,128]{1,0:T(8,128)S(1)}, u32[]{:S(2)}, u32[]{:S(2)}) collective-permute-start(f32[8,128]{1,0:T(8,128)S(1)} %add_add_fusion.1.outs_0_.mine_ref.margin_ref), channel_id=1, source_target_pairs={{0,4},{4,0},{8,12},{12,8},{16,20},{20,16},{24,28},{28,24},{1,5},{5... | collective-permute-start | bytes 12296 | tf_op jit(solution)/shard_map/ppermute | solution.py:689
  67.2 3.0 %collective-permute-start.13 = (bf16[2,256,1024]{2,1,0:T(8,128)(2,1)S(1)}, bf16[2,256,1024]{2,1,0:T(8,128)(2,1)S(1)}, u32[]{:S(2)}, u32[]{:S(2)}) collective-permute-start(bf16[2,256,1024]{2,1,0:T(8,128)(2,1)S(1)} %get-tuple-element.77), channel_id=1, source_target_pairs={{0,4},{4,0},{8,12},{12,8},{16,20},{20,16},{24,28},{28,24},{1,5},{5... | collective-permute-start | bytes 3145736 | tf_op jit(solution)/shard_map/ppermute | solution.py:689
  67.4 4.1 %collective-permute-start.14 = (bf16[2,256,1024]{2,1,0:T(8,128)(2,1)S(1)}, bf16[2,256,1024]{2,1,0:T(8,128)(2,1)S(1)}, u32[]{:S(2)}, u32[]{:S(2)}) collective-permute-start(bf16[2,256,1024]{2,1,0:T(8,128)(2,1)S(1)} %get-tuple-element.78), channel_id=1, source_target_pairs={{0,4},{4,0},{8,12},{12,8},{16,20},{20,16},{24,28},{28,24},{1,5},{5... | collective-permute-start | bytes 3145736 | tf_op jit(solution)/shard_map/ppermute | solution.py:689
  67.8 5.1 %collective-permute-start.15 = (bf16[2,256,1024]{2,1,0:T(8,128)(2,1)S(1)}, bf16[2,256,1024]{2,1,0:T(8,128)(2,1)S(1)}, u32[]{:S(2)}, u32[]{:S(2)}) collective-permute-start(bf16[2,256,1024]{2,1,0:T(8,128)(2,1)S(1)} %get-tuple-element.79), channel_id=1, source_target_pairs={{0,4},{4,0},{8,12},{12,8},{16,20},{20,16},{24,28},{28,24},{1,5},{5... | collective-permute-start | bytes 3145736 | tf_op jit(solution)/shard_map/ppermute | solution.py:689
  69.2 14.8 %collective-permute-start.21 = (bf16[256,1024]{1,0:T(8,128)(2,1)S(1)}, bf16[256,1024]{1,0:T(8,128)(2,1)S(1)}, u32[]{:S(2)}, u32[]{:S(2)}) collective-permute-start(bf16[256,1024]{1,0:T(8,128)(2,1)S(1)} %get-tuple-element.87), channel_id=1, source_target_pairs={{0,8},{4,12},{8,0},{12,4},{16,24},{20,28},{24,16},{28,20},{1,9},{5... | collective-permute-start | bytes 1572872 | tf_op jit(solution)/shard_map/ppermute | solution.py:689
  69.8 14.9 %collective-permute-start.18 = (bf16[256,1024]{1,0:T(8,128)(2,1)S(1)}, bf16[256,1024]{1,0:T(8,128)(2,1)S(1)}, u32[]{:S(2)}, u32[]{:S(2)}) collective-permute-start(bf16[256,1024]{1,0:T(8,128)(2,1)S(1)} %get-tuple-element.83), channel_id=1, source_target_pairs={{0,16},{4,20},{8,24},{12,28},{16,0},{20,4},{24,8},{28,12},{1,17},{... | collective-permute-start | bytes 1572872 | tf_op jit(solution)/shard_map/ppermute | solution.py:689
  76.3 19.6 %collective-permute-start.16 = (bf16[256,1024]{1,0:T(8,128)(2,1)S(1)}, bf16[256,1024]{1,0:T(8,128)(2,1)S(1)}, u32[]{:S(2)}, u32[]{:S(2)}) collective-permute-start(bf16[256,1024]{1,0:T(8,128)(2,1)S(1)} %get-tuple-element.81), channel_id=1, source_target_pairs={{0,16},{4,20},{8,24},{12,28},{16,0},{20,4},{24,8},{28,12},{1,17},{... | collective-permute-start | bytes 1572872 | tf_op jit(solution)/shard_map/ppermute | solution.py:689
  76.8 20.5 %collective-permute-start.20 = (bf16[256,1024]{1,0:T(8,128)(2,1)S(1)}, bf16[256,1024]{1,0:T(8,128)(2,1)S(1)}, u32[]{:S(2)}, u32[]{:S(2)}) collective-permute-start(bf16[256,1024]{1,0:T(8,128)(2,1)S(1)} %get-tuple-element.85), channel_id=1, source_target_pairs={{0,8},{4,12},{8,0},{12,4},{16,24},{20,28},{24,16},{28,20},{1,9},{5... | collective-permute-start | bytes 1572872 | tf_op jit(solution)/shard_map/ppermute | solution.py:689
  84.2 17.3 %collective-permute-start.22 = (bf16[256,512]{1,0:T(8,128)(2,1)S(1)}, bf16[256,512]{1,0:T(8,128)(2,1)S(1)}, u32[]{:S(2)}, u32[]{:S(2)}) collective-permute-start(bf16[256,512]{1,0:T(8,128)(2,1)S(1)} %get-tuple-element.110), channel_id=1, source_target_pairs={{0,16},{4,20},{8,24},{12,28},{16,0},{20,4},{24,8},{28,12},{1,17},{... | collective-permute-start | bytes 786440 | tf_op jit(solution)/shard_map/ppermute | solution.py:689
  84.9 16.6 %collective-permute-start.19 = (bf16[256,512]{1,0:T(8,128)(2,1)S(1)}, bf16[256,512]{1,0:T(8,128)(2,1)S(1)}, u32[]{:S(2)}, u32[]{:S(2)}) collective-permute-start(bf16[256,512]{1,0:T(8,128)(2,1)S(1)} %get-tuple-element.112), channel_id=1, source_target_pairs={{0,8},{4,12},{8,0},{12,4},{16,24},{20,28},{24,16},{28,20},{1,9},{5... | collective-permute-start | bytes 786440 | tf_op jit(solution)/shard_map/ppermute | solution.py:689
  86.3 20.8 %collective-permute-start.24 = (bf16[256,512]{1,0:T(8,128)(2,1)S(1)}, bf16[256,512]{1,0:T(8,128)(2,1)S(1)}, u32[]{:S(2)}, u32[]{:S(2)}) collective-permute-start(bf16[256,512]{1,0:T(8,128)(2,1)S(1)} %get-tuple-element.109), channel_id=1, source_target_pairs={{0,16},{4,20},{8,24},{12,28},{16,0},{20,4},{24,8},{28,12},{1,17},{... | collective-permute-start | bytes 786440 | tf_op jit(solution)/shard_map/ppermute | solution.py:689
  95.8 11.2 %collective-permute-start.23 = (bf16[256,512]{1,0:T(8,128)(2,1)S(1)}, bf16[256,512]{1,0:T(8,128)(2,1)S(1)}, u32[]{:S(2)}, u32[]{:S(2)}) collective-permute-start(bf16[256,512]{1,0:T(8,128)(2,1)S(1)} %get-tuple-element.111), channel_id=1, source_target_pairs={{0,8},{4,12},{8,0},{12,4},{16,24},{20,28},{24,16},{28,20},{1,9},{5... | collective-permute-start | bytes 786440 | tf_op jit(solution)/shard_map/ppermute | solution.py:689
  101.8 17.0 %collective-permute-start.29 = (bf16[2,512,256]{2,1,0:T(8,128)(2,1)S(1)}, bf16[2,512,256]{2,1,0:T(8,128)(2,1)S(1)}, u32[]{:S(2)}, u32[]{:S(2)}) collective-permute-start(bf16[2,512,256]{2,1,0:T(8,128)(2,1)S(1)} %get-tuple-element.90.refs_4_.refs_0_), channel_id=1, source_target_pairs={{0,16},{4,20},{8,24},{12,28},{16,0},{20,4},{24,8},{28,12},{1,17},{... | collective-permute-start | bytes 1572872 | tf_op jit(solution)/shard_map/ppermute | solution.py:689
  102.2 16.5 %collective-permute-start.28 = (bf16[2,512,256]{2,1,0:T(8,128)(2,1)S(1)}, bf16[2,512,256]{2,1,0:T(8,128)(2,1)S(1)}, u32[]{:S(2)}, u32[]{:S(2)}) collective-permute-start(bf16[2,512,256]{2,1,0:T(8,128)(2,1)S(1)} %get-tuple-element.90.refs_4_.refs_0_), channel_id=1, source_target_pairs={{0,8},{4,12},{8,0},{12,4},{16,24},{20,28},{24,16},{28,20},{1,9},{5... | collective-permute-start | bytes 1572872 | tf_op jit(solution)/shard_map/ppermute | solution.py:689
  107.4 21.5 %collective-permute-start.34 = (bf16[2,512,256]{2,1,0:T(8,128)(2,1)S(1)}, bf16[2,512,256]{2,1,0:T(8,128)(2,1)S(1)}, u32[]{:S(2)}, u32[]{:S(2)}) collective-permute-start(bf16[2,512,256]{2,1,0:T(8,128)(2,1)S(1)} %get-tuple-element.92.refs_5_.refs_1_), channel_id=1, source_target_pairs={{0,16},{4,20},{8,24},{12,28},{16,0},{20,4},{24,8},{28,12},{1,17},{... | collective-permute-start | bytes 1572872 | tf_op jit(solution)/shard_map/ppermute | solution.py:689
  107.9 21.1 %collective-permute-start.33 = (bf16[2,512,256]{2,1,0:T(8,128)(2,1)S(1)}, bf16[2,512,256]{2,1,0:T(8,128)(2,1)S(1)}, u32[]{:S(2)}, u32[]{:S(2)}) collective-permute-start(bf16[2,512,256]{2,1,0:T(8,128)(2,1)S(1)} %get-tuple-element.92.refs_5_.refs_1_), channel_id=1, source_target_pairs={{0,8},{4,12},{8,0},{12,4},{16,24},{20,28},{24,16},{28,20},{1,9},{5... | collective-permute-start | bytes 1572872 | tf_op jit(solution)/shard_map/ppermute | solution.py:689
  109.5 3.6 %collective-permute-start.25 = (f32[8,128]{1,0:T(8,128)S(1)}, f32[8,128]{1,0:T(8,128)S(1)}, u32[]{:S(2)}, u32[]{:S(2)}) collective-permute-start(f32[8,128]{1,0:T(8,128)S(1)} %add.49), channel_id=1, source_target_pairs={{0,1},{1,0},{2,3},{3,2},{4,5},{5,4},{6,7},{7,6},{8,9},{9,8},{10,11... | collective-permute-start | bytes 12296 | tf_op jit(solution)/shard_map/ppermute | solution.py:689
  113.1 4.5 %collective-permute-start.26 = (f32[8,128]{1,0:T(8,128)S(1)}, f32[8,128]{1,0:T(8,128)S(1)}, u32[]{:S(2)}, u32[]{:S(2)}) collective-permute-start(f32[8,128]{1,0:T(8,128)S(1)} %add.50), channel_id=1, source_target_pairs={{0,2},{1,3},{2,0},{3,1},{4,6},{5,7},{6,4},{7,5},{8,10},{9,11},{10,... | collective-permute-start | bytes 12296 | tf_op jit(solution)/shard_map/ppermute | solution.py:689
  117.6 1.2 collective-permute-start.27
  119.4 9.3 %collective-permute-start.32 = (f32[8,128]{1,0:T(8,128)S(1)}, f32[8,128]{1,0:T(8,128)S(1)}, u32[]{:S(2)}, u32[]{:S(2)}) collective-permute-start(f32[8,128]{1,0:T(8,128)S(1)} %get-tuple-element.91.refs_11_), channel_id=1, source_target_pairs={{0,24},{4,28},{8,16},{12,20},{16,8},{20,12},{24,0},{28,4},{1,25},{... | collective-permute-start | bytes 12296 | tf_op jit(solution)/shard_map/ppermute | solution.py:689
  120.9 8.0 %collective-permute-start.31 = (f32[8,128]{1,0:T(8,128)S(1)}, f32[8,128]{1,0:T(8,128)S(1)}, u32[]{:S(2)}, u32[]{:S(2)}) collective-permute-start(f32[8,128]{1,0:T(8,128)S(1)} %get-tuple-element.91.refs_11_), channel_id=1, source_target_pairs={{0,16},{4,20},{8,24},{12,28},{16,0},{20,4},{24,8},{28,12},{1,17},{... | collective-permute-start | bytes 12296 | tf_op jit(solution)/shard_map/ppermute | solution.py:689
  121.9 7.1 %collective-permute-start.30 = (f32[8,128]{1,0:T(8,128)S(1)}, f32[8,128]{1,0:T(8,128)S(1)}, u32[]{:S(2)}, u32[]{:S(2)}) collective-permute-start(f32[8,128]{1,0:T(8,128)S(1)} %get-tuple-element.91.refs_11_), channel_id=1, source_target_pairs={{0,8},{4,12},{8,0},{12,4},{16,24},{20,28},{24,16},{28,20},{1,9},{5... | collective-permute-start | bytes 12296 | tf_op jit(solution)/shard_map/ppermute | solution.py:689
  129.4 2.7 %collective-permute-start.35 = (bf16[2,1024,256]{2,1,0:T(8,128)(2,1)S(1)}, bf16[2,1024,256]{2,1,0:T(8,128)(2,1)S(1)}, u32[]{:S(2)}, u32[]{:S(2)}) collective-permute-start(bf16[2,1024,256]{2,1,0:T(8,128)(2,1)S(1)} %get-tuple-element.94), channel_id=1, source_target_pairs={{0,4},{4,0},{8,12},{12,8},{16,20},{20,16},{24,28},{28,24},{1,5},{5... | collective-permute-start | bytes 3145736 | tf_op jit(solution)/shard_map/ppermute | solution.py:689
  129.5 5.8 %collective-permute-start.37 = (bf16[2,1024,256]{2,1,0:T(8,128)(2,1)S(1)}, bf16[2,1024,256]{2,1,0:T(8,128)(2,1)S(1)}, u32[]{:S(2)}, u32[]{:S(2)}) collective-permute-start(bf16[2,1024,256]{2,1,0:T(8,128)(2,1)S(1)} %get-tuple-element.98), channel_id=1, source_target_pairs={{0,4},{4,0},{8,12},{12,8},{16,20},{20,16},{24,28},{28,24},{1,5},{5... | collective-permute-start | bytes 3145736 | tf_op jit(solution)/shard_map/ppermute | solution.py:689
  130.0 5.3 %collective-permute-start.38 = (bf16[2,1024,256]{2,1,0:T(8,128)(2,1)S(1)}, bf16[2,1024,256]{2,1,0:T(8,128)(2,1)S(1)}, u32[]{:S(2)}, u32[]{:S(2)}) collective-permute-start(bf16[2,1024,256]{2,1,0:T(8,128)(2,1)S(1)} %get-tuple-element.99), channel_id=1, source_target_pairs={{0,4},{4,0},{8,12},{12,8},{16,20},{20,16},{24,28},{28,24},{1,5},{5... | collective-permute-start | bytes 3145736 | tf_op jit(solution)/shard_map/ppermute | solution.py:689
  130.0 14.3 %collective-permute-start.40 = (bf16[1024,256]{1,0:T(8,128)(2,1)S(1)}, bf16[1024,256]{1,0:T(8,128)(2,1)S(1)}, u32[]{:S(2)}, u32[]{:S(2)}) collective-permute-start(bf16[1024,256]{1,0:T(8,128)(2,1)S(1)} %get-tuple-element.103), channel_id=1, source_target_pairs={{0,8},{4,12},{8,0},{12,4},{16,24},{20,28},{24,16},{28,20},{1,9},{5... | collective-permute-start | bytes 1572872 | tf_op jit(solution)/shard_map/ppermute | solution.py:689
  131.5 14.0 %collective-permute-start.36 = (bf16[1024,256]{1,0:T(8,128)(2,1)S(1)}, bf16[1024,256]{1,0:T(8,128)(2,1)S(1)}, u32[]{:S(2)}, u32[]{:S(2)}) collective-permute-start(bf16[1024,256]{1,0:T(8,128)(2,1)S(1)} %get-tuple-element.97), channel_id=1, source_target_pairs={{0,16},{4,20},{8,24},{12,28},{16,0},{20,4},{24,8},{28,12},{1,17},{... | collective-permute-start | bytes 1572872 | tf_op jit(solution)/shard_map/ppermute | solution.py:689
  145.5 2.7 %collective-permute-start.39 = (bf16[1024,256]{1,0:T(8,128)(2,1)S(1)}, bf16[1024,256]{1,0:T(8,128)(2,1)S(1)}, u32[]{:S(2)}, u32[]{:S(2)}) collective-permute-start(bf16[1024,256]{1,0:T(8,128)(2,1)S(1)} %collective-permute-done.36.refs_0_), channel_id=1, source_target_pairs={{0,4},{4,0},{8,12},{12,8},{16,20},{20,16},{24,28},{28,24},{1,5},{5... | collective-permute-start | bytes 1572872 | tf_op jit(solution)/shard_map/ppermute | solution.py:689
  145.5 2.7 %collective-permute-start.41 = (bf16[1024,256]{1,0:T(8,128)(2,1)S(1)}, bf16[1024,256]{1,0:T(8,128)(2,1)S(1)}, u32[]{:S(2)}, u32[]{:S(2)}) collective-permute-start(bf16[1024,256]{1,0:T(8,128)(2,1)S(1)} %collective-permute-done.40.refs_1_), channel_id=1, source_target_pairs={{0,4},{4,0},{8,12},{12,8},{16,20},{20,16},{24,28},{28,24},{1,5},{5... | collective-permute-start | bytes 1572872 | tf_op jit(solution)/shard_map/ppermute | solution.py:689

commit v5 on v4

--- a/solution.py
+++ b/solution.py
@@ -235,7 +235,8 @@
     )(*args)
 
 
-HEADS = 1
+FORWARD_HEADS = 1
+BACKWARD_HEADS = 4
 
 
 def stacked(ref, row, col, r, first, count):
@@ -258,7 +259,7 @@
 
 def attend_kernel(keep, len_ref, q_ref, k_ref, v_ref, ro_ref, *rest):
     groups = q_ref.shape[1] // k_ref.shape[1]
-    count = min(groups, HEADS)
+    count = min(groups, FORWARD_HEADS)
     if keep:
         before_ref, margin_ref, prob_ref, delta_ref = rest
     else:
@@ -329,7 +330,7 @@
 def attend_back_kernel(len_ref, q_ref, v_ref, ro_ref, prob_ref, delta_ref, table_ref, grad_ref):
     tiles = LEN // TILE
     groups = q_ref.shape[1] // v_ref.shape[1]
-    count = min(groups, HEADS)
+    count = min(groups, BACKWARD_HEADS)
 
     def one(step, carry):
         seq, h, row, col, q_col = places(step, q_ref, v_ref)

time: 151 us -> 149 us (0.987)
  Pallas kernels: 67.6 us -> 65.8 us
    pallas_call x1, Pallas kernels: 5.79 us -> 4 us  [attend_back(): pl.pallas_call(attend_back_kernel, in_specs=[SMEM] + [VMEM] * 6, out_spec...]
  transfers between devices with their start and end apart: 42 -> 42, of which waited for: 19 -> 19; matrix products, arithmetic and copies ran while one was open for 0% -> 0% of each run, Pallas kernels for 39% -> 38%
where the time goes in v5:
time: 149 us
  Pallas kernels  65.8 us (44%)
  waiting for transfers between devices  47.7 us (32%)
  starting transfers between devices  33.6 us (23%)
    ppermute x42, waiting for transfers between devices, swap(): return lax.ppermute(x, axis, [(i, i ^ bit) for i in range(size)])  47.7 us
    ppermute x42, starting transfers between devices, swap(): return lax.ppermute(x, axis, [(i, i ^ bit) for i in range(size)])  33.6 us
    pallas_call x1, Pallas kernels, norm_project(): pl.pallas_call(norm_project_kernel, in_specs=[SMEM, HBM, HBM, HBM], out_s...  17.8 us
    pallas_call x4, Pallas kernels, blend(): pl.pallas_call(functools.partial(blend_kernel, tuple(masks), first, offse...  12.3 us
    pallas_call x2, Pallas kernels, attend(): pl.pallas_call(functools.partial(attend_kernel, keep), in_specs=[SMEM] +...  8.92 us
    pallas_call x4, Pallas kernels, project(): pl.pallas_call(functools.partial(project_kernel, tuple(masks), first, las...  8.81 us
    pallas_call x4, Pallas kernels, gradient_blocks(): pl.pallas_call(functools.partial(kernel, tuple(masks)), in_specs=in_specs...  8.29 us
    pallas_call x1, Pallas kernels, attend_back(): pl.pallas_call(attend_back_kernel, in_specs=[SMEM] + [VMEM] * 6, out_spec...  4 us
  transfers between devices with their start and end apart: 42, of which 19 were waited for; matrix products, arithmetic and copies ran while one was open for 0% of the time, Pallas kernels for 38%

profile of v5, /device:TPU:0, one launch (start us, length us, event | category | flops | bytes accessed | tf_op | source)
XLA Modules:
  0.0 148.6 jit_solution(12011520288441359788)
XLA Ops:
  0.6 3.0 %collective-permute-start.1 = (bf16[2,1024,256]{2,1,0:T(8,128)(2,1)}, bf16[2,1024,256]{2,1,0:T(8,128)(2,1)S(1)}, u32[]{:S(2)}, u32[]{:S(2)}) collective-permute-start(bf16[2,1024,256]{2,1,0:T(8,128)(2,1)} %refs_0_.3), channel_id=1, source_target_pairs={{0,16},{4,20},{8,24},{12,28},{16,0},{20,4},{24,8},{28,12},{1,17},{... | collective-permute-start | bytes 3145736 | tf_op jit(solution)/shard_map/ppermute | solution.py:690
  3.7 1.5 %collective-permute-start = (bf16[2,1024,256]{2,1,0:T(8,128)(2,1)}, bf16[2,1024,256]{2,1,0:T(8,128)(2,1)S(1)}, u32[]{:S(2)}, u32[]{:S(2)}) collective-permute-start(bf16[2,1024,256]{2,1,0:T(8,128)(2,1)} %refs_0_.3), channel_id=1, source_target_pairs={{0,8},{4,12},{8,0},{12,4},{16,24},{20,28},{24,16},{28,20},{1,9},{5... | collective-permute-start | bytes 3145736 | tf_op jit(solution)/shard_map/ppermute | solution.py:690
  5.2 17.8 %norm_project.1 = (bf16[768,8192]{1,0:T(8,128)(2,1)S(1)}, bf16[768,256]{1,0:T(8,128)(2,1)S(1)}, bf16[768,256]{1,0:T(8,128)(2,1)S(1)}) custom-call(s32[1]{0:T(128)} %bitcast.idx_ref, bf16[768,8192]{1,0:T(8,128)(2,1)} %hidden_hbm.1, bf16[2,8192,256]{2,1,0:T(8,128)(2,1)} %refs_10_.1, f32[2,384,128]{2,1,0:T(8,128)} %constant.8.clone.table_hbm.refs_3_.table_ref), custom_call_target="tpu_custom_call" | custom-call | flops 1 | bytes 1 | tf_op jit(solution)/shard_map/norm_project/pallas_call | solution.py:133
  23.1 4.8 %attend.2.refs_2_.rest_0_ = f32[8,128]{1,0:T(8,128)S(1)} custom-call(s32[2]{0:T(128)S(1)} %copy-done.5, bf16[768,1024]{1,0:T(8,128)(2,1)S(1)} %copy-done.4, bf16[768,256]{1,0:T(8,128)(2,1)S(1)} %get-tuple-element.57.k_ref, bf16[768,256]{1,0:T(8,128)(2,1)S(1)} %get-tuple-element.58.v_ref, bf16[768,1024]{1,0:T(8,128)(2,1)S(1)} %copy-done), custom_call_target="tpu_custom_call" | custom-call | flops 1 | bytes 1 | tf_op jit(solution)/shard_map/attend/pallas_call | solution.py:319
  27.8 0.7 collective-permute-done.refs_0_.refs_2_
  28.5 0.5 collective-permute-start.4
  29.1 1.6 %collective-permute-start.7 = (bf16[1024,256]{1,0:T(8,128)(2,1)S(1)}, bf16[1024,256]{1,0:T(8,128)(2,1)S(1)}, u32[]{:S(2)}, u32[]{:S(2)}) collective-permute-start(bf16[1024,256]{1,0:T(8,128)(2,1)S(1)} %get-tuple-element.63), channel_id=1, source_target_pairs={{0,8},{4,12},{8,0},{12,4},{16,24},{20,28},{24,16},{28,20},{1,9},{5... | collective-permute-start | bytes 1572872 | tf_op jit(solution)/shard_map/ppermute | solution.py:690
  30.7 0.5 collective-permute-start.2
  31.2 2.0 %project.4.refs_4_ = f32[2,768,256]{2,1,0:T(8,128)S(1)} custom-call(s32[1]{0:T(128)} %bitcast.idx_ref, bf16[768,8192]{1,0:T(8,128)(2,1)S(1)} %get-tuple-element.56.x_ref, bf16[2,1024,256]{2,1,0:T(8,128)(2,1)S(1)} %copy-done.2, bf16[2,1024,256]{2,1,0:T(8,128)(2,1)S(1)} %collective-permute-done.5.refs_1_), custom_call_target="tpu_custom_call" | custom-call | flops 1 | bytes 1 | tf_op jit(solution)/shard_map/project/pallas_call | solution.py:226
  33.3 4.1 %project.5.refs_2_ = f32[2,768,256]{2,1,0:T(8,128)S(1)} custom-call(s32[1]{0:T(128)} %bitcast.idx_ref, bf16[768,8192]{1,0:T(8,128)(2,1)S(1)} %get-tuple-element.56.x_ref, bf16[2,1024,256]{2,1,0:T(8,128)(2,1)S(1)} %collective-permute-done.refs_0_.refs_2_, bf16[2,1024,256]{2,1,0:T(8,128)(2,1)S(1)} %collective-permute-done.3.refs_1_.refs_3_, ...), custom_call_target="tpu_custom_call" | custom-call | flops 1 | bytes 1 | tf_op jit(solution)/shard_map/project/pallas_call | solution.py:226
  37.4 5.7 %collective-permute-done.7.refs_1_.refs_7_ = bf16[1024,256]{1,0:T(8,128)(2,1)S(1)} collective-permute-done((bf16[1024,256]{1,0:T(8,128)(2,1)S(1)}, bf16[1024,256]{1,0:T(8,128)(2,1)S(1)}, u32[]{:S(2)}, u32[]{:S(2)}) %collective-permute-start.7) | collective-permute-done | bytes 524320 | tf_op jit(solution)/shard_map/ppermute | solution.py:690
  43.0 1.2 collective-permute-done.2.refs_0_.refs_6_
  44.2 0.5 collective-permute-start.8
  44.7 1.1 project.6.refs_2_
  46.1 0.7 collective-permute-done.8.refs_1_.refs_9_
  46.9 1.6 %project.7 = (bf16[768,256]{1,0:T(8,128)(2,1)S(1)}, bf16[768,256]{1,0:T(8,128)(2,1)S(1)}) custom-call(s32[1]{0:T(128)} %bitcast.idx_ref, bf16[768,8192]{1,0:T(8,128)(2,1)S(1)} %get-tuple-element.56.x_ref, bf16[1024,256]{1,0:T(8,128)(2,1)S(1)} %collective-permute-done.6.refs_0_.refs_8_, bf16[1024,256]{1,0:T(8,128)(2,1)S(1)} %collective-permute-done.8.refs_1_.refs_9_, ...), custom_call_target="tpu_custom_call" | custom-call | flops 1 | bytes 1 | tf_op jit(solution)/shard_map/project/pallas_call | solution.py:226
  48.5 4.2 %attend.3 = (f32[8,128]{1,0:T(8,128)S(1)}, bf16[2,2,768,512]{3,2,1,0:T(8,128)(2,1)S(1)}, f32[2,2,3,512]{3,2,1,0:T(4,128)S(1)}) custom-call(s32[2]{0:T(128)S(1)} %copy-done.5, bf16[768,1024]{1,0:T(8,128)(2,1)S(1)} %copy-done.1, bf16[768,256]{1,0:T(8,128)(2,1)S(1)} %get-tuple-element.66.k_ref, bf16[768,256]{1,0:T(8,128)(2,1)S(1)} %get-tuple-element.65.v_ref, ...), custom_call_target="tpu_custom_call" | custom-call | flops 1 | bytes 1 | tf_op jit(solution)/shard_map/attend/pallas_call | solution.py:319
  52.7 3.7 %collective-permute-start.11 = (f32[8,128]{1,0:T(8,128)S(1)}, f32[8,128]{1,0:T(8,128)S(1)}, u32[]{:S(2)}, u32[]{:S(2)}) collective-permute-start(f32[8,128]{1,0:T(8,128)S(1)} %get-tuple-element.69), channel_id=1, source_target_pairs={{0,3},{1,2},{2,1},{3,0},{4,7},{5,6},{6,5},{7,4},{8,11},{9,10},{10,... | collective-permute-start | bytes 12296 | tf_op jit(solution)/shard_map/ppermute | solution.py:690
  56.3 0.8 collective-permute-start.9
  57.1 4.0 %attend_back.1.cot_ref = bf16[2,256,768]{2,1,0:T(8,128)(2,1)S(1)} custom-call(s32[2]{0:T(128)S(1)} %copy-done.5, bf16[768,1024]{1,0:T(8,128)(2,1)S(1)} %copy-done.1, bf16[768,256]{1,0:T(8,128)(2,1)S(1)} %get-tuple-element.65.v_ref, bf16[768,1024]{1,0:T(8,128)(2,1)S(1)} %copy-done, bf16[2,2,768,512]{3,2,1,0:T(8,128)(2,1)S(1)} %get-tuple-element.67.prob_ref, ...), custom_call_target="tpu_custom_call" | custom-call | flops 1 | bytes 1 | tf_op jit(solution)/shard_map/attend_back/pallas_call | solution.py:373
  61.2 1.0 gradient_block.2
  62.3 0.5 collective-permute-start.12
  62.8 2.7 %gradient_block.3 = (bf16[2,256,1024]{2,1,0:T(8,128)(2,1)S(1)}, bf16[2,256,1024]{2,1,0:T(8,128)(2,1)S(1)}, bf16[2,256,1024]{2,1,0:T(8,128)(2,1)S(1)}) custom-call(s32[1]{0:T(128)} %bitcast.idx_ref, bf16[768,8192]{1,0:T(8,128)(2,1)S(1)} %get-tuple-element.56.x_ref, bf16[2,256,768]{2,1,0:T(8,128)(2,1)S(1)} %attend_back.1.cot_ref, ...), custom_call_target="tpu_custom_call" | custom-call | flops 1 | bytes 1 | tf_op jit(solution)/shard_map/gradient_block/pallas_call | solution.py:441
  65.6 0.4 collective-permute-start.14
  66.1 1.1 merged_block.3
  67.2 0.6 collective-permute-start.21
  68.2 1.5 collective-permute-done.14.refs_1_
  69.7 1.5 %collective-permute-done.15.refs_2_ = bf16[2,256,1024]{2,1,0:T(8,128)(2,1)S(1)} collective-permute-done((bf16[2,256,1024]{2,1,0:T(8,128)(2,1)S(1)}, bf16[2,256,1024]{2,1,0:T(8,128)(2,1)S(1)}, u32[]{:S(2)}, u32[]{:S(2)}) %collective-permute-start.15) | collective-permute-done | bytes 1048608 | tf_op jit(solution)/shard_map/ppermute | solution.py:690
  71.2 3.5 %merged_block.2 = (bf16[256,1024]{1,0:T(8,128)(2,1)S(1)}, bf16[256,1024]{1,0:T(8,128)(2,1)S(1)}, bf16[256,1024]{1,0:T(8,128)(2,1)S(1)}, bf16[256,1024]{1,0:T(8,1...) custom-call(s32[1]{0:T(128)} %bitcast.idx_ref, bf16[768,8192]{1,0:T(8,128)(2,1)S(1)} %get-tuple-element.56.x_ref, ...), custom_call_target="tpu_custom_call" | custom-call | flops 1 | bytes 1 | tf_op jit(solution)/shard_map/merged_block/pallas_call | solution.py:441
  74.7 0.6 collective-permute-start.16
  75.3 0.4 collective-permute-start.20
  75.7 6.3 %collective-permute-done.21 = bf16[256,1024]{1,0:T(8,128)(2,1)S(1)} collective-permute-done((bf16[256,1024]{1,0:T(8,128)(2,1)S(1)}, bf16[256,1024]{1,0:T(8,128)(2,1)S(1)}, u32[]{:S(2)}, u32[]{:S(2)}) %collective-permute-start.21) | collective-permute-done | bytes 524320 | tf_op jit(solution)/shard_map/ppermute | solution.py:690
  82.2 0.6 collective-permute-start.22
  82.9 1.4 collective-permute-start.19
  84.3 0.7 collective-permute-start.24
  85.0 8.8 %collective-permute-done.16.refs_1_ = bf16[256,1024]{1,0:T(8,128)(2,1)S(1)} collective-permute-done((bf16[256,1024]{1,0:T(8,128)(2,1)S(1)}, bf16[256,1024]{1,0:T(8,128)(2,1)S(1)}, u32[]{:S(2)}, u32[]{:S(2)}) %collective-permute-start.16) | collective-permute-done | bytes 524320 | tf_op jit(solution)/shard_map/ppermute | solution.py:690
  93.8 1.5 %collective-permute-start.23 = (bf16[256,512]{1,0:T(8,128)(2,1)S(1)}, bf16[256,512]{1,0:T(8,128)(2,1)S(1)}, u32[]{:S(2)}, u32[]{:S(2)}) collective-permute-start(bf16[256,512]{1,0:T(8,128)(2,1)S(1)} %get-tuple-element.111), channel_id=1, source_target_pairs={{0,8},{4,12},{8,0},{12,4},{16,24},{20,28},{24,16},{28,20},{1,9},{5... | collective-permute-start | bytes 786440 | tf_op jit(solution)/shard_map/ppermute | solution.py:690
  95.3 4.1 %collective-permute-done.22.refs_5_ = bf16[256,512]{1,0:T(8,128)(2,1)S(1)} collective-permute-done((bf16[256,512]{1,0:T(8,128)(2,1)S(1)}, bf16[256,512]{1,0:T(8,128)(2,1)S(1)}, u32[]{:S(2)}, u32[]{:S(2)}) %collective-permute-start.22) | collective-permute-done | bytes 262176 | tf_op jit(solution)/shard_map/ppermute | solution.py:690
  99.8 0.4 collective-permute-start.29
  100.2 1.6 %collective-permute-start.28 = (bf16[2,512,256]{2,1,0:T(8,128)(2,1)S(1)}, bf16[2,512,256]{2,1,0:T(8,128)(2,1)S(1)}, u32[]{:S(2)}, u32[]{:S(2)}) collective-permute-start(bf16[2,512,256]{2,1,0:T(8,128)(2,1)S(1)} %get-tuple-element.90.refs_4_.refs_0_), channel_id=1, source_target_pairs={{0,8},{4,12},{8,0},{12,4},{16,24},{20,28},{24,16},{28,20},{1,9},{5... | collective-permute-start | bytes 1572872 | tf_op jit(solution)/shard_map/ppermute | solution.py:690
  101.9 3.2 %collective-permute-done.24.refs_5_ = bf16[256,512]{1,0:T(8,128)(2,1)S(1)} collective-permute-done((bf16[256,512]{1,0:T(8,128)(2,1)S(1)}, bf16[256,512]{1,0:T(8,128)(2,1)S(1)}, u32[]{:S(2)}, u32[]{:S(2)}) %collective-permute-start.24) | collective-permute-done | bytes 262176 | tf_op jit(solution)/shard_map/ppermute | solution.py:690
  105.4 0.4 collective-permute-start.34
  105.9 1.6 %collective-permute-start.33 = (bf16[2,512,256]{2,1,0:T(8,128)(2,1)S(1)}, bf16[2,512,256]{2,1,0:T(8,128)(2,1)S(1)}, u32[]{:S(2)}, u32[]{:S(2)}) collective-permute-start(bf16[2,512,256]{2,1,0:T(8,128)(2,1)S(1)} %get-tuple-element.92.refs_5_.refs_1_), channel_id=1, source_target_pairs={{0,8},{4,12},{8,0},{12,4},{16,24},{20,28},{24,16},{28,20},{1,9},{5... | collective-permute-start | bytes 1572872 | tf_op jit(solution)/shard_map/ppermute | solution.py:690
  107.5 1.2 collective-permute-start.25
  108.7 2.4 %collective-permute-done.25 = f32[8,128]{1,0:T(8,128)S(1)} collective-permute-done((f32[8,128]{1,0:T(8,128)S(1)}, f32[8,128]{1,0:T(8,128)S(1)}, u32[]{:S(2)}, u32[]{:S(2)}) %collective-permute-start.25) | collective-permute-done | bytes 4128 | tf_op jit(solution)/shard_map/ppermute | solution.py:690
  111.1 2.1 %collective-permute-start.26 = (f32[8,128]{1,0:T(8,128)S(1)}, f32[8,128]{1,0:T(8,128)S(1)}, u32[]{:S(2)}, u32[]{:S(2)}) collective-permute-start(f32[8,128]{1,0:T(8,128)S(1)} %add.50), channel_id=1, source_target_pairs={{0,2},{1,3},{2,0},{3,1},{4,6},{5,7},{6,4},{7,5},{8,10},{9,11},{10,... | collective-permute-start | bytes 12296 | tf_op jit(solution)/shard_map/ppermute | solution.py:690
  113.2 2.4 %collective-permute-done.26 = f32[8,128]{1,0:T(8,128)S(1)} collective-permute-done((f32[8,128]{1,0:T(8,128)S(1)}, f32[8,128]{1,0:T(8,128)S(1)}, u32[]{:S(2)}, u32[]{:S(2)}) %collective-permute-start.26) | collective-permute-done | bytes 4128 | tf_op jit(solution)/shard_map/ppermute | solution.py:690
  115.6 1.2 collective-permute-done.27
  116.8 0.6 gate.1
  117.4 1.6 %collective-permute-start.32 = (f32[8,128]{1,0:T(8,128)S(1)}, f32[8,128]{1,0:T(8,128)S(1)}, u32[]{:S(2)}, u32[]{:S(2)}) collective-permute-start(f32[8,128]{1,0:T(8,128)S(1)} %get-tuple-element.91.refs_11_), channel_id=1, source_target_pairs={{0,24},{4,28},{8,16},{12,20},{16,8},{20,12},{24,0},{28,4},{1,25},{... | collective-permute-start | bytes 12296 | tf_op jit(solution)/shard_map/ppermute | solution.py:690
  118.9 1.0 collective-permute-start.31
  119.9 1.0 collective-permute-start.30
  120.9 3.8 %fetch.1 = (bf16[8,2,1024,256]{3,2,1,0:T(8,128)(2,1)S(1)}, bf16[8,2,1024,256]{3,2,1,0:T(8,128)(2,1)S(1)}) custom-call(s32[1]{0:T(128)} %bitcast.idx_ref, bf16[2,1024,256]{2,1,0:T(8,128)(2,1)S(1)} %copy-done.2, bf16[2,1024,256]{2,1,0:T(8,128)(2,1)S(1)} %collective-permute-done.5.refs_1_, bf16[2,1024,256]{2,1,0:T(8,128)(2,1)S(1)} %collective-permute-done.refs_0_.refs_2_, ...), custom_call_target="tpu_custom_call" | custom-call | flops 1 | bytes 1 | tf_op jit(solution)/shard_map/fetch/pallas_call | solution.py:575
  124.7 2.0 %collective-permute-done.32 = f32[8,128]{1,0:T(8,128)S(1)} collective-permute-done((f32[8,128]{1,0:T(8,128)S(1)}, f32[8,128]{1,0:T(8,128)S(1)}, u32[]{:S(2)}, u32[]{:S(2)}) %collective-permute-start.32) | collective-permute-done | bytes 4128 | tf_op jit(solution)/shard_map/ppermute | solution.py:690
  127.5 0.5 collective-permute-start.37
  128.0 1.5 %collective-permute-start.40 = (bf16[1024,256]{1,0:T(8,128)(2,1)S(1)}, bf16[1024,256]{1,0:T(8,128)(2,1)S(1)}, u32[]{:S(2)}, u32[]{:S(2)}) collective-permute-start(bf16[1024,256]{1,0:T(8,128)(2,1)S(1)} %get-tuple-element.103), channel_id=1, source_target_pairs={{0,8},{4,12},{8,0},{12,4},{16,24},{20,28},{24,16},{28,20},{1,9},{5... | collective-permute-start | bytes 1572872 | tf_op jit(solution)/shard_map/ppermute | solution.py:690
  129.5 0.5 collective-permute-start.36
  130.1 3.2 %blend.4 = (bf16[2,8192,256]{2,1,0:T(8,128)(2,1)}, f32[8,128]{1,0:T(8,128)}, bf16[2,1024,256]{2,1,0:T(8,128)(2,1)}) custom-call(s32[1]{0:T(128)} %bitcast.idx_ref, f32[8,128]{1,0:T(8,128)S(1)} %add_add_fusion.refs_10_.square_ref, bf16[2,512,256]{2,1,0:T(8,128)(2,1)S(1)} %get-tuple-element.90.refs_4_.refs_0_, ...), custom_call_target="tpu_custom_call" | custom-call | flops 1 | bytes 1 | tf_op jit(solution)/shard_map/blend/pallas_call | solution.py:657
  133.3 4.8 %blend.5 = (bf16[2,8192,256]{2,1,0:T(8,128)(2,1)}, f32[8,128]{1,0:T(8,128)}) custom-call(s32[1]{0:T(128)} %bitcast.idx_ref, f32[8,128]{1,0:T(8,128)S(1)} %add_add_fusion.refs_10_.square_ref, bf16[2,512,256]{2,1,0:T(8,128)(2,1)S(1)} %collective-permute-done.28.refs_0_.refs_6_, ...), custom_call_target="tpu_custom_call", output_to_operand_aliasing={{0}: (10, {})} | custom-call | flops 1 | bytes 1 | tf_op jit(solution)/shard_map/blend/pallas_call | solution.py:657
  138.1 4.2 %collective-permute-done.40.refs_1_ = bf16[1024,256]{1,0:T(8,128)(2,1)S(1)} collective-permute-done((bf16[1024,256]{1,0:T(8,128)(2,1)S(1)}, bf16[1024,256]{1,0:T(8,128)(2,1)S(1)}, u32[]{:S(2)}, u32[]{:S(2)}) %collective-permute-start.40) | collective-permute-done | bytes 524320 | tf_op jit(solution)/shard_map/ppermute | solution.py:690
  142.3 1.2 collective-permute-done.36.refs_0_
  143.5 0.5 collective-permute-start.41
  144.0 2.2 %blend.6 = (bf16[2,8192,256]{2,1,0:T(8,128)(2,1)}, f32[8,128]{1,0:T(8,128)}) custom-call(s32[1]{0:T(128)} %bitcast.idx_ref, f32[8,128]{1,0:T(8,128)S(1)} %add_add_fusion.refs_10_.square_ref, bf16[1024,256]{1,0:T(8,128)(2,1)S(1)} %collective-permute-done.36.refs_0_, ...), custom_call_target="tpu_custom_call", output_to_operand_aliasing={{0}: (6, {})} | custom-call | flops 1 | bytes 1 | tf_op jit(solution)/shard_map/blend/pallas_call | solution.py:657
  146.2 2.2 %blend.7 = (bf16[2,8192,256]{2,1,0:T(8,128)(2,1)}, f32[8,128]{1,0:T(8,128)}) custom-call(s32[1]{0:T(128)} %bitcast.idx_ref, f32[8,128]{1,0:T(8,128)S(1)} %add_add_fusion.refs_10_.square_ref, bf16[1024,256]{1,0:T(8,128)(2,1)S(1)} %collective-permute-done.39.refs_0_, ...), custom_call_target="tpu_custom_call", output_to_operand_aliasing={{0}: (6, {})} | custom-call | flops 1 | bytes 1 | tf_op jit(solution)/shard_map/blend/pallas_call | solution.py:657
  (63 shorter events, 3.1 us)
Async XLA Ops:
  0.6 27.2 %collective-permute-start.1 = (bf16[2,1024,256]{2,1,0:T(8,128)(2,1)}, bf16[2,1024,256]{2,1,0:T(8,128)(2,1)S(1)}, u32[]{:S(2)}, u32[]{:S(2)}) collective-permute-start(bf16[2,1024,256]{2,1,0:T(8,128)(2,1)} %refs_0_.3), channel_id=1, source_target_pairs={{0,16},{4,20},{8,24},{12,28},{16,0},{20,4},{24,8},{28,12},{1,17},{... | collective-permute-start | bytes 3145736 | tf_op jit(solution)/shard_map/ppermute | solution.py:690
  3.7 24.8 %collective-permute-start = (bf16[2,1024,256]{2,1,0:T(8,128)(2,1)}, bf16[2,1024,256]{2,1,0:T(8,128)(2,1)S(1)}, u32[]{:S(2)}, u32[]{:S(2)}) collective-permute-start(bf16[2,1024,256]{2,1,0:T(8,128)(2,1)} %refs_0_.3), channel_id=1, source_target_pairs={{0,8},{4,12},{8,0},{12,4},{16,24},{20,28},{24,16},{28,20},{1,9},{5... | collective-permute-start | bytes 3145736 | tf_op jit(solution)/shard_map/ppermute | solution.py:690
  5.2 26.0 %collective-permute-start.5 = (bf16[2,1024,256]{2,1,0:T(8,128)(2,1)}, bf16[2,1024,256]{2,1,0:T(8,128)(2,1)S(1)}, u32[]{:S(2)}, u32[]{:S(2)}) collective-permute-start(bf16[2,1024,256]{2,1,0:T(8,128)(2,1)} %refs_0_.3), channel_id=1, source_target_pairs={{0,4},{4,0},{8,12},{12,8},{16,20},{20,16},{24,28},{28,24},{1,5},{5... | collective-permute-start | bytes 3145736 | tf_op jit(solution)/shard_map/ppermute | solution.py:690
  5.2 17.9 %copy-start = (bf16[768,1024]{1,0:T(8,128)(2,1)S(1)}, bf16[768,1024]{1,0:T(8,128)(2,1)}, u32[]{:S(2)}) copy-start(bf16[768,1024]{1,0:T(8,128)(2,1)} %ro_ref.5) | copy-start | bytes 4718596
  5.2 17.9 %copy-start.4 = (bf16[768,1024]{1,0:T(8,128)(2,1)S(1)}, bf16[768,1024]{1,0:T(8,128)(2,1)}, u32[]{:S(2)}) copy-start(bf16[768,1024]{1,0:T(8,128)(2,1)} %q_ref.3) | copy-start | bytes 4718596
  5.2 17.9 %copy-start.5 = (s32[2]{0:T(128)S(1)}, s32[2]{0:T(128)}, u32[]{:S(2)}) copy-start(s32[2]{0:T(128)} %len_ref.5) | copy-start | bytes 28
  5.2 26.0 %copy-start.2 = (bf16[2,1024,256]{2,1,0:T(8,128)(2,1)S(1)}, bf16[2,1024,256]{2,1,0:T(8,128)(2,1)}, u32[]{:S(2)}) copy-start(bf16[2,1024,256]{2,1,0:T(8,128)(2,1)} %refs_0_.3) | copy-start | bytes 3145732
  28.5 4.8 %collective-permute-start.3 = (bf16[2,1024,256]{2,1,0:T(8,128)(2,1)S(1)}, bf16[2,1024,256]{2,1,0:T(8,128)(2,1)S(1)}, u32[]{:S(2)}, u32[]{:S(2)}) collective-permute-start(bf16[2,1024,256]{2,1,0:T(8,128)(2,1)S(1)} %collective-permute-done.refs_0_.refs_2_), channel_id=1, source_target_pairs={{0,4},{4,0},{8,12},{12,8},{16,20},{20,16},{24,28},{28,24},{1,5},{5... | collective-permute-start | bytes 3145736 | tf_op jit(solution)/shard_map/ppermute | solution.py:690
  28.5 4.8 %collective-permute-start.4 = (bf16[2,1024,256]{2,1,0:T(8,128)(2,1)S(1)}, bf16[2,1024,256]{2,1,0:T(8,128)(2,1)S(1)}, u32[]{:S(2)}, u32[]{:S(2)}) collective-permute-start(bf16[2,1024,256]{2,1,0:T(8,128)(2,1)S(1)} %collective-permute-done.1.refs_1_.refs_2_.refs_4_), channel_id=1, source_target_pairs={{0,4},{4,0},{8,12},{12,8},{16,20},{20,16},{24,28},{28,24},{1,5},{5... | collective-permute-start | bytes 3145736 | tf_op jit(solution)/shard_map/ppermute | solution.py:690
  29.1 13.9 %collective-permute-start.7 = (bf16[1024,256]{1,0:T(8,128)(2,1)S(1)}, bf16[1024,256]{1,0:T(8,128)(2,1)S(1)}, u32[]{:S(2)}, u32[]{:S(2)}) collective-permute-start(bf16[1024,256]{1,0:T(8,128)(2,1)S(1)} %get-tuple-element.63), channel_id=1, source_target_pairs={{0,8},{4,12},{8,0},{12,4},{16,24},{20,28},{24,16},{28,20},{1,9},{5... | collective-permute-start | bytes 1572872 | tf_op jit(solution)/shard_map/ppermute | solution.py:690
  30.7 13.6 %collective-permute-start.2 = (bf16[1024,256]{1,0:T(8,128)(2,1)S(1)}, bf16[1024,256]{1,0:T(8,128)(2,1)S(1)}, u32[]{:S(2)}, u32[]{:S(2)}) collective-permute-start(bf16[1024,256]{1,0:T(8,128)(2,1)S(1)} %get-tuple-element.59), channel_id=1, source_target_pairs={{0,16},{4,20},{8,24},{12,28},{16,0},{20,4},{24,8},{28,12},{1,17},{... | collective-permute-start | bytes 1572872 | tf_op jit(solution)/shard_map/ppermute | solution.py:690
  44.2 1.9 %collective-permute-start.6 = (bf16[1024,256]{1,0:T(8,128)(2,1)S(1)}, bf16[1024,256]{1,0:T(8,128)(2,1)S(1)}, u32[]{:S(2)}, u32[]{:S(2)}) collective-permute-start(bf16[1024,256]{1,0:T(8,128)(2,1)S(1)} %collective-permute-done.2.refs_0_.refs_6_), channel_id=1, source_target_pairs={{0,4},{4,0},{8,12},{12,8},{16,20},{20,16},{24,28},{28,24},{1,5},{5... | collective-permute-start | bytes 1572872 | tf_op jit(solution)/shard_map/ppermute | solution.py:690
  44.2 2.7 %collective-permute-start.8 = (bf16[1024,256]{1,0:T(8,128)(2,1)S(1)}, bf16[1024,256]{1,0:T(8,128)(2,1)S(1)}, u32[]{:S(2)}, u32[]{:S(2)}) collective-permute-start(bf16[1024,256]{1,0:T(8,128)(2,1)S(1)} %collective-permute-done.7.refs_1_.refs_7_), channel_id=1, source_target_pairs={{0,4},{4,0},{8,12},{12,8},{16,20},{20,16},{24,28},{28,24},{1,5},{5... | collective-permute-start | bytes 1572872 | tf_op jit(solution)/shard_map/ppermute | solution.py:690
  45.8 2.6 %copy-start.1 = (bf16[768,1024]{1,0:T(8,128)(2,1)S(1)}, bf16[768,1024]{1,0:T(8,128)(2,1)}, u32[]{:S(2)}) copy-start(bf16[768,1024]{1,0:T(8,128)(2,1)} %q_ref.5) | copy-start | bytes 4718596
  45.9 11.3 %copy-start.3 = (f32[2,384,128]{2,1,0:T(8,128)S(1)}, f32[2,384,128]{2,1,0:T(8,128)}, u32[]{:S(2)}) copy-start(f32[2,384,128]{2,1,0:T(8,128)} %constant.8.clone.table_hbm.refs_3_.table_ref) | copy-start | bytes 1179652
  52.7 8.5 %collective-permute-start.11 = (f32[8,128]{1,0:T(8,128)S(1)}, f32[8,128]{1,0:T(8,128)S(1)}, u32[]{:S(2)}, u32[]{:S(2)}) collective-permute-start(f32[8,128]{1,0:T(8,128)S(1)} %get-tuple-element.69), channel_id=1, source_target_pairs={{0,3},{1,2},{2,1},{3,0},{4,7},{5,6},{6,5},{7,4},{8,11},{9,10},{10,... | collective-permute-start | bytes 12296 | tf_op jit(solution)/shard_map/ppermute | solution.py:690
  56.3 4.8 %collective-permute-start.10 = (f32[8,128]{1,0:T(8,128)S(1)}, f32[8,128]{1,0:T(8,128)S(1)}, u32[]{:S(2)}, u32[]{:S(2)}) collective-permute-start(f32[8,128]{1,0:T(8,128)S(1)} %get-tuple-element.69), channel_id=1, source_target_pairs={{0,2},{1,3},{2,0},{3,1},{4,6},{5,7},{6,4},{7,5},{8,10},{9,11},{10,... | collective-permute-start | bytes 12296 | tf_op jit(solution)/shard_map/ppermute | solution.py:690
  56.3 4.8 %collective-permute-start.9 = (f32[8,128]{1,0:T(8,128)S(1)}, f32[8,128]{1,0:T(8,128)S(1)}, u32[]{:S(2)}, u32[]{:S(2)}) collective-permute-start(f32[8,128]{1,0:T(8,128)S(1)} %get-tuple-element.69), channel_id=1, source_target_pairs={{0,1},{1,0},{2,3},{3,2},{4,5},{5,4},{6,7},{7,6},{8,9},{9,8},{10,11... | collective-permute-start | bytes 12296 | tf_op jit(solution)/shard_map/ppermute | solution.py:690
  62.2 3.9 %collective-permute-start.17 = (bf16[2,256,1024]{2,1,0:T(8,128)(2,1)S(1)}, bf16[2,256,1024]{2,1,0:T(8,128)(2,1)S(1)}, u32[]{:S(2)}, u32[]{:S(2)}) collective-permute-start(bf16[2,256,1024]{2,1,0:T(8,128)(2,1)S(1)} %gradient_block.2), channel_id=1, source_target_pairs={{0,4},{4,0},{8,12},{12,8},{16,20},{20,16},{24,28},{28,24},{1,5},{5... | collective-permute-start | bytes 3145736 | tf_op jit(solution)/shard_map/ppermute | solution.py:690
  62.3 3.2 %collective-permute-start.12 = (f32[8,128]{1,0:T(8,128)S(1)}, f32[8,128]{1,0:T(8,128)S(1)}, u32[]{:S(2)}, u32[]{:S(2)}) collective-permute-start(f32[8,128]{1,0:T(8,128)S(1)} %add_add_fusion.1.outs_0_.mine_ref.margin_ref), channel_id=1, source_target_pairs={{0,4},{4,0},{8,12},{12,8},{16,20},{20,16},{24,28},{28,24},{1,5},{5... | collective-permute-start | bytes 12296 | tf_op jit(solution)/shard_map/ppermute | solution.py:690
  65.5 2.8 %collective-permute-start.13 = (bf16[2,256,1024]{2,1,0:T(8,128)(2,1)S(1)}, bf16[2,256,1024]{2,1,0:T(8,128)(2,1)S(1)}, u32[]{:S(2)}, u32[]{:S(2)}) collective-permute-start(bf16[2,256,1024]{2,1,0:T(8,128)(2,1)S(1)} %get-tuple-element.77), channel_id=1, source_target_pairs={{0,4},{4,0},{8,12},{12,8},{16,20},{20,16},{24,28},{28,24},{1,5},{5... | collective-permute-start | bytes 3145736 | tf_op jit(solution)/shard_map/ppermute | solution.py:690
  65.6 4.1 %collective-permute-start.14 = (bf16[2,256,1024]{2,1,0:T(8,128)(2,1)S(1)}, bf16[2,256,1024]{2,1,0:T(8,128)(2,1)S(1)}, u32[]{:S(2)}, u32[]{:S(2)}) collective-permute-start(bf16[2,256,1024]{2,1,0:T(8,128)(2,1)S(1)} %get-tuple-element.78), channel_id=1, source_target_pairs={{0,4},{4,0},{8,12},{12,8},{16,20},{20,16},{24,28},{28,24},{1,5},{5... | collective-permute-start | bytes 3145736 | tf_op jit(solution)/shard_map/ppermute | solution.py:690
  66.0 5.1 %collective-permute-start.15 = (bf16[2,256,1024]{2,1,0:T(8,128)(2,1)S(1)}, bf16[2,256,1024]{2,1,0:T(8,128)(2,1)S(1)}, u32[]{:S(2)}, u32[]{:S(2)}) collective-permute-start(bf16[2,256,1024]{2,1,0:T(8,128)(2,1)S(1)} %get-tuple-element.79), channel_id=1, source_target_pairs={{0,4},{4,0},{8,12},{12,8},{16,20},{20,16},{24,28},{28,24},{1,5},{5... | collective-permute-start | bytes 3145736 | tf_op jit(solution)/shard_map/ppermute | solution.py:690
  67.2 14.8 %collective-permute-start.21 = (bf16[256,1024]{1,0:T(8,128)(2,1)S(1)}, bf16[256,1024]{1,0:T(8,128)(2,1)S(1)}, u32[]{:S(2)}, u32[]{:S(2)}) collective-permute-start(bf16[256,1024]{1,0:T(8,128)(2,1)S(1)} %get-tuple-element.87), channel_id=1, source_target_pairs={{0,8},{4,12},{8,0},{12,4},{16,24},{20,28},{24,16},{28,20},{1,9},{5... | collective-permute-start | bytes 1572872 | tf_op jit(solution)/shard_map/ppermute | solution.py:690
  67.8 14.9 %collective-permute-start.18 = (bf16[256,1024]{1,0:T(8,128)(2,1)S(1)}, bf16[256,1024]{1,0:T(8,128)(2,1)S(1)}, u32[]{:S(2)}, u32[]{:S(2)}) collective-permute-start(bf16[256,1024]{1,0:T(8,128)(2,1)S(1)} %get-tuple-element.83), channel_id=1, source_target_pairs={{0,16},{4,20},{8,24},{12,28},{16,0},{20,4},{24,8},{28,12},{1,17},{... | collective-permute-start | bytes 1572872 | tf_op jit(solution)/shard_map/ppermute | solution.py:690
  74.7 19.1 %collective-permute-start.16 = (bf16[256,1024]{1,0:T(8,128)(2,1)S(1)}, bf16[256,1024]{1,0:T(8,128)(2,1)S(1)}, u32[]{:S(2)}, u32[]{:S(2)}) collective-permute-start(bf16[256,1024]{1,0:T(8,128)(2,1)S(1)} %get-tuple-element.81), channel_id=1, source_target_pairs={{0,16},{4,20},{8,24},{12,28},{16,0},{20,4},{24,8},{28,12},{1,17},{... | collective-permute-start | bytes 1572872 | tf_op jit(solution)/shard_map/ppermute | solution.py:690
  75.3 20.0 %collective-permute-start.20 = (bf16[256,1024]{1,0:T(8,128)(2,1)S(1)}, bf16[256,1024]{1,0:T(8,128)(2,1)S(1)}, u32[]{:S(2)}, u32[]{:S(2)}) collective-permute-start(bf16[256,1024]{1,0:T(8,128)(2,1)S(1)} %get-tuple-element.85), channel_id=1, source_target_pairs={{0,8},{4,12},{8,0},{12,4},{16,24},{20,28},{24,16},{28,20},{1,9},{5... | collective-permute-start | bytes 1572872 | tf_op jit(solution)/shard_map/ppermute | solution.py:690
  82.2 17.3 %collective-permute-start.22 = (bf16[256,512]{1,0:T(8,128)(2,1)S(1)}, bf16[256,512]{1,0:T(8,128)(2,1)S(1)}, u32[]{:S(2)}, u32[]{:S(2)}) collective-permute-start(bf16[256,512]{1,0:T(8,128)(2,1)S(1)} %get-tuple-element.110), channel_id=1, source_target_pairs={{0,16},{4,20},{8,24},{12,28},{16,0},{20,4},{24,8},{28,12},{1,17},{... | collective-permute-start | bytes 786440 | tf_op jit(solution)/shard_map/ppermute | solution.py:690
  82.9 16.6 %collective-permute-start.19 = (bf16[256,512]{1,0:T(8,128)(2,1)S(1)}, bf16[256,512]{1,0:T(8,128)(2,1)S(1)}, u32[]{:S(2)}, u32[]{:S(2)}) collective-permute-start(bf16[256,512]{1,0:T(8,128)(2,1)S(1)} %get-tuple-element.112), channel_id=1, source_target_pairs={{0,8},{4,12},{8,0},{12,4},{16,24},{20,28},{24,16},{28,20},{1,9},{5... | collective-permute-start | bytes 786440 | tf_op jit(solution)/shard_map/ppermute | solution.py:690
  84.3 20.8 %collective-permute-start.24 = (bf16[256,512]{1,0:T(8,128)(2,1)S(1)}, bf16[256,512]{1,0:T(8,128)(2,1)S(1)}, u32[]{:S(2)}, u32[]{:S(2)}) collective-permute-start(bf16[256,512]{1,0:T(8,128)(2,1)S(1)} %get-tuple-element.109), channel_id=1, source_target_pairs={{0,16},{4,20},{8,24},{12,28},{16,0},{20,4},{24,8},{28,12},{1,17},{... | collective-permute-start | bytes 786440 | tf_op jit(solution)/shard_map/ppermute | solution.py:690
  93.8 11.2 %collective-permute-start.23 = (bf16[256,512]{1,0:T(8,128)(2,1)S(1)}, bf16[256,512]{1,0:T(8,128)(2,1)S(1)}, u32[]{:S(2)}, u32[]{:S(2)}) collective-permute-start(bf16[256,512]{1,0:T(8,128)(2,1)S(1)} %get-tuple-element.111), channel_id=1, source_target_pairs={{0,8},{4,12},{8,0},{12,4},{16,24},{20,28},{24,16},{28,20},{1,9},{5... | collective-permute-start | bytes 786440 | tf_op jit(solution)/shard_map/ppermute | solution.py:690
  99.8 17.0 %collective-permute-start.29 = (bf16[2,512,256]{2,1,0:T(8,128)(2,1)S(1)}, bf16[2,512,256]{2,1,0:T(8,128)(2,1)S(1)}, u32[]{:S(2)}, u32[]{:S(2)}) collective-permute-start(bf16[2,512,256]{2,1,0:T(8,128)(2,1)S(1)} %get-tuple-element.90.refs_4_.refs_0_), channel_id=1, source_target_pairs={{0,16},{4,20},{8,24},{12,28},{16,0},{20,4},{24,8},{28,12},{1,17},{... | collective-permute-start | bytes 1572872 | tf_op jit(solution)/shard_map/ppermute | solution.py:690
  100.2 16.5 %collective-permute-start.28 = (bf16[2,512,256]{2,1,0:T(8,128)(2,1)S(1)}, bf16[2,512,256]{2,1,0:T(8,128)(2,1)S(1)}, u32[]{:S(2)}, u32[]{:S(2)}) collective-permute-start(bf16[2,512,256]{2,1,0:T(8,128)(2,1)S(1)} %get-tuple-element.90.refs_4_.refs_0_), channel_id=1, source_target_pairs={{0,8},{4,12},{8,0},{12,4},{16,24},{20,28},{24,16},{28,20},{1,9},{5... | collective-permute-start | bytes 1572872 | tf_op jit(solution)/shard_map/ppermute | solution.py:690
  105.4 21.5 %collective-permute-start.34 = (bf16[2,512,256]{2,1,0:T(8,128)(2,1)S(1)}, bf16[2,512,256]{2,1,0:T(8,128)(2,1)S(1)}, u32[]{:S(2)}, u32[]{:S(2)}) collective-permute-start(bf16[2,512,256]{2,1,0:T(8,128)(2,1)S(1)} %get-tuple-element.92.refs_5_.refs_1_), channel_id=1, source_target_pairs={{0,16},{4,20},{8,24},{12,28},{16,0},{20,4},{24,8},{28,12},{1,17},{... | collective-permute-start | bytes 1572872 | tf_op jit(solution)/shard_map/ppermute | solution.py:690
  105.9 21.1 %collective-permute-start.33 = (bf16[2,512,256]{2,1,0:T(8,128)(2,1)S(1)}, bf16[2,512,256]{2,1,0:T(8,128)(2,1)S(1)}, u32[]{:S(2)}, u32[]{:S(2)}) collective-permute-start(bf16[2,512,256]{2,1,0:T(8,128)(2,1)S(1)} %get-tuple-element.92.refs_5_.refs_1_), channel_id=1, source_target_pairs={{0,8},{4,12},{8,0},{12,4},{16,24},{20,28},{24,16},{28,20},{1,9},{5... | collective-permute-start | bytes 1572872 | tf_op jit(solution)/shard_map/ppermute | solution.py:690
  107.5 3.6 %collective-permute-start.25 = (f32[8,128]{1,0:T(8,128)S(1)}, f32[8,128]{1,0:T(8,128)S(1)}, u32[]{:S(2)}, u32[]{:S(2)}) collective-permute-start(f32[8,128]{1,0:T(8,128)S(1)} %add.49), channel_id=1, source_target_pairs={{0,1},{1,0},{2,3},{3,2},{4,5},{5,4},{6,7},{7,6},{8,9},{9,8},{10,11... | collective-permute-start | bytes 12296 | tf_op jit(solution)/shard_map/ppermute | solution.py:690
  111.1 4.5 %collective-permute-start.26 = (f32[8,128]{1,0:T(8,128)S(1)}, f32[8,128]{1,0:T(8,128)S(1)}, u32[]{:S(2)}, u32[]{:S(2)}) collective-permute-start(f32[8,128]{1,0:T(8,128)S(1)} %add.50), channel_id=1, source_target_pairs={{0,2},{1,3},{2,0},{3,1},{4,6},{5,7},{6,4},{7,5},{8,10},{9,11},{10,... | collective-permute-start | bytes 12296 | tf_op jit(solution)/shard_map/ppermute | solution.py:690
  115.6 1.2 collective-permute-start.27
  117.4 9.3 %collective-permute-start.32 = (f32[8,128]{1,0:T(8,128)S(1)}, f32[8,128]{1,0:T(8,128)S(1)}, u32[]{:S(2)}, u32[]{:S(2)}) collective-permute-start(f32[8,128]{1,0:T(8,128)S(1)} %get-tuple-element.91.refs_11_), channel_id=1, source_target_pairs={{0,24},{4,28},{8,16},{12,20},{16,8},{20,12},{24,0},{28,4},{1,25},{... | collective-permute-start | bytes 12296 | tf_op jit(solution)/shard_map/ppermute | solution.py:690
  118.9 8.0 %collective-permute-start.31 = (f32[8,128]{1,0:T(8,128)S(1)}, f32[8,128]{1,0:T(8,128)S(1)}, u32[]{:S(2)}, u32[]{:S(2)}) collective-permute-start(f32[8,128]{1,0:T(8,128)S(1)} %get-tuple-element.91.refs_11_), channel_id=1, source_target_pairs={{0,16},{4,20},{8,24},{12,28},{16,0},{20,4},{24,8},{28,12},{1,17},{... | collective-permute-start | bytes 12296 | tf_op jit(solution)/shard_map/ppermute | solution.py:690
  119.9 7.1 %collective-permute-start.30 = (f32[8,128]{1,0:T(8,128)S(1)}, f32[8,128]{1,0:T(8,128)S(1)}, u32[]{:S(2)}, u32[]{:S(2)}) collective-permute-start(f32[8,128]{1,0:T(8,128)S(1)} %get-tuple-element.91.refs_11_), channel_id=1, source_target_pairs={{0,8},{4,12},{8,0},{12,4},{16,24},{20,28},{24,16},{28,20},{1,9},{5... | collective-permute-start | bytes 12296 | tf_op jit(solution)/shard_map/ppermute | solution.py:690
  127.4 2.7 %collective-permute-start.35 = (bf16[2,1024,256]{2,1,0:T(8,128)(2,1)S(1)}, bf16[2,1024,256]{2,1,0:T(8,128)(2,1)S(1)}, u32[]{:S(2)}, u32[]{:S(2)}) collective-permute-start(bf16[2,1024,256]{2,1,0:T(8,128)(2,1)S(1)} %get-tuple-element.94), channel_id=1, source_target_pairs={{0,4},{4,0},{8,12},{12,8},{16,20},{20,16},{24,28},{28,24},{1,5},{5... | collective-permute-start | bytes 3145736 | tf_op jit(solution)/shard_map/ppermute | solution.py:690
  127.5 5.8 %collective-permute-start.37 = (bf16[2,1024,256]{2,1,0:T(8,128)(2,1)S(1)}, bf16[2,1024,256]{2,1,0:T(8,128)(2,1)S(1)}, u32[]{:S(2)}, u32[]{:S(2)}) collective-permute-start(bf16[2,1024,256]{2,1,0:T(8,128)(2,1)S(1)} %get-tuple-element.98), channel_id=1, source_target_pairs={{0,4},{4,0},{8,12},{12,8},{16,20},{20,16},{24,28},{28,24},{1,5},{5... | collective-permute-start | bytes 3145736 | tf_op jit(solution)/shard_map/ppermute | solution.py:690
  128.0 5.3 %collective-permute-start.38 = (bf16[2,1024,256]{2,1,0:T(8,128)(2,1)S(1)}, bf16[2,1024,256]{2,1,0:T(8,128)(2,1)S(1)}, u32[]{:S(2)}, u32[]{:S(2)}) collective-permute-start(bf16[2,1024,256]{2,1,0:T(8,128)(2,1)S(1)} %get-tuple-element.99), channel_id=1, source_target_pairs={{0,4},{4,0},{8,12},{12,8},{16,20},{20,16},{24,28},{28,24},{1,5},{5... | collective-permute-start | bytes 3145736 | tf_op jit(solution)/shard_map/ppermute | solution.py:690
  128.0 14.3 %collective-permute-start.40 = (bf16[1024,256]{1,0:T(8,128)(2,1)S(1)}, bf16[1024,256]{1,0:T(8,128)(2,1)S(1)}, u32[]{:S(2)}, u32[]{:S(2)}) collective-permute-start(bf16[1024,256]{1,0:T(8,128)(2,1)S(1)} %get-tuple-element.103), channel_id=1, source_target_pairs={{0,8},{4,12},{8,0},{12,4},{16,24},{20,28},{24,16},{28,20},{1,9},{5... | collective-permute-start | bytes 1572872 | tf_op jit(solution)/shard_map/ppermute | solution.py:690
  129.5 14.0 %collective-permute-start.36 = (bf16[1024,256]{1,0:T(8,128)(2,1)S(1)}, bf16[1024,256]{1,0:T(8,128)(2,1)S(1)}, u32[]{:S(2)}, u32[]{:S(2)}) collective-permute-start(bf16[1024,256]{1,0:T(8,128)(2,1)S(1)} %get-tuple-element.97), channel_id=1, source_target_pairs={{0,16},{4,20},{8,24},{12,28},{16,0},{20,4},{24,8},{28,12},{1,17},{... | collective-permute-start | bytes 1572872 | tf_op jit(solution)/shard_map/ppermute | solution.py:690
  143.5 2.7 %collective-permute-start.39 = (bf16[1024,256]{1,0:T(8,128)(2,1)S(1)}, bf16[1024,256]{1,0:T(8,128)(2,1)S(1)}, u32[]{:S(2)}, u32[]{:S(2)}) collective-permute-start(bf16[1024,256]{1,0:T(8,128)(2,1)S(1)} %collective-permute-done.36.refs_0_), channel_id=1, source_target_pairs={{0,4},{4,0},{8,12},{12,8},{16,20},{20,16},{24,28},{28,24},{1,5},{5... | collective-permute-start | bytes 1572872 | tf_op jit(solution)/shard_map/ppermute | solution.py:690
  143.5 2.7 %collective-permute-start.41 = (bf16[1024,256]{1,0:T(8,128)(2,1)S(1)}, bf16[1024,256]{1,0:T(8,128)(2,1)S(1)}, u32[]{:S(2)}, u32[]{:S(2)}) collective-permute-start(bf16[1024,256]{1,0:T(8,128)(2,1)S(1)} %collective-permute-done.40.refs_1_), channel_id=1, source_target_pairs={{0,4},{4,0},{8,12},{12,8},{16,20},{20,16},{24,28},{28,24},{1,5},{5... | collective-permute-start | bytes 1572872 | tf_op jit(solution)/shard_map/ppermute | solution.py:690

commit v6 on v5

--- a/solution.py
+++ b/solution.py
@@ -235,7 +235,7 @@
     )(*args)
 
 
-FORWARD_HEADS = 1
+FORWARD_HEADS = 2
 BACKWARD_HEADS = 4
 
 
@@ -268,9 +268,9 @@
     def one(step, margin):
         seq, h, row, col, q_col = places(step, q_ref, k_ref)
         length = len_ref[seq]
-        score = jnp.zeros((1, count * TILE), jnp.float32)
-        j = lax.broadcasted_iota(jnp.int32, (TILE, count * TILE), 0)
-        i = lax.broadcasted_iota(jnp.int32, (TILE, count * TILE), 1) % TILE
+        score = jnp.zeros((1, TILE), jnp.float32)
+        j = lax.broadcasted_iota(jnp.int32, (TILE, TILE), 0)
+        i = lax.broadcasted_iota(jnp.int32, (TILE, TILE), 1)
         base = 0
         for r in range(LEN // TILE):
             n = (r + 1) * TILE
@@ -278,23 +278,26 @@
             for g in range(0, groups, count):
                 q = stacked(q_ref, row, q_col, r, g, count)
                 ro = live_readout(ro_ref, row, q_col, r, g, count, length)
-                s = dot(k_ref[keys], q, NT)
-                dp = dot(v_ref[keys], ro, NT)
-                s = [s[b * TILE : (b + 1) * TILE] for b in range(r + 1)]
-                s[r] = jnp.where(j <= i, s[r], -1e30)
-                top = functools.reduce(jnp.maximum, [jnp.max(x, axis=0, keepdims=True) for x in s])
-                e = [jnp.exp2((x - top) * (logit_scale * math.log2(math.e))) for x in s]
-                inverse = 1.0 / functools.reduce(jnp.add, [jnp.sum(x, axis=0, keepdims=True) for x in e])
-                cols = slice(g * TILE, (g + count) * TILE)
-                delta = jnp.zeros((1, count * TILE), jnp.float32)
-                for b in range(r + 1):
-                    p = (e[b] * inverse).astype(jnp.bfloat16)
+                logits = dot(k_ref[keys], q, NT)
+                gains = dot(v_ref[keys], ro, NT)
+                for c in range(count):
+                    own = slice(c * TILE, (c + 1) * TILE)
+                    cols = slice((g + c) * TILE, (g + c + 1) * TILE)
+                    s = [logits[b * TILE : (b + 1) * TILE, own] for b in range(r + 1)]
+                    s[r] = jnp.where(j <= i, s[r], -1e30)
+                    top = functools.reduce(jnp.maximum, [jnp.max(x, axis=0, keepdims=True) for x in s])
+                    e = [jnp.exp2((x - top) * (logit_scale * math.log2(math.e))) for x in s]
+                    inverse = 1.0 / functools.reduce(jnp.add, [jnp.sum(x, axis=0, keepdims=True) for x in e])
+                    delta = jnp.zeros((1, TILE), jnp.float32)
+                    for b in range(r + 1):
+                        p = (e[b] * inverse).astype(jnp.bfloat16)
+                        if keep:
+                            prob_ref[seq, h, base + b * TILE : base + (b + 1) * TILE, cols] = p
+                        gain = gains[b * TILE : (b + 1) * TILE, own]
+                        delta = delta + jnp.sum(p.astype(jnp.float32) * gain, axis=0, keepdims=True)
                     if keep:
-                        prob_ref[seq, h, base + b * TILE : base + (b + 1) * TILE, cols] = p
-                    delta = delta + jnp.sum(p.astype(jnp.float32) * dp[b * TILE : (b + 1) * TILE], axis=0, keepdims=True)
-                if keep:
-                    delta_ref[seq, h, r : r + 1, cols] = delta
-                score = score + delta
+                        delta_ref[seq, h, r : r + 1, cols] = delta
+                    score = score + delta
             base += n
         side = jnp.where(seq % 2 == 0, 1.0, -1.0) * (dpo_beta / math.sqrt(QH * HD))
         return margin + jnp.sum(score, axis=1, keepdims=True) * side
@@ -347,7 +350,12 @@
                 cols = slice(g * TILE, (g + count) * TILE)
                 p = prob_ref[seq, h, base : base + n, cols]
                 dp = dot(v_ref[keys], ro, NT)
-                ds = (p.astype(jnp.float32) * (dp - delta_ref[seq, h, r : r + 1, cols])).astype(jnp.bfloat16)
+                ds = []
+                for c in range(count):
+                    own = slice(c * TILE, (c + 1) * TILE)
+                    delta = delta_ref[seq, h, r : r + 1, (g + c) * TILE : (g + c + 1) * TILE]
+                    ds.append((p[:, own].astype(jnp.float32) * (dp[:, own] - delta)).astype(jnp.bfloat16))
+                ds = jnp.concatenate(ds, axis=1)
                 tk = dot(ds, q, NN)
                 tv = dot(p, ro, NN)
                 for b in range(r + 1):

time: 149 us -> 149 us (level)
  no operation moved by 1% of the time
where the time goes in v6:
time: 149 us
  Pallas kernels  65.6 us (44%)
  waiting for transfers between devices  48 us (32%)
  starting transfers between devices  33.6 us (23%)
    ppermute x42, waiting for transfers between devices, swap(): return lax.ppermute(x, axis, [(i, i ^ bit) for i in range(size)])  48 us
    ppermute x42, starting transfers between devices, swap(): return lax.ppermute(x, axis, [(i, i ^ bit) for i in range(size)])  33.6 us
    pallas_call x1, Pallas kernels, norm_project(): pl.pallas_call(norm_project_kernel, in_specs=[SMEM, HBM, HBM, HBM], out_s...  17.8 us
    pallas_call x4, Pallas kernels, blend(): pl.pallas_call(functools.partial(blend_kernel, tuple(masks), first, offse...  12.3 us
    pallas_call x4, Pallas kernels, project(): pl.pallas_call(functools.partial(project_kernel, tuple(masks), first, las...  8.81 us
    pallas_call x2, Pallas kernels, attend(): pl.pallas_call(functools.partial(attend_kernel, keep), in_specs=[SMEM] +...  8.66 us
    pallas_call x4, Pallas kernels, gradient_blocks(): pl.pallas_call(functools.partial(kernel, tuple(masks)), in_specs=in_specs...  8.29 us
    pallas_call x1, Pallas kernels, attend_back(): pl.pallas_call(attend_back_kernel, in_specs=[SMEM] + [VMEM] * 6, out_spec...  4.02 us
  transfers between devices with their start and end apart: 42, of which 19 were waited for; matrix products, arithmetic and copies ran while one was open for 0% of the time, Pallas kernels for 38%

profile of v6, /device:TPU:0, one launch (start us, length us, event | category | flops | bytes accessed | tf_op | source)
XLA Modules:
  0.0 148.7 jit_solution(7181344868576637496)
XLA Ops:
  0.6 3.0 %collective-permute-start.1 = (bf16[2,1024,256]{2,1,0:T(8,128)(2,1)}, bf16[2,1024,256]{2,1,0:T(8,128)(2,1)S(1)}, u32[]{:S(2)}, u32[]{:S(2)}) collective-permute-start(bf16[2,1024,256]{2,1,0:T(8,128)(2,1)} %refs_0_.3), channel_id=1, source_target_pairs={{0,16},{4,20},{8,24},{12,28},{16,0},{20,4},{24,8},{28,12},{1,17},{... | collective-permute-start | bytes 3145736 | tf_op jit(solution)/shard_map/ppermute | solution.py:698
  3.7 1.5 %collective-permute-start = (bf16[2,1024,256]{2,1,0:T(8,128)(2,1)}, bf16[2,1024,256]{2,1,0:T(8,128)(2,1)S(1)}, u32[]{:S(2)}, u32[]{:S(2)}) collective-permute-start(bf16[2,1024,256]{2,1,0:T(8,128)(2,1)} %refs_0_.3), channel_id=1, source_target_pairs={{0,8},{4,12},{8,0},{12,4},{16,24},{20,28},{24,16},{28,20},{1,9},{5... | collective-permute-start | bytes 3145736 | tf_op jit(solution)/shard_map/ppermute | solution.py:698
  5.2 17.8 %norm_project.1 = (bf16[768,8192]{1,0:T(8,128)(2,1)S(1)}, bf16[768,256]{1,0:T(8,128)(2,1)S(1)}, bf16[768,256]{1,0:T(8,128)(2,1)S(1)}) custom-call(s32[1]{0:T(128)} %bitcast.idx_ref, bf16[768,8192]{1,0:T(8,128)(2,1)} %hidden_hbm.1, bf16[2,8192,256]{2,1,0:T(8,128)(2,1)} %refs_10_.1, f32[2,384,128]{2,1,0:T(8,128)} %constant.8.clone.table_hbm.refs_3_.table_ref), custom_call_target="tpu_custom_call" | custom-call | flops 1 | bytes 1 | tf_op jit(solution)/shard_map/norm_project/pallas_call | solution.py:133
  23.1 4.4 %attend.2.refs_2_.rest_0_ = f32[8,128]{1,0:T(8,128)S(1)} custom-call(s32[2]{0:T(128)S(1)} %copy-done.5, bf16[768,1024]{1,0:T(8,128)(2,1)S(1)} %copy-done.4, bf16[768,256]{1,0:T(8,128)(2,1)S(1)} %get-tuple-element.57.k_ref, bf16[768,256]{1,0:T(8,128)(2,1)S(1)} %get-tuple-element.58.v_ref, bf16[768,1024]{1,0:T(8,128)(2,1)S(1)} %copy-done), custom_call_target="tpu_custom_call" | custom-call | flops 1 | bytes 1 | tf_op jit(solution)/shard_map/attend/pallas_call | solution.py:322
  27.5 1.0 collective-permute-done.refs_0_.refs_2_
  28.5 0.5 collective-permute-start.4
  29.1 1.6 %collective-permute-start.7 = (bf16[1024,256]{1,0:T(8,128)(2,1)S(1)}, bf16[1024,256]{1,0:T(8,128)(2,1)S(1)}, u32[]{:S(2)}, u32[]{:S(2)}) collective-permute-start(bf16[1024,256]{1,0:T(8,128)(2,1)S(1)} %get-tuple-element.63), channel_id=1, source_target_pairs={{0,8},{4,12},{8,0},{12,4},{16,24},{20,28},{24,16},{28,20},{1,9},{5... | collective-permute-start | bytes 1572872 | tf_op jit(solution)/shard_map/ppermute | solution.py:698
  30.7 0.5 collective-permute-start.2
  31.2 2.0 %project.4.refs_4_ = f32[2,768,256]{2,1,0:T(8,128)S(1)} custom-call(s32[1]{0:T(128)} %bitcast.idx_ref, bf16[768,8192]{1,0:T(8,128)(2,1)S(1)} %get-tuple-element.56.x_ref, bf16[2,1024,256]{2,1,0:T(8,128)(2,1)S(1)} %copy-done.2, bf16[2,1024,256]{2,1,0:T(8,128)(2,1)S(1)} %collective-permute-done.5.refs_1_), custom_call_target="tpu_custom_call" | custom-call | flops 1 | bytes 1 | tf_op jit(solution)/shard_map/project/pallas_call | solution.py:226
  33.3 4.1 %project.5.refs_2_ = f32[2,768,256]{2,1,0:T(8,128)S(1)} custom-call(s32[1]{0:T(128)} %bitcast.idx_ref, bf16[768,8192]{1,0:T(8,128)(2,1)S(1)} %get-tuple-element.56.x_ref, bf16[2,1024,256]{2,1,0:T(8,128)(2,1)S(1)} %collective-permute-done.refs_0_.refs_2_, bf16[2,1024,256]{2,1,0:T(8,128)(2,1)S(1)} %collective-permute-done.3.refs_1_.refs_3_, ...), custom_call_target="tpu_custom_call" | custom-call | flops 1 | bytes 1 | tf_op jit(solution)/shard_map/project/pallas_call | solution.py:226
  37.4 5.7 %collective-permute-done.7.refs_1_.refs_7_ = bf16[1024,256]{1,0:T(8,128)(2,1)S(1)} collective-permute-done((bf16[1024,256]{1,0:T(8,128)(2,1)S(1)}, bf16[1024,256]{1,0:T(8,128)(2,1)S(1)}, u32[]{:S(2)}, u32[]{:S(2)}) %collective-permute-start.7) | collective-permute-done | bytes 524320 | tf_op jit(solution)/shard_map/ppermute | solution.py:698
  43.0 1.2 collective-permute-done.2.refs_0_.refs_6_
  44.2 0.5 collective-permute-start.8
  44.7 1.1 project.6.refs_2_
  46.1 0.7 collective-permute-done.8.refs_1_.refs_9_
  46.9 1.6 %project.7 = (bf16[768,256]{1,0:T(8,128)(2,1)S(1)}, bf16[768,256]{1,0:T(8,128)(2,1)S(1)}) custom-call(s32[1]{0:T(128)} %bitcast.idx_ref, bf16[768,8192]{1,0:T(8,128)(2,1)S(1)} %get-tuple-element.56.x_ref, bf16[1024,256]{1,0:T(8,128)(2,1)S(1)} %collective-permute-done.6.refs_0_.refs_8_, bf16[1024,256]{1,0:T(8,128)(2,1)S(1)} %collective-permute-done.8.refs_1_.refs_9_, ...), custom_call_target="tpu_custom_call" | custom-call | flops 1 | bytes 1 | tf_op jit(solution)/shard_map/project/pallas_call | solution.py:226
  48.5 4.2 %attend.3 = (f32[8,128]{1,0:T(8,128)S(1)}, bf16[2,2,768,512]{3,2,1,0:T(8,128)(2,1)S(1)}, f32[2,2,3,512]{3,2,1,0:T(4,128)S(1)}) custom-call(s32[2]{0:T(128)S(1)} %copy-done.5, bf16[768,1024]{1,0:T(8,128)(2,1)S(1)} %copy-done.1, bf16[768,256]{1,0:T(8,128)(2,1)S(1)} %get-tuple-element.66.k_ref, bf16[768,256]{1,0:T(8,128)(2,1)S(1)} %get-tuple-element.65.v_ref, ...), custom_call_target="tpu_custom_call" | custom-call | flops 1 | bytes 1 | tf_op jit(solution)/shard_map/attend/pallas_call | solution.py:322
  52.7 3.7 %collective-permute-start.11 = (f32[8,128]{1,0:T(8,128)S(1)}, f32[8,128]{1,0:T(8,128)S(1)}, u32[]{:S(2)}, u32[]{:S(2)}) collective-permute-start(f32[8,128]{1,0:T(8,128)S(1)} %get-tuple-element.69), channel_id=1, source_target_pairs={{0,3},{1,2},{2,1},{3,0},{4,7},{5,6},{6,5},{7,4},{8,11},{9,10},{10,... | collective-permute-start | bytes 12296 | tf_op jit(solution)/shard_map/ppermute | solution.py:698
  56.4 0.8 collective-permute-start.9
  57.2 4.0 %attend_back.1.cot_ref = bf16[2,256,768]{2,1,0:T(8,128)(2,1)S(1)} custom-call(s32[2]{0:T(128)S(1)} %copy-done.5, bf16[768,1024]{1,0:T(8,128)(2,1)S(1)} %copy-done.1, bf16[768,256]{1,0:T(8,128)(2,1)S(1)} %get-tuple-element.65.v_ref, bf16[768,1024]{1,0:T(8,128)(2,1)S(1)} %copy-done, bf16[2,2,768,512]{3,2,1,0:T(8,128)(2,1)S(1)} %get-tuple-element.67.prob_ref, ...), custom_call_target="tpu_custom_call" | custom-call | flops 1 | bytes 1 | tf_op jit(solution)/shard_map/attend_back/pallas_call | solution.py:381
  61.3 1.0 gradient_block.2
  62.4 0.5 collective-permute-start.12
  62.8 2.7 %gradient_block.3 = (bf16[2,256,1024]{2,1,0:T(8,128)(2,1)S(1)}, bf16[2,256,1024]{2,1,0:T(8,128)(2,1)S(1)}, bf16[2,256,1024]{2,1,0:T(8,128)(2,1)S(1)}) custom-call(s32[1]{0:T(128)} %bitcast.idx_ref, bf16[768,8192]{1,0:T(8,128)(2,1)S(1)} %get-tuple-element.56.x_ref, bf16[2,256,768]{2,1,0:T(8,128)(2,1)S(1)} %attend_back.1.cot_ref, ...), custom_call_target="tpu_custom_call" | custom-call | flops 1 | bytes 1 | tf_op jit(solution)/shard_map/gradient_block/pallas_call | solution.py:449
  65.7 0.4 collective-permute-start.14
  66.2 1.1 merged_block.3
  67.3 0.6 collective-permute-start.21
  68.3 1.5 collective-permute-done.14.refs_1_
  69.8 1.5 %collective-permute-done.15.refs_2_ = bf16[2,256,1024]{2,1,0:T(8,128)(2,1)S(1)} collective-permute-done((bf16[2,256,1024]{2,1,0:T(8,128)(2,1)S(1)}, bf16[2,256,1024]{2,1,0:T(8,128)(2,1)S(1)}, u32[]{:S(2)}, u32[]{:S(2)}) %collective-permute-start.15) | collective-permute-done | bytes 1048608 | tf_op jit(solution)/shard_map/ppermute | solution.py:698
  71.3 3.5 %merged_block.2 = (bf16[256,1024]{1,0:T(8,128)(2,1)S(1)}, bf16[256,1024]{1,0:T(8,128)(2,1)S(1)}, bf16[256,1024]{1,0:T(8,128)(2,1)S(1)}, bf16[256,1024]{1,0:T(8,1...) custom-call(s32[1]{0:T(128)} %bitcast.idx_ref, bf16[768,8192]{1,0:T(8,128)(2,1)S(1)} %get-tuple-element.56.x_ref, ...), custom_call_target="tpu_custom_call" | custom-call | flops 1 | bytes 1 | tf_op jit(solution)/shard_map/merged_block/pallas_call | solution.py:449
  74.8 0.6 collective-permute-start.16
  75.4 0.4 collective-permute-start.20
  75.8 6.3 %collective-permute-done.21 = bf16[256,1024]{1,0:T(8,128)(2,1)S(1)} collective-permute-done((bf16[256,1024]{1,0:T(8,128)(2,1)S(1)}, bf16[256,1024]{1,0:T(8,128)(2,1)S(1)}, u32[]{:S(2)}, u32[]{:S(2)}) %collective-permute-start.21) | collective-permute-done | bytes 524320 | tf_op jit(solution)/shard_map/ppermute | solution.py:698
  82.2 0.6 collective-permute-start.22
  83.0 1.4 collective-permute-start.19
  84.4 0.7 collective-permute-start.24
  85.1 8.8 %collective-permute-done.16.refs_1_ = bf16[256,1024]{1,0:T(8,128)(2,1)S(1)} collective-permute-done((bf16[256,1024]{1,0:T(8,128)(2,1)S(1)}, bf16[256,1024]{1,0:T(8,128)(2,1)S(1)}, u32[]{:S(2)}, u32[]{:S(2)}) %collective-permute-start.16) | collective-permute-done | bytes 524320 | tf_op jit(solution)/shard_map/ppermute | solution.py:698
  93.9 1.5 %collective-permute-start.23 = (bf16[256,512]{1,0:T(8,128)(2,1)S(1)}, bf16[256,512]{1,0:T(8,128)(2,1)S(1)}, u32[]{:S(2)}, u32[]{:S(2)}) collective-permute-start(bf16[256,512]{1,0:T(8,128)(2,1)S(1)} %get-tuple-element.111), channel_id=1, source_target_pairs={{0,8},{4,12},{8,0},{12,4},{16,24},{20,28},{24,16},{28,20},{1,9},{5... | collective-permute-start | bytes 786440 | tf_op jit(solution)/shard_map/ppermute | solution.py:698
  95.4 4.1 %collective-permute-done.22.refs_5_ = bf16[256,512]{1,0:T(8,128)(2,1)S(1)} collective-permute-done((bf16[256,512]{1,0:T(8,128)(2,1)S(1)}, bf16[256,512]{1,0:T(8,128)(2,1)S(1)}, u32[]{:S(2)}, u32[]{:S(2)}) %collective-permute-start.22) | collective-permute-done | bytes 262176 | tf_op jit(solution)/shard_map/ppermute | solution.py:698
  99.9 0.4 collective-permute-start.29
  100.3 1.6 %collective-permute-start.28 = (bf16[2,512,256]{2,1,0:T(8,128)(2,1)S(1)}, bf16[2,512,256]{2,1,0:T(8,128)(2,1)S(1)}, u32[]{:S(2)}, u32[]{:S(2)}) collective-permute-start(bf16[2,512,256]{2,1,0:T(8,128)(2,1)S(1)} %get-tuple-element.90.refs_4_.refs_0_), channel_id=1, source_target_pairs={{0,8},{4,12},{8,0},{12,4},{16,24},{20,28},{24,16},{28,20},{1,9},{5... | collective-permute-start | bytes 1572872 | tf_op jit(solution)/shard_map/ppermute | solution.py:698
  101.9 3.2 %collective-permute-done.24.refs_5_ = bf16[256,512]{1,0:T(8,128)(2,1)S(1)} collective-permute-done((bf16[256,512]{1,0:T(8,128)(2,1)S(1)}, bf16[256,512]{1,0:T(8,128)(2,1)S(1)}, u32[]{:S(2)}, u32[]{:S(2)}) %collective-permute-start.24) | collective-permute-done | bytes 262176 | tf_op jit(solution)/shard_map/ppermute | solution.py:698
  105.5 0.4 collective-permute-start.34
  105.9 1.6 %collective-permute-start.33 = (bf16[2,512,256]{2,1,0:T(8,128)(2,1)S(1)}, bf16[2,512,256]{2,1,0:T(8,128)(2,1)S(1)}, u32[]{:S(2)}, u32[]{:S(2)}) collective-permute-start(bf16[2,512,256]{2,1,0:T(8,128)(2,1)S(1)} %get-tuple-element.92.refs_5_.refs_1_), channel_id=1, source_target_pairs={{0,8},{4,12},{8,0},{12,4},{16,24},{20,28},{24,16},{28,20},{1,9},{5... | collective-permute-start | bytes 1572872 | tf_op jit(solution)/shard_map/ppermute | solution.py:698
  107.6 1.2 collective-permute-start.25
  108.8 2.4 %collective-permute-done.25 = f32[8,128]{1,0:T(8,128)S(1)} collective-permute-done((f32[8,128]{1,0:T(8,128)S(1)}, f32[8,128]{1,0:T(8,128)S(1)}, u32[]{:S(2)}, u32[]{:S(2)}) %collective-permute-start.25) | collective-permute-done | bytes 4128 | tf_op jit(solution)/shard_map/ppermute | solution.py:698
  111.2 2.1 %collective-permute-start.26 = (f32[8,128]{1,0:T(8,128)S(1)}, f32[8,128]{1,0:T(8,128)S(1)}, u32[]{:S(2)}, u32[]{:S(2)}) collective-permute-start(f32[8,128]{1,0:T(8,128)S(1)} %add.50), channel_id=1, source_target_pairs={{0,2},{1,3},{2,0},{3,1},{4,6},{5,7},{6,4},{7,5},{8,10},{9,11},{10,... | collective-permute-start | bytes 12296 | tf_op jit(solution)/shard_map/ppermute | solution.py:698
  113.3 2.4 %collective-permute-done.26 = f32[8,128]{1,0:T(8,128)S(1)} collective-permute-done((f32[8,128]{1,0:T(8,128)S(1)}, f32[8,128]{1,0:T(8,128)S(1)}, u32[]{:S(2)}, u32[]{:S(2)}) %collective-permute-start.26) | collective-permute-done | bytes 4128 | tf_op jit(solution)/shard_map/ppermute | solution.py:698
  115.7 1.2 collective-permute-done.27
  116.9 0.6 gate.1
  117.4 1.6 %collective-permute-start.32 = (f32[8,128]{1,0:T(8,128)S(1)}, f32[8,128]{1,0:T(8,128)S(1)}, u32[]{:S(2)}, u32[]{:S(2)}) collective-permute-start(f32[8,128]{1,0:T(8,128)S(1)} %get-tuple-element.91.refs_11_), channel_id=1, source_target_pairs={{0,24},{4,28},{8,16},{12,20},{16,8},{20,12},{24,0},{28,4},{1,25},{... | collective-permute-start | bytes 12296 | tf_op jit(solution)/shard_map/ppermute | solution.py:698
  119.0 1.0 collective-permute-start.31
  120.0 1.0 collective-permute-start.30
  121.0 3.8 %fetch.1 = (bf16[8,2,1024,256]{3,2,1,0:T(8,128)(2,1)S(1)}, bf16[8,2,1024,256]{3,2,1,0:T(8,128)(2,1)S(1)}) custom-call(s32[1]{0:T(128)} %bitcast.idx_ref, bf16[2,1024,256]{2,1,0:T(8,128)(2,1)S(1)} %copy-done.2, bf16[2,1024,256]{2,1,0:T(8,128)(2,1)S(1)} %collective-permute-done.5.refs_1_, bf16[2,1024,256]{2,1,0:T(8,128)(2,1)S(1)} %collective-permute-done.refs_0_.refs_2_, ...), custom_call_target="tpu_custom_call" | custom-call | flops 1 | bytes 1 | tf_op jit(solution)/shard_map/fetch/pallas_call | solution.py:583
  124.8 2.0 %collective-permute-done.32 = f32[8,128]{1,0:T(8,128)S(1)} collective-permute-done((f32[8,128]{1,0:T(8,128)S(1)}, f32[8,128]{1,0:T(8,128)S(1)}, u32[]{:S(2)}, u32[]{:S(2)}) %collective-permute-start.32) | collective-permute-done | bytes 4128 | tf_op jit(solution)/shard_map/ppermute | solution.py:698
  127.5 0.5 collective-permute-start.37
  128.1 1.5 %collective-permute-start.40 = (bf16[1024,256]{1,0:T(8,128)(2,1)S(1)}, bf16[1024,256]{1,0:T(8,128)(2,1)S(1)}, u32[]{:S(2)}, u32[]{:S(2)}) collective-permute-start(bf16[1024,256]{1,0:T(8,128)(2,1)S(1)} %get-tuple-element.103), channel_id=1, source_target_pairs={{0,8},{4,12},{8,0},{12,4},{16,24},{20,28},{24,16},{28,20},{1,9},{5... | collective-permute-start | bytes 1572872 | tf_op jit(solution)/shard_map/ppermute | solution.py:698
  129.6 0.5 collective-permute-start.36
  130.2 3.2 %blend.4 = (bf16[2,8192,256]{2,1,0:T(8,128)(2,1)}, f32[8,128]{1,0:T(8,128)}, bf16[2,1024,256]{2,1,0:T(8,128)(2,1)}) custom-call(s32[1]{0:T(128)} %bitcast.idx_ref, f32[8,128]{1,0:T(8,128)S(1)} %add_add_fusion.refs_10_.square_ref, bf16[2,512,256]{2,1,0:T(8,128)(2,1)S(1)} %get-tuple-element.90.refs_4_.refs_0_, ...), custom_call_target="tpu_custom_call" | custom-call | flops 1 | bytes 1 | tf_op jit(solution)/shard_map/blend/pallas_call | solution.py:665
  133.4 4.8 %blend.5 = (bf16[2,8192,256]{2,1,0:T(8,128)(2,1)}, f32[8,128]{1,0:T(8,128)}) custom-call(s32[1]{0:T(128)} %bitcast.idx_ref, f32[8,128]{1,0:T(8,128)S(1)} %add_add_fusion.refs_10_.square_ref, bf16[2,512,256]{2,1,0:T(8,128)(2,1)S(1)} %collective-permute-done.28.refs_0_.refs_6_, ...), custom_call_target="tpu_custom_call", output_to_operand_aliasing={{0}: (10, {})} | custom-call | flops 1 | bytes 1 | tf_op jit(solution)/shard_map/blend/pallas_call | solution.py:665
  138.2 4.2 %collective-permute-done.40.refs_1_ = bf16[1024,256]{1,0:T(8,128)(2,1)S(1)} collective-permute-done((bf16[1024,256]{1,0:T(8,128)(2,1)S(1)}, bf16[1024,256]{1,0:T(8,128)(2,1)S(1)}, u32[]{:S(2)}, u32[]{:S(2)}) %collective-permute-start.40) | collective-permute-done | bytes 524320 | tf_op jit(solution)/shard_map/ppermute | solution.py:698
  142.4 1.2 collective-permute-done.36.refs_0_
  143.6 0.5 collective-permute-start.41
  144.1 2.2 %blend.6 = (bf16[2,8192,256]{2,1,0:T(8,128)(2,1)}, f32[8,128]{1,0:T(8,128)}) custom-call(s32[1]{0:T(128)} %bitcast.idx_ref, f32[8,128]{1,0:T(8,128)S(1)} %add_add_fusion.refs_10_.square_ref, bf16[1024,256]{1,0:T(8,128)(2,1)S(1)} %collective-permute-done.36.refs_0_, ...), custom_call_target="tpu_custom_call", output_to_operand_aliasing={{0}: (6, {})} | custom-call | flops 1 | bytes 1 | tf_op jit(solution)/shard_map/blend/pallas_call | solution.py:665
  146.3 2.2 %blend.7 = (bf16[2,8192,256]{2,1,0:T(8,128)(2,1)}, f32[8,128]{1,0:T(8,128)}) custom-call(s32[1]{0:T(128)} %bitcast.idx_ref, f32[8,128]{1,0:T(8,128)S(1)} %add_add_fusion.refs_10_.square_ref, bf16[1024,256]{1,0:T(8,128)(2,1)S(1)} %collective-permute-done.39.refs_0_, ...), custom_call_target="tpu_custom_call", output_to_operand_aliasing={{0}: (6, {})} | custom-call | flops 1 | bytes 1 | tf_op jit(solution)/shard_map/blend/pallas_call | solution.py:665
  (63 shorter events, 3.1 us)
Async XLA Ops:
  0.6 26.9 %collective-permute-start.1 = (bf16[2,1024,256]{2,1,0:T(8,128)(2,1)}, bf16[2,1024,256]{2,1,0:T(8,128)(2,1)S(1)}, u32[]{:S(2)}, u32[]{:S(2)}) collective-permute-start(bf16[2,1024,256]{2,1,0:T(8,128)(2,1)} %refs_0_.3), channel_id=1, source_target_pairs={{0,16},{4,20},{8,24},{12,28},{16,0},{20,4},{24,8},{28,12},{1,17},{... | collective-permute-start | bytes 3145736 | tf_op jit(solution)/shard_map/ppermute | solution.py:698
  3.7 24.8 %collective-permute-start = (bf16[2,1024,256]{2,1,0:T(8,128)(2,1)}, bf16[2,1024,256]{2,1,0:T(8,128)(2,1)S(1)}, u32[]{:S(2)}, u32[]{:S(2)}) collective-permute-start(bf16[2,1024,256]{2,1,0:T(8,128)(2,1)} %refs_0_.3), channel_id=1, source_target_pairs={{0,8},{4,12},{8,0},{12,4},{16,24},{20,28},{24,16},{28,20},{1,9},{5... | collective-permute-start | bytes 3145736 | tf_op jit(solution)/shard_map/ppermute | solution.py:698
  5.2 26.0 %collective-permute-start.5 = (bf16[2,1024,256]{2,1,0:T(8,128)(2,1)}, bf16[2,1024,256]{2,1,0:T(8,128)(2,1)S(1)}, u32[]{:S(2)}, u32[]{:S(2)}) collective-permute-start(bf16[2,1024,256]{2,1,0:T(8,128)(2,1)} %refs_0_.3), channel_id=1, source_target_pairs={{0,4},{4,0},{8,12},{12,8},{16,20},{20,16},{24,28},{28,24},{1,5},{5... | collective-permute-start | bytes 3145736 | tf_op jit(solution)/shard_map/ppermute | solution.py:698
  5.2 17.9 %copy-start = (bf16[768,1024]{1,0:T(8,128)(2,1)S(1)}, bf16[768,1024]{1,0:T(8,128)(2,1)}, u32[]{:S(2)}) copy-start(bf16[768,1024]{1,0:T(8,128)(2,1)} %ro_ref.5) | copy-start | bytes 4718596
  5.2 17.9 %copy-start.4 = (bf16[768,1024]{1,0:T(8,128)(2,1)S(1)}, bf16[768,1024]{1,0:T(8,128)(2,1)}, u32[]{:S(2)}) copy-start(bf16[768,1024]{1,0:T(8,128)(2,1)} %q_ref.3) | copy-start | bytes 4718596
  5.2 17.9 %copy-start.5 = (s32[2]{0:T(128)S(1)}, s32[2]{0:T(128)}, u32[]{:S(2)}) copy-start(s32[2]{0:T(128)} %len_ref.5) | copy-start | bytes 28
  5.2 26.0 %copy-start.2 = (bf16[2,1024,256]{2,1,0:T(8,128)(2,1)S(1)}, bf16[2,1024,256]{2,1,0:T(8,128)(2,1)}, u32[]{:S(2)}) copy-start(bf16[2,1024,256]{2,1,0:T(8,128)(2,1)} %refs_0_.3) | copy-start | bytes 3145732
  28.5 4.8 %collective-permute-start.3 = (bf16[2,1024,256]{2,1,0:T(8,128)(2,1)S(1)}, bf16[2,1024,256]{2,1,0:T(8,128)(2,1)S(1)}, u32[]{:S(2)}, u32[]{:S(2)}) collective-permute-start(bf16[2,1024,256]{2,1,0:T(8,128)(2,1)S(1)} %collective-permute-done.refs_0_.refs_2_), channel_id=1, source_target_pairs={{0,4},{4,0},{8,12},{12,8},{16,20},{20,16},{24,28},{28,24},{1,5},{5... | collective-permute-start | bytes 3145736 | tf_op jit(solution)/shard_map/ppermute | solution.py:698
  28.5 4.8 %collective-permute-start.4 = (bf16[2,1024,256]{2,1,0:T(8,128)(2,1)S(1)}, bf16[2,1024,256]{2,1,0:T(8,128)(2,1)S(1)}, u32[]{:S(2)}, u32[]{:S(2)}) collective-permute-start(bf16[2,1024,256]{2,1,0:T(8,128)(2,1)S(1)} %collective-permute-done.1.refs_1_.refs_2_.refs_4_), channel_id=1, source_target_pairs={{0,4},{4,0},{8,12},{12,8},{16,20},{20,16},{24,28},{28,24},{1,5},{5... | collective-permute-start | bytes 3145736 | tf_op jit(solution)/shard_map/ppermute | solution.py:698
  29.1 13.9 %collective-permute-start.7 = (bf16[1024,256]{1,0:T(8,128)(2,1)S(1)}, bf16[1024,256]{1,0:T(8,128)(2,1)S(1)}, u32[]{:S(2)}, u32[]{:S(2)}) collective-permute-start(bf16[1024,256]{1,0:T(8,128)(2,1)S(1)} %get-tuple-element.63), channel_id=1, source_target_pairs={{0,8},{4,12},{8,0},{12,4},{16,24},{20,28},{24,16},{28,20},{1,9},{5... | collective-permute-start | bytes 1572872 | tf_op jit(solution)/shard_map/ppermute | solution.py:698
  30.7 13.6 %collective-permute-start.2 = (bf16[1024,256]{1,0:T(8,128)(2,1)S(1)}, bf16[1024,256]{1,0:T(8,128)(2,1)S(1)}, u32[]{:S(2)}, u32[]{:S(2)}) collective-permute-start(bf16[1024,256]{1,0:T(8,128)(2,1)S(1)} %get-tuple-element.59), channel_id=1, source_target_pairs={{0,16},{4,20},{8,24},{12,28},{16,0},{20,4},{24,8},{28,12},{1,17},{... | collective-permute-start | bytes 1572872 | tf_op jit(solution)/shard_map/ppermute | solution.py:698
  44.2 1.9 %collective-permute-start.6 = (bf16[1024,256]{1,0:T(8,128)(2,1)S(1)}, bf16[1024,256]{1,0:T(8,128)(2,1)S(1)}, u32[]{:S(2)}, u32[]{:S(2)}) collective-permute-start(bf16[1024,256]{1,0:T(8,128)(2,1)S(1)} %collective-permute-done.2.refs_0_.refs_6_), channel_id=1, source_target_pairs={{0,4},{4,0},{8,12},{12,8},{16,20},{20,16},{24,28},{28,24},{1,5},{5... | collective-permute-start | bytes 1572872 | tf_op jit(solution)/shard_map/ppermute | solution.py:698
  44.2 2.7 %collective-permute-start.8 = (bf16[1024,256]{1,0:T(8,128)(2,1)S(1)}, bf16[1024,256]{1,0:T(8,128)(2,1)S(1)}, u32[]{:S(2)}, u32[]{:S(2)}) collective-permute-start(bf16[1024,256]{1,0:T(8,128)(2,1)S(1)} %collective-permute-done.7.refs_1_.refs_7_), channel_id=1, source_target_pairs={{0,4},{4,0},{8,12},{12,8},{16,20},{20,16},{24,28},{28,24},{1,5},{5... | collective-permute-start | bytes 1572872 | tf_op jit(solution)/shard_map/ppermute | solution.py:698
  45.8 2.6 %copy-start.1 = (bf16[768,1024]{1,0:T(8,128)(2,1)S(1)}, bf16[768,1024]{1,0:T(8,128)(2,1)}, u32[]{:S(2)}) copy-start(bf16[768,1024]{1,0:T(8,128)(2,1)} %q_ref.5) | copy-start | bytes 4718596
  45.9 11.3 %copy-start.3 = (f32[2,384,128]{2,1,0:T(8,128)S(1)}, f32[2,384,128]{2,1,0:T(8,128)}, u32[]{:S(2)}) copy-start(f32[2,384,128]{2,1,0:T(8,128)} %constant.8.clone.table_hbm.refs_3_.table_ref) | copy-start | bytes 1179652
  52.7 8.5 %collective-permute-start.11 = (f32[8,128]{1,0:T(8,128)S(1)}, f32[8,128]{1,0:T(8,128)S(1)}, u32[]{:S(2)}, u32[]{:S(2)}) collective-permute-start(f32[8,128]{1,0:T(8,128)S(1)} %get-tuple-element.69), channel_id=1, source_target_pairs={{0,3},{1,2},{2,1},{3,0},{4,7},{5,6},{6,5},{7,4},{8,11},{9,10},{10,... | collective-permute-start | bytes 12296 | tf_op jit(solution)/shard_map/ppermute | solution.py:698
  56.4 4.8 %collective-permute-start.10 = (f32[8,128]{1,0:T(8,128)S(1)}, f32[8,128]{1,0:T(8,128)S(1)}, u32[]{:S(2)}, u32[]{:S(2)}) collective-permute-start(f32[8,128]{1,0:T(8,128)S(1)} %get-tuple-element.69), channel_id=1, source_target_pairs={{0,2},{1,3},{2,0},{3,1},{4,6},{5,7},{6,4},{7,5},{8,10},{9,11},{10,... | collective-permute-start | bytes 12296 | tf_op jit(solution)/shard_map/ppermute | solution.py:698
  56.4 4.8 %collective-permute-start.9 = (f32[8,128]{1,0:T(8,128)S(1)}, f32[8,128]{1,0:T(8,128)S(1)}, u32[]{:S(2)}, u32[]{:S(2)}) collective-permute-start(f32[8,128]{1,0:T(8,128)S(1)} %get-tuple-element.69), channel_id=1, source_target_pairs={{0,1},{1,0},{2,3},{3,2},{4,5},{5,4},{6,7},{7,6},{8,9},{9,8},{10,11... | collective-permute-start | bytes 12296 | tf_op jit(solution)/shard_map/ppermute | solution.py:698
  62.3 3.9 %collective-permute-start.17 = (bf16[2,256,1024]{2,1,0:T(8,128)(2,1)S(1)}, bf16[2,256,1024]{2,1,0:T(8,128)(2,1)S(1)}, u32[]{:S(2)}, u32[]{:S(2)}) collective-permute-start(bf16[2,256,1024]{2,1,0:T(8,128)(2,1)S(1)} %gradient_block.2), channel_id=1, source_target_pairs={{0,4},{4,0},{8,12},{12,8},{16,20},{20,16},{24,28},{28,24},{1,5},{5... | collective-permute-start | bytes 3145736 | tf_op jit(solution)/shard_map/ppermute | solution.py:698
  62.4 3.2 %collective-permute-start.12 = (f32[8,128]{1,0:T(8,128)S(1)}, f32[8,128]{1,0:T(8,128)S(1)}, u32[]{:S(2)}, u32[]{:S(2)}) collective-permute-start(f32[8,128]{1,0:T(8,128)S(1)} %add_add_fusion.1.outs_0_.mine_ref.margin_ref), channel_id=1, source_target_pairs={{0,4},{4,0},{8,12},{12,8},{16,20},{20,16},{24,28},{28,24},{1,5},{5... | collective-permute-start | bytes 12296 | tf_op jit(solution)/shard_map/ppermute | solution.py:698
  65.5 2.7 %collective-permute-start.13 = (bf16[2,256,1024]{2,1,0:T(8,128)(2,1)S(1)}, bf16[2,256,1024]{2,1,0:T(8,128)(2,1)S(1)}, u32[]{:S(2)}, u32[]{:S(2)}) collective-permute-start(bf16[2,256,1024]{2,1,0:T(8,128)(2,1)S(1)} %get-tuple-element.77), channel_id=1, source_target_pairs={{0,4},{4,0},{8,12},{12,8},{16,20},{20,16},{24,28},{28,24},{1,5},{5... | collective-permute-start | bytes 3145736 | tf_op jit(solution)/shard_map/ppermute | solution.py:698
  65.7 4.1 %collective-permute-start.14 = (bf16[2,256,1024]{2,1,0:T(8,128)(2,1)S(1)}, bf16[2,256,1024]{2,1,0:T(8,128)(2,1)S(1)}, u32[]{:S(2)}, u32[]{:S(2)}) collective-permute-start(bf16[2,256,1024]{2,1,0:T(8,128)(2,1)S(1)} %get-tuple-element.78), channel_id=1, source_target_pairs={{0,4},{4,0},{8,12},{12,8},{16,20},{20,16},{24,28},{28,24},{1,5},{5... | collective-permute-start | bytes 3145736 | tf_op jit(solution)/shard_map/ppermute | solution.py:698
  66.1 5.1 %collective-permute-start.15 = (bf16[2,256,1024]{2,1,0:T(8,128)(2,1)S(1)}, bf16[2,256,1024]{2,1,0:T(8,128)(2,1)S(1)}, u32[]{:S(2)}, u32[]{:S(2)}) collective-permute-start(bf16[2,256,1024]{2,1,0:T(8,128)(2,1)S(1)} %get-tuple-element.79), channel_id=1, source_target_pairs={{0,4},{4,0},{8,12},{12,8},{16,20},{20,16},{24,28},{28,24},{1,5},{5... | collective-permute-start | bytes 3145736 | tf_op jit(solution)/shard_map/ppermute | solution.py:698
  67.3 14.8 %collective-permute-start.21 = (bf16[256,1024]{1,0:T(8,128)(2,1)S(1)}, bf16[256,1024]{1,0:T(8,128)(2,1)S(1)}, u32[]{:S(2)}, u32[]{:S(2)}) collective-permute-start(bf16[256,1024]{1,0:T(8,128)(2,1)S(1)} %get-tuple-element.87), channel_id=1, source_target_pairs={{0,8},{4,12},{8,0},{12,4},{16,24},{20,28},{24,16},{28,20},{1,9},{5... | collective-permute-start | bytes 1572872 | tf_op jit(solution)/shard_map/ppermute | solution.py:698
  67.9 14.9 %collective-permute-start.18 = (bf16[256,1024]{1,0:T(8,128)(2,1)S(1)}, bf16[256,1024]{1,0:T(8,128)(2,1)S(1)}, u32[]{:S(2)}, u32[]{:S(2)}) collective-permute-start(bf16[256,1024]{1,0:T(8,128)(2,1)S(1)} %get-tuple-element.83), channel_id=1, source_target_pairs={{0,16},{4,20},{8,24},{12,28},{16,0},{20,4},{24,8},{28,12},{1,17},{... | collective-permute-start | bytes 1572872 | tf_op jit(solution)/shard_map/ppermute | solution.py:698
  74.8 19.1 %collective-permute-start.16 = (bf16[256,1024]{1,0:T(8,128)(2,1)S(1)}, bf16[256,1024]{1,0:T(8,128)(2,1)S(1)}, u32[]{:S(2)}, u32[]{:S(2)}) collective-permute-start(bf16[256,1024]{1,0:T(8,128)(2,1)S(1)} %get-tuple-element.81), channel_id=1, source_target_pairs={{0,16},{4,20},{8,24},{12,28},{16,0},{20,4},{24,8},{28,12},{1,17},{... | collective-permute-start | bytes 1572872 | tf_op jit(solution)/shard_map/ppermute | solution.py:698
  75.4 20.1 %collective-permute-start.20 = (bf16[256,1024]{1,0:T(8,128)(2,1)S(1)}, bf16[256,1024]{1,0:T(8,128)(2,1)S(1)}, u32[]{:S(2)}, u32[]{:S(2)}) collective-permute-start(bf16[256,1024]{1,0:T(8,128)(2,1)S(1)} %get-tuple-element.85), channel_id=1, source_target_pairs={{0,8},{4,12},{8,0},{12,4},{16,24},{20,28},{24,16},{28,20},{1,9},{5... | collective-permute-start | bytes 1572872 | tf_op jit(solution)/shard_map/ppermute | solution.py:698
  82.2 17.3 %collective-permute-start.22 = (bf16[256,512]{1,0:T(8,128)(2,1)S(1)}, bf16[256,512]{1,0:T(8,128)(2,1)S(1)}, u32[]{:S(2)}, u32[]{:S(2)}) collective-permute-start(bf16[256,512]{1,0:T(8,128)(2,1)S(1)} %get-tuple-element.110), channel_id=1, source_target_pairs={{0,16},{4,20},{8,24},{12,28},{16,0},{20,4},{24,8},{28,12},{1,17},{... | collective-permute-start | bytes 786440 | tf_op jit(solution)/shard_map/ppermute | solution.py:698
  83.0 16.6 %collective-permute-start.19 = (bf16[256,512]{1,0:T(8,128)(2,1)S(1)}, bf16[256,512]{1,0:T(8,128)(2,1)S(1)}, u32[]{:S(2)}, u32[]{:S(2)}) collective-permute-start(bf16[256,512]{1,0:T(8,128)(2,1)S(1)} %get-tuple-element.112), channel_id=1, source_target_pairs={{0,8},{4,12},{8,0},{12,4},{16,24},{20,28},{24,16},{28,20},{1,9},{5... | collective-permute-start | bytes 786440 | tf_op jit(solution)/shard_map/ppermute | solution.py:698
  84.4 20.8 %collective-permute-start.24 = (bf16[256,512]{1,0:T(8,128)(2,1)S(1)}, bf16[256,512]{1,0:T(8,128)(2,1)S(1)}, u32[]{:S(2)}, u32[]{:S(2)}) collective-permute-start(bf16[256,512]{1,0:T(8,128)(2,1)S(1)} %get-tuple-element.109), channel_id=1, source_target_pairs={{0,16},{4,20},{8,24},{12,28},{16,0},{20,4},{24,8},{28,12},{1,17},{... | collective-permute-start | bytes 786440 | tf_op jit(solution)/shard_map/ppermute | solution.py:698
  93.9 11.2 %collective-permute-start.23 = (bf16[256,512]{1,0:T(8,128)(2,1)S(1)}, bf16[256,512]{1,0:T(8,128)(2,1)S(1)}, u32[]{:S(2)}, u32[]{:S(2)}) collective-permute-start(bf16[256,512]{1,0:T(8,128)(2,1)S(1)} %get-tuple-element.111), channel_id=1, source_target_pairs={{0,8},{4,12},{8,0},{12,4},{16,24},{20,28},{24,16},{28,20},{1,9},{5... | collective-permute-start | bytes 786440 | tf_op jit(solution)/shard_map/ppermute | solution.py:698
  99.9 17.0 %collective-permute-start.29 = (bf16[2,512,256]{2,1,0:T(8,128)(2,1)S(1)}, bf16[2,512,256]{2,1,0:T(8,128)(2,1)S(1)}, u32[]{:S(2)}, u32[]{:S(2)}) collective-permute-start(bf16[2,512,256]{2,1,0:T(8,128)(2,1)S(1)} %get-tuple-element.90.refs_4_.refs_0_), channel_id=1, source_target_pairs={{0,16},{4,20},{8,24},{12,28},{16,0},{20,4},{24,8},{28,12},{1,17},{... | collective-permute-start | bytes 1572872 | tf_op jit(solution)/shard_map/ppermute | solution.py:698
  100.3 16.5 %collective-permute-start.28 = (bf16[2,512,256]{2,1,0:T(8,128)(2,1)S(1)}, bf16[2,512,256]{2,1,0:T(8,128)(2,1)S(1)}, u32[]{:S(2)}, u32[]{:S(2)}) collective-permute-start(bf16[2,512,256]{2,1,0:T(8,128)(2,1)S(1)} %get-tuple-element.90.refs_4_.refs_0_), channel_id=1, source_target_pairs={{0,8},{4,12},{8,0},{12,4},{16,24},{20,28},{24,16},{28,20},{1,9},{5... | collective-permute-start | bytes 1572872 | tf_op jit(solution)/shard_map/ppermute | solution.py:698
  105.5 21.5 %collective-permute-start.34 = (bf16[2,512,256]{2,1,0:T(8,128)(2,1)S(1)}, bf16[2,512,256]{2,1,0:T(8,128)(2,1)S(1)}, u32[]{:S(2)}, u32[]{:S(2)}) collective-permute-start(bf16[2,512,256]{2,1,0:T(8,128)(2,1)S(1)} %get-tuple-element.92.refs_5_.refs_1_), channel_id=1, source_target_pairs={{0,16},{4,20},{8,24},{12,28},{16,0},{20,4},{24,8},{28,12},{1,17},{... | collective-permute-start | bytes 1572872 | tf_op jit(solution)/shard_map/ppermute | solution.py:698
  105.9 21.1 %collective-permute-start.33 = (bf16[2,512,256]{2,1,0:T(8,128)(2,1)S(1)}, bf16[2,512,256]{2,1,0:T(8,128)(2,1)S(1)}, u32[]{:S(2)}, u32[]{:S(2)}) collective-permute-start(bf16[2,512,256]{2,1,0:T(8,128)(2,1)S(1)} %get-tuple-element.92.refs_5_.refs_1_), channel_id=1, source_target_pairs={{0,8},{4,12},{8,0},{12,4},{16,24},{20,28},{24,16},{28,20},{1,9},{5... | collective-permute-start | bytes 1572872 | tf_op jit(solution)/shard_map/ppermute | solution.py:698
  107.6 3.6 %collective-permute-start.25 = (f32[8,128]{1,0:T(8,128)S(1)}, f32[8,128]{1,0:T(8,128)S(1)}, u32[]{:S(2)}, u32[]{:S(2)}) collective-permute-start(f32[8,128]{1,0:T(8,128)S(1)} %add.49), channel_id=1, source_target_pairs={{0,1},{1,0},{2,3},{3,2},{4,5},{5,4},{6,7},{7,6},{8,9},{9,8},{10,11... | collective-permute-start | bytes 12296 | tf_op jit(solution)/shard_map/ppermute | solution.py:698
  111.2 4.5 %collective-permute-start.26 = (f32[8,128]{1,0:T(8,128)S(1)}, f32[8,128]{1,0:T(8,128)S(1)}, u32[]{:S(2)}, u32[]{:S(2)}) collective-permute-start(f32[8,128]{1,0:T(8,128)S(1)} %add.50), channel_id=1, source_target_pairs={{0,2},{1,3},{2,0},{3,1},{4,6},{5,7},{6,4},{7,5},{8,10},{9,11},{10,... | collective-permute-start | bytes 12296 | tf_op jit(solution)/shard_map/ppermute | solution.py:698
  115.7 1.2 collective-permute-start.27
  117.4 9.3 %collective-permute-start.32 = (f32[8,128]{1,0:T(8,128)S(1)}, f32[8,128]{1,0:T(8,128)S(1)}, u32[]{:S(2)}, u32[]{:S(2)}) collective-permute-start(f32[8,128]{1,0:T(8,128)S(1)} %get-tuple-element.91.refs_11_), channel_id=1, source_target_pairs={{0,24},{4,28},{8,16},{12,20},{16,8},{20,12},{24,0},{28,4},{1,25},{... | collective-permute-start | bytes 12296 | tf_op jit(solution)/shard_map/ppermute | solution.py:698
  119.0 8.0 %collective-permute-start.31 = (f32[8,128]{1,0:T(8,128)S(1)}, f32[8,128]{1,0:T(8,128)S(1)}, u32[]{:S(2)}, u32[]{:S(2)}) collective-permute-start(f32[8,128]{1,0:T(8,128)S(1)} %get-tuple-element.91.refs_11_), channel_id=1, source_target_pairs={{0,16},{4,20},{8,24},{12,28},{16,0},{20,4},{24,8},{28,12},{1,17},{... | collective-permute-start | bytes 12296 | tf_op jit(solution)/shard_map/ppermute | solution.py:698
  120.0 7.1 %collective-permute-start.30 = (f32[8,128]{1,0:T(8,128)S(1)}, f32[8,128]{1,0:T(8,128)S(1)}, u32[]{:S(2)}, u32[]{:S(2)}) collective-permute-start(f32[8,128]{1,0:T(8,128)S(1)} %get-tuple-element.91.refs_11_), channel_id=1, source_target_pairs={{0,8},{4,12},{8,0},{12,4},{16,24},{20,28},{24,16},{28,20},{1,9},{5... | collective-permute-start | bytes 12296 | tf_op jit(solution)/shard_map/ppermute | solution.py:698
  127.5 2.7 %collective-permute-start.35 = (bf16[2,1024,256]{2,1,0:T(8,128)(2,1)S(1)}, bf16[2,1024,256]{2,1,0:T(8,128)(2,1)S(1)}, u32[]{:S(2)}, u32[]{:S(2)}) collective-permute-start(bf16[2,1024,256]{2,1,0:T(8,128)(2,1)S(1)} %get-tuple-element.94), channel_id=1, source_target_pairs={{0,4},{4,0},{8,12},{12,8},{16,20},{20,16},{24,28},{28,24},{1,5},{5... | collective-permute-start | bytes 3145736 | tf_op jit(solution)/shard_map/ppermute | solution.py:698
  127.5 5.8 %collective-permute-start.37 = (bf16[2,1024,256]{2,1,0:T(8,128)(2,1)S(1)}, bf16[2,1024,256]{2,1,0:T(8,128)(2,1)S(1)}, u32[]{:S(2)}, u32[]{:S(2)}) collective-permute-start(bf16[2,1024,256]{2,1,0:T(8,128)(2,1)S(1)} %get-tuple-element.98), channel_id=1, source_target_pairs={{0,4},{4,0},{8,12},{12,8},{16,20},{20,16},{24,28},{28,24},{1,5},{5... | collective-permute-start | bytes 3145736 | tf_op jit(solution)/shard_map/ppermute | solution.py:698
  128.0 5.3 %collective-permute-start.38 = (bf16[2,1024,256]{2,1,0:T(8,128)(2,1)S(1)}, bf16[2,1024,256]{2,1,0:T(8,128)(2,1)S(1)}, u32[]{:S(2)}, u32[]{:S(2)}) collective-permute-start(bf16[2,1024,256]{2,1,0:T(8,128)(2,1)S(1)} %get-tuple-element.99), channel_id=1, source_target_pairs={{0,4},{4,0},{8,12},{12,8},{16,20},{20,16},{24,28},{28,24},{1,5},{5... | collective-permute-start | bytes 3145736 | tf_op jit(solution)/shard_map/ppermute | solution.py:698
  128.1 14.3 %collective-permute-start.40 = (bf16[1024,256]{1,0:T(8,128)(2,1)S(1)}, bf16[1024,256]{1,0:T(8,128)(2,1)S(1)}, u32[]{:S(2)}, u32[]{:S(2)}) collective-permute-start(bf16[1024,256]{1,0:T(8,128)(2,1)S(1)} %get-tuple-element.103), channel_id=1, source_target_pairs={{0,8},{4,12},{8,0},{12,4},{16,24},{20,28},{24,16},{28,20},{1,9},{5... | collective-permute-start | bytes 1572872 | tf_op jit(solution)/shard_map/ppermute | solution.py:698
  129.6 14.0 %collective-permute-start.36 = (bf16[1024,256]{1,0:T(8,128)(2,1)S(1)}, bf16[1024,256]{1,0:T(8,128)(2,1)S(1)}, u32[]{:S(2)}, u32[]{:S(2)}) collective-permute-start(bf16[1024,256]{1,0:T(8,128)(2,1)S(1)} %get-tuple-element.97), channel_id=1, source_target_pairs={{0,16},{4,20},{8,24},{12,28},{16,0},{20,4},{24,8},{28,12},{1,17},{... | collective-permute-start | bytes 1572872 | tf_op jit(solution)/shard_map/ppermute | solution.py:698
  143.6 2.7 %collective-permute-start.39 = (bf16[1024,256]{1,0:T(8,128)(2,1)S(1)}, bf16[1024,256]{1,0:T(8,128)(2,1)S(1)}, u32[]{:S(2)}, u32[]{:S(2)}) collective-permute-start(bf16[1024,256]{1,0:T(8,128)(2,1)S(1)} %collective-permute-done.36.refs_0_), channel_id=1, source_target_pairs={{0,4},{4,0},{8,12},{12,8},{16,20},{20,16},{24,28},{28,24},{1,5},{5... | collective-permute-start | bytes 1572872 | tf_op jit(solution)/shard_map/ppermute | solution.py:698
  143.6 2.7 %collective-permute-start.41 = (bf16[1024,256]{1,0:T(8,128)(2,1)S(1)}, bf16[1024,256]{1,0:T(8,128)(2,1)S(1)}, u32[]{:S(2)}, u32[]{:S(2)}) collective-permute-start(bf16[1024,256]{1,0:T(8,128)(2,1)S(1)} %collective-permute-done.40.refs_1_), channel_id=1, source_target_pairs={{0,4},{4,0},{8,12},{12,8},{16,20},{20,16},{24,28},{28,24},{1,5},{5... | collective-permute-start | bytes 1572872 | tf_op jit(solution)/shard_map/ppermute | solution.py:698

commit v7 on v5

--- a/solution.py
+++ b/solution.py
@@ -623,7 +623,7 @@
                     o[n, i, j] = mixed.astype(jnp.bfloat16)
                 return carry
 
-            lax.fori_loop(0, half // step, mix, 0, unroll=2)
+            lax.fori_loop(0, half // step, mix, 0, unroll=4)
             at = pl.ds(pl.multiple_of((idx_ref[0] ^ masks[n]) * rows + part * half, half), half)
             writes.append(pltpu.make_async_copy(o.at[n, :, pl.ds(part * half, half), :], out_hbm.at[:, at, :], out_sem.at[part, n]))
             writes[-1].start()

time: 149 us -> 149 us (level)
  no operation moved by 1% of the time
where the time goes in v7:
time: 149 us
  Pallas kernels  65.7 us (44%)
  waiting for transfers between devices  47.7 us (32%)
  starting transfers between devices  33.6 us (23%)
    ppermute x42, waiting for transfers between devices, swap(): return lax.ppermute(x, axis, [(i, i ^ bit) for i in range(size)])  47.7 us
    ppermute x42, starting transfers between devices, swap(): return lax.ppermute(x, axis, [(i, i ^ bit) for i in range(size)])  33.6 us
    pallas_call x1, Pallas kernels, norm_project(): pl.pallas_call(norm_project_kernel, in_specs=[SMEM, HBM, HBM, HBM], out_s...  17.8 us
    pallas_call x4, Pallas kernels, blend(): pl.pallas_call(functools.partial(blend_kernel, tuple(masks), first, offse...  12.3 us
    pallas_call x2, Pallas kernels, attend(): pl.pallas_call(functools.partial(attend_kernel, keep), in_specs=[SMEM] +...  8.92 us
    pallas_call x4, Pallas kernels, project(): pl.pallas_call(functools.partial(project_kernel, tuple(masks), first, las...  8.81 us
    pallas_call x4, Pallas kernels, gradient_blocks(): pl.pallas_call(functools.partial(kernel, tuple(masks)), in_specs=in_specs...  8.29 us
    pallas_call x1, Pallas kernels, attend_back(): pl.pallas_call(attend_back_kernel, in_specs=[SMEM] + [VMEM] * 6, out_spec...  4 us
  transfers between devices with their start and end apart: 42, of which 19 were waited for; matrix products, arithmetic and copies ran while one was open for 0% of the time, Pallas kernels for 38%

profile of v7, /device:TPU:0, one launch (start us, length us, event | category | flops | bytes accessed | tf_op | source)
XLA Modules:
  0.0 148.6 jit_solution(18443552960853846535)
XLA Ops:
  0.6 3.0 %collective-permute-start.1 = (bf16[2,1024,256]{2,1,0:T(8,128)(2,1)}, bf16[2,1024,256]{2,1,0:T(8,128)(2,1)S(1)}, u32[]{:S(2)}, u32[]{:S(2)}) collective-permute-start(bf16[2,1024,256]{2,1,0:T(8,128)(2,1)} %refs_0_.3), channel_id=1, source_target_pairs={{0,16},{4,20},{8,24},{12,28},{16,0},{20,4},{24,8},{28,12},{1,17},{... | collective-permute-start | bytes 3145736 | tf_op jit(solution)/shard_map/ppermute | solution.py:690
  3.7 1.5 %collective-permute-start = (bf16[2,1024,256]{2,1,0:T(8,128)(2,1)}, bf16[2,1024,256]{2,1,0:T(8,128)(2,1)S(1)}, u32[]{:S(2)}, u32[]{:S(2)}) collective-permute-start(bf16[2,1024,256]{2,1,0:T(8,128)(2,1)} %refs_0_.3), channel_id=1, source_target_pairs={{0,8},{4,12},{8,0},{12,4},{16,24},{20,28},{24,16},{28,20},{1,9},{5... | collective-permute-start | bytes 3145736 | tf_op jit(solution)/shard_map/ppermute | solution.py:690
  5.2 17.8 %norm_project.1 = (bf16[768,8192]{1,0:T(8,128)(2,1)S(1)}, bf16[768,256]{1,0:T(8,128)(2,1)S(1)}, bf16[768,256]{1,0:T(8,128)(2,1)S(1)}) custom-call(s32[1]{0:T(128)} %bitcast.idx_ref, bf16[768,8192]{1,0:T(8,128)(2,1)} %hidden_hbm.1, bf16[2,8192,256]{2,1,0:T(8,128)(2,1)} %refs_10_.1, f32[2,384,128]{2,1,0:T(8,128)} %constant.8.clone.table_hbm.refs_3_.table_ref), custom_call_target="tpu_custom_call" | custom-call | flops 1 | bytes 1 | tf_op jit(solution)/shard_map/norm_project/pallas_call | solution.py:133
  23.1 4.8 %attend.2.refs_2_.rest_0_ = f32[8,128]{1,0:T(8,128)S(1)} custom-call(s32[2]{0:T(128)S(1)} %copy-done.5, bf16[768,1024]{1,0:T(8,128)(2,1)S(1)} %copy-done.4, bf16[768,256]{1,0:T(8,128)(2,1)S(1)} %get-tuple-element.57.k_ref, bf16[768,256]{1,0:T(8,128)(2,1)S(1)} %get-tuple-element.58.v_ref, bf16[768,1024]{1,0:T(8,128)(2,1)S(1)} %copy-done), custom_call_target="tpu_custom_call" | custom-call | flops 1 | bytes 1 | tf_op jit(solution)/shard_map/attend/pallas_call | solution.py:319
  27.8 0.7 collective-permute-done.refs_0_.refs_2_
  28.5 0.5 collective-permute-start.4
  29.1 1.6 %collective-permute-start.7 = (bf16[1024,256]{1,0:T(8,128)(2,1)S(1)}, bf16[1024,256]{1,0:T(8,128)(2,1)S(1)}, u32[]{:S(2)}, u32[]{:S(2)}) collective-permute-start(bf16[1024,256]{1,0:T(8,128)(2,1)S(1)} %get-tuple-element.63), channel_id=1, source_target_pairs={{0,8},{4,12},{8,0},{12,4},{16,24},{20,28},{24,16},{28,20},{1,9},{5... | collective-permute-start | bytes 1572872 | tf_op jit(solution)/shard_map/ppermute | solution.py:690
  30.7 0.5 collective-permute-start.2
  31.2 2.0 %project.4.refs_4_ = f32[2,768,256]{2,1,0:T(8,128)S(1)} custom-call(s32[1]{0:T(128)} %bitcast.idx_ref, bf16[768,8192]{1,0:T(8,128)(2,1)S(1)} %get-tuple-element.56.x_ref, bf16[2,1024,256]{2,1,0:T(8,128)(2,1)S(1)} %copy-done.2, bf16[2,1024,256]{2,1,0:T(8,128)(2,1)S(1)} %collective-permute-done.5.refs_1_), custom_call_target="tpu_custom_call" | custom-call | flops 1 | bytes 1 | tf_op jit(solution)/shard_map/project/pallas_call | solution.py:226
  33.3 4.1 %project.5.refs_2_ = f32[2,768,256]{2,1,0:T(8,128)S(1)} custom-call(s32[1]{0:T(128)} %bitcast.idx_ref, bf16[768,8192]{1,0:T(8,128)(2,1)S(1)} %get-tuple-element.56.x_ref, bf16[2,1024,256]{2,1,0:T(8,128)(2,1)S(1)} %collective-permute-done.refs_0_.refs_2_, bf16[2,1024,256]{2,1,0:T(8,128)(2,1)S(1)} %collective-permute-done.3.refs_1_.refs_3_, ...), custom_call_target="tpu_custom_call" | custom-call | flops 1 | bytes 1 | tf_op jit(solution)/shard_map/project/pallas_call | solution.py:226
  37.4 5.7 %collective-permute-done.7.refs_1_.refs_7_ = bf16[1024,256]{1,0:T(8,128)(2,1)S(1)} collective-permute-done((bf16[1024,256]{1,0:T(8,128)(2,1)S(1)}, bf16[1024,256]{1,0:T(8,128)(2,1)S(1)}, u32[]{:S(2)}, u32[]{:S(2)}) %collective-permute-start.7) | collective-permute-done | bytes 524320 | tf_op jit(solution)/shard_map/ppermute | solution.py:690
  43.0 1.2 collective-permute-done.2.refs_0_.refs_6_
  44.2 0.5 collective-permute-start.8
  44.7 1.1 project.6.refs_2_
  46.1 0.7 collective-permute-done.8.refs_1_.refs_9_
  46.9 1.6 %project.7 = (bf16[768,256]{1,0:T(8,128)(2,1)S(1)}, bf16[768,256]{1,0:T(8,128)(2,1)S(1)}) custom-call(s32[1]{0:T(128)} %bitcast.idx_ref, bf16[768,8192]{1,0:T(8,128)(2,1)S(1)} %get-tuple-element.56.x_ref, bf16[1024,256]{1,0:T(8,128)(2,1)S(1)} %collective-permute-done.6.refs_0_.refs_8_, bf16[1024,256]{1,0:T(8,128)(2,1)S(1)} %collective-permute-done.8.refs_1_.refs_9_, ...), custom_call_target="tpu_custom_call" | custom-call | flops 1 | bytes 1 | tf_op jit(solution)/shard_map/project/pallas_call | solution.py:226
  48.5 4.2 %attend.3 = (f32[8,128]{1,0:T(8,128)S(1)}, bf16[2,2,768,512]{3,2,1,0:T(8,128)(2,1)S(1)}, f32[2,2,3,512]{3,2,1,0:T(4,128)S(1)}) custom-call(s32[2]{0:T(128)S(1)} %copy-done.5, bf16[768,1024]{1,0:T(8,128)(2,1)S(1)} %copy-done.1, bf16[768,256]{1,0:T(8,128)(2,1)S(1)} %get-tuple-element.66.k_ref, bf16[768,256]{1,0:T(8,128)(2,1)S(1)} %get-tuple-element.65.v_ref, ...), custom_call_target="tpu_custom_call" | custom-call | flops 1 | bytes 1 | tf_op jit(solution)/shard_map/attend/pallas_call | solution.py:319
  52.7 3.7 %collective-permute-start.11 = (f32[8,128]{1,0:T(8,128)S(1)}, f32[8,128]{1,0:T(8,128)S(1)}, u32[]{:S(2)}, u32[]{:S(2)}) collective-permute-start(f32[8,128]{1,0:T(8,128)S(1)} %get-tuple-element.69), channel_id=1, source_target_pairs={{0,3},{1,2},{2,1},{3,0},{4,7},{5,6},{6,5},{7,4},{8,11},{9,10},{10,... | collective-permute-start | bytes 12296 | tf_op jit(solution)/shard_map/ppermute | solution.py:690
  56.3 0.8 collective-permute-start.9
  57.1 4.0 %attend_back.1.cot_ref = bf16[2,256,768]{2,1,0:T(8,128)(2,1)S(1)} custom-call(s32[2]{0:T(128)S(1)} %copy-done.5, bf16[768,1024]{1,0:T(8,128)(2,1)S(1)} %copy-done.1, bf16[768,256]{1,0:T(8,128)(2,1)S(1)} %get-tuple-element.65.v_ref, bf16[768,1024]{1,0:T(8,128)(2,1)S(1)} %copy-done, bf16[2,2,768,512]{3,2,1,0:T(8,128)(2,1)S(1)} %get-tuple-element.67.prob_ref, ...), custom_call_target="tpu_custom_call" | custom-call | flops 1 | bytes 1 | tf_op jit(solution)/shard_map/attend_back/pallas_call | solution.py:373
  61.2 1.0 gradient_block.2
  62.3 0.5 collective-permute-start.12
  62.8 2.7 %gradient_block.3 = (bf16[2,256,1024]{2,1,0:T(8,128)(2,1)S(1)}, bf16[2,256,1024]{2,1,0:T(8,128)(2,1)S(1)}, bf16[2,256,1024]{2,1,0:T(8,128)(2,1)S(1)}) custom-call(s32[1]{0:T(128)} %bitcast.idx_ref, bf16[768,8192]{1,0:T(8,128)(2,1)S(1)} %get-tuple-element.56.x_ref, bf16[2,256,768]{2,1,0:T(8,128)(2,1)S(1)} %attend_back.1.cot_ref, ...), custom_call_target="tpu_custom_call" | custom-call | flops 1 | bytes 1 | tf_op jit(solution)/shard_map/gradient_block/pallas_call | solution.py:441
  65.6 0.4 collective-permute-start.14
  66.1 1.1 merged_block.3
  67.2 0.6 collective-permute-start.21
  68.2 1.5 collective-permute-done.14.refs_1_
  69.7 1.5 %collective-permute-done.15.refs_2_ = bf16[2,256,1024]{2,1,0:T(8,128)(2,1)S(1)} collective-permute-done((bf16[2,256,1024]{2,1,0:T(8,128)(2,1)S(1)}, bf16[2,256,1024]{2,1,0:T(8,128)(2,1)S(1)}, u32[]{:S(2)}, u32[]{:S(2)}) %collective-permute-start.15) | collective-permute-done | bytes 1048608 | tf_op jit(solution)/shard_map/ppermute | solution.py:690
  71.2 3.5 %merged_block.2 = (bf16[256,1024]{1,0:T(8,128)(2,1)S(1)}, bf16[256,1024]{1,0:T(8,128)(2,1)S(1)}, bf16[256,1024]{1,0:T(8,128)(2,1)S(1)}, bf16[256,1024]{1,0:T(8,1...) custom-call(s32[1]{0:T(128)} %bitcast.idx_ref, bf16[768,8192]{1,0:T(8,128)(2,1)S(1)} %get-tuple-element.56.x_ref, ...), custom_call_target="tpu_custom_call" | custom-call | flops 1 | bytes 1 | tf_op jit(solution)/shard_map/merged_block/pallas_call | solution.py:441
  74.7 0.6 collective-permute-start.16
  75.3 0.4 collective-permute-start.20
  75.7 6.3 %collective-permute-done.21 = bf16[256,1024]{1,0:T(8,128)(2,1)S(1)} collective-permute-done((bf16[256,1024]{1,0:T(8,128)(2,1)S(1)}, bf16[256,1024]{1,0:T(8,128)(2,1)S(1)}, u32[]{:S(2)}, u32[]{:S(2)}) %collective-permute-start.21) | collective-permute-done | bytes 524320 | tf_op jit(solution)/shard_map/ppermute | solution.py:690
  82.2 0.6 collective-permute-start.22
  82.9 1.4 collective-permute-start.19
  84.3 0.7 collective-permute-start.24
  85.0 8.8 %collective-permute-done.16.refs_1_ = bf16[256,1024]{1,0:T(8,128)(2,1)S(1)} collective-permute-done((bf16[256,1024]{1,0:T(8,128)(2,1)S(1)}, bf16[256,1024]{1,0:T(8,128)(2,1)S(1)}, u32[]{:S(2)}, u32[]{:S(2)}) %collective-permute-start.16) | collective-permute-done | bytes 524320 | tf_op jit(solution)/shard_map/ppermute | solution.py:690
  93.8 1.5 %collective-permute-start.23 = (bf16[256,512]{1,0:T(8,128)(2,1)S(1)}, bf16[256,512]{1,0:T(8,128)(2,1)S(1)}, u32[]{:S(2)}, u32[]{:S(2)}) collective-permute-start(bf16[256,512]{1,0:T(8,128)(2,1)S(1)} %get-tuple-element.111), channel_id=1, source_target_pairs={{0,8},{4,12},{8,0},{12,4},{16,24},{20,28},{24,16},{28,20},{1,9},{5... | collective-permute-start | bytes 786440 | tf_op jit(solution)/shard_map/ppermute | solution.py:690
  95.3 4.1 %collective-permute-done.22.refs_5_ = bf16[256,512]{1,0:T(8,128)(2,1)S(1)} collective-permute-done((bf16[256,512]{1,0:T(8,128)(2,1)S(1)}, bf16[256,512]{1,0:T(8,128)(2,1)S(1)}, u32[]{:S(2)}, u32[]{:S(2)}) %collective-permute-start.22) | collective-permute-done | bytes 262176 | tf_op jit(solution)/shard_map/ppermute | solution.py:690
  99.8 0.4 collective-permute-start.29
  100.2 1.6 %collective-permute-start.28 = (bf16[2,512,256]{2,1,0:T(8,128)(2,1)S(1)}, bf16[2,512,256]{2,1,0:T(8,128)(2,1)S(1)}, u32[]{:S(2)}, u32[]{:S(2)}) collective-permute-start(bf16[2,512,256]{2,1,0:T(8,128)(2,1)S(1)} %get-tuple-element.90.refs_4_.refs_0_), channel_id=1, source_target_pairs={{0,8},{4,12},{8,0},{12,4},{16,24},{20,28},{24,16},{28,20},{1,9},{5... | collective-permute-start | bytes 1572872 | tf_op jit(solution)/shard_map/ppermute | solution.py:690
  101.9 3.2 %collective-permute-done.24.refs_5_ = bf16[256,512]{1,0:T(8,128)(2,1)S(1)} collective-permute-done((bf16[256,512]{1,0:T(8,128)(2,1)S(1)}, bf16[256,512]{1,0:T(8,128)(2,1)S(1)}, u32[]{:S(2)}, u32[]{:S(2)}) %collective-permute-start.24) | collective-permute-done | bytes 262176 | tf_op jit(solution)/shard_map/ppermute | solution.py:690
  105.4 0.4 collective-permute-start.34
  105.9 1.6 %collective-permute-start.33 = (bf16[2,512,256]{2,1,0:T(8,128)(2,1)S(1)}, bf16[2,512,256]{2,1,0:T(8,128)(2,1)S(1)}, u32[]{:S(2)}, u32[]{:S(2)}) collective-permute-start(bf16[2,512,256]{2,1,0:T(8,128)(2,1)S(1)} %get-tuple-element.92.refs_5_.refs_1_), channel_id=1, source_target_pairs={{0,8},{4,12},{8,0},{12,4},{16,24},{20,28},{24,16},{28,20},{1,9},{5... | collective-permute-start | bytes 1572872 | tf_op jit(solution)/shard_map/ppermute | solution.py:690
  107.5 1.2 collective-permute-start.25
  108.7 2.4 %collective-permute-done.25 = f32[8,128]{1,0:T(8,128)S(1)} collective-permute-done((f32[8,128]{1,0:T(8,128)S(1)}, f32[8,128]{1,0:T(8,128)S(1)}, u32[]{:S(2)}, u32[]{:S(2)}) %collective-permute-start.25) | collective-permute-done | bytes 4128 | tf_op jit(solution)/shard_map/ppermute | solution.py:690
  111.1 2.1 %collective-permute-start.26 = (f32[8,128]{1,0:T(8,128)S(1)}, f32[8,128]{1,0:T(8,128)S(1)}, u32[]{:S(2)}, u32[]{:S(2)}) collective-permute-start(f32[8,128]{1,0:T(8,128)S(1)} %add.50), channel_id=1, source_target_pairs={{0,2},{1,3},{2,0},{3,1},{4,6},{5,7},{6,4},{7,5},{8,10},{9,11},{10,... | collective-permute-start | bytes 12296 | tf_op jit(solution)/shard_map/ppermute | solution.py:690
  113.2 2.4 %collective-permute-done.26 = f32[8,128]{1,0:T(8,128)S(1)} collective-permute-done((f32[8,128]{1,0:T(8,128)S(1)}, f32[8,128]{1,0:T(8,128)S(1)}, u32[]{:S(2)}, u32[]{:S(2)}) %collective-permute-start.26) | collective-permute-done | bytes 4128 | tf_op jit(solution)/shard_map/ppermute | solution.py:690
  115.6 1.2 collective-permute-done.27
  116.8 0.6 gate.1
  117.4 1.6 %collective-permute-start.32 = (f32[8,128]{1,0:T(8,128)S(1)}, f32[8,128]{1,0:T(8,128)S(1)}, u32[]{:S(2)}, u32[]{:S(2)}) collective-permute-start(f32[8,128]{1,0:T(8,128)S(1)} %get-tuple-element.91.refs_11_), channel_id=1, source_target_pairs={{0,24},{4,28},{8,16},{12,20},{16,8},{20,12},{24,0},{28,4},{1,25},{... | collective-permute-start | bytes 12296 | tf_op jit(solution)/shard_map/ppermute | solution.py:690
  118.9 1.0 collective-permute-start.31
  119.9 1.0 collective-permute-start.30
  120.9 3.8 %fetch.1 = (bf16[8,2,1024,256]{3,2,1,0:T(8,128)(2,1)S(1)}, bf16[8,2,1024,256]{3,2,1,0:T(8,128)(2,1)S(1)}) custom-call(s32[1]{0:T(128)} %bitcast.idx_ref, bf16[2,1024,256]{2,1,0:T(8,128)(2,1)S(1)} %copy-done.2, bf16[2,1024,256]{2,1,0:T(8,128)(2,1)S(1)} %collective-permute-done.5.refs_1_, bf16[2,1024,256]{2,1,0:T(8,128)(2,1)S(1)} %collective-permute-done.refs_0_.refs_2_, ...), custom_call_target="tpu_custom_call" | custom-call | flops 1 | bytes 1 | tf_op jit(solution)/shard_map/fetch/pallas_call | solution.py:575
  124.7 2.0 %collective-permute-done.32 = f32[8,128]{1,0:T(8,128)S(1)} collective-permute-done((f32[8,128]{1,0:T(8,128)S(1)}, f32[8,128]{1,0:T(8,128)S(1)}, u32[]{:S(2)}, u32[]{:S(2)}) %collective-permute-start.32) | collective-permute-done | bytes 4128 | tf_op jit(solution)/shard_map/ppermute | solution.py:690
  127.5 0.5 collective-permute-start.37
  128.0 1.5 %collective-permute-start.40 = (bf16[1024,256]{1,0:T(8,128)(2,1)S(1)}, bf16[1024,256]{1,0:T(8,128)(2,1)S(1)}, u32[]{:S(2)}, u32[]{:S(2)}) collective-permute-start(bf16[1024,256]{1,0:T(8,128)(2,1)S(1)} %get-tuple-element.103), channel_id=1, source_target_pairs={{0,8},{4,12},{8,0},{12,4},{16,24},{20,28},{24,16},{28,20},{1,9},{5... | collective-permute-start | bytes 1572872 | tf_op jit(solution)/shard_map/ppermute | solution.py:690
  129.5 0.5 collective-permute-start.36
  130.1 3.2 %blend.4 = (bf16[2,8192,256]{2,1,0:T(8,128)(2,1)}, f32[8,128]{1,0:T(8,128)}, bf16[2,1024,256]{2,1,0:T(8,128)(2,1)}) custom-call(s32[1]{0:T(128)} %bitcast.idx_ref, f32[8,128]{1,0:T(8,128)S(1)} %add_add_fusion.refs_10_.square_ref, bf16[2,512,256]{2,1,0:T(8,128)(2,1)S(1)} %get-tuple-element.90.refs_4_.refs_0_, ...), custom_call_target="tpu_custom_call" | custom-call | flops 1 | bytes 1 | tf_op jit(solution)/shard_map/blend/pallas_call | solution.py:657
  133.3 4.8 %blend.5 = (bf16[2,8192,256]{2,1,0:T(8,128)(2,1)}, f32[8,128]{1,0:T(8,128)}) custom-call(s32[1]{0:T(128)} %bitcast.idx_ref, f32[8,128]{1,0:T(8,128)S(1)} %add_add_fusion.refs_10_.square_ref, bf16[2,512,256]{2,1,0:T(8,128)(2,1)S(1)} %collective-permute-done.28.refs_0_.refs_6_, ...), custom_call_target="tpu_custom_call", output_to_operand_aliasing={{0}: (10, {})} | custom-call | flops 1 | bytes 1 | tf_op jit(solution)/shard_map/blend/pallas_call | solution.py:657
  138.1 4.2 %collective-permute-done.40.refs_1_ = bf16[1024,256]{1,0:T(8,128)(2,1)S(1)} collective-permute-done((bf16[1024,256]{1,0:T(8,128)(2,1)S(1)}, bf16[1024,256]{1,0:T(8,128)(2,1)S(1)}, u32[]{:S(2)}, u32[]{:S(2)}) %collective-permute-start.40) | collective-permute-done | bytes 524320 | tf_op jit(solution)/shard_map/ppermute | solution.py:690
  142.3 1.2 collective-permute-done.36.refs_0_
  143.5 0.5 collective-permute-start.41
  144.0 2.2 %blend.6 = (bf16[2,8192,256]{2,1,0:T(8,128)(2,1)}, f32[8,128]{1,0:T(8,128)}) custom-call(s32[1]{0:T(128)} %bitcast.idx_ref, f32[8,128]{1,0:T(8,128)S(1)} %add_add_fusion.refs_10_.square_ref, bf16[1024,256]{1,0:T(8,128)(2,1)S(1)} %collective-permute-done.36.refs_0_, ...), custom_call_target="tpu_custom_call", output_to_operand_aliasing={{0}: (6, {})} | custom-call | flops 1 | bytes 1 | tf_op jit(solution)/shard_map/blend/pallas_call | solution.py:657
  146.2 2.2 %blend.7 = (bf16[2,8192,256]{2,1,0:T(8,128)(2,1)}, f32[8,128]{1,0:T(8,128)}) custom-call(s32[1]{0:T(128)} %bitcast.idx_ref, f32[8,128]{1,0:T(8,128)S(1)} %add_add_fusion.refs_10_.square_ref, bf16[1024,256]{1,0:T(8,128)(2,1)S(1)} %collective-permute-done.39.refs_0_, ...), custom_call_target="tpu_custom_call", output_to_operand_aliasing={{0}: (6, {})} | custom-call | flops 1 | bytes 1 | tf_op jit(solution)/shard_map/blend/pallas_call | solution.py:657
  (63 shorter events, 3.1 us)
Async XLA Ops:
  0.6 27.2 %collective-permute-start.1 = (bf16[2,1024,256]{2,1,0:T(8,128)(2,1)}, bf16[2,1024,256]{2,1,0:T(8,128)(2,1)S(1)}, u32[]{:S(2)}, u32[]{:S(2)}) collective-permute-start(bf16[2,1024,256]{2,1,0:T(8,128)(2,1)} %refs_0_.3), channel_id=1, source_target_pairs={{0,16},{4,20},{8,24},{12,28},{16,0},{20,4},{24,8},{28,12},{1,17},{... | collective-permute-start | bytes 3145736 | tf_op jit(solution)/shard_map/ppermute | solution.py:690
  3.7 24.8 %collective-permute-start = (bf16[2,1024,256]{2,1,0:T(8,128)(2,1)}, bf16[2,1024,256]{2,1,0:T(8,128)(2,1)S(1)}, u32[]{:S(2)}, u32[]{:S(2)}) collective-permute-start(bf16[2,1024,256]{2,1,0:T(8,128)(2,1)} %refs_0_.3), channel_id=1, source_target_pairs={{0,8},{4,12},{8,0},{12,4},{16,24},{20,28},{24,16},{28,20},{1,9},{5... | collective-permute-start | bytes 3145736 | tf_op jit(solution)/shard_map/ppermute | solution.py:690
  5.2 26.0 %collective-permute-start.5 = (bf16[2,1024,256]{2,1,0:T(8,128)(2,1)}, bf16[2,1024,256]{2,1,0:T(8,128)(2,1)S(1)}, u32[]{:S(2)}, u32[]{:S(2)}) collective-permute-start(bf16[2,1024,256]{2,1,0:T(8,128)(2,1)} %refs_0_.3), channel_id=1, source_target_pairs={{0,4},{4,0},{8,12},{12,8},{16,20},{20,16},{24,28},{28,24},{1,5},{5... | collective-permute-start | bytes 3145736 | tf_op jit(solution)/shard_map/ppermute | solution.py:690
  5.2 17.9 %copy-start = (bf16[768,1024]{1,0:T(8,128)(2,1)S(1)}, bf16[768,1024]{1,0:T(8,128)(2,1)}, u32[]{:S(2)}) copy-start(bf16[768,1024]{1,0:T(8,128)(2,1)} %ro_ref.5) | copy-start | bytes 4718596
  5.2 17.9 %copy-start.4 = (bf16[768,1024]{1,0:T(8,128)(2,1)S(1)}, bf16[768,1024]{1,0:T(8,128)(2,1)}, u32[]{:S(2)}) copy-start(bf16[768,1024]{1,0:T(8,128)(2,1)} %q_ref.3) | copy-start | bytes 4718596
  5.2 17.9 %copy-start.5 = (s32[2]{0:T(128)S(1)}, s32[2]{0:T(128)}, u32[]{:S(2)}) copy-start(s32[2]{0:T(128)} %len_ref.5) | copy-start | bytes 28
  5.2 26.0 %copy-start.2 = (bf16[2,1024,256]{2,1,0:T(8,128)(2,1)S(1)}, bf16[2,1024,256]{2,1,0:T(8,128)(2,1)}, u32[]{:S(2)}) copy-start(bf16[2,1024,256]{2,1,0:T(8,128)(2,1)} %refs_0_.3) | copy-start | bytes 3145732
  28.5 4.8 %collective-permute-start.3 = (bf16[2,1024,256]{2,1,0:T(8,128)(2,1)S(1)}, bf16[2,1024,256]{2,1,0:T(8,128)(2,1)S(1)}, u32[]{:S(2)}, u32[]{:S(2)}) collective-permute-start(bf16[2,1024,256]{2,1,0:T(8,128)(2,1)S(1)} %collective-permute-done.refs_0_.refs_2_), channel_id=1, source_target_pairs={{0,4},{4,0},{8,12},{12,8},{16,20},{20,16},{24,28},{28,24},{1,5},{5... | collective-permute-start | bytes 3145736 | tf_op jit(solution)/shard_map/ppermute | solution.py:690
  28.5 4.8 %collective-permute-start.4 = (bf16[2,1024,256]{2,1,0:T(8,128)(2,1)S(1)}, bf16[2,1024,256]{2,1,0:T(8,128)(2,1)S(1)}, u32[]{:S(2)}, u32[]{:S(2)}) collective-permute-start(bf16[2,1024,256]{2,1,0:T(8,128)(2,1)S(1)} %collective-permute-done.1.refs_1_.refs_2_.refs_4_), channel_id=1, source_target_pairs={{0,4},{4,0},{8,12},{12,8},{16,20},{20,16},{24,28},{28,24},{1,5},{5... | collective-permute-start | bytes 3145736 | tf_op jit(solution)/shard_map/ppermute | solution.py:690
  29.1 13.9 %collective-permute-start.7 = (bf16[1024,256]{1,0:T(8,128)(2,1)S(1)}, bf16[1024,256]{1,0:T(8,128)(2,1)S(1)}, u32[]{:S(2)}, u32[]{:S(2)}) collective-permute-start(bf16[1024,256]{1,0:T(8,128)(2,1)S(1)} %get-tuple-element.63), channel_id=1, source_target_pairs={{0,8},{4,12},{8,0},{12,4},{16,24},{20,28},{24,16},{28,20},{1,9},{5... | collective-permute-start | bytes 1572872 | tf_op jit(solution)/shard_map/ppermute | solution.py:690
  30.7 13.6 %collective-permute-start.2 = (bf16[1024,256]{1,0:T(8,128)(2,1)S(1)}, bf16[1024,256]{1,0:T(8,128)(2,1)S(1)}, u32[]{:S(2)}, u32[]{:S(2)}) collective-permute-start(bf16[1024,256]{1,0:T(8,128)(2,1)S(1)} %get-tuple-element.59), channel_id=1, source_target_pairs={{0,16},{4,20},{8,24},{12,28},{16,0},{20,4},{24,8},{28,12},{1,17},{... | collective-permute-start | bytes 1572872 | tf_op jit(solution)/shard_map/ppermute | solution.py:690
  44.2 1.9 %collective-permute-start.6 = (bf16[1024,256]{1,0:T(8,128)(2,1)S(1)}, bf16[1024,256]{1,0:T(8,128)(2,1)S(1)}, u32[]{:S(2)}, u32[]{:S(2)}) collective-permute-start(bf16[1024,256]{1,0:T(8,128)(2,1)S(1)} %collective-permute-done.2.refs_0_.refs_6_), channel_id=1, source_target_pairs={{0,4},{4,0},{8,12},{12,8},{16,20},{20,16},{24,28},{28,24},{1,5},{5... | collective-permute-start | bytes 1572872 | tf_op jit(solution)/shard_map/ppermute | solution.py:690
  44.2 2.7 %collective-permute-start.8 = (bf16[1024,256]{1,0:T(8,128)(2,1)S(1)}, bf16[1024,256]{1,0:T(8,128)(2,1)S(1)}, u32[]{:S(2)}, u32[]{:S(2)}) collective-permute-start(bf16[1024,256]{1,0:T(8,128)(2,1)S(1)} %collective-permute-done.7.refs_1_.refs_7_), channel_id=1, source_target_pairs={{0,4},{4,0},{8,12},{12,8},{16,20},{20,16},{24,28},{28,24},{1,5},{5... | collective-permute-start | bytes 1572872 | tf_op jit(solution)/shard_map/ppermute | solution.py:690
  45.8 2.6 %copy-start.1 = (bf16[768,1024]{1,0:T(8,128)(2,1)S(1)}, bf16[768,1024]{1,0:T(8,128)(2,1)}, u32[]{:S(2)}) copy-start(bf16[768,1024]{1,0:T(8,128)(2,1)} %q_ref.5) | copy-start | bytes 4718596
  45.9 11.3 %copy-start.3 = (f32[2,384,128]{2,1,0:T(8,128)S(1)}, f32[2,384,128]{2,1,0:T(8,128)}, u32[]{:S(2)}) copy-start(f32[2,384,128]{2,1,0:T(8,128)} %constant.8.clone.table_hbm.refs_3_.table_ref) | copy-start | bytes 1179652
  52.7 8.5 %collective-permute-start.11 = (f32[8,128]{1,0:T(8,128)S(1)}, f32[8,128]{1,0:T(8,128)S(1)}, u32[]{:S(2)}, u32[]{:S(2)}) collective-permute-start(f32[8,128]{1,0:T(8,128)S(1)} %get-tuple-element.69), channel_id=1, source_target_pairs={{0,3},{1,2},{2,1},{3,0},{4,7},{5,6},{6,5},{7,4},{8,11},{9,10},{10,... | collective-permute-start | bytes 12296 | tf_op jit(solution)/shard_map/ppermute | solution.py:690
  56.3 4.8 %collective-permute-start.10 = (f32[8,128]{1,0:T(8,128)S(1)}, f32[8,128]{1,0:T(8,128)S(1)}, u32[]{:S(2)}, u32[]{:S(2)}) collective-permute-start(f32[8,128]{1,0:T(8,128)S(1)} %get-tuple-element.69), channel_id=1, source_target_pairs={{0,2},{1,3},{2,0},{3,1},{4,6},{5,7},{6,4},{7,5},{8,10},{9,11},{10,... | collective-permute-start | bytes 12296 | tf_op jit(solution)/shard_map/ppermute | solution.py:690
  56.3 4.8 %collective-permute-start.9 = (f32[8,128]{1,0:T(8,128)S(1)}, f32[8,128]{1,0:T(8,128)S(1)}, u32[]{:S(2)}, u32[]{:S(2)}) collective-permute-start(f32[8,128]{1,0:T(8,128)S(1)} %get-tuple-element.69), channel_id=1, source_target_pairs={{0,1},{1,0},{2,3},{3,2},{4,5},{5,4},{6,7},{7,6},{8,9},{9,8},{10,11... | collective-permute-start | bytes 12296 | tf_op jit(solution)/shard_map/ppermute | solution.py:690
  62.2 3.9 %collective-permute-start.17 = (bf16[2,256,1024]{2,1,0:T(8,128)(2,1)S(1)}, bf16[2,256,1024]{2,1,0:T(8,128)(2,1)S(1)}, u32[]{:S(2)}, u32[]{:S(2)}) collective-permute-start(bf16[2,256,1024]{2,1,0:T(8,128)(2,1)S(1)} %gradient_block.2), channel_id=1, source_target_pairs={{0,4},{4,0},{8,12},{12,8},{16,20},{20,16},{24,28},{28,24},{1,5},{5... | collective-permute-start | bytes 3145736 | tf_op jit(solution)/shard_map/ppermute | solution.py:690
  62.3 3.2 %collective-permute-start.12 = (f32[8,128]{1,0:T(8,128)S(1)}, f32[8,128]{1,0:T(8,128)S(1)}, u32[]{:S(2)}, u32[]{:S(2)}) collective-permute-start(f32[8,128]{1,0:T(8,128)S(1)} %add_add_fusion.1.outs_0_.mine_ref.margin_ref), channel_id=1, source_target_pairs={{0,4},{4,0},{8,12},{12,8},{16,20},{20,16},{24,28},{28,24},{1,5},{5... | collective-permute-start | bytes 12296 | tf_op jit(solution)/shard_map/ppermute | solution.py:690
  65.5 2.8 %collective-permute-start.13 = (bf16[2,256,1024]{2,1,0:T(8,128)(2,1)S(1)}, bf16[2,256,1024]{2,1,0:T(8,128)(2,1)S(1)}, u32[]{:S(2)}, u32[]{:S(2)}) collective-permute-start(bf16[2,256,1024]{2,1,0:T(8,128)(2,1)S(1)} %get-tuple-element.77), channel_id=1, source_target_pairs={{0,4},{4,0},{8,12},{12,8},{16,20},{20,16},{24,28},{28,24},{1,5},{5... | collective-permute-start | bytes 3145736 | tf_op jit(solution)/shard_map/ppermute | solution.py:690
  65.6 4.1 %collective-permute-start.14 = (bf16[2,256,1024]{2,1,0:T(8,128)(2,1)S(1)}, bf16[2,256,1024]{2,1,0:T(8,128)(2,1)S(1)}, u32[]{:S(2)}, u32[]{:S(2)}) collective-permute-start(bf16[2,256,1024]{2,1,0:T(8,128)(2,1)S(1)} %get-tuple-element.78), channel_id=1, source_target_pairs={{0,4},{4,0},{8,12},{12,8},{16,20},{20,16},{24,28},{28,24},{1,5},{5... | collective-permute-start | bytes 3145736 | tf_op jit(solution)/shard_map/ppermute | solution.py:690
  66.0 5.1 %collective-permute-start.15 = (bf16[2,256,1024]{2,1,0:T(8,128)(2,1)S(1)}, bf16[2,256,1024]{2,1,0:T(8,128)(2,1)S(1)}, u32[]{:S(2)}, u32[]{:S(2)}) collective-permute-start(bf16[2,256,1024]{2,1,0:T(8,128)(2,1)S(1)} %get-tuple-element.79), channel_id=1, source_target_pairs={{0,4},{4,0},{8,12},{12,8},{16,20},{20,16},{24,28},{28,24},{1,5},{5... | collective-permute-start | bytes 3145736 | tf_op jit(solution)/shard_map/ppermute | solution.py:690
  67.2 14.8 %collective-permute-start.21 = (bf16[256,1024]{1,0:T(8,128)(2,1)S(1)}, bf16[256,1024]{1,0:T(8,128)(2,1)S(1)}, u32[]{:S(2)}, u32[]{:S(2)}) collective-permute-start(bf16[256,1024]{1,0:T(8,128)(2,1)S(1)} %get-tuple-element.87), channel_id=1, source_target_pairs={{0,8},{4,12},{8,0},{12,4},{16,24},{20,28},{24,16},{28,20},{1,9},{5... | collective-permute-start | bytes 1572872 | tf_op jit(solution)/shard_map/ppermute | solution.py:690
  67.8 14.9 %collective-permute-start.18 = (bf16[256,1024]{1,0:T(8,128)(2,1)S(1)}, bf16[256,1024]{1,0:T(8,128)(2,1)S(1)}, u32[]{:S(2)}, u32[]{:S(2)}) collective-permute-start(bf16[256,1024]{1,0:T(8,128)(2,1)S(1)} %get-tuple-element.83), channel_id=1, source_target_pairs={{0,16},{4,20},{8,24},{12,28},{16,0},{20,4},{24,8},{28,12},{1,17},{... | collective-permute-start | bytes 1572872 | tf_op jit(solution)/shard_map/ppermute | solution.py:690
  74.7 19.1 %collective-permute-start.16 = (bf16[256,1024]{1,0:T(8,128)(2,1)S(1)}, bf16[256,1024]{1,0:T(8,128)(2,1)S(1)}, u32[]{:S(2)}, u32[]{:S(2)}) collective-permute-start(bf16[256,1024]{1,0:T(8,128)(2,1)S(1)} %get-tuple-element.81), channel_id=1, source_target_pairs={{0,16},{4,20},{8,24},{12,28},{16,0},{20,4},{24,8},{28,12},{1,17},{... | collective-permute-start | bytes 1572872 | tf_op jit(solution)/shard_map/ppermute | solution.py:690
  75.3 20.0 %collective-permute-start.20 = (bf16[256,1024]{1,0:T(8,128)(2,1)S(1)}, bf16[256,1024]{1,0:T(8,128)(2,1)S(1)}, u32[]{:S(2)}, u32[]{:S(2)}) collective-permute-start(bf16[256,1024]{1,0:T(8,128)(2,1)S(1)} %get-tuple-element.85), channel_id=1, source_target_pairs={{0,8},{4,12},{8,0},{12,4},{16,24},{20,28},{24,16},{28,20},{1,9},{5... | collective-permute-start | bytes 1572872 | tf_op jit(solution)/shard_map/ppermute | solution.py:690
  82.2 17.3 %collective-permute-start.22 = (bf16[256,512]{1,0:T(8,128)(2,1)S(1)}, bf16[256,512]{1,0:T(8,128)(2,1)S(1)}, u32[]{:S(2)}, u32[]{:S(2)}) collective-permute-start(bf16[256,512]{1,0:T(8,128)(2,1)S(1)} %get-tuple-element.110), channel_id=1, source_target_pairs={{0,16},{4,20},{8,24},{12,28},{16,0},{20,4},{24,8},{28,12},{1,17},{... | collective-permute-start | bytes 786440 | tf_op jit(solution)/shard_map/ppermute | solution.py:690
  82.9 16.6 %collective-permute-start.19 = (bf16[256,512]{1,0:T(8,128)(2,1)S(1)}, bf16[256,512]{1,0:T(8,128)(2,1)S(1)}, u32[]{:S(2)}, u32[]{:S(2)}) collective-permute-start(bf16[256,512]{1,0:T(8,128)(2,1)S(1)} %get-tuple-element.112), channel_id=1, source_target_pairs={{0,8},{4,12},{8,0},{12,4},{16,24},{20,28},{24,16},{28,20},{1,9},{5... | collective-permute-start | bytes 786440 | tf_op jit(solution)/shard_map/ppermute | solution.py:690
  84.3 20.8 %collective-permute-start.24 = (bf16[256,512]{1,0:T(8,128)(2,1)S(1)}, bf16[256,512]{1,0:T(8,128)(2,1)S(1)}, u32[]{:S(2)}, u32[]{:S(2)}) collective-permute-start(bf16[256,512]{1,0:T(8,128)(2,1)S(1)} %get-tuple-element.109), channel_id=1, source_target_pairs={{0,16},{4,20},{8,24},{12,28},{16,0},{20,4},{24,8},{28,12},{1,17},{... | collective-permute-start | bytes 786440 | tf_op jit(solution)/shard_map/ppermute | solution.py:690
  93.8 11.2 %collective-permute-start.23 = (bf16[256,512]{1,0:T(8,128)(2,1)S(1)}, bf16[256,512]{1,0:T(8,128)(2,1)S(1)}, u32[]{:S(2)}, u32[]{:S(2)}) collective-permute-start(bf16[256,512]{1,0:T(8,128)(2,1)S(1)} %get-tuple-element.111), channel_id=1, source_target_pairs={{0,8},{4,12},{8,0},{12,4},{16,24},{20,28},{24,16},{28,20},{1,9},{5... | collective-permute-start | bytes 786440 | tf_op jit(solution)/shard_map/ppermute | solution.py:690
  99.8 17.0 %collective-permute-start.29 = (bf16[2,512,256]{2,1,0:T(8,128)(2,1)S(1)}, bf16[2,512,256]{2,1,0:T(8,128)(2,1)S(1)}, u32[]{:S(2)}, u32[]{:S(2)}) collective-permute-start(bf16[2,512,256]{2,1,0:T(8,128)(2,1)S(1)} %get-tuple-element.90.refs_4_.refs_0_), channel_id=1, source_target_pairs={{0,16},{4,20},{8,24},{12,28},{16,0},{20,4},{24,8},{28,12},{1,17},{... | collective-permute-start | bytes 1572872 | tf_op jit(solution)/shard_map/ppermute | solution.py:690
  100.2 16.5 %collective-permute-start.28 = (bf16[2,512,256]{2,1,0:T(8,128)(2,1)S(1)}, bf16[2,512,256]{2,1,0:T(8,128)(2,1)S(1)}, u32[]{:S(2)}, u32[]{:S(2)}) collective-permute-start(bf16[2,512,256]{2,1,0:T(8,128)(2,1)S(1)} %get-tuple-element.90.refs_4_.refs_0_), channel_id=1, source_target_pairs={{0,8},{4,12},{8,0},{12,4},{16,24},{20,28},{24,16},{28,20},{1,9},{5... | collective-permute-start | bytes 1572872 | tf_op jit(solution)/shard_map/ppermute | solution.py:690
  105.4 21.5 %collective-permute-start.34 = (bf16[2,512,256]{2,1,0:T(8,128)(2,1)S(1)}, bf16[2,512,256]{2,1,0:T(8,128)(2,1)S(1)}, u32[]{:S(2)}, u32[]{:S(2)}) collective-permute-start(bf16[2,512,256]{2,1,0:T(8,128)(2,1)S(1)} %get-tuple-element.92.refs_5_.refs_1_), channel_id=1, source_target_pairs={{0,16},{4,20},{8,24},{12,28},{16,0},{20,4},{24,8},{28,12},{1,17},{... | collective-permute-start | bytes 1572872 | tf_op jit(solution)/shard_map/ppermute | solution.py:690
  105.9 21.1 %collective-permute-start.33 = (bf16[2,512,256]{2,1,0:T(8,128)(2,1)S(1)}, bf16[2,512,256]{2,1,0:T(8,128)(2,1)S(1)}, u32[]{:S(2)}, u32[]{:S(2)}) collective-permute-start(bf16[2,512,256]{2,1,0:T(8,128)(2,1)S(1)} %get-tuple-element.92.refs_5_.refs_1_), channel_id=1, source_target_pairs={{0,8},{4,12},{8,0},{12,4},{16,24},{20,28},{24,16},{28,20},{1,9},{5... | collective-permute-start | bytes 1572872 | tf_op jit(solution)/shard_map/ppermute | solution.py:690
  107.5 3.6 %collective-permute-start.25 = (f32[8,128]{1,0:T(8,128)S(1)}, f32[8,128]{1,0:T(8,128)S(1)}, u32[]{:S(2)}, u32[]{:S(2)}) collective-permute-start(f32[8,128]{1,0:T(8,128)S(1)} %add.49), channel_id=1, source_target_pairs={{0,1},{1,0},{2,3},{3,2},{4,5},{5,4},{6,7},{7,6},{8,9},{9,8},{10,11... | collective-permute-start | bytes 12296 | tf_op jit(solution)/shard_map/ppermute | solution.py:690
  111.1 4.5 %collective-permute-start.26 = (f32[8,128]{1,0:T(8,128)S(1)}, f32[8,128]{1,0:T(8,128)S(1)}, u32[]{:S(2)}, u32[]{:S(2)}) collective-permute-start(f32[8,128]{1,0:T(8,128)S(1)} %add.50), channel_id=1, source_target_pairs={{0,2},{1,3},{2,0},{3,1},{4,6},{5,7},{6,4},{7,5},{8,10},{9,11},{10,... | collective-permute-start | bytes 12296 | tf_op jit(solution)/shard_map/ppermute | solution.py:690
  115.6 1.2 collective-permute-start.27
  117.4 9.3 %collective-permute-start.32 = (f32[8,128]{1,0:T(8,128)S(1)}, f32[8,128]{1,0:T(8,128)S(1)}, u32[]{:S(2)}, u32[]{:S(2)}) collective-permute-start(f32[8,128]{1,0:T(8,128)S(1)} %get-tuple-element.91.refs_11_), channel_id=1, source_target_pairs={{0,24},{4,28},{8,16},{12,20},{16,8},{20,12},{24,0},{28,4},{1,25},{... | collective-permute-start | bytes 12296 | tf_op jit(solution)/shard_map/ppermute | solution.py:690
  118.9 8.0 %collective-permute-start.31 = (f32[8,128]{1,0:T(8,128)S(1)}, f32[8,128]{1,0:T(8,128)S(1)}, u32[]{:S(2)}, u32[]{:S(2)}) collective-permute-start(f32[8,128]{1,0:T(8,128)S(1)} %get-tuple-element.91.refs_11_), channel_id=1, source_target_pairs={{0,16},{4,20},{8,24},{12,28},{16,0},{20,4},{24,8},{28,12},{1,17},{... | collective-permute-start | bytes 12296 | tf_op jit(solution)/shard_map/ppermute | solution.py:690
  119.9 7.1 %collective-permute-start.30 = (f32[8,128]{1,0:T(8,128)S(1)}, f32[8,128]{1,0:T(8,128)S(1)}, u32[]{:S(2)}, u32[]{:S(2)}) collective-permute-start(f32[8,128]{1,0:T(8,128)S(1)} %get-tuple-element.91.refs_11_), channel_id=1, source_target_pairs={{0,8},{4,12},{8,0},{12,4},{16,24},{20,28},{24,16},{28,20},{1,9},{5... | collective-permute-start | bytes 12296 | tf_op jit(solution)/shard_map/ppermute | solution.py:690
  127.4 2.7 %collective-permute-start.35 = (bf16[2,1024,256]{2,1,0:T(8,128)(2,1)S(1)}, bf16[2,1024,256]{2,1,0:T(8,128)(2,1)S(1)}, u32[]{:S(2)}, u32[]{:S(2)}) collective-permute-start(bf16[2,1024,256]{2,1,0:T(8,128)(2,1)S(1)} %get-tuple-element.94), channel_id=1, source_target_pairs={{0,4},{4,0},{8,12},{12,8},{16,20},{20,16},{24,28},{28,24},{1,5},{5... | collective-permute-start | bytes 3145736 | tf_op jit(solution)/shard_map/ppermute | solution.py:690
  127.5 5.8 %collective-permute-start.37 = (bf16[2,1024,256]{2,1,0:T(8,128)(2,1)S(1)}, bf16[2,1024,256]{2,1,0:T(8,128)(2,1)S(1)}, u32[]{:S(2)}, u32[]{:S(2)}) collective-permute-start(bf16[2,1024,256]{2,1,0:T(8,128)(2,1)S(1)} %get-tuple-element.98), channel_id=1, source_target_pairs={{0,4},{4,0},{8,12},{12,8},{16,20},{20,16},{24,28},{28,24},{1,5},{5... | collective-permute-start | bytes 3145736 | tf_op jit(solution)/shard_map/ppermute | solution.py:690
  128.0 5.3 %collective-permute-start.38 = (bf16[2,1024,256]{2,1,0:T(8,128)(2,1)S(1)}, bf16[2,1024,256]{2,1,0:T(8,128)(2,1)S(1)}, u32[]{:S(2)}, u32[]{:S(2)}) collective-permute-start(bf16[2,1024,256]{2,1,0:T(8,128)(2,1)S(1)} %get-tuple-element.99), channel_id=1, source_target_pairs={{0,4},{4,0},{8,12},{12,8},{16,20},{20,16},{24,28},{28,24},{1,5},{5... | collective-permute-start | bytes 3145736 | tf_op jit(solution)/shard_map/ppermute | solution.py:690
  128.0 14.3 %collective-permute-start.40 = (bf16[1024,256]{1,0:T(8,128)(2,1)S(1)}, bf16[1024,256]{1,0:T(8,128)(2,1)S(1)}, u32[]{:S(2)}, u32[]{:S(2)}) collective-permute-start(bf16[1024,256]{1,0:T(8,128)(2,1)S(1)} %get-tuple-element.103), channel_id=1, source_target_pairs={{0,8},{4,12},{8,0},{12,4},{16,24},{20,28},{24,16},{28,20},{1,9},{5... | collective-permute-start | bytes 1572872 | tf_op jit(solution)/shard_map/ppermute | solution.py:690
  129.5 14.0 %collective-permute-start.36 = (bf16[1024,256]{1,0:T(8,128)(2,1)S(1)}, bf16[1024,256]{1,0:T(8,128)(2,1)S(1)}, u32[]{:S(2)}, u32[]{:S(2)}) collective-permute-start(bf16[1024,256]{1,0:T(8,128)(2,1)S(1)} %get-tuple-element.97), channel_id=1, source_target_pairs={{0,16},{4,20},{8,24},{12,28},{16,0},{20,4},{24,8},{28,12},{1,17},{... | collective-permute-start | bytes 1572872 | tf_op jit(solution)/shard_map/ppermute | solution.py:690
  143.5 2.7 %collective-permute-start.39 = (bf16[1024,256]{1,0:T(8,128)(2,1)S(1)}, bf16[1024,256]{1,0:T(8,128)(2,1)S(1)}, u32[]{:S(2)}, u32[]{:S(2)}) collective-permute-start(bf16[1024,256]{1,0:T(8,128)(2,1)S(1)} %collective-permute-done.36.refs_0_), channel_id=1, source_target_pairs={{0,4},{4,0},{8,12},{12,8},{16,20},{20,16},{24,28},{28,24},{1,5},{5... | collective-permute-start | bytes 1572872 | tf_op jit(solution)/shard_map/ppermute | solution.py:690
  143.5 2.7 %collective-permute-start.41 = (bf16[1024,256]{1,0:T(8,128)(2,1)S(1)}, bf16[1024,256]{1,0:T(8,128)(2,1)S(1)}, u32[]{:S(2)}, u32[]{:S(2)}) collective-permute-start(bf16[1024,256]{1,0:T(8,128)(2,1)S(1)} %collective-permute-done.40.refs_1_), channel_id=1, source_target_pairs={{0,4},{4,0},{8,12},{12,8},{16,20},{20,16},{24,28},{28,24},{1,5},{5... | collective-permute-start | bytes 1572872 | tf_op jit(solution)/shard_map/ppermute | solution.py:690
